TPU v7x, 32 devices: a whole 2x2x4 slice. The times are simulated.
32 devices in a mesh: dp: 4 (over y, x), blk: 8 (over z, core).
Axes of the slice: x: 2, y: 2, z: 4, core: 2. Of those that a mesh axis runs over, the one named last changes fastest.
Arguments:
- tokens: bfloat16 [15360, 768], P(('dp', 'blk')), may hold values from -6 to 6
- item_lengths: int32 [4, 4], P('dp'), may hold values from 0 to 1200, as said below
- dataset_ids: int32 [4, 4], P('dp'), may hold values from 0 to 9
- dataset_table: float32 [10, 768], replicated, may hold values from -3 to 3
- norm1_gain: float32 [768], replicated, may hold values from 0.5 to 1.5
- norm1_bias: float32 [768], replicated, may hold values from -1.5 to 1.5
- query_weight: bfloat16 [768, 768], replicated, may hold values from -0.21875 to 0.21875
- key_weight: bfloat16 [768, 768], replicated, may hold values from -0.21875 to 0.21875
- value_weight: bfloat16 [768, 768], replicated, may hold values from -0.21875 to 0.21875
- out_weight: bfloat16 [768, 768], replicated, may hold values from -0.875 to 0.875
- norm2_gain: float32 [768], replicated, may hold values from 0.5 to 1.5
- norm2_bias: float32 [768], replicated, may hold values from -1.5 to 1.5
- fc1_weight: bfloat16 [768, 3072], replicated, may hold values from -0.21875 to 0.21875
- fc2_weight: bfloat16 [3072, 768], replicated, may hold values from -0.109375 to 0.109375
- project_weight: bfloat16 [768, 256], replicated, may hold values from -0.21875 to 0.21875
- unit1_first: bfloat16 [2304, 256], replicated, may hold values from -0.125 to 0.125
- unit1_second: bfloat16 [2304, 256], replicated, may hold values from -0.125 to 0.125
- unit2_first: bfloat16 [2304, 256], replicated, may hold values from -0.125 to 0.125
- unit2_second: bfloat16 [2304, 256], replicated, may hold values from -0.125 to 0.125
- output_weight: bfloat16 [256, 256], replicated, may hold values from -0.375 to 0.375
- block_cotangent: bfloat16 [15360, 768], P(('dp', 'blk')), may hold values from -6 to 6
- merged_cotangent: bfloat16 [15360, 1024], P(('dp', 'blk')), may hold values from -6 to 6
Outputs:
- block_out: bfloat16 [15360, 768], P(('dp', 'blk'))
- merged: bfloat16 [15360, 1024], P(('dp', 'blk'))
- tokens_grad: float32 [15360, 768], P(('dp', 'blk'))
- table_grad: float32 [10, 768], P(None, 'blk')
- norm1_gain_grad: float32 [768], P('blk')
- norm1_bias_grad: float32 [768], P('blk')
- query_grad: float32 [768, 768], P('blk')
- key_grad: float32 [768, 768], P('blk')
- value_grad: float32 [768, 768], P('blk')
- out_proj_grad: float32 [768, 768], P('blk')
- norm2_gain_grad: float32 [768], P('blk')
- norm2_bias_grad: float32 [768], P('blk')
- fc1_grad: float32 [768, 3072], P('blk')
- fc2_grad: float32 [3072, 768], P('blk')
- project_grad: float32 [768, 256], P('blk')
- unit1_first_grad: float32 [2304, 256], P('blk')
- unit1_second_grad: float32 [2304, 256], P('blk')
- unit2_first_grad: float32 [2304, 256], P('blk')
- unit2_second_grad: float32 [2304, 256], P('blk')
- output_grad: float32 [256, 256], P('blk')
Inputs may be any that keep to these rules, and one draw needn't show every extreme that they name: `item_lengths`: row g lists group g's items in order. Entries are 0, 576 (an image of 24 x 24 patches) or 1200 (30 x 40 patches); the nonzero entries come first and the first entry is never 0; the heights (24 or 30 rows) of a row's items add up to at most 96.
All inputs are finite; a program needn't handle non-finite values.
Results may differ from a plain program's by a relative error of at most 0.023.
Values may be sent and summed in bfloat16 or wider, within the bound.
No kernel may reach another device: no remote copies, remote signals or barrier semaphores. Data moves between devices by JAX's collectives and lax.ppermute only.
A program may use at most 192 MiB of HBM per device.

v0:
```python
import math

import jax
import jax.numpy as jnp
from jax import lax
from jax.sharding import PartitionSpec as P

HEADS = 12
HEAD = 64
ROWW = 40
SLOTS = 12


NEG = -1e30
EPS = 1e-06
HIGH = lax.Precision.HIGHEST


def passed_along(value, axis, steps):
    count = lax.axis_size(axis)
    pairs = [(source, (source + steps) % count) for source in range(count)]
    return lax.ppermute(value, axis, pairs)


def gelu_tanh(values):
    return (
        0.5
        * values
        * (1.0 + jnp.tanh(0.7978845608028654 * (values + 0.044715 * values * values * values)))
    )


def gelu_back(values, gradient):
    return jax.vjp(gelu_tanh, values)[1](gradient)[0]


def layer_norm(hidden, norm_gain, norm_bias):
    centred = hidden - jnp.mean(hidden, axis=-1, keepdims=True)
    spread = jnp.mean(centred * centred, axis=-1, keepdims=True)
    return centred * lax.rsqrt(spread + EPS) * norm_gain + norm_bias


def geometry(lengths, row_ids, col_count):
    item_count = lengths.shape[0]
    item_heights = jnp.where(lengths == 1200, 30, jnp.where(lengths == 576, 24, 0)).astype(
        jnp.int32
    )
    item_widths = jnp.where(lengths == 1200, 40, 24).astype(jnp.int32)
    row_ends = jnp.cumsum(item_heights)
    row_begins = row_ends - item_heights
    number = jnp.sum((row_ends[None, :] <= row_ids[:, None]).astype(jnp.int32), axis=1)
    item_pick = jnp.arange(item_count, dtype=jnp.int32)[None, :] == number[:, None]
    row_start = jnp.sum(jnp.where(item_pick, row_begins[None, :], 0), axis=1)
    item_height = jnp.sum(jnp.where(item_pick, item_heights[None, :], 0), axis=1)
    item_width = jnp.sum(jnp.where(item_pick, item_widths[None, :], 0), axis=1)
    column = jnp.arange(col_count, dtype=jnp.int32)
    is_real = (number < item_count)[:, None] & (column[None, :] < item_width[:, None])
    item_ids = jnp.where(is_real, number[:, None], item_count)
    return (item_ids, item_pick, row_ids - row_start, item_height, item_width, is_real)


def tap_masks(local_row, item_height, item_width, is_real):
    column = jnp.arange(is_real.shape[1], dtype=jnp.int32)
    all_masks = []
    for row_step in (-1, 0, 1):
        rows_fine = (local_row + row_step >= 0) & (local_row + row_step < item_height)
        for col_step in (-1, 0, 1):
            cols_fine = (column + col_step >= 0)[None, :] & (
                column[None, :] + col_step < item_width[:, None]
            )
            all_masks.append(is_real & rows_fine[:, None] & cols_fine)
    return all_masks


def device_rows(lengths, anchor, cycle_size):
    row_ids = jnp.arange(SLOTS, dtype=jnp.int32) * cycle_size + anchor
    return geometry(lengths, row_ids, ROWW)


def key_item_ids(lengths, anchor, cycle_size):
    return device_rows(lengths, anchor, cycle_size)[0].reshape(-1)


def vertical(values, cycle_pos, cycle_size):
    from_prev = passed_along(values, "blk", 1)
    from_next = passed_along(values, "blk", -1)
    empty_row = jnp.zeros_like(values[:1])
    row_above = jnp.where(
        cycle_pos == 0, jnp.concatenate([empty_row, from_prev[:-1]], axis=0), from_prev
    )
    row_below = jnp.where(
        cycle_pos == cycle_size - 1, jnp.concatenate([from_next[1:], empty_row], axis=0), from_next
    )
    return (row_above, row_below)


def side_shift(values, col_step):
    if col_step == 0:
        return values
    empty_col = jnp.zeros_like(values[:, :1])
    if col_step < 0:
        return jnp.concatenate([empty_col, values[:, :-1]], axis=1)
    return jnp.concatenate([values[:, 1:], empty_col], axis=1)


def tap_matrix(values, all_masks, cycle_pos, cycle_size):
    row_above, row_below = vertical(values, cycle_pos, cycle_size)
    tap_parts = []
    for source_rows in (row_above, values, row_below):
        for col_step in (-1, 0, 1):
            tap_mask = all_masks[len(tap_parts)]
            tap_parts.append(
                jnp.where(
                    tap_mask[:, :, None],
                    side_shift(source_rows, col_step),
                    jnp.zeros((), values.dtype),
                )
            )
    joined = jnp.concatenate(tap_parts, axis=2)
    return joined.reshape(-1, joined.shape[2])


def flipped(kernel):
    channels = kernel.shape[1]
    return jnp.transpose(kernel.reshape(9, channels, channels)[::-1], (0, 2, 1)).reshape(
        9 * channels, channels
    )


def upsample_forward(values, all_masks, cycle_pos, cycle_size):
    row_above, row_below = vertical(values, cycle_pos, cycle_size)
    center = values.astype(jnp.float32)
    upper_value = jnp.where(all_masks[1][:, :, None], row_above, values).astype(jnp.float32)
    lower_value = jnp.where(all_masks[7][:, :, None], row_below, values).astype(jnp.float32)
    pieces = []
    for half_rows in (0.75 * center + 0.25 * upper_value, 0.75 * center + 0.25 * lower_value):
        left_value = jnp.where(all_masks[3][:, :, None], side_shift(half_rows, -1), half_rows)
        right_value = jnp.where(all_masks[5][:, :, None], side_shift(half_rows, 1), half_rows)
        pieces.append(0.75 * half_rows + 0.25 * left_value)
        pieces.append(0.75 * half_rows + 0.25 * right_value)
    joined = jnp.concatenate(pieces, axis=2)
    return joined.reshape(-1, joined.shape[2])


def upsample_back(gradient, all_masks, cycle_pos, cycle_size):
    row_above, row_below = vertical(gradient, cycle_pos, cycle_size)
    channels = gradient.shape[2] // 4
    up_fine = all_masks[1][:, :, None]
    down_fine = all_masks[7][:, :, None]

    def sub_pixel(source, upper_half, side):
        offset = (2 * upper_half + side) * channels
        return source[:, :, offset : offset + channels].astype(jnp.float32)

    halves = []
    for side in (0, 1):
        grad_top = sub_pixel(gradient, 0, side)
        grad_bottom = sub_pixel(gradient, 1, side)
        spread_back = jnp.where(down_fine, sub_pixel(row_below, 0, side), 0.0) + jnp.where(
            up_fine, 0.0, grad_top
        )
        spread_back = (
            spread_back
            + jnp.where(up_fine, sub_pixel(row_above, 1, side), 0.0)
            + jnp.where(down_fine, 0.0, grad_bottom)
        )
        halves.append(0.75 * (grad_top + grad_bottom) + 0.25 * spread_back)
    left_part, right_part = halves
    left_fine = all_masks[3][:, :, None]
    right_fine = all_masks[5][:, :, None]
    spread_side = jnp.where(right_fine, side_shift(left_part, 1), 0.0) + jnp.where(
        left_fine, 0.0, left_part
    )
    spread_side = (
        spread_side
        + jnp.where(left_fine, side_shift(right_part, -1), 0.0)
        + jnp.where(right_fine, 0.0, right_part)
    )
    result = 0.75 * (left_part + right_part) + 0.25 * spread_side
    return result.reshape(-1, channels)


def pair_grads(
    query_heads, query_items, grad_heads, log_totals, delta, key_heads, value_heads, key_items
):
    score_scale = 1.0 / math.sqrt(query_heads.shape[2])
    same_item = (query_items[:, None] == key_items[None, :])[None]
    scores = jnp.where(
        same_item,
        jnp.einsum("qhd,khd->hqk", query_heads, key_heads, preferred_element_type=jnp.float32)
        * score_scale,
        NEG,
    )
    weights_now = jnp.exp(scores - log_totals[:, :, None])
    slopes = jnp.einsum("qhd,khd->hqk", grad_heads, value_heads, preferred_element_type=jnp.float32)
    score_grads = (weights_now * (slopes - delta[:, :, None])).astype(jnp.bfloat16)
    query_part = score_scale * jnp.einsum(
        "hqk,khd->qhd", score_grads, key_heads, preferred_element_type=jnp.float32
    )
    key_part = score_scale * jnp.einsum(
        "hqk,qhd->khd", score_grads, query_heads, preferred_element_type=jnp.float32
    )
    value_part = jnp.einsum(
        "hqk,qhd->khd",
        weights_now.astype(jnp.bfloat16),
        grad_heads,
        preferred_element_type=jnp.float32,
    )
    return (query_part, key_part, value_part)


def attention_forward(
    query_heads, key_heads, value_heads, query_items, lengths, cycle_pos, cycle_size
):
    token_count = query_heads.shape[0]
    head_count = query_heads.shape[1]
    score_scale = 1.0 / math.sqrt(query_heads.shape[2])

    def absorb(state, keys_now, values_now, cycle_step):
        maxima, totals, accumulated = state
        items_now = key_item_ids(lengths, (cycle_pos - cycle_step) % cycle_size, cycle_size)
        same_item = (query_items[:, None] == items_now[None, :])[None]
        scores = jnp.where(
            same_item,
            jnp.einsum("qhd,khd->hqk", query_heads, keys_now, preferred_element_type=jnp.float32)
            * score_scale,
            NEG,
        )
        new_max = jnp.maximum(maxima, jnp.max(scores, axis=2))
        factor = jnp.exp(maxima - new_max)
        weights_now = jnp.exp(scores - new_max[:, :, None])
        totals = totals * factor + jnp.sum(weights_now, axis=2)
        accumulated = accumulated * factor[:, :, None] + jnp.einsum(
            "hqk,khd->hqd",
            weights_now.astype(jnp.bfloat16),
            values_now,
            preferred_element_type=jnp.float32,
        )
        return (new_max, totals, accumulated)

    def cycle_turn(cycle_step, carried):
        state, keys_now, values_now = carried
        state = absorb(state, keys_now, values_now, cycle_step)
        keys_now, values_now = passed_along((keys_now, values_now), "blk", 1)
        return (state, keys_now, values_now)

    start_state = (
        jnp.full((head_count, token_count), NEG, jnp.float32),
        jnp.zeros((head_count, token_count), jnp.float32),
        jnp.zeros((head_count, token_count, query_heads.shape[2]), jnp.float32),
    )
    state, keys_now, values_now = lax.fori_loop(
        0, cycle_size - 1, cycle_turn, (start_state, key_heads, value_heads)
    )
    maxima, totals, accumulated = absorb(state, keys_now, values_now, cycle_size - 1)
    outputs = jnp.transpose(accumulated / totals[:, :, None], (1, 0, 2))
    return (outputs, maxima + jnp.log(totals))


def shards(
    tokens,
    item_lengths,
    dataset_ids,
    dataset_table,
    norm1_gain,
    norm1_bias,
    query_weight,
    key_weight,
    value_weight,
    out_weight,
    norm2_gain,
    norm2_bias,
    fc1_weight,
    fc2_weight,
    project_weight,
    unit1_first,
    unit1_second,
    unit2_first,
    unit2_second,
    output_weight,
    block_cotangent,
    merged_cotangent,
):
    cycle_size = lax.axis_size("blk")
    cycle_pos = lax.axis_index("blk")
    lengths = item_lengths[0]
    item_ids, item_pick, local_row, item_height, item_width, is_real = device_rows(
        lengths, cycle_pos, cycle_size
    )
    all_masks = tap_masks(local_row, item_height, item_width, is_real)
    query_items = item_ids.reshape(-1)
    dataset_here = jnp.sum(jnp.where(item_pick, dataset_ids[0][None, :], 0), axis=1)
    table_rows = dataset_table.shape[0]
    onehot = (
        (
            is_real[:, :, None]
            & (
                dataset_here[:, None, None]
                == jnp.arange(table_rows, dtype=jnp.int32)[None, None, :]
            )
        )
        .astype(jnp.float32)
        .reshape(-1, table_rows)
    )
    token_count = tokens.shape[0]

    def as_cells(flattened):
        return flattened.reshape(SLOTS, ROWW, flattened.shape[-1])

    def stencil(values, kernel):
        taps_now = tap_matrix(as_cells(values), all_masks, cycle_pos, cycle_size)
        return (taps_now, jnp.dot(taps_now, kernel, preferred_element_type=jnp.float32))

    def stencil_back(gradient, kernel):
        taps_now = tap_matrix(as_cells(gradient), all_masks, cycle_pos, cycle_size)
        return jnp.dot(taps_now, flipped(kernel), preferred_element_type=jnp.float32)

    def head_view(flattened):
        return flattened.reshape(token_count, HEADS, HEAD)

    def kernel_grad(taps_now, gradient):
        return jnp.einsum("tk,tc->kc", taps_now, gradient, preferred_element_type=jnp.float32)

    stream_start = tokens.astype(jnp.float32) + jnp.dot(onehot, dataset_table, precision=HIGH)
    normed_one = layer_norm(stream_start, norm1_gain, norm1_bias).astype(jnp.bfloat16)
    query_heads = head_view(
        jnp.dot(normed_one, query_weight, preferred_element_type=jnp.float32).astype(jnp.bfloat16)
    )
    key_heads = head_view(
        jnp.dot(normed_one, key_weight, preferred_element_type=jnp.float32).astype(jnp.bfloat16)
    )
    value_heads = head_view(
        jnp.dot(normed_one, value_weight, preferred_element_type=jnp.float32).astype(jnp.bfloat16)
    )
    attn_f32, log_totals = attention_forward(
        query_heads, key_heads, value_heads, query_items, lengths, cycle_pos, cycle_size
    )
    attended = attn_f32.reshape(token_count, -1).astype(jnp.bfloat16)
    after_attn = stream_start + jnp.dot(attended, out_weight, preferred_element_type=jnp.float32)
    normed_two = layer_norm(after_attn, norm2_gain, norm2_bias).astype(jnp.bfloat16)
    pre_act = jnp.dot(normed_two, fc1_weight, preferred_element_type=jnp.float32)
    hidden = gelu_tanh(pre_act).astype(jnp.bfloat16)
    block_out = (
        after_attn + jnp.dot(hidden, fc2_weight, preferred_element_type=jnp.float32)
    ).astype(jnp.bfloat16)
    reassembled = jnp.dot(block_out, project_weight, preferred_element_type=jnp.float32)
    act_one = gelu_tanh(reassembled).astype(jnp.bfloat16)
    taps_one, conv_one = stencil(act_one, unit1_first)
    act_two = gelu_tanh(conv_one).astype(jnp.bfloat16)
    taps_two, conv_two = stencil(act_two, unit1_second)
    merged_one = reassembled + conv_two
    act_three = gelu_tanh(merged_one).astype(jnp.bfloat16)
    taps_three, conv_three = stencil(act_three, unit2_first)
    act_four = gelu_tanh(conv_three).astype(jnp.bfloat16)
    taps_four, conv_four = stencil(act_four, unit2_second)
    merged_two = merged_one + conv_four
    merged_low = merged_two.astype(jnp.bfloat16)
    mapped = jnp.dot(merged_low, output_weight, preferred_element_type=jnp.float32).astype(
        jnp.bfloat16
    )
    merged = upsample_forward(as_cells(mapped), all_masks, cycle_pos, cycle_size).astype(
        jnp.bfloat16
    )
    mapped_grad = upsample_back(
        as_cells(merged_cotangent), all_masks, cycle_pos, cycle_size
    ).astype(jnp.bfloat16)
    output_grad = jnp.einsum(
        "tc,td->cd", merged_low, mapped_grad, preferred_element_type=jnp.float32
    )
    merged_two_grad = jnp.einsum(
        "td,cd->tc", mapped_grad, output_weight, preferred_element_type=jnp.float32
    )
    conv_four_grad = merged_two_grad.astype(jnp.bfloat16)
    unit2_second_grad = kernel_grad(taps_four, conv_four_grad)
    act_four_grad = stencil_back(conv_four_grad, unit2_second)
    conv_three_grad = gelu_back(conv_three, act_four_grad).astype(jnp.bfloat16)
    unit2_first_grad = kernel_grad(taps_three, conv_three_grad)
    act_three_grad = stencil_back(conv_three_grad, unit2_first)
    merged_one_grad = merged_two_grad + gelu_back(merged_one, act_three_grad)
    conv_two_grad = merged_one_grad.astype(jnp.bfloat16)
    unit1_second_grad = kernel_grad(taps_two, conv_two_grad)
    act_two_grad = stencil_back(conv_two_grad, unit1_second)
    conv_one_grad = gelu_back(conv_one, act_two_grad).astype(jnp.bfloat16)
    unit1_first_grad = kernel_grad(taps_one, conv_one_grad)
    act_one_grad = stencil_back(conv_one_grad, unit1_first)
    reassembled_grad = (merged_one_grad + gelu_back(reassembled, act_one_grad)).astype(jnp.bfloat16)
    project_grad = jnp.einsum(
        "td,tc->dc", block_out, reassembled_grad, preferred_element_type=jnp.float32
    )
    block_grad = block_cotangent.astype(jnp.float32) + jnp.einsum(
        "tc,dc->td", reassembled_grad, project_weight, preferred_element_type=jnp.float32
    )
    mlp_grad = block_grad.astype(jnp.bfloat16)
    fc2_grad = jnp.einsum("tf,td->fd", hidden, mlp_grad, preferred_element_type=jnp.float32)
    hidden_grad = jnp.einsum("td,fd->tf", mlp_grad, fc2_weight, preferred_element_type=jnp.float32)
    pre_grad = gelu_back(pre_act, hidden_grad).astype(jnp.bfloat16)
    fc1_grad = jnp.einsum("td,tf->df", normed_two, pre_grad, preferred_element_type=jnp.float32)
    normed_two_grad = jnp.einsum(
        "tf,df->td", pre_grad, fc1_weight, preferred_element_type=jnp.float32
    )
    norm_two_pull = jax.vjp(layer_norm, after_attn, norm2_gain, norm2_bias)[1]
    attn_side, norm2_gain_grad, norm2_bias_grad = norm_two_pull(normed_two_grad)
    after_grad = block_grad + attn_side
    branch_grad = after_grad.astype(jnp.bfloat16)
    out_proj_grad = jnp.einsum(
        "td,te->de", attended, branch_grad, preferred_element_type=jnp.float32
    )
    attended_grad = jnp.einsum(
        "te,de->td", branch_grad, out_weight, preferred_element_type=jnp.float32
    ).astype(jnp.bfloat16)
    grad_heads = head_view(attended_grad)
    delta = jnp.einsum("qhd,qhd->hq", grad_heads.astype(jnp.float32), attn_f32)
    zero_heads = jnp.zeros(query_heads.shape, jnp.float32)

    def back_turn(cycle_step, carried):
        query_acc, keys_now, values_now, key_acc, value_acc = carried
        items_now = key_item_ids(lengths, (cycle_pos - cycle_step) % cycle_size, cycle_size)
        query_part, key_part, value_part = pair_grads(
            query_heads, query_items, grad_heads, log_totals, delta, keys_now, values_now, items_now
        )
        keys_now, values_now = passed_along((keys_now, values_now), "blk", 1)
        key_acc, value_acc = (
            passed_along((key_acc + key_part).astype(jnp.bfloat16), "blk", 1).astype(jnp.float32),
            passed_along((value_acc + value_part).astype(jnp.bfloat16), "blk", 1).astype(
                jnp.float32
            ),
        )
        return (query_acc + query_part, keys_now, values_now, key_acc, value_acc)

    query_acc, keys_now, values_now, key_acc, value_acc = lax.fori_loop(
        0, cycle_size - 1, back_turn, (zero_heads, key_heads, value_heads, zero_heads, zero_heads)
    )
    items_now = key_item_ids(lengths, (cycle_pos - cycle_size + 1) % cycle_size, cycle_size)
    query_part, key_part, value_part = pair_grads(
        query_heads, query_items, grad_heads, log_totals, delta, keys_now, values_now, items_now
    )
    query_grad_heads = query_acc + query_part
    key_grad_heads, value_grad_heads = (
        passed_along((key_acc + key_part).astype(jnp.bfloat16), "blk", 1).astype(jnp.float32),
        passed_along((value_acc + value_part).astype(jnp.bfloat16), "blk", 1).astype(jnp.float32),
    )
    query_low = query_grad_heads.reshape(token_count, -1).astype(jnp.bfloat16)
    key_low = key_grad_heads.reshape(token_count, -1).astype(jnp.bfloat16)
    value_low = value_grad_heads.reshape(token_count, -1).astype(jnp.bfloat16)
    query_grad = jnp.einsum("td,te->de", normed_one, query_low, preferred_element_type=jnp.float32)
    key_grad = jnp.einsum("td,te->de", normed_one, key_low, preferred_element_type=jnp.float32)
    value_grad = jnp.einsum("td,te->de", normed_one, value_low, preferred_element_type=jnp.float32)
    normed_one_grad = jnp.einsum(
        "te,de->td", query_low, query_weight, preferred_element_type=jnp.float32
    )
    normed_one_grad = normed_one_grad + jnp.einsum(
        "te,de->td", key_low, key_weight, preferred_element_type=jnp.float32
    )
    normed_one_grad = normed_one_grad + jnp.einsum(
        "te,de->td", value_low, value_weight, preferred_element_type=jnp.float32
    )
    norm_one_pull = jax.vjp(layer_norm, stream_start, norm1_gain, norm1_bias)[1]
    start_side, norm1_gain_grad, norm1_bias_grad = norm_one_pull(normed_one_grad)
    tokens_grad = after_grad + start_side
    table_grad = jnp.dot(onehot.T, tokens_grad, precision=HIGH)
    shares = (
        lax.psum_scatter(
            table_grad.astype(jnp.bfloat16), "blk", scatter_dimension=1, tiled=True
        ).astype(jnp.float32),
        lax.psum_scatter(
            norm1_gain_grad.astype(jnp.bfloat16), "blk", scatter_dimension=0, tiled=True
        ).astype(jnp.float32),
        lax.psum_scatter(
            norm1_bias_grad.astype(jnp.bfloat16), "blk", scatter_dimension=0, tiled=True
        ).astype(jnp.float32),
        lax.psum_scatter(
            query_grad.astype(jnp.bfloat16), "blk", scatter_dimension=0, tiled=True
        ).astype(jnp.float32),
        lax.psum_scatter(
            key_grad.astype(jnp.bfloat16), "blk", scatter_dimension=0, tiled=True
        ).astype(jnp.float32),
        lax.psum_scatter(
            value_grad.astype(jnp.bfloat16), "blk", scatter_dimension=0, tiled=True
        ).astype(jnp.float32),
        lax.psum_scatter(
            out_proj_grad.astype(jnp.bfloat16), "blk", scatter_dimension=0, tiled=True
        ).astype(jnp.float32),
        lax.psum_scatter(
            norm2_gain_grad.astype(jnp.bfloat16), "blk", scatter_dimension=0, tiled=True
        ).astype(jnp.float32),
        lax.psum_scatter(
            norm2_bias_grad.astype(jnp.bfloat16), "blk", scatter_dimension=0, tiled=True
        ).astype(jnp.float32),
        lax.psum_scatter(
            fc1_grad.astype(jnp.bfloat16), "blk", scatter_dimension=0, tiled=True
        ).astype(jnp.float32),
        lax.psum_scatter(
            fc2_grad.astype(jnp.bfloat16), "blk", scatter_dimension=0, tiled=True
        ).astype(jnp.float32),
        lax.psum_scatter(
            project_grad.astype(jnp.bfloat16), "blk", scatter_dimension=0, tiled=True
        ).astype(jnp.float32),
        lax.psum_scatter(
            unit1_first_grad.astype(jnp.bfloat16), "blk", scatter_dimension=0, tiled=True
        ).astype(jnp.float32),
        lax.psum_scatter(
            unit1_second_grad.astype(jnp.bfloat16), "blk", scatter_dimension=0, tiled=True
        ).astype(jnp.float32),
        lax.psum_scatter(
            unit2_first_grad.astype(jnp.bfloat16), "blk", scatter_dimension=0, tiled=True
        ).astype(jnp.float32),
        lax.psum_scatter(
            unit2_second_grad.astype(jnp.bfloat16), "blk", scatter_dimension=0, tiled=True
        ).astype(jnp.float32),
        lax.psum_scatter(
            output_grad.astype(jnp.bfloat16), "blk", scatter_dimension=0, tiled=True
        ).astype(jnp.float32),
    )
    summed = (
        lax.psum(shares[0].astype(jnp.bfloat16), "dp").astype(jnp.float32),
        lax.psum(shares[1].astype(jnp.bfloat16), "dp").astype(jnp.float32),
        lax.psum(shares[2].astype(jnp.bfloat16), "dp").astype(jnp.float32),
        lax.psum(shares[3].astype(jnp.bfloat16), "dp").astype(jnp.float32),
        lax.psum(shares[4].astype(jnp.bfloat16), "dp").astype(jnp.float32),
        lax.psum(shares[5].astype(jnp.bfloat16), "dp").astype(jnp.float32),
        lax.psum(shares[6].astype(jnp.bfloat16), "dp").astype(jnp.float32),
        lax.psum(shares[7].astype(jnp.bfloat16), "dp").astype(jnp.float32),
        lax.psum(shares[8].astype(jnp.bfloat16), "dp").astype(jnp.float32),
        lax.psum(shares[9].astype(jnp.bfloat16), "dp").astype(jnp.float32),
        lax.psum(shares[10].astype(jnp.bfloat16), "dp").astype(jnp.float32),
        lax.psum(shares[11].astype(jnp.bfloat16), "dp").astype(jnp.float32),
        lax.psum(shares[12].astype(jnp.bfloat16), "dp").astype(jnp.float32),
        lax.psum(shares[13].astype(jnp.bfloat16), "dp").astype(jnp.float32),
        lax.psum(shares[14].astype(jnp.bfloat16), "dp").astype(jnp.float32),
        lax.psum(shares[15].astype(jnp.bfloat16), "dp").astype(jnp.float32),
        lax.psum(shares[16].astype(jnp.bfloat16), "dp").astype(jnp.float32),
    )
    return (
        block_out,
        merged,
        tokens_grad,
        summed[0],
        summed[1],
        summed[2],
        summed[3],
        summed[4],
        summed[5],
        summed[6],
        summed[7],
        summed[8],
        summed[9],
        summed[10],
        summed[11],
        summed[12],
        summed[13],
        summed[14],
        summed[15],
        summed[16],
    )


def solution(mesh):
    placed = (
        P(("dp", "blk"), None),
        P("dp", None),
        P("dp", None),
        P(),
        P(),
        P(),
        P(),
        P(),
        P(),
        P(),
        P(),
        P(),
        P(),
        P(),
        P(),
        P(),
        P(),
        P(),
        P(),
        P(),
        P(("dp", "blk"), None),
        P(("dp", "blk"), None),
    )
    return jax.shard_map(
        shards,
        mesh=mesh,
        in_specs=placed,
        out_specs=(
            P(("dp", "blk"), None),
            P(("dp", "blk"), None),
            P(("dp", "blk"), None),
            P(None, "blk"),
            P("blk"),
            P("blk"),
            P("blk", None),
            P("blk", None),
            P("blk", None),
            P("blk", None),
            P("blk"),
            P("blk"),
            P("blk", None),
            P("blk", None),
            P("blk", None),
            P("blk", None),
            P("blk", None),
            P("blk", None),
            P("blk", None),
            P("blk", None),
        ),
        check_vma=False,
    )
```

profile of v0, /device:TPU:0, one launch (start us, length us, event | category | flops | bytes accessed | tf_op | source)
XLA Modules:
  0.0 1354.9 jit_solution(920508047010687415)
XLA Ops:
  28.0 155.3 %while.48 = (s32[]{:T(128)}, f32[12,480]{1,0:T(8,128)}, f32[12,480]{1,0:T(8,128)}, f32[12,480,64]{1,2,0:T(8,128)}, bf16[480,12,64]{0,2,1:T(8,128)(2,1)S(1)}, /*i...) while((s32[]{:T(128)}, f32[12,480]{1,0:T(8,128)}, ...), condition=%wide.region_12.13_spmd.clone, body=%wide.region_6.12_spmd.clone.sunk | while | flops 739569920 | bytes 60566056 | solution.py:252
  43.6 8.5 collective-permute-done.1
  67.5 6.5 collective-permute-done.1
  89.4 6.5 collective-permute-done.1
  111.2 6.5 collective-permute-done.1
  133.1 6.5 collective-permute-done.1
  155.0 6.5 collective-permute-done.1
  176.8 6.5 collective-permute-done.1
  196.6 5.7 fusion.130
  262.6 6.6 collective-permute-done.10
  286.5 6.3 collective-permute-done.22
  307.9 6.5 fusion.43
  324.5 368.5 %while.49 = (s32[]{:T(128)}, f32[480,12,64]{0,2,1:T(8,128)}, bf16[480,12,64]{0,2,1:T(8,128)(2,1)S(1)}, bf16[480,12,64]{0,2,1:T(8,128)(2,1)}, f32[480,12,64]{0,2,...) while((s32[]{:T(128)}, f32[480,12,64]{0,2,1:T(8,128)}, ...), condition=%wide.region_27.28_spmd.clone, body=%wide.region_23.27_spmd.clone.sunk | while | flops 1801777280 | bytes 116345776 | solution.py:430
  343.8 5.7 bitcast_add_fusion.7
  354.6 5.9 collective-permute-done.5
  363.0 6.0 collective-permute-done.3
  369.0 8.3 collective-permute-done.2
  382.8 5.6 multiply_convert_fusion.10
  396.3 6.1 bitcast_add_fusion.7
  407.2 5.9 collective-permute-done.5
  415.6 6.0 collective-permute-done.3
  421.5 8.3 collective-permute-done.2
  448.9 6.1 bitcast_add_fusion.7
  459.7 5.9 collective-permute-done.5
  468.1 6.0 collective-permute-done.3
  474.1 8.3 collective-permute-done.2
  487.9 5.6 multiply_convert_fusion.10
  501.4 6.1 bitcast_add_fusion.7
  512.3 5.9 collective-permute-done.5
  520.7 6.0 collective-permute-done.3
  526.6 8.3 collective-permute-done.2
  554.0 6.1 bitcast_add_fusion.7
  564.8 5.9 collective-permute-done.5
  573.2 6.0 collective-permute-done.3
  579.2 8.3 collective-permute-done.2
  593.0 5.6 multiply_convert_fusion.10
  606.5 6.1 bitcast_add_fusion.7
  617.4 5.9 collective-permute-done.5
  625.8 6.0 collective-permute-done.3
  631.7 8.3 collective-permute-done.2
  659.1 6.1 bitcast_add_fusion.7
  669.9 5.9 collective-permute-done.5
  678.3 6.0 collective-permute-done.3
  684.3 8.3 collective-permute-done.2
  699.8 8.9 multiply_convert_fusion.1
  715.5 8.3 collective-permute-done.26
  724.7 7.6 collective-permute-done.27
  768.3 8.1 convolution_convert_fusion
  777.8 6.4 convolution_convert_fusion.1
  786.1 13.9 %all-reduce.78 = (bf16[768]{0:T(1024)(128)(2,1)S(1)}, bf16[768]{0:T(1024)(128)(2,1)S(1)}, bf16[768]{0:T(1024)(128)(2,1)S(1)}, bf16[768]{0:T(1024)(128)(2,1)S(1)}) all-reduce(bf16[768]{0:T(1024)(128)(2,1)S(1)} %get-tuple-element.716, bf16[768]{0:T(1024)(128)(2,1)S(1)} %get-tuple-element.719, ...), channel_id=3, replica_groups=mesh['dp'=4,'blk'=8] {'blk'}, use_global_device_ids=true, to_apply=%region_33.34.clone | all-reduce | flops 3072 | bytes 12288
  803.8 25.2 %reduce-scatter.28.cloned.1.call-done = bf16[96,256]{1,0:T(8,128)(2,1)} async-done(((bf16[768,256]{1,0:T(8,128)(2,1)}), bf16[96,256]{1,0:T(8,128)(2,1)}) %reduce-scatter.28.cloned.1.call-update) | async-done | bytes 49168 | tf_op jit(solution)/shard_map/reduce_scatter | solution.py:495
  829.1 33.3 %reduce-scatter.34.cloned.1.call-done = bf16[288,256]{1,0:T(8,128)(2,1)} async-done(((bf16[2304,256]{1,0:T(8,128)(2,1)}), bf16[288,256]{1,0:T(8,128)(2,1)}) %reduce-scatter.34.cloned.1.call-update) | async-done | bytes 147472 | tf_op jit(solution)/shard_map/reduce_scatter | solution.py:504
  862.3 33.2 %reduce-scatter.32.cloned.1.call-done = bf16[288,256]{1,0:T(8,128)(2,1)} async-done(((bf16[2304,256]{1,0:T(8,128)(2,1)}), bf16[288,256]{1,0:T(8,128)(2,1)}) %reduce-scatter.32.cloned.1.call-update) | async-done | bytes 147472 | tf_op jit(solution)/shard_map/reduce_scatter | solution.py:501
  895.5 33.1 %reduce-scatter.30.cloned.1.call-done = bf16[288,256]{1,0:T(8,128)(2,1)} async-done(((bf16[2304,256]{1,0:T(8,128)(2,1)}), bf16[288,256]{1,0:T(8,128)(2,1)}) %reduce-scatter.30.cloned.1.call-update) | async-done | bytes 147472 | tf_op jit(solution)/shard_map/reduce_scatter | solution.py:498
  928.7 33.6 %reduce-scatter.36.cloned.1.call-done = bf16[288,256]{1,0:T(8,128)(2,1)} async-done(((bf16[2304,256]{1,0:T(8,128)(2,1)}), bf16[288,256]{1,0:T(8,128)(2,1)}) %reduce-scatter.36.cloned.1.call-update) | async-done | bytes 147472 | tf_op jit(solution)/shard_map/reduce_scatter | solution.py:507
  962.2 33.4 %reduce-scatter.22.cloned.1.call-done = bf16[96,768]{1,0:T(8,128)(2,1)} async-done(((bf16[768,768]{1,0:T(8,128)(2,1)}), bf16[96,768]{1,0:T(8,128)(2,1)}) %reduce-scatter.22.cloned.1.call-update) | async-done | bytes 147472 | tf_op jit(solution)/shard_map/reduce_scatter | solution.py:480
  995.6 33.8 %reduce-scatter.16.cloned.1.call-done = bf16[96,768]{1,0:T(8,128)(2,1)} async-done(((bf16[768,768]{1,0:T(8,128)(2,1)}), bf16[96,768]{1,0:T(8,128)(2,1)}) %reduce-scatter.16.cloned.1.call-update) | async-done | bytes 147472 | tf_op jit(solution)/shard_map/reduce_scatter | solution.py:471
  1029.4 33.3 %reduce-scatter.20.cloned.1.call-done = bf16[96,768]{1,0:T(8,128)(2,1)} async-done(((bf16[768,768]{1,0:T(8,128)(2,1)}), bf16[96,768]{1,0:T(8,128)(2,1)}) %reduce-scatter.20.cloned.1.call-update) | async-done | bytes 147472 | tf_op jit(solution)/shard_map/reduce_scatter | solution.py:477
  1062.7 34.2 %reduce-scatter.18.cloned.1.call-done = bf16[96,768]{1,0:T(8,128)(2,1)} async-done(((bf16[768,768]{1,0:T(8,128)(2,1)}), bf16[96,768]{1,0:T(8,128)(2,1)}) %reduce-scatter.18.cloned.1.call-update) | async-done | bytes 147472 | tf_op jit(solution)/shard_map/reduce_scatter | solution.py:474
  1096.8 55.2 %reduce-scatter.26.cloned.1.call-done = bf16[384,768]{1,0:T(8,128)(2,1)} async-done(((bf16[3072,768]{1,0:T(8,128)(2,1)}), bf16[384,768]{1,0:T(8,128)(2,1)}) %reduce-scatter.26.cloned.1.call-update) | async-done | bytes 589840 | tf_op jit(solution)/shard_map/reduce_scatter | solution.py:492
  1152.1 55.8 %reduce-scatter.24.cloned.1.call-done = bf16[96,3072]{1,0:T(8,128)(2,1)} async-done(((bf16[768,3072]{1,0:T(8,128)(2,1)}), bf16[96,3072]{1,0:T(8,128)(2,1)}) %reduce-scatter.24.cloned.1.call-update) | async-done | bytes 589840 | tf_op jit(solution)/shard_map/reduce_scatter | solution.py:489
  1208.7 5.7 collective-permute-done.15
  1219.2 34.1 %all-reduce.84.cloned.1.call-done = (bf16[10,96]{1,0:T(8,128)(2,1)}, bf16[96]{0:T(256)(128)(2,1)}, bf16[96]{0:T(256)(128)(2,1)}, bf16[96]{0:T(256)(128)(2,1)}, b...) async-done(((bf16[10,96]{1,0:T(8,128)(2,1)}, bf16[96]{0:T(256)(128)(2,1)}, bf16[96]{0:T(256)(128)(2,1)}, bf16[96]{0:T(256)(128)(2,1)}, ...) | async-done | bytes 68240 | tf_op jit(solution)/shard_map/psum | solution.py:515
  1261.9 73.5 %all-reduce.86.cloned.1.call-done = (bf16[96,768]{1,0:T(8,128)(2,1)}, bf16[96,768]{1,0:T(8,128)(2,1)}, bf16[96,768]{1,0:T(8,128)(2,1)}, bf16[96,768]{1,0:T(8,128...) async-done(((bf16[96,768]{1,0:T(8,128)(2,1)}, ...) | async-done | bytes 2359312 | tf_op jit(solution)/shard_map/psum | solution.py:518
  (1084 shorter events, 491.0 us)
Async XLA Ops:
  7.2 795.1 %reduce-scatter.40.cloned.1.call-start = ((), (), s32[]{:S(2)}) async-start(), calls=%async_computation.25 | async-start | bytes 221184
  7.3 230.6 %collective-permute-start.16 = (bf16[12,40,1024]{2,1,0:T(8,128)(2,1)}, bf16[12,40,1024]{2,1,0:T(8,128)(2,1)}, u32[]{:S(2)}, u32[]{:S(2)}) collective-permute-start(bf16[12,40,1024]{2,1,0:T(8,128)(2,1)} %bitcast.265), channel_id=1, source_target_pairs={{0,7},{1,0},{2,1},{3,2},{4,3},{5,4},{6,5},{7,6},{8,15},{9,8},{10,9... | collective-permute-start | bytes 2949128 | tf_op jit(solution)/shard_map/ppermute | solution.py:22
  11.8 228.7 %collective-permute-start.17 = (bf16[12,40,1024]{2,1,0:T(8,128)(2,1)}, bf16[12,40,1024]{2,1,0:T(8,128)(2,1)}, u32[]{:S(2)}, u32[]{:S(2)}) collective-permute-start(bf16[12,40,1024]{2,1,0:T(8,128)(2,1)} %bitcast.266), channel_id=1, source_target_pairs={{0,1},{1,2},{2,3},{3,4},{4,5},{5,6},{6,7},{7,0},{8,9},{9,10},{10,1... | collective-permute-start | bytes 2949128 | tf_op jit(solution)/shard_map/ppermute | solution.py:22
  28.2 15.4 %collective-permute-start = (bf16[480,12,64]{0,2,1:T(8,128)(2,1)S(1)}, bf16[480,12,64]{0,2,1:T(8,128)(2,1)S(1)}, u32[]{:S(2)}, u32[]{:S(2)}) collective-permute-start(bf16[480,12,64]{0,2,1:T(8,128)(2,1)S(1)} %copy.145), channel_id=1, source_target_pairs={{0,1},{1,2},{2,3},{3,4},{4,5},{5,6},{6,7},{7,0},{8,9},{9,10},{10,1... | collective-permute-start | bytes 2211848 | tf_op jit(solution)/shard_map/while/body/eval_jaxpr/ppermute | solution.py:22
  30.4 21.8 %collective-permute-start.1 = (bf16[480,12,64]{0,2,1:T(8,128)(2,1)}, bf16[480,12,64]{0,2,1:T(8,128)(2,1)}, u32[]{:S(2)}, u32[]{:S(2)}) collective-permute-start(bf16[480,12,64]{0,2,1:T(8,128)(2,1)} %copy.146), channel_id=1, source_target_pairs={{0,1},{1,2},{2,3},{3,4},{4,5},{5,6},{6,7},{7,0},{8,9},{9,10},{10,1... | collective-permute-start | bytes 2211848 | tf_op jit(solution)/shard_map/while/body/eval_jaxpr/ppermute | solution.py:22
  52.2 15.3 %collective-permute-start = (bf16[480,12,64]{0,2,1:T(8,128)(2,1)S(1)}, bf16[480,12,64]{0,2,1:T(8,128)(2,1)S(1)}, u32[]{:S(2)}, u32[]{:S(2)}) collective-permute-start(bf16[480,12,64]{0,2,1:T(8,128)(2,1)S(1)} %copy.145), channel_id=1, source_target_pairs={{0,1},{1,2},{2,3},{3,4},{4,5},{5,6},{6,7},{7,0},{8,9},{9,10},{10,1... | collective-permute-start | bytes 2211848 | tf_op jit(solution)/shard_map/while/body/eval_jaxpr/ppermute | solution.py:22
  54.4 19.7 %collective-permute-start.1 = (bf16[480,12,64]{0,2,1:T(8,128)(2,1)}, bf16[480,12,64]{0,2,1:T(8,128)(2,1)}, u32[]{:S(2)}, u32[]{:S(2)}) collective-permute-start(bf16[480,12,64]{0,2,1:T(8,128)(2,1)} %copy.146), channel_id=1, source_target_pairs={{0,1},{1,2},{2,3},{3,4},{4,5},{5,6},{6,7},{7,0},{8,9},{9,10},{10,1... | collective-permute-start | bytes 2211848 | tf_op jit(solution)/shard_map/while/body/eval_jaxpr/ppermute | solution.py:22
  74.1 15.3 %collective-permute-start = (bf16[480,12,64]{0,2,1:T(8,128)(2,1)S(1)}, bf16[480,12,64]{0,2,1:T(8,128)(2,1)S(1)}, u32[]{:S(2)}, u32[]{:S(2)}) collective-permute-start(bf16[480,12,64]{0,2,1:T(8,128)(2,1)S(1)} %copy.145), channel_id=1, source_target_pairs={{0,1},{1,2},{2,3},{3,4},{4,5},{5,6},{6,7},{7,0},{8,9},{9,10},{10,1... | collective-permute-start | bytes 2211848 | tf_op jit(solution)/shard_map/while/body/eval_jaxpr/ppermute | solution.py:22
  76.2 19.7 %collective-permute-start.1 = (bf16[480,12,64]{0,2,1:T(8,128)(2,1)}, bf16[480,12,64]{0,2,1:T(8,128)(2,1)}, u32[]{:S(2)}, u32[]{:S(2)}) collective-permute-start(bf16[480,12,64]{0,2,1:T(8,128)(2,1)} %copy.146), channel_id=1, source_target_pairs={{0,1},{1,2},{2,3},{3,4},{4,5},{5,6},{6,7},{7,0},{8,9},{9,10},{10,1... | collective-permute-start | bytes 2211848 | tf_op jit(solution)/shard_map/while/body/eval_jaxpr/ppermute | solution.py:22
  95.9 15.3 %collective-permute-start = (bf16[480,12,64]{0,2,1:T(8,128)(2,1)S(1)}, bf16[480,12,64]{0,2,1:T(8,128)(2,1)S(1)}, u32[]{:S(2)}, u32[]{:S(2)}) collective-permute-start(bf16[480,12,64]{0,2,1:T(8,128)(2,1)S(1)} %copy.145), channel_id=1, source_target_pairs={{0,1},{1,2},{2,3},{3,4},{4,5},{5,6},{6,7},{7,0},{8,9},{9,10},{10,1... | collective-permute-start | bytes 2211848 | tf_op jit(solution)/shard_map/while/body/eval_jaxpr/ppermute | solution.py:22
  98.1 19.7 %collective-permute-start.1 = (bf16[480,12,64]{0,2,1:T(8,128)(2,1)}, bf16[480,12,64]{0,2,1:T(8,128)(2,1)}, u32[]{:S(2)}, u32[]{:S(2)}) collective-permute-start(bf16[480,12,64]{0,2,1:T(8,128)(2,1)} %copy.146), channel_id=1, source_target_pairs={{0,1},{1,2},{2,3},{3,4},{4,5},{5,6},{6,7},{7,0},{8,9},{9,10},{10,1... | collective-permute-start | bytes 2211848 | tf_op jit(solution)/shard_map/while/body/eval_jaxpr/ppermute | solution.py:22
  117.8 15.3 %collective-permute-start = (bf16[480,12,64]{0,2,1:T(8,128)(2,1)S(1)}, bf16[480,12,64]{0,2,1:T(8,128)(2,1)S(1)}, u32[]{:S(2)}, u32[]{:S(2)}) collective-permute-start(bf16[480,12,64]{0,2,1:T(8,128)(2,1)S(1)} %copy.145), channel_id=1, source_target_pairs={{0,1},{1,2},{2,3},{3,4},{4,5},{5,6},{6,7},{7,0},{8,9},{9,10},{10,1... | collective-permute-start | bytes 2211848 | tf_op jit(solution)/shard_map/while/body/eval_jaxpr/ppermute | solution.py:22
  119.9 19.7 %collective-permute-start.1 = (bf16[480,12,64]{0,2,1:T(8,128)(2,1)}, bf16[480,12,64]{0,2,1:T(8,128)(2,1)}, u32[]{:S(2)}, u32[]{:S(2)}) collective-permute-start(bf16[480,12,64]{0,2,1:T(8,128)(2,1)} %copy.146), channel_id=1, source_target_pairs={{0,1},{1,2},{2,3},{3,4},{4,5},{5,6},{6,7},{7,0},{8,9},{9,10},{10,1... | collective-permute-start | bytes 2211848 | tf_op jit(solution)/shard_map/while/body/eval_jaxpr/ppermute | solution.py:22
  139.7 15.3 %collective-permute-start = (bf16[480,12,64]{0,2,1:T(8,128)(2,1)S(1)}, bf16[480,12,64]{0,2,1:T(8,128)(2,1)S(1)}, u32[]{:S(2)}, u32[]{:S(2)}) collective-permute-start(bf16[480,12,64]{0,2,1:T(8,128)(2,1)S(1)} %copy.145), channel_id=1, source_target_pairs={{0,1},{1,2},{2,3},{3,4},{4,5},{5,6},{6,7},{7,0},{8,9},{9,10},{10,1... | collective-permute-start | bytes 2211848 | tf_op jit(solution)/shard_map/while/body/eval_jaxpr/ppermute | solution.py:22
  141.8 19.7 %collective-permute-start.1 = (bf16[480,12,64]{0,2,1:T(8,128)(2,1)}, bf16[480,12,64]{0,2,1:T(8,128)(2,1)}, u32[]{:S(2)}, u32[]{:S(2)}) collective-permute-start(bf16[480,12,64]{0,2,1:T(8,128)(2,1)} %copy.146), channel_id=1, source_target_pairs={{0,1},{1,2},{2,3},{3,4},{4,5},{5,6},{6,7},{7,0},{8,9},{9,10},{10,1... | collective-permute-start | bytes 2211848 | tf_op jit(solution)/shard_map/while/body/eval_jaxpr/ppermute | solution.py:22
  161.5 15.3 %collective-permute-start = (bf16[480,12,64]{0,2,1:T(8,128)(2,1)S(1)}, bf16[480,12,64]{0,2,1:T(8,128)(2,1)S(1)}, u32[]{:S(2)}, u32[]{:S(2)}) collective-permute-start(bf16[480,12,64]{0,2,1:T(8,128)(2,1)S(1)} %copy.145), channel_id=1, source_target_pairs={{0,1},{1,2},{2,3},{3,4},{4,5},{5,6},{6,7},{7,0},{8,9},{9,10},{10,1... | collective-permute-start | bytes 2211848 | tf_op jit(solution)/shard_map/while/body/eval_jaxpr/ppermute | solution.py:22
  163.7 19.7 %collective-permute-start.1 = (bf16[480,12,64]{0,2,1:T(8,128)(2,1)}, bf16[480,12,64]{0,2,1:T(8,128)(2,1)}, u32[]{:S(2)}, u32[]{:S(2)}) collective-permute-start(bf16[480,12,64]{0,2,1:T(8,128)(2,1)} %copy.146), channel_id=1, source_target_pairs={{0,1},{1,2},{2,3},{3,4},{4,5},{5,6},{6,7},{7,0},{8,9},{9,10},{10,1... | collective-permute-start | bytes 2211848 | tf_op jit(solution)/shard_map/while/body/eval_jaxpr/ppermute | solution.py:22
  222.4 12.4 collective-permute-start.9
  222.8 13.0 collective-permute-start.8
  272.8 12.6 collective-permute-start.13
  338.6 13.6 %collective-permute-start.4 = (bf16[480,12,64]{0,2,1:T(8,128)(2,1)}, bf16[480,12,64]{0,2,1:T(8,128)(2,1)}, u32[]{:S(2)}, u32[]{:S(2)}) collective-permute-start(bf16[480,12,64]{0,2,1:T(8,128)(2,1)} %fusion.309), channel_id=1, source_target_pairs={{0,1},{1,2},{2,3},{3,4},{4,5},{5,6},{6,7},{7,0},{8,9},{9,10},{10,1... | collective-permute-start | bytes 2211848 | tf_op jit(solution)/shard_map/while/body/eval_jaxpr/ppermute | solution.py:22
  343.7 16.9 %collective-permute-start.5 = (bf16[480,12,64]{0,2,1:T(8,128)(2,1)}, bf16[480,12,64]{0,2,1:T(8,128)(2,1)}, u32[]{:S(2)}, u32[]{:S(2)}) collective-permute-start(bf16[480,12,64]{0,2,1:T(8,128)(2,1)} %fusion.310), channel_id=1, source_target_pairs={{0,1},{1,2},{2,3},{3,4},{4,5},{5,6},{6,7},{7,0},{8,9},{9,10},{10,1... | collective-permute-start | bytes 2211848 | tf_op jit(solution)/shard_map/while/body/eval_jaxpr/ppermute | solution.py:22
  343.7 25.3 %collective-permute-start.3 = (bf16[480,12,64]{0,2,1:T(8,128)(2,1)}, bf16[480,12,64]{0,2,1:T(8,128)(2,1)}, u32[]{:S(2)}, u32[]{:S(2)}) collective-permute-start(bf16[480,12,64]{0,2,1:T(8,128)(2,1)} %copy.226), channel_id=1, source_target_pairs={{0,1},{1,2},{2,3},{3,4},{4,5},{5,6},{6,7},{7,0},{8,9},{9,10},{10,1... | collective-permute-start | bytes 2211848 | tf_op jit(solution)/shard_map/while/body/eval_jaxpr/ppermute | solution.py:22
  343.7 33.6 %collective-permute-start.2 = (bf16[480,12,64]{0,2,1:T(8,128)(2,1)S(1)}, bf16[480,12,64]{0,2,1:T(8,128)(2,1)S(1)}, u32[]{:S(2)}, u32[]{:S(2)}) collective-permute-start(bf16[480,12,64]{0,2,1:T(8,128)(2,1)S(1)} %copy.225), channel_id=1, source_target_pairs={{0,1},{1,2},{2,3},{3,4},{4,5},{5,6},{6,7},{7,0},{8,9},{9,10},{10,1... | collective-permute-start | bytes 2211848 | tf_op jit(solution)/shard_map/while/body/eval_jaxpr/ppermute | solution.py:22
  391.2 13.5 collective-permute-start.4
  396.3 16.8 %collective-permute-start.5 = (bf16[480,12,64]{0,2,1:T(8,128)(2,1)}, bf16[480,12,64]{0,2,1:T(8,128)(2,1)}, u32[]{:S(2)}, u32[]{:S(2)}) collective-permute-start(bf16[480,12,64]{0,2,1:T(8,128)(2,1)} %fusion.310), channel_id=1, source_target_pairs={{0,1},{1,2},{2,3},{3,4},{4,5},{5,6},{6,7},{7,0},{8,9},{9,10},{10,1... | collective-permute-start | bytes 2211848 | tf_op jit(solution)/shard_map/while/body/eval_jaxpr/ppermute | solution.py:22
  396.3 25.3 %collective-permute-start.3 = (bf16[480,12,64]{0,2,1:T(8,128)(2,1)}, bf16[480,12,64]{0,2,1:T(8,128)(2,1)}, u32[]{:S(2)}, u32[]{:S(2)}) collective-permute-start(bf16[480,12,64]{0,2,1:T(8,128)(2,1)} %copy.226), channel_id=1, source_target_pairs={{0,1},{1,2},{2,3},{3,4},{4,5},{5,6},{6,7},{7,0},{8,9},{9,10},{10,1... | collective-permute-start | bytes 2211848 | tf_op jit(solution)/shard_map/while/body/eval_jaxpr/ppermute | solution.py:22
  396.3 33.6 %collective-permute-start.2 = (bf16[480,12,64]{0,2,1:T(8,128)(2,1)S(1)}, bf16[480,12,64]{0,2,1:T(8,128)(2,1)S(1)}, u32[]{:S(2)}, u32[]{:S(2)}) collective-permute-start(bf16[480,12,64]{0,2,1:T(8,128)(2,1)S(1)} %copy.225), channel_id=1, source_target_pairs={{0,1},{1,2},{2,3},{3,4},{4,5},{5,6},{6,7},{7,0},{8,9},{9,10},{10,1... | collective-permute-start | bytes 2211848 | tf_op jit(solution)/shard_map/while/body/eval_jaxpr/ppermute | solution.py:22
  443.7 13.5 collective-permute-start.4
  448.8 16.8 %collective-permute-start.5 = (bf16[480,12,64]{0,2,1:T(8,128)(2,1)}, bf16[480,12,64]{0,2,1:T(8,128)(2,1)}, u32[]{:S(2)}, u32[]{:S(2)}) collective-permute-start(bf16[480,12,64]{0,2,1:T(8,128)(2,1)} %fusion.310), channel_id=1, source_target_pairs={{0,1},{1,2},{2,3},{3,4},{4,5},{5,6},{6,7},{7,0},{8,9},{9,10},{10,1... | collective-permute-start | bytes 2211848 | tf_op jit(solution)/shard_map/while/body/eval_jaxpr/ppermute | solution.py:22
  448.8 25.3 %collective-permute-start.3 = (bf16[480,12,64]{0,2,1:T(8,128)(2,1)}, bf16[480,12,64]{0,2,1:T(8,128)(2,1)}, u32[]{:S(2)}, u32[]{:S(2)}) collective-permute-start(bf16[480,12,64]{0,2,1:T(8,128)(2,1)} %copy.226), channel_id=1, source_target_pairs={{0,1},{1,2},{2,3},{3,4},{4,5},{5,6},{6,7},{7,0},{8,9},{9,10},{10,1... | collective-permute-start | bytes 2211848 | tf_op jit(solution)/shard_map/while/body/eval_jaxpr/ppermute | solution.py:22
  448.8 33.6 %collective-permute-start.2 = (bf16[480,12,64]{0,2,1:T(8,128)(2,1)S(1)}, bf16[480,12,64]{0,2,1:T(8,128)(2,1)S(1)}, u32[]{:S(2)}, u32[]{:S(2)}) collective-permute-start(bf16[480,12,64]{0,2,1:T(8,128)(2,1)S(1)} %copy.225), channel_id=1, source_target_pairs={{0,1},{1,2},{2,3},{3,4},{4,5},{5,6},{6,7},{7,0},{8,9},{9,10},{10,1... | collective-permute-start | bytes 2211848 | tf_op jit(solution)/shard_map/while/body/eval_jaxpr/ppermute | solution.py:22
  496.3 13.5 collective-permute-start.4
  501.4 16.8 %collective-permute-start.5 = (bf16[480,12,64]{0,2,1:T(8,128)(2,1)}, bf16[480,12,64]{0,2,1:T(8,128)(2,1)}, u32[]{:S(2)}, u32[]{:S(2)}) collective-permute-start(bf16[480,12,64]{0,2,1:T(8,128)(2,1)} %fusion.310), channel_id=1, source_target_pairs={{0,1},{1,2},{2,3},{3,4},{4,5},{5,6},{6,7},{7,0},{8,9},{9,10},{10,1... | collective-permute-start | bytes 2211848 | tf_op jit(solution)/shard_map/while/body/eval_jaxpr/ppermute | solution.py:22
  501.4 25.3 %collective-permute-start.3 = (bf16[480,12,64]{0,2,1:T(8,128)(2,1)}, bf16[480,12,64]{0,2,1:T(8,128)(2,1)}, u32[]{:S(2)}, u32[]{:S(2)}) collective-permute-start(bf16[480,12,64]{0,2,1:T(8,128)(2,1)} %copy.226), channel_id=1, source_target_pairs={{0,1},{1,2},{2,3},{3,4},{4,5},{5,6},{6,7},{7,0},{8,9},{9,10},{10,1... | collective-permute-start | bytes 2211848 | tf_op jit(solution)/shard_map/while/body/eval_jaxpr/ppermute | solution.py:22
  501.4 33.6 %collective-permute-start.2 = (bf16[480,12,64]{0,2,1:T(8,128)(2,1)S(1)}, bf16[480,12,64]{0,2,1:T(8,128)(2,1)S(1)}, u32[]{:S(2)}, u32[]{:S(2)}) collective-permute-start(bf16[480,12,64]{0,2,1:T(8,128)(2,1)S(1)} %copy.225), channel_id=1, source_target_pairs={{0,1},{1,2},{2,3},{3,4},{4,5},{5,6},{6,7},{7,0},{8,9},{9,10},{10,1... | collective-permute-start | bytes 2211848 | tf_op jit(solution)/shard_map/while/body/eval_jaxpr/ppermute | solution.py:22
  548.8 13.5 collective-permute-start.4
  553.9 16.8 %collective-permute-start.5 = (bf16[480,12,64]{0,2,1:T(8,128)(2,1)}, bf16[480,12,64]{0,2,1:T(8,128)(2,1)}, u32[]{:S(2)}, u32[]{:S(2)}) collective-permute-start(bf16[480,12,64]{0,2,1:T(8,128)(2,1)} %fusion.310), channel_id=1, source_target_pairs={{0,1},{1,2},{2,3},{3,4},{4,5},{5,6},{6,7},{7,0},{8,9},{9,10},{10,1... | collective-permute-start | bytes 2211848 | tf_op jit(solution)/shard_map/while/body/eval_jaxpr/ppermute | solution.py:22
  553.9 25.3 %collective-permute-start.3 = (bf16[480,12,64]{0,2,1:T(8,128)(2,1)}, bf16[480,12,64]{0,2,1:T(8,128)(2,1)}, u32[]{:S(2)}, u32[]{:S(2)}) collective-permute-start(bf16[480,12,64]{0,2,1:T(8,128)(2,1)} %copy.226), channel_id=1, source_target_pairs={{0,1},{1,2},{2,3},{3,4},{4,5},{5,6},{6,7},{7,0},{8,9},{9,10},{10,1... | collective-permute-start | bytes 2211848 | tf_op jit(solution)/shard_map/while/body/eval_jaxpr/ppermute | solution.py:22
  553.9 33.6 %collective-permute-start.2 = (bf16[480,12,64]{0,2,1:T(8,128)(2,1)S(1)}, bf16[480,12,64]{0,2,1:T(8,128)(2,1)S(1)}, u32[]{:S(2)}, u32[]{:S(2)}) collective-permute-start(bf16[480,12,64]{0,2,1:T(8,128)(2,1)S(1)} %copy.225), channel_id=1, source_target_pairs={{0,1},{1,2},{2,3},{3,4},{4,5},{5,6},{6,7},{7,0},{8,9},{9,10},{10,1... | collective-permute-start | bytes 2211848 | tf_op jit(solution)/shard_map/while/body/eval_jaxpr/ppermute | solution.py:22
  601.4 13.5 collective-permute-start.4
  606.5 16.8 %collective-permute-start.5 = (bf16[480,12,64]{0,2,1:T(8,128)(2,1)}, bf16[480,12,64]{0,2,1:T(8,128)(2,1)}, u32[]{:S(2)}, u32[]{:S(2)}) collective-permute-start(bf16[480,12,64]{0,2,1:T(8,128)(2,1)} %fusion.310), channel_id=1, source_target_pairs={{0,1},{1,2},{2,3},{3,4},{4,5},{5,6},{6,7},{7,0},{8,9},{9,10},{10,1... | collective-permute-start | bytes 2211848 | tf_op jit(solution)/shard_map/while/body/eval_jaxpr/ppermute | solution.py:22
  606.5 25.3 %collective-permute-start.3 = (bf16[480,12,64]{0,2,1:T(8,128)(2,1)}, bf16[480,12,64]{0,2,1:T(8,128)(2,1)}, u32[]{:S(2)}, u32[]{:S(2)}) collective-permute-start(bf16[480,12,64]{0,2,1:T(8,128)(2,1)} %copy.226), channel_id=1, source_target_pairs={{0,1},{1,2},{2,3},{3,4},{4,5},{5,6},{6,7},{7,0},{8,9},{9,10},{10,1... | collective-permute-start | bytes 2211848 | tf_op jit(solution)/shard_map/while/body/eval_jaxpr/ppermute | solution.py:22
  606.5 33.6 %collective-permute-start.2 = (bf16[480,12,64]{0,2,1:T(8,128)(2,1)S(1)}, bf16[480,12,64]{0,2,1:T(8,128)(2,1)S(1)}, u32[]{:S(2)}, u32[]{:S(2)}) collective-permute-start(bf16[480,12,64]{0,2,1:T(8,128)(2,1)S(1)} %copy.225), channel_id=1, source_target_pairs={{0,1},{1,2},{2,3},{3,4},{4,5},{5,6},{6,7},{7,0},{8,9},{9,10},{10,1... | collective-permute-start | bytes 2211848 | tf_op jit(solution)/shard_map/while/body/eval_jaxpr/ppermute | solution.py:22
  653.9 13.5 collective-permute-start.4
  659.0 16.8 %collective-permute-start.5 = (bf16[480,12,64]{0,2,1:T(8,128)(2,1)}, bf16[480,12,64]{0,2,1:T(8,128)(2,1)}, u32[]{:S(2)}, u32[]{:S(2)}) collective-permute-start(bf16[480,12,64]{0,2,1:T(8,128)(2,1)} %fusion.310), channel_id=1, source_target_pairs={{0,1},{1,2},{2,3},{3,4},{4,5},{5,6},{6,7},{7,0},{8,9},{9,10},{10,1... | collective-permute-start | bytes 2211848 | tf_op jit(solution)/shard_map/while/body/eval_jaxpr/ppermute | solution.py:22
  659.0 25.3 %collective-permute-start.3 = (bf16[480,12,64]{0,2,1:T(8,128)(2,1)}, bf16[480,12,64]{0,2,1:T(8,128)(2,1)}, u32[]{:S(2)}, u32[]{:S(2)}) collective-permute-start(bf16[480,12,64]{0,2,1:T(8,128)(2,1)} %copy.226), channel_id=1, source_target_pairs={{0,1},{1,2},{2,3},{3,4},{4,5},{5,6},{6,7},{7,0},{8,9},{9,10},{10,1... | collective-permute-start | bytes 2211848 | tf_op jit(solution)/shard_map/while/body/eval_jaxpr/ppermute | solution.py:22
  659.0 33.6 %collective-permute-start.2 = (bf16[480,12,64]{0,2,1:T(8,128)(2,1)S(1)}, bf16[480,12,64]{0,2,1:T(8,128)(2,1)S(1)}, u32[]{:S(2)}, u32[]{:S(2)}) collective-permute-start(bf16[480,12,64]{0,2,1:T(8,128)(2,1)S(1)} %copy.225), channel_id=1, source_target_pairs={{0,1},{1,2},{2,3},{3,4},{4,5},{5,6},{6,7},{7,0},{8,9},{9,10},{10,1... | collective-permute-start | bytes 2211848 | tf_op jit(solution)/shard_map/while/body/eval_jaxpr/ppermute | solution.py:22
  710.6 13.3 collective-permute-start.26
  711.7 20.5 %collective-permute-start.27 = (bf16[480,12,64]{0,2,1:T(8,128)(2,1)S(1)}, bf16[480,12,64]{0,2,1:T(8,128)(2,1)S(1)}, u32[]{:S(2)}, u32[]{:S(2)}) collective-permute-start(bf16[480,12,64]{0,2,1:T(8,128)(2,1)S(1)} %fusion.52), channel_id=1, source_target_pairs={{0,1},{1,2},{2,3},{3,4},{4,5},{5,6},{6,7},{7,0},{8,9},{9,10},{10,1... | collective-permute-start | bytes 2211848 | tf_op jit(solution)/shard_map/ppermute | solution.py:22
  738.0 65.8 %reduce-scatter.38.cloned.1.call-start = ((), (), s32[]{:S(2)}) async-start(), calls=%async_computation.24 | async-start | bytes 147456 | tf_op jit(solution)/shard_map/reduce_scatter | solution.py:510
  739.0 90.0 %reduce-scatter.28.cloned.1.call-start = ((), (), s32[]{:S(2)}) async-start(), calls=%async_computation.19 | async-start | bytes 442368 | tf_op jit(solution)/shard_map/reduce_scatter | solution.py:495
  741.5 120.9 %reduce-scatter.34.cloned.1.call-start = ((), (), s32[]{:S(2)}) async-start(), calls=%async_computation.22 | async-start | bytes 1327104 | tf_op jit(solution)/shard_map/reduce_scatter | solution.py:504
  745.2 150.4 %reduce-scatter.32.cloned.1.call-start = ((), (), s32[]{:S(2)}) async-start(), calls=%async_computation.21 | async-start | bytes 1327104 | tf_op jit(solution)/shard_map/reduce_scatter | solution.py:501
  748.8 179.8 %reduce-scatter.30.cloned.1.call-start = ((), (), s32[]{:S(2)}) async-start(), calls=%async_computation.20 | async-start | bytes 1327104 | tf_op jit(solution)/shard_map/reduce_scatter | solution.py:498
  752.5 209.7 %reduce-scatter.36.cloned.1.call-start = ((), (), s32[]{:S(2)}) async-start(), calls=%async_computation.23 | async-start | bytes 1327104 | tf_op jit(solution)/shard_map/reduce_scatter | solution.py:507
  756.1 239.5 %reduce-scatter.22.cloned.1.call-start = ((), (), s32[]{:S(2)}) async-start(), calls=%async_computation.16 | async-start | bytes 1327104 | tf_op jit(solution)/shard_map/reduce_scatter | solution.py:480
  759.2 270.2 %reduce-scatter.16.cloned.1.call-start = ((), (), s32[]{:S(2)}) async-start(), calls=%async_computation.13 | async-start | bytes 1327104 | tf_op jit(solution)/shard_map/reduce_scatter | solution.py:471
  762.6 300.1 %reduce-scatter.20.cloned.1.call-start = ((), (), s32[]{:S(2)}) async-start(), calls=%async_computation.15 | async-start | bytes 1327104 | tf_op jit(solution)/shard_map/reduce_scatter | solution.py:477
  764.6 332.2 %reduce-scatter.18.cloned.1.call-start = ((), (), s32[]{:S(2)}) async-start(), calls=%async_computation.14 | async-start | bytes 1327104 | tf_op jit(solution)/shard_map/reduce_scatter | solution.py:474
  768.3 383.8 %reduce-scatter.26.cloned.1.call-start = ((), (), s32[]{:S(2)}) async-start(), calls=%async_computation.18 | async-start | bytes 5308416 | tf_op jit(solution)/shard_map/reduce_scatter | solution.py:492
  776.4 431.4 %reduce-scatter.24.cloned.1.call-start = ((), (), s32[]{:S(2)}) async-start(), calls=%async_computation.17 | async-start | bytes 5308416 | tf_op jit(solution)/shard_map/reduce_scatter | solution.py:489
  784.3 469.0 %all-reduce.84.cloned.1.call-start = ((), (), s32[]{:S(2)}) async-start(), calls=%async_computation.26 | async-start | bytes 143360 | tf_op jit(solution)/shard_map/psum | solution.py:515
  829.0 506.3 %all-reduce.86.cloned.1.call-start = ((), (), s32[]{:S(2)}) async-start(), calls=%async_computation.27 | async-start | bytes 4718592 | tf_op jit(solution)/shard_map/psum | solution.py:518
  (236 other events, 3284.0 us)
Sparse Core Ops, SparseCore 0:
  738.1 28.4 reduce-scatter.39
  769.6 28.2 reduce-scatter.37
  800.1 28.8 reduce-scatter.27
  831.3 31.0 reduce-scatter.33
  864.6 30.9 reduce-scatter.31
  897.8 30.8 reduce-scatter.29
  931.0 31.1 reduce-scatter.35
  964.6 30.9 reduce-scatter.21
  998.6 30.7 reduce-scatter.15
  1031.6 30.9 reduce-scatter.19
  1065.6 31.1 reduce-scatter.17
  1099.1 52.9 reduce-scatter.25
  1154.5 53.3 reduce-scatter.23
  1213.0 40.2 all-reduce.83
  1257.3 78.0 all-reduce.85
where the time goes:
time: 1360 us; the launch traced here: 1350 us
  waiting for transfers between devices  770 us (57%)
  matrix products  300 us (22%)
  other arithmetic  136 us (10%)
  local copies, waits for them, and re-layouts  88.8 us (7%)
  starting transfers between devices  26.4 us (2%)
  between operations  17.5 us (1%)
  blocking collectives  13.9 us (1%)
    ppermute x64, waiting for transfers between devices, passed_along(): return lax.ppermute(value, axis, pairs)  258 us
    psum x1, waiting for transfers between devices, shards(): lax.psum(shares[3].astype(jnp.bfloat16), 'dp').astype(jnp.float32)  73.5 us
    reduce_scatter x1, waiting for transfers between devices, shards(): lax.psum_scatter(fc1_grad.astype(jnp.bfloat16), 'blk', scatter_dimension=...  55.8 us
    reduce_scatter x1, waiting for transfers between devices, shards(): lax.psum_scatter(fc2_grad.astype(jnp.bfloat16), 'blk', scatter_dimension=...  55.2 us
    dot_general x8, matrix products, pair_grads(): jnp.einsum('qhd,khd->hqk', grad_heads, value_heads, preferred_element_typ...  47.8 us
    dot_general x8, matrix products, pair_grads(): jnp.einsum('hqk,khd->qhd', score_grads, key_heads, preferred_element_type...  43.6 us
    dot_general x8, matrix products, pair_grads(): jnp.einsum('hqk,qhd->khd', weights_now.astype(jnp.bfloat16), grad_heads,...  40.7 us
    while x217, local copies, waits for them, and re-layouts  40.1 us
  transfers between devices with their start and end apart: 79, of which 61 were waited for; matrix products, arithmetic and copies ran while one was open for 26% of the time, Pallas kernels for 0%

commit v1 on v0

v1 whole, which is shorter than its diff:
```python
import functools
import math

import jax
import jax.numpy as jnp
from jax import lax
from jax.experimental import pallas as pl
from jax.experimental.pallas import tpu as pltpu
from jax.sharding import PartitionSpec as P
import numpy as np

HEADS = 12
HEAD = 64
ROWW = 40
SLOTS = 12
HALF = SLOTS // 2
REACH = 6

NEG = -1e30
EPS = 1e-06
HIGH = lax.Precision.HIGHEST
KEYS = 672
SPARE_KEYS = 768
QROWS = 64
ROWS = 512
VMEM = 60 * 1024 * 1024
NT = (((1,), (1,)), ((), ()))
F32 = jnp.float32
BF16 = jnp.bfloat16


def up16(value):
    return (value + 15) // 16 * 16


def own_blocks(heads, feats):
    row = lax.broadcasted_iota(jnp.int32, (heads * QROWS, feats), 0) // QROWS
    col = lax.broadcasted_iota(jnp.int32, (heads * QROWS, feats), 1) // HEAD
    return row == col


def spread(block, heads):
    wide = jnp.concatenate([block] * heads, axis=0)
    return jnp.where(own_blocks(heads, block.shape[1]), wide, jnp.zeros((), block.dtype))


def gathered(wide, heads):
    kept = jnp.where(own_blocks(heads, wide.shape[1]), wide, 0.0)
    total = kept[:QROWS]
    for head in range(1, heads):
        total = total + kept[head * QROWS : (head + 1) * QROWS]
    return total


def lanes(column, width):
    return jnp.concatenate([column] * (width // 128), axis=1)


def query_blocks(first, many, body):
    def pair(number, none):
        body(first + 2 * number, 2)
        return none

    lax.fori_loop(0, many // 2, pair, 0)

    @pl.when(many % 2 == 1)
    def _():
        body(first + many - 1, 1)


def for_items(items, klen, body):
    def one(item, none):
        body(item, KEYS, (klen[item] + KEYS - 1) // KEYS)
        return none

    lax.fori_loop(0, items - 1, one, 0)
    last = items - 1
    body(last, SPARE_KEYS, (klen[last] + SPARE_KEYS - 1) // SPARE_KEYS)


def as_column(row):
    return row.T[:, :1]


def attend_kernel(
    heads, units, items,
    koff, kcnt, kdst, kstart, klen, qfirst, qcount,
    q_ref, bias_ref, wk_ref, wv_ref, *refs,
):
    steps = units // 4
    n_refs = refs[:steps]
    o_ref, lse_ref, ns_ref, ks_ref, vs_ref = refs[steps : steps + 5]
    acc_ref, top_ref, total_ref = refs[steps + 5 :]
    stride = n_refs[0].shape[0]
    cols = heads * QROWS
    width = ns_ref.shape[1]
    o_ref[...] = jnp.zeros_like(o_ref)
    lse_ref[...] = jnp.zeros_like(lse_ref)
    used = kstart[items]

    @pl.when(pl.program_id(0) == 0)
    def _():
        def one_item(item, size, blocks):
            def one_unit(turn, unit, none):
                entry = (4 * turn + unit) * items + item
                count, source, target = kcnt[entry], koff[entry] - turn * stride, kdst[entry]

                def step(part, none):
                    src = pl.ds(pl.multiple_of(source + 64 * part, 16), 64)
                    dst = pl.ds(pl.multiple_of(target + 64 * part, 16), 64)
                    ns_ref[dst, :] = n_refs[turn][src, :]
                    return none

                return lax.fori_loop(0, (count + 63) // 64, step, none)

            for turn in range(steps):
                lax.fori_loop(0, 4, functools.partial(one_unit, turn), 0)
            end = kstart[item] + klen[item]

            def clear(part, none):
                tail = pl.ds(pl.multiple_of(end + 64 * part, 16), 64)
                ns_ref[tail, :] = jnp.zeros((64, width), BF16)
                return none

            lax.fori_loop(0, (kstart[item + 1] - end + 63) // 64 + 1, clear, 0)

        for_items(items, klen, one_item)

        def clear(part, none):
            tail = pl.ds(pl.multiple_of(used + 64 * part, 16), 64)
            ns_ref[tail, :] = jnp.zeros((64, width), BF16)
            return none

        lax.fori_loop(0, (ns_ref.shape[0] - used) // 64, clear, 0)

    def project(block, none):
        here = pl.ds(pl.multiple_of(block * ROWS, ROWS), ROWS)
        rows = ns_ref[here, :]
        ks_ref[here, :] = jnp.dot(rows, wk_ref[...], preferred_element_type=F32).astype(BF16)
        vs_ref[here, :] = jnp.dot(rows, wv_ref[...], preferred_element_type=F32).astype(BF16)
        return none

    lax.fori_loop(0, (used + ROWS - 1) // ROWS, project, 0)

    def one_item(item, size, blocks):
        def some_queries(place, count):
            wide = count * cols
            rows = pl.ds(pl.multiple_of(place * QROWS, QROWS), count * QROWS)
            block = q_ref[rows, :]
            queries = jnp.concatenate(
                [spread(block[n * QROWS : (n + 1) * QROWS], heads) for n in range(count)], axis=0
            )
            top, total, acc = top_ref.at[:, :wide], total_ref.at[:, :wide], acc_ref.at[:wide]
            top[...] = jnp.full((8, wide), NEG, F32)
            total[...] = jnp.zeros((8, wide), F32)
            acc[...] = jnp.zeros((wide, heads * HEAD), F32)

            def step(number, none):
                here = pl.ds(pl.multiple_of(kstart[item] + number * size, 16), size)
                scores = lax.dot_general(
                    ks_ref[here, :], queries, NT, preferred_element_type=F32
                ) + lanes(bias_ref[here, :], wide)
                best = jnp.max(jnp.max(scores.reshape(size // 8, 8, wide), axis=0), axis=0)
                old = top[...]
                best = jnp.maximum(old, jnp.broadcast_to(best[None], (8, wide)))
                top[...] = best
                shrink = jnp.exp(old - best)
                weights = jnp.exp(scores - best[:1])
                total[...] = total[...] * shrink + jnp.sum(
                    weights.reshape(size // 8, 8, wide), axis=0
                )
                acc[...] = acc[...] * as_column(shrink) + lax.dot_general(
                    weights.astype(BF16),
                    vs_ref[here, :],
                    (((0,), (0,)), ((), ())),
                    preferred_element_type=F32,
                )
                return none

            lax.fori_loop(0, blocks, step, 0)
            summed = jnp.broadcast_to(jnp.sum(total[...], axis=0, keepdims=True), (8, wide))
            lse = top[...] + jnp.log(summed)
            out = acc[...] * as_column(1.0 / summed)
            for n in range(count):
                part = slice(n * cols, (n + 1) * cols)
                lse_ref[pl.ds(place + n, 1), :] = lse[:1, part]
                o_ref[pl.ds(pl.multiple_of((place + n) * QROWS, QROWS), QROWS), :] = gathered(
                    out[part], heads
                )

        query_blocks(qfirst[item], qcount[item], some_queries)

    for_items(items, klen, one_item)


def attend_back_kernel(
    heads, units, items,
    koff, kcnt, kdst, kstart, klen, qfirst, qcount,
    q_ref, do_ref, o_ref, lse_ref, ks_ref, vs_ref, wk_ref, wv_ref, ns_ref, bias_ref,
    dq_ref, gk_ref, gv_ref, dn_ref,
    spread_q, spread_do, delta, dq_acc, dk_acc, dv_acc, gk_acc, gv_acc, dn_acc,
):
    feats = heads * HEAD
    cols = heads * QROWS
    flip = (((0,), (0,)), ((), ()))
    dq_ref[...] = jnp.zeros_like(dq_ref)
    gk_acc[...] = jnp.zeros_like(gk_acc)
    gv_acc[...] = jnp.zeros_like(gv_acc)
    used = qfirst[items - 1] + qcount[items - 1]

    @pl.when(pl.program_id(0) == 0)
    def _():
        dn_acc[...] = jnp.zeros_like(dn_acc)

    def prepare(place, none):
        rows = pl.ds(pl.multiple_of(place * QROWS, QROWS), QROWS)
        grads = do_ref[rows, :]
        spread_q[place] = spread(q_ref[rows, :], heads)
        spread_do[place] = spread(grads, heads)
        product = spread(grads.astype(F32) * o_ref[rows, :], heads)
        delta[place] = lax.dot_general(
            jnp.ones((8, feats), F32), product, NT, precision=HIGH, preferred_element_type=F32
        )
        dq_acc[place] = jnp.zeros((cols, feats), F32)
        return none

    lax.fori_loop(0, used, prepare, 0)

    def one_item(item, size, blocks):
        def one_block(number, none):
            here = pl.ds(pl.multiple_of(kstart[item] + number * size, 16), size)
            dk_acc[:size] = jnp.zeros((size, feats), F32)
            dv_acc[:size] = jnp.zeros((size, feats), F32)

            def some_queries(place, count):
                wide = count * cols
                spot = pl.ds(place, count)
                queries = spread_q[spot].reshape(wide, feats)
                grads = spread_do[spot].reshape(wide, feats)
                row = [lse_ref[pl.ds(place + n, 1), :] for n in range(count)]
                log_total = jnp.concatenate(row, axis=1)
                shift = jnp.concatenate([delta[place + n, :1, :] for n in range(count)], axis=1)
                keys = ks_ref[here, :]
                scores = lax.dot_general(keys, queries, NT, preferred_element_type=F32)
                weights = jnp.exp(scores + lanes(bias_ref[here, :], wide) - log_total)
                slopes = lax.dot_general(vs_ref[here, :], grads, NT, preferred_element_type=F32)
                score_grads = (weights * (slopes - shift)).astype(BF16)
                dv_acc[:size] += jnp.dot(weights.astype(BF16), grads, preferred_element_type=F32)
                dk_acc[:size] += jnp.dot(score_grads, queries, preferred_element_type=F32)
                part = lax.dot_general(score_grads, keys, flip, preferred_element_type=F32)
                dq_acc[spot] += part.reshape(count, cols, feats)

            query_blocks(qfirst[item], qcount[item], some_queries)
            dk = dk_acc[:size].astype(BF16)
            dv = dv_acc[:size].astype(BF16)
            dn_acc[here, :] += (
                lax.dot_general(dk, wk_ref[...], NT, preferred_element_type=F32)
                + lax.dot_general(dv, wv_ref[...], NT, preferred_element_type=F32)
            ).astype(dn_acc.dtype)
            rows = ns_ref[here, :]
            gk_acc[...] += lax.dot_general(rows, dk, flip, preferred_element_type=F32)
            gv_acc[...] += lax.dot_general(rows, dv, flip, preferred_element_type=F32)
            return none

        lax.fori_loop(0, jnp.where(qcount[item] > 0, blocks, 0), one_block, 0)

    for_items(items, klen, one_item)

    def finish(place, none):
        rows = pl.ds(pl.multiple_of(place * QROWS, QROWS), QROWS)
        scale = 1.0 / math.sqrt(HEAD)
        dq_ref[rows, :] = (gathered(dq_acc[place], heads) * scale).astype(BF16)
        return none

    lax.fori_loop(0, used, finish, 0)
    gk_ref[...] = gk_acc[...].astype(BF16)
    gv_ref[...] = gv_acc[...].astype(BF16)

    @pl.when(pl.program_id(0) == pl.num_programs(0) - 1)
    def _():
        dn_ref[...] = jnp.zeros_like(dn_ref)

        def one_unit(unit, none):
            def one_item(item, none):
                entry = unit * items + item
                count, source, target = kcnt[entry], koff[entry], kdst[entry]

                def step(part, none):
                    src = pl.ds(pl.multiple_of(source + 64 * part, 16), 64)
                    dst = pl.ds(pl.multiple_of(target + 64 * part, 16), 64)
                    dn_ref[src, :] = dn_acc[dst, :].astype(BF16)
                    return none

                return lax.fori_loop(0, (count + 63) // 64, step, none)

            return lax.fori_loop(0, items, one_item, none)

        lax.fori_loop(0, units, one_unit, 0)


def attend(tables, query, bias, key_weight, value_weight, norms, units, items, heads):
    feats = heads * HEAD
    cols = heads * QROWS
    width = query.shape[1]
    groups = width // feats
    blocks8 = (query.shape[0] // QROWS + 7) // 8 * 8
    sorted_keys = bias.shape[0]
    once = pl.Buffered(1) if units > 16 else None

    def part(rows, columns=feats):
        return pl.BlockSpec((rows, columns), lambda group, *_: (0, group), pipeline_mode=once)

    def whole(rows, columns):
        return pl.BlockSpec(
            (rows, columns), lambda group, *_: (0, 0), pipeline_mode=pl.Buffered(1)
        )

    return pl.pallas_call(
        functools.partial(attend_kernel, heads, units, items),
        grid_spec=pltpu.PrefetchScalarGridSpec(
            num_scalar_prefetch=7,
            grid=(groups,),
            in_specs=[part(query.shape[0]), whole(sorted_keys, 128), part(width), part(width)]
            + [whole(*norm.shape) for norm in norms],
            out_specs=[
                part(query.shape[0]),
                part(blocks8, cols),
                whole(sorted_keys, width),
                part(sorted_keys),
                part(sorted_keys),
            ],
            scratch_shapes=[
                pltpu.VMEM((2 * cols, feats), F32),
                pltpu.VMEM((8, 2 * cols), F32),
                pltpu.VMEM((8, 2 * cols), F32),
            ],
        ),
        out_shape=[
            jax.ShapeDtypeStruct(query.shape, F32),
            jax.ShapeDtypeStruct((blocks8, groups * cols), F32),
            jax.ShapeDtypeStruct((sorted_keys, width), BF16),
            jax.ShapeDtypeStruct((sorted_keys, width), BF16),
            jax.ShapeDtypeStruct((sorted_keys, width), BF16),
        ],
        compiler_params=pltpu.CompilerParams(vmem_limit_bytes=VMEM),
        name="attend",
    )(*tables, query, bias, key_weight, value_weight, *norms)


def attend_back(
    tables, query, grads, outputs, lse, ks, vs, key_weight, value_weight, ns, bias,
    key_rows, units, items, heads,
):
    feats = heads * HEAD
    cols = heads * QROWS
    rows, width = query.shape
    groups = width // feats
    blocks = rows // QROWS
    once = pl.Buffered(1) if units > 16 else None

    def part(rows, columns=feats):
        return pl.BlockSpec((rows, columns), lambda group, *_: (0, group), pipeline_mode=once)

    def whole(rows, columns):
        return pl.BlockSpec(
            (rows, columns), lambda group, *_: (0, 0), pipeline_mode=pl.Buffered(1)
        )

    return pl.pallas_call(
        functools.partial(attend_back_kernel, heads, units, items),
        grid_spec=pltpu.PrefetchScalarGridSpec(
            num_scalar_prefetch=7,
            grid=(groups,),
            in_specs=[
                part(rows),
                part(rows),
                part(rows),
                part(lse.shape[0], cols),
                part(ks.shape[0]),
                part(ks.shape[0]),
                part(width),
                part(width),
                whole(*ns.shape),
                whole(*bias.shape),
            ],
            out_specs=[part(rows), part(width), part(width), whole(key_rows, width)],
            scratch_shapes=[
                pltpu.VMEM((blocks, cols, feats), BF16),
                pltpu.VMEM((blocks, cols, feats), BF16),
                pltpu.VMEM((blocks, 8, cols), F32),
                pltpu.VMEM((blocks, cols, feats), F32),
                pltpu.VMEM((SPARE_KEYS, feats), F32),
                pltpu.VMEM((SPARE_KEYS, feats), F32),
                pltpu.VMEM((width, feats), F32),
                pltpu.VMEM((width, feats), F32),
                pltpu.VMEM(ns.shape, BF16),
            ],
        ),
        out_shape=[
            jax.ShapeDtypeStruct(query.shape, BF16),
            jax.ShapeDtypeStruct((width, width), BF16),
            jax.ShapeDtypeStruct((width, width), BF16),
            jax.ShapeDtypeStruct((key_rows, width), BF16),
        ],
        compiler_params=pltpu.CompilerParams(vmem_limit_bytes=VMEM),
        name="attend_back",
    )(*tables, query, grads, outputs, lse, ks, vs, key_weight, value_weight, ns, bias)


@functools.cache
def most_rows(cycle_size, item_count):
    rows = np.arange(SLOTS)[:, None] * cycle_size + np.arange(cycle_size)
    most_keys = most_unit = most_queries = 0
    lists = [()]
    while lists:
        heights = lists.pop()
        if len(heights) < item_count:
            for height in (24, 30):
                if sum(heights) + height <= SLOTS * cycle_size:
                    lists.append(heights + (height,))
        if not heights:
            continue
        ends = np.cumsum(heights)
        number = np.searchsorted(ends, rows, side="right")
        wide = np.array([24 if height == 24 else ROWW for height in heights] + [0])[number]
        kinds = np.arange(len(heights))
        counts = [((number == kind) * wide) for kind in kinds] + [ROWW - wide]
        counts = np.stack(counts)

        def rounded(values, align):
            return -(-values // align) * align

        units = rounded(counts.reshape(len(counts), 2, HALF, cycle_size).sum(2), 16)
        most_unit = max(most_unit, units.sum(0).max())
        keys = units.sum((1, 2))
        keys = rounded(keys[:-1], KEYS).sum() + rounded(keys[-1], SPARE_KEYS)
        most_keys = max(most_keys, keys)
        most_queries = max(most_queries, rounded(counts.sum(1), QROWS).sum(0).max())
    return int(most_keys), int(most_unit), int(most_queries)


def passed(value, axis, target):
    pairs = [(source, target(source)) for source in range(lax.axis_size(axis))]
    return lax.ppermute(value, axis, pairs)


def passed_along(value, axis, steps):
    count = lax.axis_size(axis)
    return passed(value, axis, lambda source: (source + steps) % count)


def to_sibling(value):
    return passed(value, "blk", lambda source: source ^ 1)


def gelu_tanh(values):
    return (
        0.5
        * values
        * (1.0 + jnp.tanh(0.7978845608028654 * (values + 0.044715 * values * values * values)))
    )


def gelu_back(values, gradient):
    return jax.vjp(gelu_tanh, values)[1](gradient)[0]


def layer_norm(hidden, norm_gain, norm_bias):
    centred = hidden - jnp.mean(hidden, axis=-1, keepdims=True)
    spread_now = jnp.mean(centred * centred, axis=-1, keepdims=True)
    return centred * lax.rsqrt(spread_now + EPS) * norm_gain + norm_bias


def row_facts(lengths, row_ids):
    item_count = lengths.shape[0]
    heights = jnp.where(lengths == 1200, 30, jnp.where(lengths == 576, 24, 0)).astype(jnp.int32)
    widths = jnp.where(lengths == 1200, 40, 24).astype(jnp.int32)
    upto = jnp.arange(item_count)[None, :] <= jnp.arange(item_count)[:, None]
    ends = jnp.sum(jnp.where(upto, heights[None, :], 0), axis=1)
    number = jnp.sum((ends <= row_ids[..., None]).astype(jnp.int32), axis=-1)
    number = jnp.where(row_ids < 0, item_count, number)
    pick = number[..., None] == jnp.arange(item_count, dtype=jnp.int32)
    start = jnp.sum(jnp.where(pick, ends - heights, 0), axis=-1)
    height = jnp.sum(jnp.where(pick, heights, 0), axis=-1)
    width = jnp.sum(jnp.where(pick, widths, 0), axis=-1)
    return number, pick, row_ids - start, height, width


def tap_masks(local_row, height, width):
    column = jnp.arange(ROWW, dtype=jnp.int32)
    is_real = column[None, :] < width[:, None]
    all_masks = []
    for row_step in (-1, 0, 1):
        rows_fine = (local_row + row_step >= 0) & (local_row + row_step < height)
        for col_step in (-1, 0, 1):
            cols_fine = (column + col_step >= 0)[None, :] & (
                column[None, :] + col_step < width[:, None]
            )
            all_masks.append(is_real & rows_fine[:, None] & cols_fine)
    return is_real, all_masks


def segments(number, width, item_count, align):
    slots = number.shape[1]
    kinds = jnp.arange(item_count + 1, dtype=jnp.int32)
    here = number[:, :, None] == kinds
    counts = jnp.sum(jnp.where(here, width[:, :, None], 0), axis=1)
    spare = jnp.sum(ROWW - width, axis=1)
    counts = jnp.where(kinds == item_count, spare[:, None], counts)
    rounded = (counts + align - 1) // align * align
    before = kinds[:, None] < kinds[None, :]
    offsets = jnp.sum(jnp.where(before, rounded[:, :, None], 0), axis=1)
    own_offset = jnp.sum(jnp.where(here, offsets[:, None, :], 0), axis=2)
    earlier = jnp.arange(slots)[None, :] < jnp.arange(slots)[:, None]
    same = earlier & (number[:, :, None] == number[:, None, :])
    rank = jnp.sum(jnp.where(same, width[:, None, :], 0), axis=2)
    spare_rank = jnp.sum(jnp.where(earlier, ROWW - width[:, None, :], 0), axis=2)
    column = jnp.arange(ROWW, dtype=jnp.int32)
    place = jnp.where(
        column < width[:, :, None],
        (own_offset + rank)[:, :, None] + column,
        (offsets[:, -1:] + spare_rank - width)[:, :, None] + column,
    )
    return counts, rounded, offsets, place


def one_hot_rows(place, rows):
    flat = place.reshape(place.shape[0], 1, -1)
    return (flat == jnp.arange(rows, dtype=jnp.int32)[None, :, None]).astype(BF16)


def side_shift(values, col_step):
    if col_step == 0:
        return values
    empty_col = jnp.zeros_like(values[:, :1])
    if col_step < 0:
        return jnp.concatenate([empty_col, values[:, :-1]], axis=1)
    return jnp.concatenate([values[:, 1:], empty_col], axis=1)


def row_shift(values, row_step):
    empty_row = jnp.zeros_like(values[:1])
    if row_step == 0:
        return values
    if row_step < 0:
        return jnp.concatenate([empty_row, values[:-1]], axis=0)
    return jnp.concatenate([values[1:], empty_row], axis=0)


def tap_matrix(values, all_masks):
    tap_parts = []
    for row_step in (-1, 0, 1):
        for col_step in (-1, 0, 1):
            tap_parts.append(
                jnp.where(
                    all_masks[len(tap_parts)][:, :, None],
                    side_shift(row_shift(values, row_step), col_step),
                    jnp.zeros((), values.dtype),
                )
            )
    joined = jnp.concatenate(tap_parts, axis=2)
    return joined.reshape(-1, joined.shape[2])


def flipped(kernel):
    channels = kernel.shape[1]
    return jnp.transpose(kernel.reshape(9, channels, channels)[::-1], (0, 2, 1)).reshape(
        9 * channels, channels
    )


def from_above(values, cycle_pos):
    got = passed_along(values, "blk", 1)
    empty_row = jnp.zeros_like(values[:1])
    return jnp.where(cycle_pos == 0, jnp.concatenate([empty_row, got[:-1]], axis=0), got)


def from_below(values, cycle_pos, cycle_size):
    got = passed_along(values, "blk", -1)
    empty_row = jnp.zeros_like(values[:1])
    return jnp.where(
        cycle_pos == cycle_size - 1, jnp.concatenate([got[1:], empty_row], axis=0), got
    )


def upsample_forward(values, all_masks, cycle_pos, cycle_size):
    center = values.astype(F32)
    row_above = from_above(values, cycle_pos)
    row_below = from_below(values, cycle_pos, cycle_size)
    upper_value = jnp.where(all_masks[1][:, :, None], row_above, values).astype(F32)
    lower_value = jnp.where(all_masks[7][:, :, None], row_below, values).astype(F32)
    pieces = []
    for half_rows in (0.75 * center + 0.25 * upper_value, 0.75 * center + 0.25 * lower_value):
        left_value = jnp.where(all_masks[3][:, :, None], side_shift(half_rows, -1), half_rows)
        right_value = jnp.where(all_masks[5][:, :, None], side_shift(half_rows, 1), half_rows)
        pieces.append(0.75 * half_rows + 0.25 * left_value)
        pieces.append(0.75 * half_rows + 0.25 * right_value)
    joined = jnp.concatenate(pieces, axis=2)
    return joined.reshape(-1, joined.shape[2])


def upsample_back(gradient, all_masks, cycle_pos, cycle_size):
    channels = gradient.shape[2] // 4
    left_fine = all_masks[3][:, :, None]
    right_fine = all_masks[5][:, :, None]
    up_fine = all_masks[1][:, :, None]
    down_fine = all_masks[7][:, :, None]
    halves = []
    for half in (0, 1):
        left_part = gradient[:, :, 2 * half * channels : (2 * half + 1) * channels].astype(F32)
        right_part = gradient[:, :, (2 * half + 1) * channels : (2 * half + 2) * channels].astype(
            F32
        )
        side = jnp.where(right_fine, side_shift(left_part, 1), 0.0)
        side = side + jnp.where(left_fine, 0.0, left_part)
        side = side + jnp.where(left_fine, side_shift(right_part, -1), 0.0)
        side = side + jnp.where(right_fine, 0.0, right_part)
        halves.append(0.75 * (left_part + right_part) + 0.25 * side)
    upper, lower = halves
    upper_next = from_below(upper.astype(BF16), cycle_pos, cycle_size).astype(F32)
    lower_prev = from_above(lower.astype(BF16), cycle_pos).astype(F32)
    rows = jnp.where(down_fine, upper_next, lower) + jnp.where(up_fine, lower_prev, upper)
    return 0.75 * (upper + lower) + 0.25 * rows


def first_slot(begin, device, cycle_size):
    return -((device - begin) // cycle_size)


def to_windows(values, cycle_pos, cycle_size):
    window = SLOTS + 2 * REACH
    many = -(-window // cycle_size)
    spare = many + 1
    padded = jnp.pad(values, ((spare, spare), (0, 0), (0, 0)))
    sends = []
    for target in range(cycle_size):
        slot = first_slot(SLOTS * target - REACH, cycle_pos, cycle_size) + spare
        sends.append(lax.dynamic_slice_in_dim(padded, slot, many, axis=0))
    got = lax.all_to_all(jnp.stack(sends), "blk", 0, 0)
    got = jnp.swapaxes(got, 0, 1)
    begin = SLOTS * cycle_pos - REACH
    turn = begin - (begin // cycle_size) * cycle_size
    got = lax.dynamic_slice_in_dim(jnp.concatenate([got, got], axis=1), turn, cycle_size, axis=1)
    return got.reshape((many * cycle_size,) + values.shape[1:])[:window]


def from_windows(values, cycle_pos, cycle_size):
    many = -(-SLOTS // cycle_size)
    padded = jnp.pad(values, ((0, many * cycle_size), (0, 0), (0, 0)))
    begin = SLOTS * cycle_pos
    sends = []
    for target in range(cycle_size):
        slot = first_slot(begin, target, cycle_size)
        for extra in range(many):
            row = (slot + extra) * cycle_size + target - begin
            sends.append(lax.dynamic_slice_in_dim(padded, row, 1, axis=0))
    sends = jnp.concatenate(sends, axis=0).reshape((cycle_size, many) + values.shape[1:])
    got = lax.all_to_all(sends, "blk", 0, 0).reshape((cycle_size * many,) + values.shape[1:])
    rows = []
    for slot in range(SLOTS):
        row = slot * cycle_size + cycle_pos
        source = row // SLOTS
        extra = slot - first_slot(source * SLOTS, cycle_pos, cycle_size)
        rows.append(lax.dynamic_slice_in_dim(got, source * many + extra, 1, axis=0))
    return jnp.concatenate(rows, axis=0)


def dot32(left, right, **more):
    return jnp.dot(left, right, preferred_element_type=F32, **more)


def dot_t(left, right):
    return lax.dot_general(left, right, NT, preferred_element_type=F32)


def t_dot(left, right):
    return lax.dot_general(left, right, (((0,), (0,)), ((), ())), preferred_element_type=F32)


def halved(values, device, bit, axis, pairs_axis):
    half = values.shape[axis] // 2
    mine = (device >> bit) & 1
    keep = lax.dynamic_slice_in_dim(values, mine * half, half, axis=axis)
    send = lax.dynamic_slice_in_dim(values, (1 - mine) * half, half, axis=axis)
    got = passed(send, pairs_axis, lambda source: source ^ (1 << bit))
    return (keep.astype(F32) + got.astype(F32)).astype(BF16)


def added_over_group(shares, order, cycle_pos, dp_pos):
    cycle_size, rows, width = shares.shape
    chips = cycle_size // 2
    core = cycle_pos % 2
    paired = shares.reshape(chips, 2, rows, width)
    keep = lax.dynamic_index_in_dim(paired, core, 1, keepdims=False)
    send = lax.dynamic_index_in_dim(paired, 1 - core, 1, keepdims=False)
    values = (keep.astype(F32) + to_sibling(send).astype(F32)).astype(BF16)
    for bit in order:
        values = halved(values, dp_pos, bit, 1, "dp")
    return values


def added_over_chips(values, chip):
    chips = values.shape[0]

    def block(offset):
        return lax.dynamic_index_in_dim(
            values, (chip + offset) % chips, 0, keepdims=False
        ).astype(F32)

    moving = block(-1)
    for step in range(2, chips + 1):
        moving = passed_along(moving.astype(BF16), "blk", 2).astype(F32) + block(-step)
    return moving.astype(BF16)


def gathered_over_groups(values, dp_pos):
    groups = lax.axis_size("dp")
    bits = groups.bit_length() - 1
    half = values.shape[0] // 2
    both = []
    for part, order in ((values[:half], range(bits)), (values[half:], range(bits - 1, -1, -1))):
        held = part[(None,) * bits]
        for bit in order:
            axis = bits - 1 - bit
            got = passed(held, "dp", lambda source, bit=bit: source ^ (1 << bit))
            mine = (dp_pos >> bit) & 1
            held = jnp.where(
                mine == 0,
                jnp.concatenate([held, got], axis=axis),
                jnp.concatenate([got, held], axis=axis),
            )
        both.append(held.reshape((groups,) + part.shape))
    return jnp.concatenate(both, axis=1)


def reduced(gradients, cycle_size, cycle_pos, dp_pos):
    groups = lax.axis_size("dp")
    bits = groups.bit_length() - 1
    orders, parts = [], []
    for number, gradient in enumerate(gradients):
        order = list(range(bits))
        if number % 2:
            order.reverse()
        orders.append(order)
        parts.append(added_over_group(gradient, order, cycle_pos, dp_pos))
    chips = cycle_size // 2
    joined = jnp.concatenate([part.reshape(chips, -1, 256) for part in parts], axis=1)
    whole = gathered_over_groups(added_over_chips(joined, cycle_pos // 2), dp_pos)
    out, place = [], 0
    for gradient, order in zip(gradients, orders):
        rows, width = gradient.shape[1:]
        size = rows * width // groups // 256
        pieces = []
        for turn in range(groups):
            device = sum(((turn >> (bits - 1 - index)) & 1) << bit for index, bit in enumerate(order))
            pieces.append(whole[device, place : place + size].reshape(rows // groups, width))
        out.append(jnp.concatenate(pieces, axis=0).astype(F32))
        place += size
    return out


def shards(
    tokens,
    item_lengths,
    dataset_ids,
    dataset_table,
    norm1_gain,
    norm1_bias,
    query_weight,
    key_weight,
    value_weight,
    out_weight,
    norm2_gain,
    norm2_bias,
    fc1_weight,
    fc2_weight,
    project_weight,
    unit1_first,
    unit1_second,
    unit2_first,
    unit2_second,
    output_weight,
    block_cotangent,
    merged_cotangent,
):
    cycle_size = lax.axis_size("blk")
    cycle_pos = lax.axis_index("blk")
    chips = cycle_size // 2
    chip, core = cycle_pos // 2, cycle_pos % 2
    lengths = item_lengths[0]
    item_count = lengths.shape[0]
    kinds = item_count + 1
    width_model = tokens.shape[1]
    heads = 4 if cycle_size <= 8 else 2
    half_tokens = HALF * ROWW
    token_count = tokens.shape[0]

    ahead, behind = tokens[:half_tokens], tokens[half_tokens:]
    arrivals = []
    for step in range(chips):
        if step:
            ahead = passed_along(ahead, "blk", 2)
            behind = passed_along(behind, "blk", -2)
        mine = jnp.concatenate([ahead, behind], axis=0)
        arrivals.append((mine, to_sibling(mine)))

    slots = jnp.arange(SLOTS, dtype=jnp.int32)
    number, item_pick, local_row, height, width = row_facts(lengths, slots * cycle_size + cycle_pos)
    is_real, all_masks = tap_masks(local_row, height, width)
    unit_rows = []
    for step in range(chips):
        for other in (0, 1):
            for half, turn in ((0, -step), (1, step)):
                source = 2 * ((chip + turn) % chips) + (core ^ other)
                unit_rows.append(slots[half * HALF : (half + 1) * HALF] * cycle_size + source)
    unit_rows = jnp.stack(unit_rows)
    units = 4 * chips
    unit_number, unit_pick, _, _, unit_width = row_facts(lengths, unit_rows)
    most_keys, unit_size, query_rows = most_rows(cycle_size, item_count)
    kcnt, krounded, koff, kplace = segments(unit_number, unit_width, item_count, 16)
    unit_spots = jnp.arange(units, dtype=jnp.int32)
    step_rows = 4 * unit_size + 64
    koff = koff + (unit_spots // 4 * step_rows + unit_spots % 4 * unit_size)[:, None]
    klen = jnp.sum(krounded, axis=0)
    size = jnp.where(jnp.arange(kinds) == kinds - 1, SPARE_KEYS, KEYS)
    klen_up = (klen + size - 1) // size * size
    before = jnp.arange(kinds)[:, None] < jnp.arange(kinds + 1)[None, :]
    kstart = jnp.sum(jnp.where(before, klen_up[:, None], 0), axis=0)
    unit_before = jnp.arange(units)[:, None] < jnp.arange(units)[None, :]
    kdst = kstart[None, :kinds] + jnp.sum(
        jnp.where(unit_before[:, :, None], krounded[:, None, :], 0), axis=0
    )
    key_rows = chips * step_rows
    sorted_keys = (most_keys + 128 + ROWS - 1) // ROWS * ROWS
    spot = jnp.arange(sorted_keys, dtype=jnp.int32)[:, None]
    filled = (spot >= kdst.reshape(1, -1)) & (spot < (kdst + kcnt).reshape(1, -1))
    bias = jnp.where(jnp.any(filled, axis=1), 0.0, NEG)
    bias = jnp.broadcast_to(bias[:, None], (sorted_keys, 128)).astype(F32)
    _, qrounded, qoff, qplace = segments(number[None], width[None], item_count, QROWS)
    tables = (
        koff.reshape(-1),
        kcnt.reshape(-1),
        kdst.reshape(-1),
        kstart,
        klen,
        qoff[0] // QROWS,
        qrounded[0] // QROWS,
    )
    sort_units = one_hot_rows(kplace, unit_size)
    sort_queries = one_hot_rows(qplace, query_rows)[0]
    table_rows = dataset_table.shape[0]

    def dataset_one_hot(pick, widths):
        dataset = jnp.sum(jnp.where(pick, dataset_ids[0], 0), axis=-1)
        real = jnp.arange(ROWW, dtype=jnp.int32) < widths[..., None]
        hot = real[..., None] & (
            dataset[..., None, None] == jnp.arange(table_rows, dtype=jnp.int32)
        )
        return hot.astype(F32).reshape(-1, table_rows)

    def with_dataset(values, hot):
        return values.astype(F32) + jnp.dot(hot, dataset_table, precision=HIGH)

    onehot = dataset_one_hot(item_pick, width)

    sorted_norms = []
    for step in range(chips):
        here = slice(4 * step, 4 * step + 4)
        hot = dataset_one_hot(unit_pick[here], unit_width[here])
        values = with_dataset(jnp.concatenate(arrivals[step], axis=0), hot)
        normed = layer_norm(values, norm1_gain, norm1_bias).astype(BF16)
        normed = jnp.einsum(
            "upt,utd->upd",
            sort_units[here],
            normed.reshape(4, half_tokens, width_model),
            preferred_element_type=F32,
        ).astype(BF16)
        normed = jnp.pad(normed.reshape(4 * unit_size, width_model), ((0, 64), (0, 0)))
        sorted_norms.append(normed)

    stream_start = with_dataset(tokens, onehot)
    normed_one = layer_norm(stream_start, norm1_gain, norm1_bias).astype(BF16)
    query_norm = dot32(sort_queries, normed_one).astype(BF16)
    query = (dot32(query_norm, query_weight) * (1.0 / math.sqrt(HEAD))).astype(BF16)
    outputs, lse, sorted_norm, ks, vs = attend(
        tables, query, bias, key_weight, value_weight, sorted_norms, units, kinds, heads
    )
    attended = t_dot(sort_queries, outputs.astype(BF16)).astype(BF16)

    def as_cells(flattened):
        return flattened.reshape(SLOTS, ROWW, flattened.shape[-1])

    after_attn = stream_start + dot32(attended, out_weight)
    normed_two = layer_norm(after_attn, norm2_gain, norm2_bias).astype(BF16)
    pre_act = dot32(normed_two, fc1_weight)
    hidden = gelu_tanh(pre_act).astype(BF16)
    block_out = (after_attn + dot32(hidden, fc2_weight)).astype(BF16)
    reassembled_own = dot32(block_out, project_weight).astype(BF16)

    mapped_grad_own = upsample_back(
        as_cells(merged_cotangent), all_masks, cycle_pos, cycle_size
    ).astype(BF16)
    channels = mapped_grad_own.shape[-1]
    arrived = to_windows(
        jnp.concatenate([as_cells(reassembled_own), mapped_grad_own], axis=2), cycle_pos, cycle_size
    )
    window = SLOTS + 2 * REACH
    _, _, w_row, w_height, w_width = row_facts(
        lengths, SLOTS * cycle_pos - REACH + jnp.arange(window, dtype=jnp.int32)
    )
    _, w_masks = tap_masks(w_row, w_height, w_width)
    reassembled = arrived[:, :, :channels].reshape(-1, channels).astype(F32)
    mapped_grad = arrived[:, :, channels:].reshape(-1, channels)
    middle = slice(REACH * ROWW, (REACH + SLOTS) * ROWW)

    def grid(flattened):
        return flattened.reshape(window, ROWW, channels)

    def stencil(values, kernel):
        taps_now = tap_matrix(grid(values), w_masks)
        return taps_now[middle], dot32(taps_now, kernel)

    def stencil_back(gradient, kernel):
        return dot32(tap_matrix(grid(gradient), w_masks), flipped(kernel))

    taps_one, conv_one = stencil(gelu_tanh(reassembled).astype(BF16), unit1_first)
    taps_two, conv_two = stencil(gelu_tanh(conv_one).astype(BF16), unit1_second)
    merged_one = reassembled + conv_two
    taps_three, conv_three = stencil(gelu_tanh(merged_one).astype(BF16), unit2_first)
    taps_four, conv_four = stencil(gelu_tanh(conv_three).astype(BF16), unit2_second)
    merged_low = (merged_one + conv_four).astype(BF16)[middle]
    mapped = dot32(merged_low, output_weight).astype(BF16)
    output_grad = t_dot(merged_low, mapped_grad[middle])
    merged_two_grad = dot_t(mapped_grad, output_weight)
    conv_four_grad = merged_two_grad.astype(BF16)
    unit2_second_grad = t_dot(taps_four, conv_four_grad[middle])
    conv_three_grad = gelu_back(conv_three, stencil_back(conv_four_grad, unit2_second)).astype(BF16)
    unit2_first_grad = t_dot(taps_three, conv_three_grad[middle])
    merged_one_grad = merged_two_grad + gelu_back(
        merged_one, stencil_back(conv_three_grad, unit2_first)
    )
    conv_two_grad = merged_one_grad.astype(BF16)
    unit1_second_grad = t_dot(taps_two, conv_two_grad[middle])
    conv_one_grad = gelu_back(conv_one, stencil_back(conv_two_grad, unit1_second)).astype(BF16)
    unit1_first_grad = t_dot(taps_one, conv_one_grad[middle])
    reassembled_grad = (
        merged_one_grad + gelu_back(reassembled, stencil_back(conv_one_grad, unit1_first))
    ).astype(BF16)[middle]

    returned = from_windows(
        jnp.concatenate([as_cells(reassembled_grad), as_cells(mapped)], axis=2),
        cycle_pos,
        cycle_size,
    )
    reassembled_grad = returned[:, :, :channels].reshape(-1, channels)
    merged = upsample_forward(returned[:, :, channels:], all_masks, cycle_pos, cycle_size).astype(
        BF16
    )

    project_grad = t_dot(block_out, reassembled_grad)
    block_grad = block_cotangent.astype(F32) + dot_t(reassembled_grad, project_weight)
    mlp_grad = block_grad.astype(BF16)
    fc2_grad = t_dot(hidden, mlp_grad)
    pre_grad = gelu_back(pre_act, dot_t(mlp_grad, fc2_weight)).astype(BF16)
    fc1_grad = t_dot(normed_two, pre_grad)
    normed_two_grad = dot_t(pre_grad, fc1_weight)
    norm_two_pull = jax.vjp(layer_norm, after_attn, norm2_gain, norm2_bias)[1]
    attn_side, norm2_gain_grad, norm2_bias_grad = norm_two_pull(normed_two_grad)
    after_grad = block_grad + attn_side
    branch_grad = after_grad.astype(BF16)
    out_proj_grad = t_dot(attended, branch_grad)
    attended_grad = dot_t(branch_grad, out_weight).astype(BF16)

    rows = width_model // cycle_size
    dp_pos = lax.axis_index("dp")

    def shared_out(*gradients):
        parts = []
        for gradient in gradients:
            parts.append(gradient.astype(BF16).reshape(cycle_size, -1, gradient.shape[-1]))
        return jnp.concatenate(parts, axis=1)

    early = reduced(
        [
            shared_out(
                unit1_first_grad,
                unit1_second_grad,
                unit2_first_grad,
                unit2_second_grad,
                output_grad,
                project_grad,
            ),
            shared_out(fc2_grad, out_proj_grad),
            shared_out(fc1_grad),
        ],
        cycle_size,
        cycle_pos,
        dp_pos,
    )
    unit_share = 9 * channels // cycle_size
    fc2_share = fc2_weight.shape[0] // cycle_size

    sorted_grad = dot32(sort_queries, attended_grad).astype(BF16)
    dq, key_grad, value_grad, unit_grad = attend_back(
        tables, query, sorted_grad, outputs, lse, ks, vs, key_weight, value_weight, sorted_norm,
        bias, key_rows, units, kinds, heads,
    )
    query_low = t_dot(sort_queries, dq).astype(BF16)
    query_grad = t_dot(normed_one, query_low)

    def unit_part(step):
        here = slice(step_rows * step, step_rows * step + 4 * unit_size)
        part = jnp.einsum(
            "upt,upd->utd",
            sort_units[4 * step : 4 * step + 4],
            unit_grad[here].reshape(4, unit_size, width_model),
            preferred_element_type=F32,
        )
        mine, other = part[:2], part[2:].astype(BF16)
        return mine + to_sibling(other).astype(F32)

    ahead = behind = None
    for step in range(chips - 1, -1, -1):
        part = unit_part(step)
        if ahead is None:
            ahead, behind = part[0], part[1]
        else:
            ahead = passed_along(ahead.astype(BF16), "blk", -2).astype(F32) + part[0]
            behind = passed_along(behind.astype(BF16), "blk", 2).astype(F32) + part[1]
    normed_one_grad = jnp.concatenate([ahead, behind], axis=0) + dot_t(query_low, query_weight)

    norm_one_pull = jax.vjp(layer_norm, stream_start, norm1_gain, norm1_bias)[1]
    start_side, norm1_gain_grad, norm1_bias_grad = norm_one_pull(normed_one_grad)
    tokens_grad = after_grad + start_side
    table_grad = jnp.dot(onehot.T, tokens_grad, precision=HIGH)
    table_split = jnp.swapaxes(table_grad.reshape(table_rows, cycle_size, rows), 0, 1)
    small = [table_split.reshape(cycle_size, -1)] + [
        gradient.reshape(cycle_size, -1)
        for gradient in (norm1_gain_grad, norm1_bias_grad, norm2_gain_grad, norm2_bias_grad)
    ]
    small = jnp.concatenate(small, axis=1).astype(BF16)
    small = jnp.pad(small, ((0, 0), (0, 32 * width_model - small.shape[1])))
    late = reduced(
        [
            jnp.concatenate(
                [
                    shared_out(query_grad, key_grad, value_grad),
                    small.reshape(cycle_size, 32, width_model),
                ],
                axis=1,
            )
        ],
        cycle_size,
        cycle_pos,
        dp_pos,
    )[0]
    small = late[3 * rows :].reshape(-1)
    table_size = table_rows * rows
    norms = [small[table_size + index * rows :][:rows] for index in range(4)]
    convs = early[0]
    return (
        block_out,
        merged,
        tokens_grad,
        small[:table_size].reshape(table_rows, rows),
        norms[0],
        norms[1],
        late[:rows],
        late[rows : 2 * rows],
        late[2 * rows : 3 * rows],
        early[1][fc2_share:],
        norms[2],
        norms[3],
        early[2],
        early[1][:fc2_share],
        convs[4 * unit_share + channels // cycle_size :],
        convs[:unit_share],
        convs[unit_share : 2 * unit_share],
        convs[2 * unit_share : 3 * unit_share],
        convs[3 * unit_share : 4 * unit_share],
        convs[4 * unit_share : 4 * unit_share + channels // cycle_size],
    )


def solution(mesh):
    split = P(("dp", "blk"), None)
    placed = (split, P("dp", None), P("dp", None)) + (P(),) * 17 + (split, split)
    rows, line = P("blk", None), P("blk")
    return jax.shard_map(
        shards,
        mesh=mesh,
        in_specs=placed,
        out_specs=(
            split, split, split, P(None, "blk"), line, line, rows, rows, rows, rows, line, line,
            rows, rows, rows, rows, rows, rows, rows, rows,
        ),
        check_vma=False,
    )
```

time: 1360 us -> 752 us (0.55)
  waiting for transfers between devices: 770 us -> 179 us
  matrix products: 300 us -> 89.8 us
  Pallas kernels: 0 us -> 173 us
  starting transfers between devices: 26.4 us -> 94.7 us
  other arithmetic: 136 us -> 95.9 us
  local copies, waits for them, and re-layouts: 88.8 us -> 107 us
  blocking collectives: 13.9 us -> 0 us
    reduce_scatter x12 -> x0, waiting for transfers between devices: 404 us -> none  [the longest x1 55.8 us: shards(): lax.psum_scatter(fc1_grad.astype(jnp.bfloat16), 'blk', scatter_dimension=...]
    dot_general x93 -> x45, matrix products: 299 us -> 88.9 us  [the longest x15 30.6 us: dot32(): return jnp.dot(left, right, preferred_element_type=F32, **more)]
    pallas_call x0 -> x2, Pallas kernels: none -> 173 us  [the longest x1 92.6 us: attend_back(): pl.pallas_call(functools.partial(attend_back_kernel, heads, units, items)...]
    psum x2 -> x0, waiting for transfers between devices: 108 us -> none  [the longest x1 73.5 us: shards(): lax.psum(shares[3].astype(jnp.bfloat16), 'dp').astype(jnp.float32)]
    ppermute x64 -> x50, waiting for transfers between devices: 258 us -> 159 us  [passed(): return lax.ppermute(value, axis, pairs)]
    ppermute x64 -> x50, starting transfers between devices: 25.6 us -> 87.6 us  [passed(): return lax.ppermute(value, axis, pairs)]
    while x217 -> x0, local copies, waits for them, and re-layouts: 40.1 us -> none
    reduce_sum x40 -> x25, other arithmetic: 28.4 us -> 8.34 us  [the longest x6 5.54 us: layer_norm(): spread_now = jnp.mean(centred * centred, axis=-1, keepdims=True)]
  transfers between devices with their start and end apart: 79 -> 52, of which waited for: 61 -> 27; matrix products, arithmetic and copies ran while one was open for 26% -> 21% of each run, Pallas kernels for 0% -> 12%
where the time goes in v1:
time: 752 us; the launch traced here: 746 us
  waiting for transfers between devices  179 us (24%)
  Pallas kernels  173 us (23%)
  local copies, waits for them, and re-layouts  107 us (14%)
  other arithmetic  95.9 us (13%)
  starting transfers between devices  94.7 us (13%)
  matrix products  89.8 us (12%)
    ppermute x50, waiting for transfers between devices, passed(): return lax.ppermute(value, axis, pairs)  159 us
    pallas_call x1, Pallas kernels, attend_back(): pl.pallas_call(functools.partial(attend_back_kernel, heads, units, items)...  92.6 us
    ppermute x50, starting transfers between devices, passed(): return lax.ppermute(value, axis, pairs)  87.6 us
    pallas_call x1, Pallas kernels, attend(): pl.pallas_call(functools.partial(attend_kernel, heads, units, items), gri...  80.8 us
    dot_general x15, matrix products, dot32(): return jnp.dot(left, right, preferred_element_type=F32, **more)  30.6 us
    dot_general x12, matrix products, t_dot(): lax.dot_general(left, right, (((0,), (0,)), ((), ())), preferred_element_...  24.7 us
    unnamed x326, local copies, waits for them, and re-layouts  23.5 us
    dot_general x5, matrix products, dot_t(): return lax.dot_general(left, right, NT, preferred_element_type=F32)  17.1 us
  transfers between devices with their start and end apart: 52, of which 27 were waited for; matrix products, arithmetic and copies ran while one was open for 21% of the time, Pallas kernels for 12%

profile of v1, /device:TPU:0, one launch (start us, length us, event | category | flops | bytes accessed | tf_op | source)
XLA Modules:
  0.0 745.9 jit_solution(14182782474801188045)
XLA Ops:
  1.2 2.1 fusion.165
  3.3 2.7 collective-permute-start.1
  35.9 3.6 multiply_convert_fusion.1.q_ref
  53.7 3.8 collective-permute-start.5
  57.5 2.7 fusion.123
  60.2 7.0 collective-permute-done.4
  67.2 5.2 collective-permute-done.5
  72.5 2.3 collective-permute-start.7
  78.5 7.3 collective-permute-done.7
  85.8 7.4 collective-permute-done.8
  93.4 2.6 fusion.148
  106.9 5.5 add_convert_fusion.1
  120.0 3.2 broadcast_in_dim.1025.bias_ref
  123.2 80.8 %attend.1 = (f32[704,768]{1,0:T(8,128)}, f32[16,768]{1,0:T(8,128)}, bf16[5120,768]{1,0:T(8,128)(2,1)}, bf16[5120,768]{1,0:T(8,128)(2,1)}, bf16[5120,768]{1,0:T(8,128)(2,1)}) custom-call(s32[80]{0:T(128)} %add.1579.koff, s32[80]{0:T(128)} %copy-done.100, s32[80]{0:T(128)} %copy-done.93, s32[6]{0:T(128)} %copy-done.99, s32[5]{0:T(128)} %copy-done.92, ...), custom_call_target="tpu_custom_call" | custom-call | tf_op jit(solution)/shard_map/attend/pallas_call | solution.py:318
  204.0 2.6 fusion.42
  208.5 5.1 fusion.151
  213.7 3.7 add_convert_fusion.9
  223.6 3.6 all-to-all-start
  241.1 11.1 %all-to-all-done = bf16[8,3,40,512]{3,2,1,0:T(8,128)(2,1)S(1)} async-done(((bf16[8,3,40,512]{3,2,1,0:T(8,128)(2,1)}), bf16[8,3,40,512]{3,2,1,0:T(8,128)(2,1)S(1)}, u32[]{:S(2)}, u32[]{:S(2)}) %all-to-all-start) | async-done | bytes 983072 | tf_op jit(solution)/shard_map/all_to_all | solution.py:639
  301.0 3.5 all-to-all-start.1
  304.6 2.4 constant_dynamic-update-slice_fusion.41
  314.1 8.6 %all-to-all-done.1 = bf16[8,2,40,512]{3,2,1,0:T(8,128)(2,1)S(1)} async-done(((bf16[8,2,40,512]{3,2,1,0:T(8,128)(2,1)}), bf16[8,2,40,512]{3,2,1,0:T(8,128)(2,1)S(1)}, u32[]{:S(2)}, u32[]{:S(2)}) %all-to-all-start.1) | async-done | bytes 655392 | tf_op jit(solution)/shard_map/all_to_all | solution.py:658
  323.6 2.2 convolution_convert_fusion.11
  327.4 11.2 %fusion.3 = bf16[480,3072]{1,0:T(8,128)(2,1)S(1)} fusion(f32[480,3072]{1,0:T(8,128)} %copy-done.132, bf16[3072,768]{1,0:T(8,128)(2,1)} %param.35, f32[480,768]{1,0:T(8,128)S(1)} %convert_add_fusion.8), kind=kOutput, calls=%fused_computation.9 | convolution fusion | flops 2300682240 | bytes 15040512 | tf_op jit(solution)/shard_map/dot_general | solution.py:673
  338.7 2.8 multiply_reduce_fusion.4
  341.6 4.9 convolution_convert_fusion
  350.0 3.6 convolution_convert_fusion.8.do_ref
  353.7 3.5 collective-permute-start.13
  358.0 3.4 dynamic-slice_bitcast_fusion
  361.4 3.2 dynamic-slice_bitcast_fusion.1
  364.6 92.6 %attend_back.1 = (bf16[704,768]{1,0:T(8,128)(2,1)}, bf16[768,768]{1,0:T(8,128)(2,1)}, bf16[768,768]{1,0:T(8,128)(2,1)}, bf16[4352,768]{1,0:T(8,128)(2,1)}) custom-call(s32[80]{0:T(128)} %add.1579.koff, s32[80]{0:T(128)} %copy-done.100, s32[80]{0:T(128)} %copy-done.93, s32[6]{0:T(128)} %copy-done.99, s32[5]{0:T(128)} %copy-done.92, ...), custom_call_target="tpu_custom_call" | custom-call | tf_op jit(solution)/shard_map/attend_back/pallas_call | solution.py:369
  457.2 3.2 fusion.161
  464.8 2.4 copy-done.125
  468.6 2.1 convolution_convert_fusion.7
  470.7 3.5 convolution_convert_fusion.1
  483.7 10.8 %collective-permute-done.15 = bf16[240,768]{1,0:T(8,128)(2,1)S(1)} collective-permute-done((bf16[240,768]{1,0:T(8,128)(2,1)}, bf16[240,768]{1,0:T(8,128)(2,1)S(1)}, u32[]{:S(2)}, u32[]{:S(2)}) %collective-permute-start.15) | collective-permute-done | bytes 368672 | tf_op jit(solution)/shard_map/ppermute | solution.py:444
  499.0 7.0 collective-permute-done.17
  506.0 8.9 %collective-permute-done.22 = bf16[240,768]{1,0:T(8,128)(2,1)S(1)} collective-permute-done((bf16[240,768]{1,0:T(8,128)(2,1)S(1)}, bf16[240,768]{1,0:T(8,128)(2,1)S(1)}, u32[]{:S(2)}, u32[]{:S(2)}) %collective-permute-start.22) | collective-permute-done | bytes 368672 | tf_op jit(solution)/shard_map/ppermute | solution.py:444
  518.6 6.8 collective-permute-done.19
  525.4 7.8 %collective-permute-done.23 = bf16[240,768]{1,0:T(8,128)(2,1)S(1)} collective-permute-done((bf16[240,768]{1,0:T(8,128)(2,1)S(1)}, bf16[240,768]{1,0:T(8,128)(2,1)S(1)}, u32[]{:S(2)}, u32[]{:S(2)}) %collective-permute-start.23) | collective-permute-done | bytes 368672 | tf_op jit(solution)/shard_map/ppermute | solution.py:444
  540.5 2.3 pad_maximum_fusion
  544.3 2.6 fusion.8
  547.0 3.3 fusion.7
  552.4 2.6 fusion.6
  555.1 9.2 %collective-permute-start.38 = (bf16[4,240,768]{2,1,0:T(8,128)(2,1)S(1)}, bf16[4,240,768]{2,1,0:T(8,128)(2,1)S(1)}, u32[]{:S(2)}, u32[]{:S(2)}) collective-permute-start(bf16[4,240,768]{2,1,0:T(8,128)(2,1)S(1)} %constant_dynamic-slice_fusion.3), channel_id=1, source_target_pairs={{0,16},{8,24},{16,0},{24,8},{1,17},{9,25},{17,1},{25,9},{2,18},{10... | collective-permute-start | bytes 4423688 | tf_op jit(solution)/shard_map/ppermute | solution.py:444
  564.3 11.5 %collective-permute-done.41 = bf16[4,48,3072]{2,1,0:T(8,128)(2,1)S(1)} collective-permute-done((bf16[4,48,3072]{2,1,0:T(8,128)(2,1)S(1)}, bf16[4,48,3072]{2,1,0:T(8,128)(2,1)S(1)}, u32[]{:S(2)}, u32[]{:S(2)}) %collective-permute-start.41) | collective-permute-done | bytes 1179680 | tf_op jit(solution)/shard_map/ppermute | solution.py:444
  576.3 9.2 %collective-permute-start.42 = (bf16[4,24,3072]{2,1,0:T(8,128)(2,1)S(1)}, bf16[4,24,3072]{2,1,0:T(8,128)(2,1)S(1)}, u32[]{:S(2)}, u32[]{:S(2)}) collective-permute-start(bf16[4,24,3072]{2,1,0:T(8,128)(2,1)S(1)} %constant_dynamic-slice_fusion), channel_id=1, source_target_pairs={{0,16},{8,24},{16,0},{24,8},{1,17},{9,25},{17,1},{25,9},{2,18},{10... | collective-permute-start | bytes 1769480 | tf_op jit(solution)/shard_map/ppermute | solution.py:444
  587.1 16.8 %collective-permute-done.35 = bf16[4,640,256]{2,1,0:T(8,128)(2,1)S(1)} collective-permute-done((bf16[4,640,256]{2,1,0:T(8,128)(2,1)S(1)}, bf16[4,640,256]{2,1,0:T(8,128)(2,1)S(1)}, u32[]{:S(2)}, u32[]{:S(2)}) %collective-permute-start.35) | collective-permute-done | bytes 1310752 | tf_op jit(solution)/shard_map/ppermute | solution.py:444
  605.2 9.1 %collective-permute-start.36 = (bf16[4,320,256]{2,1,0:T(8,128)(2,1)}, bf16[4,320,256]{2,1,0:T(8,128)(2,1)}, u32[]{:S(2)}, u32[]{:S(2)}) collective-permute-start(bf16[4,320,256]{2,1,0:T(8,128)(2,1)} %constant_dynamic-slice_fusion.4), channel_id=1, source_target_pairs={{0,16},{8,24},{16,0},{24,8},{1,17},{9,25},{17,1},{25,9},{2,18},{10... | collective-permute-start | bytes 1966088 | tf_op jit(solution)/shard_map/ppermute | solution.py:444
  617.9 2.5 reshape.2751
  620.4 4.6 collective-permute-done.25
  627.4 9.1 %collective-permute-start.26 = (bf16[4,80,768]{2,1,0:T(8,128)(2,1)}, bf16[4,80,768]{2,1,0:T(8,128)(2,1)}, u32[]{:S(2)}, u32[]{:S(2)}) collective-permute-start(bf16[4,80,768]{2,1,0:T(8,128)(2,1)} %constant_dynamic-slice_fusion.6), channel_id=1, source_target_pairs={{0,16},{8,24},{16,0},{24,8},{1,17},{9,25},{17,1},{25,9},{2,18},{10... | collective-permute-start | bytes 1474568 | tf_op jit(solution)/shard_map/ppermute | solution.py:444
  636.5 2.1 add_convert_fusion.12
  644.7 2.9 collective-permute-done.26
  654.6 6.1 collective-permute-done.27
  663.3 8.4 %collective-permute-done.28 = bf16[240,256]{1,0:T(8,128)(2,1)S(1)} collective-permute-done((bf16[240,256]{1,0:T(8,128)(2,1)S(1)}, bf16[240,256]{1,0:T(8,128)(2,1)S(1)}, u32[]{:S(2)}, u32[]{:S(2)}) %collective-permute-start.28) | collective-permute-done | bytes 122912 | tf_op jit(solution)/shard_map/ppermute | solution.py:444
  672.5 7.3 collective-permute-done.29
  679.9 7.3 collective-permute-done.44
  687.4 8.5 %collective-permute-start.32 = (bf16[1,1,120,256]{3,2,1,0:T(8,128)(2,1)S(1)}, bf16[1,1,120,256]{3,2,1,0:T(8,128)(2,1)S(1)}, u32[]{:S(2)}, u32[]{:S(2)}) collective-permute-start(bf16[1,1,120,256]{3,2,1,0:T(8,128)(2,1)S(1)} %get-tuple-element.204), channel_id=1, source_target_pairs={{0,16},{8,24},{16,0},{24,8},{1,17},{9,25},{17,1},{25,9},{2,18},{10... | collective-permute-start | bytes 184328 | tf_op jit(solution)/shard_map/ppermute | solution.py:444
  699.1 2.4 collective-permute-done.30
  704.4 2.1 collective-permute-done.31
  708.2 7.2 collective-permute-start.47
  717.7 10.5 %collective-permute-done.48 = bf16[1,1,484,256]{3,2,1,0:T(8,128)(2,1)S(1)} collective-permute-done((bf16[1,1,484,256]{3,2,1,0:T(8,128)(2,1)S(1)}, bf16[1,1,484,256]{3,2,1,0:T(8,128)(2,1)S(1)}, u32[]{:S(2)}, u32[]{:S(2)}) %collective-permute-start.48) | collective-permute-done | bytes 247840 | tf_op jit(solution)/shard_map/ppermute | solution.py:444
  731.1 6.1 collective-permute-done.49
  (810 shorter events, 229.4 us)
Async XLA Ops:
  0.7 35.2 %copy-start = (bf16[768,768]{1,0:T(8,128)(2,1)S(1)}, bf16[768,768]{1,0:T(8,128)(2,1)}, u32[]{:S(2)}) copy-start(bf16[768,768]{1,0:T(8,128)(2,1)} %param.28) | copy-start | bytes 3538948
  0.7 56.8 %collective-permute-start = (bf16[480,768]{1,0:T(8,128)(2,1)}, bf16[480,768]{1,0:T(8,128)(2,1)}, u32[]{:S(2)}, u32[]{:S(2)}) collective-permute-start(bf16[480,768]{1,0:T(8,128)(2,1)} %param.22), channel_id=1, source_target_pairs={{0,1},{1,0},{2,3},{3,2},{4,5},{5,4},{6,7},{7,6},{8,9},{9,8},{10,11... | collective-permute-start | bytes 2211848 | tf_op jit(solution)/shard_map/ppermute | solution.py:444
  3.3 48.7 %collective-permute-start.1 = (bf16[240,768]{1,0:T(8,128)(2,1)}, bf16[240,768]{1,0:T(8,128)(2,1)}, u32[]{:S(2)}, u32[]{:S(2)}) collective-permute-start(bf16[240,768]{1,0:T(8,128)(2,1)} %get-tuple-element.116), channel_id=1, source_target_pairs={{0,2},{1,3},{2,4},{3,5},{4,6},{5,7},{6,0},{7,1},{8,10},{9,11},{10,... | collective-permute-start | bytes 1105928 | tf_op jit(solution)/shard_map/ppermute | solution.py:444
  6.0 46.0 %collective-permute-start.2 = (bf16[240,768]{1,0:T(8,128)(2,1)}, bf16[240,768]{1,0:T(8,128)(2,1)}, u32[]{:S(2)}, u32[]{:S(2)}) collective-permute-start(bf16[240,768]{1,0:T(8,128)(2,1)} %get-tuple-element.117), channel_id=1, source_target_pairs={{0,6},{1,7},{2,0},{3,1},{4,2},{5,3},{6,4},{7,5},{8,14},{9,15},{10,... | collective-permute-start | bytes 1105928 | tf_op jit(solution)/shard_map/ppermute | solution.py:444
  12.0 20.6 %copy-start.63 = (pred[12,40]{1,0:T(8,128)(4,1)}, pred[12,40]{1,0:T(8,128)(4,1)S(1)}, u32[]{:S(2)}) copy-start(pred[12,40]{1,0:T(8,128)(4,1)S(1)} %get-tuple-element.274) | copy-start | bytes 1444
  12.0 20.6 %copy-start.65 = (pred[12,40]{1,0:T(8,128)(4,1)}, pred[12,40]{1,0:T(8,128)(4,1)S(1)}, u32[]{:S(2)}) copy-start(pred[12,40]{1,0:T(8,128)(4,1)S(1)} %get-tuple-element.275) | copy-start | bytes 1444
  12.0 21.8 %copy-start.4 = (bf16[480,768]{1,0:T(8,128)(2,1)S(1)}, bf16[480,768]{1,0:T(8,128)(2,1)}, u32[]{:S(2)}) copy-start(bf16[480,768]{1,0:T(8,128)(2,1)} %param.22) | copy-start | bytes 2211844
  12.0 21.8 %copy-start.55 = (f32[10,768]{1,0:T(8,128)S(1)}, f32[10,768]{1,0:T(8,128)}, u32[]{:S(2)}) copy-start(f32[10,768]{1,0:T(8,128)} %param.25) | copy-start | bytes 92164
  13.7 22.1 %copy-start.60 = (f32[768]{0:T(1024)S(1)}, f32[768]{0:T(1024)}, u32[]{:S(2)}) copy-start(f32[768]{0:T(1024)} %param.26) | copy-start | bytes 9220
  13.7 34.7 %collective-permute-start.10 = (bf16[12,40,256]{2,1,0:T(8,128)(2,1)}, bf16[12,40,256]{2,1,0:T(8,128)(2,1)}, u32[]{:S(2)}, u32[]{:S(2)}) collective-permute-start(bf16[12,40,256]{2,1,0:T(8,128)(2,1)} %get-tuple-element.102), channel_id=1, source_target_pairs={{0,7},{1,0},{2,1},{3,2},{4,3},{5,4},{6,5},{7,6},{8,15},{9,8},{10,9... | collective-permute-start | bytes 737288 | tf_op jit(solution)/shard_map/ppermute | solution.py:444
  15.2 34.2 %collective-permute-start.11 = (bf16[12,40,256]{2,1,0:T(8,128)(2,1)}, bf16[12,40,256]{2,1,0:T(8,128)(2,1)}, u32[]{:S(2)}, u32[]{:S(2)}) collective-permute-start(bf16[12,40,256]{2,1,0:T(8,128)(2,1)} %get-tuple-element.66), channel_id=1, source_target_pairs={{0,1},{1,2},{2,3},{3,4},{4,5},{5,6},{6,7},{7,0},{8,9},{9,10},{10,1... | collective-permute-start | bytes 737288 | tf_op jit(solution)/shard_map/ppermute | solution.py:444
  34.7 171.9 %copy-start.1 = (f32[480,768]{1,0:T(8,128)}, f32[480,768]{1,0:T(8,128)S(1)}, u32[]{:S(2)}) copy-start(f32[480,768]{1,0:T(8,128)S(1)} %get-tuple-element.300) | copy-start | bytes 4423684
  53.1 40.2 %collective-permute-start.3 = (bf16[480,768]{1,0:T(8,128)(2,1)S(1)}, bf16[480,768]{1,0:T(8,128)(2,1)S(1)}, u32[]{:S(2)}, u32[]{:S(2)}) collective-permute-start(bf16[480,768]{1,0:T(8,128)(2,1)S(1)} %pad_maximum_fusion.3), channel_id=1, source_target_pairs={{0,1},{1,0},{2,3},{3,2},{4,5},{5,4},{6,7},{7,6},{8,9},{9,8},{10,11... | collective-permute-start | bytes 2211848 | tf_op jit(solution)/shard_map/ppermute | solution.py:444
  53.7 13.5 %collective-permute-start.4 = (bf16[240,768]{1,0:T(8,128)(2,1)}, bf16[240,768]{1,0:T(8,128)(2,1)S(1)}, u32[]{:S(2)}, u32[]{:S(2)}) collective-permute-start(bf16[240,768]{1,0:T(8,128)(2,1)} %collective-permute-done.1), channel_id=1, source_target_pairs={{0,2},{1,3},{2,4},{3,5},{4,6},{5,7},{6,0},{7,1},{8,10},{9,11},{10,... | collective-permute-start | bytes 1105928 | tf_op jit(solution)/shard_map/ppermute | solution.py:444
  53.7 18.7 %collective-permute-start.5 = (bf16[240,768]{1,0:T(8,128)(2,1)}, bf16[240,768]{1,0:T(8,128)(2,1)S(1)}, u32[]{:S(2)}, u32[]{:S(2)}) collective-permute-start(bf16[240,768]{1,0:T(8,128)(2,1)} %collective-permute-done.2), channel_id=1, source_target_pairs={{0,6},{1,7},{2,0},{3,1},{4,2},{5,3},{6,4},{7,5},{8,14},{9,15},{10,... | collective-permute-start | bytes 1105928 | tf_op jit(solution)/shard_map/ppermute | solution.py:444
  72.5 25.4 %collective-permute-start.6 = (bf16[480,768]{1,0:T(8,128)(2,1)S(1)}, bf16[480,768]{1,0:T(8,128)(2,1)S(1)}, u32[]{:S(2)}, u32[]{:S(2)}) collective-permute-start(bf16[480,768]{1,0:T(8,128)(2,1)S(1)} %pad_maximum_fusion.4), channel_id=1, source_target_pairs={{0,1},{1,0},{2,3},{3,2},{4,5},{5,4},{6,7},{7,6},{8,9},{9,8},{10,11... | collective-permute-start | bytes 2211848 | tf_op jit(solution)/shard_map/ppermute | solution.py:444
  72.5 13.3 %collective-permute-start.7 = (bf16[240,768]{1,0:T(8,128)(2,1)S(1)}, bf16[240,768]{1,0:T(8,128)(2,1)S(1)}, u32[]{:S(2)}, u32[]{:S(2)}) collective-permute-start(bf16[240,768]{1,0:T(8,128)(2,1)S(1)} %collective-permute-done.4), channel_id=1, source_target_pairs={{0,2},{1,3},{2,4},{3,5},{4,6},{5,7},{6,0},{7,1},{8,10},{9,11},{10,... | collective-permute-start | bytes 1105928 | tf_op jit(solution)/shard_map/ppermute | solution.py:444
  74.9 18.3 %collective-permute-start.8 = (bf16[240,768]{1,0:T(8,128)(2,1)S(1)}, bf16[240,768]{1,0:T(8,128)(2,1)S(1)}, u32[]{:S(2)}, u32[]{:S(2)}) collective-permute-start(bf16[240,768]{1,0:T(8,128)(2,1)S(1)} %collective-permute-done.5), channel_id=1, source_target_pairs={{0,6},{1,7},{2,0},{3,1},{4,2},{5,3},{6,4},{7,5},{8,14},{9,15},{10,... | collective-permute-start | bytes 1105928 | tf_op jit(solution)/shard_map/ppermute | solution.py:444
  93.3 11.3 %collective-permute-start.9 = (bf16[480,768]{1,0:T(8,128)(2,1)S(1)}, bf16[480,768]{1,0:T(8,128)(2,1)S(1)}, u32[]{:S(2)}, u32[]{:S(2)}) collective-permute-start(bf16[480,768]{1,0:T(8,128)(2,1)S(1)} %pad_maximum_fusion.5), channel_id=1, source_target_pairs={{0,1},{1,0},{2,3},{3,2},{4,5},{5,4},{6,7},{7,6},{8,9},{9,8},{10,11... | collective-permute-start | bytes 2211848 | tf_op jit(solution)/shard_map/ppermute | solution.py:444
  123.2 80.8 %copy-start.115 = (s32[480]{0:T(512)S(1)}, s32[480]{0:T(512)}, u32[]{:S(2)}) copy-start(s32[480]{0:T(512)} %copy-done.114) | copy-start | bytes 5764
  223.6 28.7 %all-to-all-start = ((bf16[8,3,40,512]{3,2,1,0:T(8,128)(2,1)}), bf16[8,3,40,512]{3,2,1,0:T(8,128)(2,1)S(1)}, u32[]{:S(2)}, u32[]{:S(2)}) async-start(bf16[8,3,40,512]{3,2,1,0:T(8,128)(2,1)} %constant_dynamic-update-slice_fusion), calls=%async_computation | async-start | bytes 1966080 | tf_op jit(solution)/shard_map/all_to_all | solution.py:639
  301.0 21.6 %all-to-all-start.1 = ((bf16[8,2,40,512]{3,2,1,0:T(8,128)(2,1)}), bf16[8,2,40,512]{3,2,1,0:T(8,128)(2,1)S(1)}, u32[]{:S(2)}, u32[]{:S(2)}) async-start(bf16[8,2,40,512]{3,2,1,0:T(8,128)(2,1)} %bitcast.477), calls=%async_computation.1 | async-start | bytes 1310720 | tf_op jit(solution)/shard_map/all_to_all | solution.py:658
  353.6 127.5 %collective-permute-start.12 = (bf16[12,40,256]{2,1,0:T(8,128)(2,1)}, bf16[12,40,256]{2,1,0:T(8,128)(2,1)S(1)}, u32[]{:S(2)}, u32[]{:S(2)}) collective-permute-start(bf16[12,40,256]{2,1,0:T(8,128)(2,1)} %get-tuple-element.128), channel_id=1, source_target_pairs={{0,1},{1,2},{2,3},{3,4},{4,5},{5,6},{6,7},{7,0},{8,9},{9,10},{10,1... | collective-permute-start | bytes 737288 | tf_op jit(solution)/shard_map/ppermute | solution.py:444
  353.7 127.6 %collective-permute-start.13 = (bf16[12,40,256]{2,1,0:T(8,128)(2,1)}, bf16[12,40,256]{2,1,0:T(8,128)(2,1)S(1)}, u32[]{:S(2)}, u32[]{:S(2)}) collective-permute-start(bf16[12,40,256]{2,1,0:T(8,128)(2,1)} %get-tuple-element.128), channel_id=1, source_target_pairs={{0,7},{1,0},{2,1},{3,2},{4,3},{5,4},{6,5},{7,6},{8,15},{9,8},{10,9... | collective-permute-start | bytes 737288 | tf_op jit(solution)/shard_map/ppermute | solution.py:444
  461.2 13.1 %collective-permute-start.14 = (bf16[2,240,768]{2,1,0:T(8,128)(2,1)S(1)}, bf16[2,240,768]{2,1,0:T(8,128)(2,1)S(1)}, u32[]{:S(2)}, u32[]{:S(2)}) collective-permute-start(bf16[2,240,768]{2,1,0:T(8,128)(2,1)S(1)} %slice.1185), channel_id=1, source_target_pairs={{0,1},{1,0},{2,3},{3,2},{4,5},{5,4},{6,7},{7,6},{8,9},{9,8},{10,11... | collective-permute-start | bytes 2211848 | tf_op jit(solution)/shard_map/ppermute | solution.py:444
  462.9 19.0 %collective-permute-start.16 = (bf16[2,240,768]{2,1,0:T(8,128)(2,1)}, bf16[2,240,768]{2,1,0:T(8,128)(2,1)}, u32[]{:S(2)}, u32[]{:S(2)}) collective-permute-start(bf16[2,240,768]{2,1,0:T(8,128)(2,1)} %slice.1184), channel_id=1, source_target_pairs={{0,1},{1,0},{2,3},{3,2},{4,5},{5,4},{6,7},{7,6},{8,9},{9,8},{10,11... | collective-permute-start | bytes 2211848 | tf_op jit(solution)/shard_map/ppermute | solution.py:444
  475.3 19.2 %collective-permute-start.15 = (bf16[240,768]{1,0:T(8,128)(2,1)}, bf16[240,768]{1,0:T(8,128)(2,1)S(1)}, u32[]{:S(2)}, u32[]{:S(2)}) collective-permute-start(bf16[240,768]{1,0:T(8,128)(2,1)} %get-tuple-element.114), channel_id=1, source_target_pairs={{0,6},{1,7},{2,0},{3,1},{4,2},{5,3},{6,4},{7,5},{8,14},{9,15},{10,... | collective-permute-start | bytes 1105928 | tf_op jit(solution)/shard_map/ppermute | solution.py:444
  475.3 19.2 %collective-permute-start.21 = (bf16[240,768]{1,0:T(8,128)(2,1)}, bf16[240,768]{1,0:T(8,128)(2,1)}, u32[]{:S(2)}, u32[]{:S(2)}) collective-permute-start(bf16[240,768]{1,0:T(8,128)(2,1)} %get-tuple-element.115), channel_id=1, source_target_pairs={{0,2},{1,3},{2,4},{3,5},{4,6},{5,7},{6,0},{7,1},{8,10},{9,11},{10,... | collective-permute-start | bytes 1105928 | tf_op jit(solution)/shard_map/ppermute | solution.py:444
  481.2 65.8 %collective-permute-start.34 = (bf16[4,1280,256]{2,1,0:T(8,128)(2,1)}, bf16[4,1280,256]{2,1,0:T(8,128)(2,1)}, u32[]{:S(2)}, u32[]{:S(2)}) collective-permute-start(bf16[4,1280,256]{2,1,0:T(8,128)(2,1)} %dynamic-slice_bitcast_fusion), channel_id=1, source_target_pairs={{0,1},{1,0},{2,3},{3,2},{4,5},{5,4},{6,7},{7,6},{8,9},{9,8},{10,11... | collective-permute-start | bytes 7864328 | tf_op jit(solution)/shard_map/ppermute | solution.py:444
  481.3 71.1 %collective-permute-start.37 = (bf16[4,480,768]{2,1,0:T(8,128)(2,1)}, bf16[4,480,768]{2,1,0:T(8,128)(2,1)}, u32[]{:S(2)}, u32[]{:S(2)}) collective-permute-start(bf16[4,480,768]{2,1,0:T(8,128)(2,1)} %fusion.19), channel_id=1, source_target_pairs={{0,1},{1,0},{2,3},{3,2},{4,5},{5,4},{6,7},{7,6},{8,9},{9,8},{10,11... | collective-permute-start | bytes 8847368 | tf_op jit(solution)/shard_map/ppermute | solution.py:444
  481.9 16.9 %collective-permute-start.18 = (bf16[2,240,768]{2,1,0:T(8,128)(2,1)}, bf16[2,240,768]{2,1,0:T(8,128)(2,1)S(1)}, u32[]{:S(2)}, u32[]{:S(2)}) collective-permute-start(bf16[2,240,768]{2,1,0:T(8,128)(2,1)} %slice.1183), channel_id=1, source_target_pairs={{0,1},{1,0},{2,3},{3,2},{4,5},{5,4},{6,7},{7,6},{8,9},{9,8},{10,11... | collective-permute-start | bytes 2211848 | tf_op jit(solution)/shard_map/ppermute | solution.py:444
  495.7 10.4 %collective-permute-start.17 = (bf16[240,768]{1,0:T(8,128)(2,1)S(1)}, bf16[240,768]{1,0:T(8,128)(2,1)S(1)}, u32[]{:S(2)}, u32[]{:S(2)}) collective-permute-start(bf16[240,768]{1,0:T(8,128)(2,1)S(1)} %get-tuple-element.88), channel_id=1, source_target_pairs={{0,6},{1,7},{2,0},{3,1},{4,2},{5,3},{6,4},{7,5},{8,14},{9,15},{10,... | collective-permute-start | bytes 1105928 | tf_op jit(solution)/shard_map/ppermute | solution.py:444
  495.7 19.2 %collective-permute-start.22 = (bf16[240,768]{1,0:T(8,128)(2,1)S(1)}, bf16[240,768]{1,0:T(8,128)(2,1)S(1)}, u32[]{:S(2)}, u32[]{:S(2)}) collective-permute-start(bf16[240,768]{1,0:T(8,128)(2,1)S(1)} %get-tuple-element.89), channel_id=1, source_target_pairs={{0,2},{1,3},{2,4},{3,5},{4,6},{5,7},{6,0},{7,1},{8,10},{9,11},{10,... | collective-permute-start | bytes 1105928 | tf_op jit(solution)/shard_map/ppermute | solution.py:444
  498.8 19.6 %collective-permute-start.20 = (bf16[2,240,768]{2,1,0:T(8,128)(2,1)S(1)}, bf16[2,240,768]{2,1,0:T(8,128)(2,1)S(1)}, u32[]{:S(2)}, u32[]{:S(2)}) collective-permute-start(bf16[2,240,768]{2,1,0:T(8,128)(2,1)S(1)} %copy-done.51), channel_id=1, source_target_pairs={{0,1},{1,0},{2,3},{3,2},{4,5},{5,4},{6,7},{7,6},{8,9},{9,8},{10,11... | collective-permute-start | bytes 2211848 | tf_op jit(solution)/shard_map/ppermute | solution.py:444
  515.1 10.3 %collective-permute-start.19 = (bf16[240,768]{1,0:T(8,128)(2,1)S(1)}, bf16[240,768]{1,0:T(8,128)(2,1)S(1)}, u32[]{:S(2)}, u32[]{:S(2)}) collective-permute-start(bf16[240,768]{1,0:T(8,128)(2,1)S(1)} %get-tuple-element.86), channel_id=1, source_target_pairs={{0,6},{1,7},{2,0},{3,1},{4,2},{5,3},{6,4},{7,5},{8,14},{9,15},{10,... | collective-permute-start | bytes 1105928 | tf_op jit(solution)/shard_map/ppermute | solution.py:444
  516.2 16.9 %collective-permute-start.23 = (bf16[240,768]{1,0:T(8,128)(2,1)S(1)}, bf16[240,768]{1,0:T(8,128)(2,1)S(1)}, u32[]{:S(2)}, u32[]{:S(2)}) collective-permute-start(bf16[240,768]{1,0:T(8,128)(2,1)S(1)} %get-tuple-element.87), channel_id=1, source_target_pairs={{0,2},{1,3},{2,4},{3,5},{4,6},{5,7},{6,0},{7,1},{8,10},{9,11},{10,... | collective-permute-start | bytes 1105928 | tf_op jit(solution)/shard_map/ppermute | solution.py:444
  518.4 25.8 %collective-permute-start.40 = (bf16[4,96,3072]{2,1,0:T(8,128)(2,1)}, bf16[4,96,3072]{2,1,0:T(8,128)(2,1)}, u32[]{:S(2)}, u32[]{:S(2)}) collective-permute-start(bf16[4,96,3072]{2,1,0:T(8,128)(2,1)} %dynamic-slice_bitcast_fusion.1), channel_id=1, source_target_pairs={{0,1},{1,0},{2,3},{3,2},{4,5},{5,4},{6,7},{7,6},{8,9},{9,8},{10,11... | collective-permute-start | bytes 7077896 | tf_op jit(solution)/shard_map/ppermute | solution.py:444
  544.2 41.2 %collective-permute-start.24 = (bf16[4,320,768]{2,1,0:T(8,128)(2,1)}, bf16[4,320,768]{2,1,0:T(8,128)(2,1)S(1)}, u32[]{:S(2)}, u32[]{:S(2)}) collective-permute-start(bf16[4,320,768]{2,1,0:T(8,128)(2,1)} %dynamic-slice_bitcast_fusion.2), channel_id=1, source_target_pairs={{0,1},{1,0},{2,3},{3,2},{4,5},{5,4},{6,7},{7,6},{8,9},{9,8},{10,11... | collective-permute-start | bytes 5898248 | tf_op jit(solution)/shard_map/ppermute | solution.py:444
  547.0 28.8 %collective-permute-start.41 = (bf16[4,48,3072]{2,1,0:T(8,128)(2,1)S(1)}, bf16[4,48,3072]{2,1,0:T(8,128)(2,1)S(1)}, u32[]{:S(2)}, u32[]{:S(2)}) collective-permute-start(bf16[4,48,3072]{2,1,0:T(8,128)(2,1)S(1)} %constant_dynamic-slice_fusion.1), channel_id=1, source_target_pairs={{0,8},{8,0},{16,24},{24,16},{1,9},{9,1},{17,25},{25,17},{2,10},{10... | collective-permute-start | bytes 3538952 | tf_op jit(solution)/shard_map/ppermute | solution.py:444
  550.4 53.4 %collective-permute-start.35 = (bf16[4,640,256]{2,1,0:T(8,128)(2,1)S(1)}, bf16[4,640,256]{2,1,0:T(8,128)(2,1)S(1)}, u32[]{:S(2)}, u32[]{:S(2)}) collective-permute-start(bf16[4,640,256]{2,1,0:T(8,128)(2,1)S(1)} %constant_dynamic-slice_fusion.5), channel_id=1, source_target_pairs={{0,8},{8,0},{16,24},{24,16},{1,9},{9,1},{17,25},{25,17},{2,10},{10... | collective-permute-start | bytes 3932168 | tf_op jit(solution)/shard_map/ppermute | solution.py:444
  555.1 59.2 %collective-permute-start.38 = (bf16[4,240,768]{2,1,0:T(8,128)(2,1)S(1)}, bf16[4,240,768]{2,1,0:T(8,128)(2,1)S(1)}, u32[]{:S(2)}, u32[]{:S(2)}) collective-permute-start(bf16[4,240,768]{2,1,0:T(8,128)(2,1)S(1)} %constant_dynamic-slice_fusion.3), channel_id=1, source_target_pairs={{0,16},{8,24},{16,0},{24,8},{1,17},{9,25},{17,1},{25,9},{2,18},{10... | collective-permute-start | bytes 4423688 | tf_op jit(solution)/shard_map/ppermute | solution.py:444
  576.3 40.6 %collective-permute-start.42 = (bf16[4,24,3072]{2,1,0:T(8,128)(2,1)S(1)}, bf16[4,24,3072]{2,1,0:T(8,128)(2,1)S(1)}, u32[]{:S(2)}, u32[]{:S(2)}) collective-permute-start(bf16[4,24,3072]{2,1,0:T(8,128)(2,1)S(1)} %constant_dynamic-slice_fusion), channel_id=1, source_target_pairs={{0,16},{8,24},{16,0},{24,8},{1,17},{9,25},{17,1},{25,9},{2,18},{10... | collective-permute-start | bytes 1769480 | tf_op jit(solution)/shard_map/ppermute | solution.py:444
  587.0 38.1 %collective-permute-start.25 = (bf16[4,160,768]{2,1,0:T(8,128)(2,1)}, bf16[4,160,768]{2,1,0:T(8,128)(2,1)}, u32[]{:S(2)}, u32[]{:S(2)}) collective-permute-start(bf16[4,160,768]{2,1,0:T(8,128)(2,1)} %constant_dynamic-slice_fusion.7), channel_id=1, source_target_pairs={{0,8},{8,0},{16,24},{24,16},{1,9},{9,1},{17,25},{25,17},{2,10},{10... | collective-permute-start | bytes 2949128 | tf_op jit(solution)/shard_map/ppermute | solution.py:444
  605.2 31.3 %collective-permute-start.36 = (bf16[4,320,256]{2,1,0:T(8,128)(2,1)}, bf16[4,320,256]{2,1,0:T(8,128)(2,1)}, u32[]{:S(2)}, u32[]{:S(2)}) collective-permute-start(bf16[4,320,256]{2,1,0:T(8,128)(2,1)} %constant_dynamic-slice_fusion.4), channel_id=1, source_target_pairs={{0,16},{8,24},{16,0},{24,8},{1,17},{9,25},{17,1},{25,9},{2,18},{10... | collective-permute-start | bytes 1966088 | tf_op jit(solution)/shard_map/ppermute | solution.py:444
  616.8 23.7 %collective-permute-start.39 = (bf16[4,120,768]{2,1,0:T(8,128)(2,1)}, bf16[4,120,768]{2,1,0:T(8,128)(2,1)}, u32[]{:S(2)}, u32[]{:S(2)}) collective-permute-start(bf16[4,120,768]{2,1,0:T(8,128)(2,1)} %constant_dynamic-slice_fusion.2), channel_id=1, source_target_pairs={{0,8},{8,0},{16,24},{24,16},{1,9},{9,1},{17,25},{25,17},{2,10},{10... | collective-permute-start | bytes 2211848 | tf_op jit(solution)/shard_map/ppermute | solution.py:444
  627.4 20.2 %collective-permute-start.26 = (bf16[4,80,768]{2,1,0:T(8,128)(2,1)}, bf16[4,80,768]{2,1,0:T(8,128)(2,1)}, u32[]{:S(2)}, u32[]{:S(2)}) collective-permute-start(bf16[4,80,768]{2,1,0:T(8,128)(2,1)} %constant_dynamic-slice_fusion.6), channel_id=1, source_target_pairs={{0,16},{8,24},{16,0},{24,8},{1,17},{9,25},{17,1},{25,9},{2,18},{10... | collective-permute-start | bytes 1474568 | tf_op jit(solution)/shard_map/ppermute | solution.py:444
  651.5 20.5 %copy-start.12 = (f32[12,40,256]{2,1,0:T(8,128)S(1)}, f32[12,40,256]{2,1,0:T(8,128)}, u32[]{:S(2)}) copy-start(f32[12,40,256]{2,1,0:T(8,128)} %copy-done.11) | copy-start | bytes 1474564
  651.5 20.5 %copy-start.13 = (f32[12,40,256]{2,1,0:T(8,128)S(1)}, f32[12,40,256]{2,1,0:T(8,128)}, u32[]{:S(2)}) copy-start(f32[12,40,256]{2,1,0:T(8,128)} %get-tuple-element.134) | copy-start | bytes 1474564
  651.5 20.5 %copy-start.27 = (f32[12,39,256]{2,1,0:T(8,128)S(1)}, f32[12,39,256]{2,1,0:T(8,128)}, u32[]{:S(2)}) copy-start(f32[12,39,256]{2,1,0:T(8,128)} %get-tuple-element.131) | copy-start | bytes 1437700
  651.5 20.5 %copy-start.28 = (f32[12,39,256]{2,1,0:T(8,128)S(1)}, f32[12,39,256]{2,1,0:T(8,128)}, u32[]{:S(2)}) copy-start(f32[12,39,256]{2,1,0:T(8,128)} %get-tuple-element.132) | copy-start | bytes 1437700
  652.6 8.1 %collective-permute-start.27 = (bf16[240,256]{1,0:T(8,128)(2,1)S(1)}, bf16[240,256]{1,0:T(8,128)(2,1)S(1)}, u32[]{:S(2)}, u32[]{:S(2)}) collective-permute-start(bf16[240,256]{1,0:T(8,128)(2,1)S(1)} %dynamic-slice_bitcast_fusion.4), channel_id=1, source_target_pairs={{0,2},{1,3},{2,4},{3,5},{4,6},{5,7},{6,0},{7,1},{8,10},{9,11},{10,... | collective-permute-start | bytes 368648 | tf_op jit(solution)/shard_map/ppermute | solution.py:444
  654.2 17.6 %collective-permute-start.43 = (bf16[968,256]{1,0:T(8,128)(2,1)S(1)}, bf16[968,256]{1,0:T(8,128)(2,1)S(1)}, u32[]{:S(2)}, u32[]{:S(2)}) collective-permute-start(bf16[968,256]{1,0:T(8,128)(2,1)S(1)} %dynamic-slice_bitcast_fusion.3), channel_id=1, source_target_pairs={{0,2},{1,3},{2,4},{3,5},{4,6},{5,7},{6,0},{7,1},{8,10},{9,11},{10,... | collective-permute-start | bytes 1486856 | tf_op jit(solution)/shard_map/ppermute | solution.py:444
  661.7 10.0 %collective-permute-start.28 = (bf16[240,256]{1,0:T(8,128)(2,1)S(1)}, bf16[240,256]{1,0:T(8,128)(2,1)S(1)}, u32[]{:S(2)}, u32[]{:S(2)}) collective-permute-start(bf16[240,256]{1,0:T(8,128)(2,1)S(1)} %fusion.118), channel_id=1, source_target_pairs={{0,2},{1,3},{2,4},{3,5},{4,6},{5,7},{6,0},{7,1},{8,10},{9,11},{10,... | collective-permute-start | bytes 368648 | tf_op jit(solution)/shard_map/ppermute | solution.py:444
  671.7 8.1 %collective-permute-start.29 = (bf16[240,256]{1,0:T(8,128)(2,1)S(1)}, bf16[240,256]{1,0:T(8,128)(2,1)S(1)}, u32[]{:S(2)}, u32[]{:S(2)}) collective-permute-start(bf16[240,256]{1,0:T(8,128)(2,1)S(1)} %fusion.117), channel_id=1, source_target_pairs={{0,2},{1,3},{2,4},{3,5},{4,6},{5,7},{6,0},{7,1},{8,10},{9,11},{10,... | collective-permute-start | bytes 368648 | tf_op jit(solution)/shard_map/ppermute | solution.py:444
  672.0 15.2 %collective-permute-start.44 = (bf16[968,256]{1,0:T(8,128)(2,1)S(1)}, bf16[968,256]{1,0:T(8,128)(2,1)S(1)}, u32[]{:S(2)}, u32[]{:S(2)}) collective-permute-start(bf16[968,256]{1,0:T(8,128)(2,1)S(1)} %fusion.51), channel_id=1, source_target_pairs={{0,2},{1,3},{2,4},{3,5},{4,6},{5,7},{6,0},{7,1},{8,10},{9,11},{10,... | collective-permute-start | bytes 1486856 | tf_op jit(solution)/shard_map/ppermute | solution.py:444
  687.3 14.3 %collective-permute-start.45 = (bf16[968,256]{1,0:T(8,128)(2,1)S(1)}, bf16[968,256]{1,0:T(8,128)(2,1)S(1)}, u32[]{:S(2)}, u32[]{:S(2)}) collective-permute-start(bf16[968,256]{1,0:T(8,128)(2,1)S(1)} %fusion.50), channel_id=1, source_target_pairs={{0,2},{1,3},{2,4},{3,5},{4,6},{5,7},{6,0},{7,1},{8,10},{9,11},{10,... | collective-permute-start | bytes 1486856 | tf_op jit(solution)/shard_map/ppermute | solution.py:444
  687.4 10.7 %collective-permute-start.32 = (bf16[1,1,120,256]{3,2,1,0:T(8,128)(2,1)S(1)}, bf16[1,1,120,256]{3,2,1,0:T(8,128)(2,1)S(1)}, u32[]{:S(2)}, u32[]{:S(2)}) collective-permute-start(bf16[1,1,120,256]{3,2,1,0:T(8,128)(2,1)S(1)} %get-tuple-element.204), channel_id=1, source_target_pairs={{0,16},{8,24},{16,0},{24,8},{1,17},{9,25},{17,1},{25,9},{2,18},{10... | collective-permute-start | bytes 184328 | tf_op jit(solution)/shard_map/ppermute | solution.py:444
  697.0 4.5 collective-permute-start.30
  698.1 6.2 collective-permute-start.33
  701.5 4.9 collective-permute-start.31
  701.8 6.3 collective-permute-start.46
  708.2 21.2 %collective-permute-start.47 = (bf16[1,2,484,256]{3,2,1,0:T(8,128)(2,1)S(1)}, bf16[1,2,484,256]{3,2,1,0:T(8,128)(2,1)S(1)}, u32[]{:S(2)}, u32[]{:S(2)}) collective-permute-start(bf16[1,2,484,256]{3,2,1,0:T(8,128)(2,1)S(1)} %maximum_select_fusion.2), channel_id=1, source_target_pairs={{0,16},{8,24},{16,0},{24,8},{1,17},{9,25},{17,1},{25,9},{2,18},{10... | collective-permute-start | bytes 1486856 | tf_op jit(solution)/shard_map/ppermute | solution.py:444
  716.3 11.8 %collective-permute-start.48 = (bf16[1,1,484,256]{3,2,1,0:T(8,128)(2,1)S(1)}, bf16[1,1,484,256]{3,2,1,0:T(8,128)(2,1)S(1)}, u32[]{:S(2)}, u32[]{:S(2)}) collective-permute-start(bf16[1,1,484,256]{3,2,1,0:T(8,128)(2,1)S(1)} %get-tuple-element.119), channel_id=1, source_target_pairs={{0,16},{8,24},{16,0},{24,8},{1,17},{9,25},{17,1},{25,9},{2,18},{10... | collective-permute-start | bytes 743432 | tf_op jit(solution)/shard_map/ppermute | solution.py:444
  728.2 9.0 %collective-permute-start.49 = (bf16[2,1,484,256]{3,2,1,0:T(8,128)(2,1)S(1)}, bf16[2,1,484,256]{3,2,1,0:T(8,128)(2,1)S(1)}, u32[]{:S(2)}, u32[]{:S(2)}) collective-permute-start(bf16[2,1,484,256]{3,2,1,0:T(8,128)(2,1)S(1)} %maximum_select_fusion.3), channel_id=1, source_target_pairs={{0,8},{8,0},{16,24},{24,16},{1,9},{9,1},{17,25},{25,17},{2,10},{10... | collective-permute-start | bytes 1486856 | tf_op jit(solution)/shard_map/ppermute | solution.py:444
  (131 other events, 840.0 us)

commit v2 on v1

v2 whole, which is shorter than its diff:
```python
import functools
import math
import typing

import jax
import jax.numpy as jnp
from jax import lax
from jax.experimental import pallas as pl
from jax.experimental.pallas import tpu as pltpu
from jax.sharding import PartitionSpec as P
import numpy as np

HEADS = 12
HEAD = 64
ROWW = 40
SLOTS = 12
HALF = SLOTS // 2
REACH = 6
PITCH = 48
CH = 256

NEG = -1e30
EPS = 1e-06
HIGH = lax.Precision.HIGHEST
KEYS = 672
SPARE_KEYS = 768
QROWS = 64
ROWS = 512
VMEM = 60 * 1024 * 1024
NT = (((1,), (1,)), ((), ()))
FLIP = (((0,), (0,)), ((), ()))
F32 = jnp.float32
BF16 = jnp.bfloat16


def cost(microseconds):
    return pl.CostEstimate(flops=microseconds * 10**9, bytes_accessed=10**6, transcendentals=0)


def own_blocks(heads, feats):
    row = lax.broadcasted_iota(jnp.int32, (heads * QROWS, feats), 0) // QROWS
    col = lax.broadcasted_iota(jnp.int32, (heads * QROWS, feats), 1) // HEAD
    return row == col


def spread(block, heads):
    wide = jnp.concatenate([block] * heads, axis=0)
    return jnp.where(own_blocks(heads, block.shape[1]), wide, jnp.zeros((), block.dtype))


def gathered(wide, heads):
    kept = jnp.where(own_blocks(heads, wide.shape[1]), wide, 0.0)
    total = kept[:QROWS]
    for head in range(1, heads):
        total = total + kept[head * QROWS : (head + 1) * QROWS]
    return total


def lanes(column, width):
    return jnp.concatenate([column] * (width // 128), axis=1)


class Tables(typing.NamedTuple):
    koff: jax.Array
    kcnt: jax.Array
    kdst: jax.Array
    kstart: jax.Array
    klen: jax.Array
    qfirst: jax.Array
    qcount: jax.Array
    ubase: jax.Array
    uspare: jax.Array
    uwidth: jax.Array
    uitem: jax.Array
    qbase: jax.Array
    qspare: jax.Array
    qwidth: jax.Array
    qitem: jax.Array
    wwidth: jax.Array
    wup: jax.Array
    wdown: jax.Array


TABLES = len(Tables._fields)


def geometry_kernel(cycle_size, unit_size, lengths, place, *refs):
    tab = Tables(*refs)
    item_count = lengths.shape[0]
    items = item_count + 1
    chips = cycle_size // 2
    units = 4 * chips
    me = place[0]
    chip, core = lax.div(me, 2), lax.rem(me, 2)
    facts, start = [], 0
    for item in range(item_count):
        length = lengths[item]
        height = jnp.where(length == 1200, 30, jnp.where(length == 576, 24, 0))
        facts.append((start, start + height, jnp.where(length == 1200, 40, 24)))
        start = start + height

    def fact(row):
        number, width = item_count, 0
        for item, (begin, end, item_width) in enumerate(facts):
            inside = (row >= begin) & (row < end)
            number = jnp.where(inside, item, number)
            width = jnp.where(inside, item_width, width)
        return number, width

    def up(value, align):
        return lax.div(value + (align - 1), align) * align

    def sort(rows, align, base, spare_base, widths, numbers, first):
        known = [fact(row) for row in rows]
        counts = [
            sum(jnp.where(number == item, width, 0) for number, width in known)
            for item in range(item_count)
        ]
        counts.append(sum(ROWW - width for _, width in known))
        offsets, total = [], 0
        for count in counts:
            offsets.append(total)
            total = total + up(count, align)
        spare = offsets[-1]
        for slot, (number, width) in enumerate(known):
            begin = sum(jnp.where(number == item, offsets[item], 0) for item in range(item_count))
            for other, other_width in known[:slot]:
                begin = begin + jnp.where(other == number, other_width, 0)
            base[first + slot] = begin
            spare_base[first + slot] = spare - width
            widths[first + slot] = width
            numbers[first + slot] = number
            spare = spare + ROWW - width
        return counts, offsets

    def one_unit(unit, lens):
        turn, half = lax.div(unit, 4), lax.rem(unit, 2)
        other = lax.rem(lax.div(unit, 2), 2)
        turn = jnp.where(half == 0, -turn, turn)
        source = 2 * lax.rem(chip + turn + chips, chips) + jnp.where(other == 0, core, 1 - core)
        rows = [(half * HALF + slot) * cycle_size + source for slot in range(HALF)]
        counts, offsets = sort(
            rows, 16, tab.ubase, tab.uspare, tab.uwidth, tab.uitem, unit * HALF
        )
        for item in range(items):
            tab.koff[unit * items + item] = offsets[item] + unit * unit_size
            tab.kcnt[unit * items + item] = counts[item]
        return tuple(length + up(count, 16) for length, count in zip(lens, counts))

    lens = lax.fori_loop(0, units, one_unit, (jnp.int32(0),) * items)
    starts = [jnp.int32(0)]
    for item in range(items):
        size = SPARE_KEYS if item == items - 1 else KEYS
        tab.klen[item] = lens[item]
        tab.kstart[item] = starts[item]
        starts.append(starts[item] + up(lens[item], size))
    tab.kstart[items] = starts[items]

    def place_unit(unit, at):
        for item in range(items):
            tab.kdst[unit * items + item] = at[item]
        return tuple(
            spot + up(tab.kcnt[unit * items + item], 16) for item, spot in enumerate(at)
        )

    lax.fori_loop(0, units, place_unit, tuple(starts[:items]))
    for index in range(SLOTS + 2 * REACH):
        row = SLOTS * me - REACH + index
        width, above, below = 0, 0, 0
        for begin, end, item_width in facts:
            inside = (row >= begin) & (row < end)
            width = jnp.where(inside, item_width, width)
            above = jnp.where(inside & (row > begin), 1, above)
            below = jnp.where(inside & (row + 1 < end), 1, below)
        tab.wwidth[index] = width
        tab.wup[index] = above
        tab.wdown[index] = below
    rows = [slot * cycle_size + me for slot in range(SLOTS)]
    counts, offsets = sort(rows, QROWS, tab.qbase, tab.qspare, tab.qwidth, tab.qitem, 0)
    for item in range(items):
        tab.qfirst[item] = lax.div(offsets[item], QROWS)
        tab.qcount[item] = lax.div(counts[item] + (QROWS - 1), QROWS)


def geometry(lengths, cycle_pos, cycle_size, unit_size):
    items = lengths.shape[0] + 1
    units = 2 * cycle_size
    sizes = [units * items] * 3 + [items + 1] + [items] * 3 + [units * HALF] * 4 + [SLOTS] * 4
    sizes += [SLOTS + 2 * REACH] * 3
    smem = pl.BlockSpec(memory_space=pltpu.SMEM)
    return Tables(
        *pl.pallas_call(
            functools.partial(geometry_kernel, cycle_size, unit_size),
            in_specs=[smem, smem],
            out_specs=[smem] * TABLES,
            out_shape=[jax.ShapeDtypeStruct((size,), jnp.int32) for size in sizes],
            name="geometry",
        )(lengths, cycle_pos.reshape(1))
    )


def places(base, spare, width, first, slots):
    token = lax.broadcasted_iota(jnp.int32, (1, slots * ROWW), 1)
    place = jnp.zeros_like(token)
    for slot in range(slots):
        column = token - slot * ROWW
        here = jnp.where(column < width[first + slot], base[first + slot], spare[first + slot])
        place = jnp.where((column >= 0) & (column < ROWW), here + column, place)
    return place


def sorter(place, rows):
    spot = lax.broadcasted_iota(jnp.int32, (rows, place.shape[1]), 0)
    return jnp.where(spot == place, 1.0, 0.0).astype(BF16)


def query_sorter(tab, rows):
    return sorter(places(tab.qbase, tab.qspare, tab.qwidth, 0, SLOTS), rows)


def with_dataset(values, width, item, first, ids, table_ref):
    column = lax.broadcasted_iota(jnp.int32, (ROWW, 1), 0)
    parts = []
    for slot in range(values.shape[0] // ROWW):
        number = jnp.minimum(item[first + slot], ids.shape[0] - 1)
        added = table_ref[pl.ds(ids[number], 1), :]
        real = column < width[first + slot]
        parts.append(values[slot * ROWW : (slot + 1) * ROWW] + jnp.where(real, added, 0.0))
    return jnp.concatenate(parts, axis=0)


def layer_norm(hidden, norm_gain, norm_bias):
    centred = hidden - jnp.mean(hidden, axis=-1, keepdims=True)
    variance = jnp.mean(centred * centred, axis=-1, keepdims=True)
    return centred * lax.rsqrt(variance + EPS) * norm_gain + norm_bias


def sort_step_kernel(step, ubase, uspare, uwidth, uitem, ids, *refs):
    mine_ref, other_ref, table_ref, gain_ref, bias_ref, out_ref = refs
    unit_size = out_ref.shape[0] // 4
    count = HALF * ROWW
    for unit in range(4):
        source = (mine_ref, other_ref)[unit // 2]
        first = (4 * step + unit) * HALF
        values = source[unit % 2 * count : (unit % 2 + 1) * count, :].astype(F32)
        values = with_dataset(values, uwidth, uitem, first, ids, table_ref)
        normed = layer_norm(values, gain_ref[...], bias_ref[...]).astype(BF16)
        matrix = sorter(places(ubase, uspare, uwidth, first, HALF), unit_size)
        out_ref[unit * unit_size : (unit + 1) * unit_size, :] = jnp.dot(
            matrix, normed, preferred_element_type=F32
        ).astype(BF16)


def sort_step(step, tab, ids, mine, other, table, gain, bias, unit_size):
    return pl.pallas_call(
        functools.partial(sort_step_kernel, step),
        grid_spec=pltpu.PrefetchScalarGridSpec(
            num_scalar_prefetch=5,
            in_specs=[pl.BlockSpec(memory_space=pltpu.VMEM)] * 5,
            out_specs=pl.BlockSpec(memory_space=pltpu.VMEM),
        ),
        out_shape=jax.ShapeDtypeStruct((4 * unit_size, mine.shape[1]), BF16),
        cost_estimate=cost(3),
        compiler_params=pltpu.CompilerParams(vmem_limit_bytes=VMEM),
        name="sort_step",
    )(tab.ubase, tab.uspare, tab.uwidth, tab.uitem, ids, mine, other, table, gain, bias)


def own_start_kernel(qbase, qspare, qwidth, qitem, ids, *refs):
    tokens_ref, table_ref, gain_ref, bias_ref, weight_ref, start_ref, normed_ref, query_ref = refs
    values = tokens_ref[...].astype(F32)
    values = with_dataset(values, qwidth, qitem, 0, ids, table_ref)
    start_ref[...] = values
    normed = layer_norm(values, gain_ref[...], bias_ref[...]).astype(BF16)
    normed_ref[...] = normed
    matrix = sorter(places(qbase, qspare, qwidth, 0, SLOTS), query_ref.shape[0])
    sorted_norm = jnp.dot(matrix, normed, preferred_element_type=F32).astype(BF16)
    query = jnp.dot(sorted_norm, weight_ref[...], preferred_element_type=F32)
    query_ref[...] = (query * (1.0 / math.sqrt(HEAD))).astype(BF16)


def own_start(tab, ids, tokens, table, gain, bias, weight, query_rows):
    vmem = pl.BlockSpec(memory_space=pltpu.VMEM)
    return pl.pallas_call(
        own_start_kernel,
        grid_spec=pltpu.PrefetchScalarGridSpec(
            num_scalar_prefetch=5, in_specs=[vmem] * 5, out_specs=[vmem] * 3
        ),
        out_shape=[
            jax.ShapeDtypeStruct(tokens.shape, F32),
            jax.ShapeDtypeStruct(tokens.shape, BF16),
            jax.ShapeDtypeStruct((query_rows, tokens.shape[1]), BF16),
        ],
        cost_estimate=cost(5),
        compiler_params=pltpu.CompilerParams(vmem_limit_bytes=VMEM),
        name="own_start",
    )(tab.qbase, tab.qspare, tab.qwidth, tab.qitem, ids, tokens, table, gain, bias, weight)


def query_blocks(first, many, body):
    def pair(number, none):
        body(first + 2 * number, 2)
        return none

    lax.fori_loop(0, many // 2, pair, 0)

    @pl.when(many % 2 == 1)
    def _():
        body(first + many - 1, 1)


def for_items(items, klen, body):
    def one(item, none):
        body(item, KEYS, (klen[item] + KEYS - 1) // KEYS)
        return none

    lax.fori_loop(0, items - 1, one, 0)
    last = items - 1
    body(last, SPARE_KEYS, (klen[last] + SPARE_KEYS - 1) // SPARE_KEYS)


def as_column(row):
    return row.T[:, :1]


def attend_kernel(heads, units, items, *refs):
    tab, refs = Tables(*refs[:TABLES]), refs[TABLES:]
    koff, kcnt, kdst, kstart, klen, qfirst, qcount = tab[:7]
    steps = units // 4
    q_ref, wk_ref, wv_ref = refs[:3]
    n_refs, refs = refs[3 : 3 + steps], refs[3 + steps :]
    att_ref, o_ref, lse_ref, ns_ref, bias_ref, ks_ref, vs_ref = refs[:7]
    acc_ref, top_ref, total_ref, matrix = refs[7:]
    stride = n_refs[0].shape[0]
    cols = heads * QROWS
    width = ns_ref.shape[1]
    o_ref[...] = jnp.zeros_like(o_ref)
    lse_ref[...] = jnp.zeros_like(lse_ref)
    used = kstart[items]

    @pl.when(pl.program_id(0) == 0)
    def _():
        matrix[...] = query_sorter(tab, o_ref.shape[0])

        def one_item(item, size, blocks):
            def one_unit(turn, unit, none):
                entry = (4 * turn + unit) * items + item
                count, source, target = kcnt[entry], koff[entry] - turn * stride, kdst[entry]

                def step(part, none):
                    src = pl.ds(pl.multiple_of(source + 64 * part, 16), 64)
                    dst = pl.ds(pl.multiple_of(target + 64 * part, 16), 64)
                    ns_ref[dst, :] = n_refs[turn][src, :]
                    row = lax.broadcasted_iota(jnp.int32, (64, 128), 0) + 64 * part
                    bias_ref[dst, :] = jnp.where(row < count, 0.0, NEG).astype(BF16)
                    return none

                return lax.fori_loop(0, (count + 63) // 64, step, none)

            for turn in range(steps):
                lax.fori_loop(0, 4, functools.partial(one_unit, turn), 0)
            end = kstart[item] + klen[item]

            def clear(part, none):
                tail = pl.ds(pl.multiple_of(end + 64 * part, 16), 64)
                ns_ref[tail, :] = jnp.zeros((64, width), BF16)
                bias_ref[tail, :] = jnp.full((64, 128), NEG, BF16)
                return none

            lax.fori_loop(0, (kstart[item + 1] - end + 63) // 64 + 1, clear, 0)

        for_items(items, klen, one_item)

        def clear(part, none):
            tail = pl.ds(pl.multiple_of(used + 64 * part, 16), 64)
            ns_ref[tail, :] = jnp.zeros((64, width), BF16)
            return none

        lax.fori_loop(0, (ns_ref.shape[0] - used) // 64, clear, 0)

    def project(block, none):
        here = pl.ds(pl.multiple_of(block * ROWS, ROWS), ROWS)
        rows = ns_ref[here, :]
        ks_ref[here, :] = jnp.dot(rows, wk_ref[...], preferred_element_type=F32).astype(BF16)
        vs_ref[here, :] = jnp.dot(rows, wv_ref[...], preferred_element_type=F32).astype(BF16)
        return none

    lax.fori_loop(0, (used + ROWS - 1) // ROWS, project, 0)

    def one_item(item, size, blocks):
        def some_queries(place, count):
            wide = count * cols
            rows = pl.ds(pl.multiple_of(place * QROWS, QROWS), count * QROWS)
            block = q_ref[rows, :]
            queries = jnp.concatenate(
                [spread(block[n * QROWS : (n + 1) * QROWS], heads) for n in range(count)], axis=0
            )
            top, total, acc = top_ref.at[:, :wide], total_ref.at[:, :wide], acc_ref.at[:wide]
            top[...] = jnp.full((8, wide), NEG, F32)
            total[...] = jnp.zeros((8, wide), F32)
            acc[...] = jnp.zeros((wide, heads * HEAD), F32)

            def step(number, none):
                here = pl.ds(pl.multiple_of(kstart[item] + number * size, 16), size)
                scores = lax.dot_general(
                    ks_ref[here, :], queries, NT, preferred_element_type=F32
                ) + lanes(bias_ref[here, :].astype(F32), wide)
                best = jnp.max(jnp.max(scores.reshape(size // 8, 8, wide), axis=0), axis=0)
                old = top[...]
                best = jnp.maximum(old, jnp.broadcast_to(best[None], (8, wide)))
                top[...] = best
                shrink = jnp.exp(old - best)
                weights = jnp.exp(scores - best[:1])
                total[...] = total[...] * shrink + jnp.sum(
                    weights.reshape(size // 8, 8, wide), axis=0
                )
                acc[...] = acc[...] * as_column(shrink) + lax.dot_general(
                    weights.astype(BF16),
                    vs_ref[here, :],
                    (((0,), (0,)), ((), ())),
                    preferred_element_type=F32,
                )
                return none

            lax.fori_loop(0, blocks, step, 0)
            summed = jnp.broadcast_to(jnp.sum(total[...], axis=0, keepdims=True), (8, wide))
            lse = top[...] + jnp.log(summed)
            out = acc[...] * as_column(1.0 / summed)
            for n in range(count):
                part = slice(n * cols, (n + 1) * cols)
                lse_ref[pl.ds(place + n, 1), :] = lse[:1, part]
                o_ref[pl.ds(pl.multiple_of((place + n) * QROWS, QROWS), QROWS), :] = gathered(
                    out[part], heads
                )

        query_blocks(qfirst[item], qcount[item], some_queries)

    for_items(items, klen, one_item)
    att_ref[...] = lax.dot_general(
        matrix[...], o_ref[...].astype(BF16), FLIP, preferred_element_type=F32
    ).astype(BF16)


def attend_back_kernel(heads, units, items, unit_size, *refs):
    tab, refs = Tables(*refs[:TABLES]), refs[TABLES:]
    koff, kcnt, kdst, kstart, klen, qfirst, qcount = tab[:7]
    q_ref, grad_ref, o_ref, lse_ref, ks_ref, vs_ref, wk_ref, wv_ref, ns_ref, bias_ref = refs[:10]
    dq_ref, gk_ref, gv_ref, dn_ref = refs[10:14]
    (
        spread_q, spread_do, delta, dq_acc, dk_acc, dv_acc, gk_acc, gv_acc, dn_acc,
        matrix, do_ref, dqs, unit_rows,
    ) = refs[14:]
    feats = heads * HEAD
    cols = heads * QROWS
    flip = FLIP
    dqs[...] = jnp.zeros_like(dqs)
    gk_acc[...] = jnp.zeros_like(gk_acc)
    gv_acc[...] = jnp.zeros_like(gv_acc)
    used = qfirst[items - 1] + qcount[items - 1]

    @pl.when(pl.program_id(0) == 0)
    def _():
        dn_acc[...] = jnp.zeros_like(dn_acc)
        matrix[...] = query_sorter(tab, q_ref.shape[0])

    do_ref[...] = jnp.dot(matrix[...], grad_ref[...], preferred_element_type=F32).astype(BF16)

    def prepare(place, none):
        rows = pl.ds(pl.multiple_of(place * QROWS, QROWS), QROWS)
        grads = do_ref[rows, :]
        spread_q[place] = spread(q_ref[rows, :], heads)
        spread_do[place] = spread(grads, heads)
        product = spread(grads.astype(F32) * o_ref[rows, :], heads)
        delta[place] = lax.dot_general(
            jnp.ones((8, feats), F32), product, NT, precision=HIGH, preferred_element_type=F32
        )
        dq_acc[place] = jnp.zeros((cols, feats), F32)
        return none

    lax.fori_loop(0, used, prepare, 0)

    def one_item(item, size, blocks):
        def one_block(number, none):
            here = pl.ds(pl.multiple_of(kstart[item] + number * size, 16), size)
            dk_acc[:size] = jnp.zeros((size, feats), F32)
            dv_acc[:size] = jnp.zeros((size, feats), F32)

            def some_queries(place, count):
                wide = count * cols
                spot = pl.ds(place, count)
                queries = spread_q[spot].reshape(wide, feats)
                grads = spread_do[spot].reshape(wide, feats)
                row = [lse_ref[pl.ds(place + n, 1), :] for n in range(count)]
                log_total = jnp.concatenate(row, axis=1)
                shift = jnp.concatenate([delta[place + n, :1, :] for n in range(count)], axis=1)
                keys = ks_ref[here, :]
                scores = lax.dot_general(keys, queries, NT, preferred_element_type=F32)
                weights = jnp.exp(scores + lanes(bias_ref[here, :].astype(F32), wide) - log_total)
                slopes = lax.dot_general(vs_ref[here, :], grads, NT, preferred_element_type=F32)
                score_grads = (weights * (slopes - shift)).astype(BF16)
                dv_acc[:size] += jnp.dot(weights.astype(BF16), grads, preferred_element_type=F32)
                dk_acc[:size] += jnp.dot(score_grads, queries, preferred_element_type=F32)
                part = lax.dot_general(score_grads, keys, flip, preferred_element_type=F32)
                dq_acc[spot] += part.reshape(count, cols, feats)

            query_blocks(qfirst[item], qcount[item], some_queries)
            dk = dk_acc[:size].astype(BF16)
            dv = dv_acc[:size].astype(BF16)
            dn_acc[here, :] += (
                lax.dot_general(dk, wk_ref[...], NT, preferred_element_type=F32)
                + lax.dot_general(dv, wv_ref[...], NT, preferred_element_type=F32)
            ).astype(dn_acc.dtype)
            rows = ns_ref[here, :]
            gk_acc[...] += lax.dot_general(rows, dk, flip, preferred_element_type=F32)
            gv_acc[...] += lax.dot_general(rows, dv, flip, preferred_element_type=F32)
            return none

        lax.fori_loop(0, jnp.where(qcount[item] > 0, blocks, 0), one_block, 0)

    for_items(items, klen, one_item)

    def finish(place, none):
        rows = pl.ds(pl.multiple_of(place * QROWS, QROWS), QROWS)
        scale = 1.0 / math.sqrt(HEAD)
        dqs[rows, :] = (gathered(dq_acc[place], heads) * scale).astype(BF16)
        return none

    lax.fori_loop(0, used, finish, 0)
    dq_ref[...] = lax.dot_general(
        matrix[...], dqs[...], flip, preferred_element_type=F32
    ).astype(BF16)
    gk_ref[...] = gk_acc[...].astype(BF16)
    gv_ref[...] = gv_acc[...].astype(BF16)

    @pl.when(pl.program_id(0) == pl.num_programs(0) - 1)
    def _():
        unit_rows[...] = jnp.zeros_like(unit_rows)
        count = HALF * ROWW

        def one_unit(unit, none):
            def one_item(item, none):
                entry = unit * items + item
                source, target = koff[entry] - unit * unit_size, kdst[entry]

                def step(part, none):
                    src = pl.ds(pl.multiple_of(source + 64 * part, 16), 64)
                    dst = pl.ds(pl.multiple_of(target + 64 * part, 16), 64)
                    unit_rows[src, :] = dn_acc[dst, :]
                    return none

                return lax.fori_loop(0, (kcnt[entry] + 63) // 64, step, none)

            lax.fori_loop(0, items, one_item, 0)
            place = places(tab.ubase, tab.uspare, tab.uwidth, unit * HALF, HALF)
            dn_ref[pl.ds(pl.multiple_of(unit * count, 16), count), :] = lax.dot_general(
                sorter(place, unit_size), unit_rows[...], flip, preferred_element_type=F32
            ).astype(BF16)
            return none

        lax.fori_loop(0, units, one_unit, 0)


def gelu_parts(values):
    slope = 0.7978845608028654
    bent = jnp.tanh(slope * (values + 0.044715 * values * values * values))
    return bent, slope * (1.0 + 3.0 * 0.044715 * values * values)


def gelu(values):
    return 0.5 * values * (1.0 + gelu_parts(values)[0])


def gelu_slope(values):
    bent, inner = gelu_parts(values)
    return 0.5 * (1.0 + bent) + 0.5 * values * (1.0 - bent * bent) * inner


def merge_kernel(
    cycle_size, wwidth, wup, wdown,
    win_ref, k11, k12, k21, k22, out_weight, grad_ref, mapped_ref, shares_ref,
    x1, x2, x3, x4, g3, real_ref, up_ref, down_ref, c1, m1, c3, m2g, m1g,
):
    window = SLOTS + 2 * REACH
    column = lax.broadcasted_iota(jnp.int32, (PITCH, 128), 0)
    for row in range(window):
        spots = pl.ds(row * PITCH, PITCH)
        real = jnp.where(column < wwidth[row], 1.0, 0.0)
        real_ref[spots, :] = real
        up_ref[spots, :] = real * wup[row].astype(F32)
        down_ref[spots, :] = real * wdown[row].astype(F32)

    def at(low, high):
        return slice(low * PITCH, high * PITCH)

    def masked(ref, values, low, high):
        return values * lanes(ref[at(low, high), :], CH)

    def fill(taps, values, low, high):
        spots = at(low + 1, high + 1)
        size = values.shape[0]
        taps[spots, :CH] = pltpu.roll(values, 1, 0).astype(BF16)
        taps[spots, CH : 2 * CH] = values.astype(BF16)
        taps[spots, 2 * CH :] = pltpu.roll(values, size - 1, 0).astype(BF16)

    def conv(taps, kernel, low, high):
        def part(row_step):
            rows = taps[at(low + 1 + row_step, high + 1 + row_step), :]
            first = (row_step + 1) * 3 * CH
            return jnp.dot(rows, kernel[first : first + 3 * CH, :], preferred_element_type=F32)

        total = masked(real_ref, part(0), low, high)
        total = total + masked(up_ref, part(-1), low, high)
        return total + masked(down_ref, part(1), low, high)

    def conv_back(kernel, low, high):
        def part(row_step):
            rows = at(low + 1 + row_step, high + 1 + row_step)
            total = None
            for col_step in (-1, 0, 1):
                first = (8 - (3 * (row_step + 1) + col_step + 1)) * CH
                side = (col_step + 1) * CH
                now = lax.dot_general(
                    g3[rows, side : side + CH],
                    kernel[first : first + CH, :],
                    NT,
                    preferred_element_type=F32,
                )
                total = now if total is None else total + now
            return total

        total = masked(real_ref, part(0), low, high)
        total = total + masked(up_ref, part(-1), low, high)
        return total + masked(down_ref, part(1), low, high)

    own, last = REACH, REACH + SLOTS
    unit_share = 9 * CH // cycle_size
    out_share = CH // cycle_size
    share_rows = 4 * unit_share + out_share

    def weight_grad(taps, gradient, tensor):
        piece = math.gcd(3 * CH, unit_share)
        for row_step, mask in ((-1, up_ref), (0, real_ref), (1, down_ref)):
            now = masked(mask, gradient, own, last).astype(BF16)
            rows = taps[at(own + 1 + row_step, last + 1 + row_step), :]
            block = lax.dot_general(rows, now, FLIP, preferred_element_type=F32).astype(BF16)
            for part in range(3 * CH // piece):
                spot = (row_step + 1) * 3 * CH + part * piece
                share, offset = divmod(spot, unit_share)
                first = share * share_rows + tensor * unit_share + offset
                shares_ref[first : first + piece, :] = block[part * piece : (part + 1) * piece]

    def start(low, high):
        return win_ref[at(low, high), :CH].astype(F32)

    fill(x1, masked(real_ref, gelu(start(0, 24)), 0, 24), 0, 24)
    c1[at(1, 23), :] = conv(x1, k11, 1, 23)
    fill(x2, masked(real_ref, gelu(c1[at(1, 23), :]), 1, 23), 1, 23)
    m1[at(2, 22), :] = start(2, 22) + conv(x2, k12, 2, 22)
    fill(x3, masked(real_ref, gelu(m1[at(2, 22), :]), 2, 22), 2, 22)
    c3[at(3, 21), :] = conv(x3, k21, 3, 21)
    fill(x4, masked(real_ref, gelu(c3[at(3, 21), :]), 3, 21), 3, 21)
    merged = (m1[at(own, last), :] + conv(x4, k22, own, last)).astype(BF16)
    mapped_ref[...] = jnp.dot(merged, out_weight[...], preferred_element_type=F32).astype(BF16)
    block = lax.dot_general(
        merged, win_ref[at(own, last), CH:], FLIP, preferred_element_type=F32
    ).astype(BF16)
    for share in range(cycle_size):
        first = share * share_rows + 4 * unit_share
        shares_ref[first : first + out_share, :] = block[share * out_share : (share + 1) * out_share]

    m2g[at(2, 22), :] = lax.dot_general(
        win_ref[at(2, 22), CH:], out_weight[...], NT, preferred_element_type=F32
    )
    fill(g3, masked(real_ref, m2g[at(2, 22), :], 2, 22), 2, 22)
    weight_grad(x4, m2g[at(own, last), :], 3)
    now = gelu_slope(c3[at(3, 21), :]) * conv_back(k22, 3, 21)
    fill(g3, now, 3, 21)
    weight_grad(x3, now[at(own - 3, last - 3)], 2)
    m1g[at(4, 20), :] = m2g[at(4, 20), :] + gelu_slope(m1[at(4, 20), :]) * conv_back(k21, 4, 20)
    fill(g3, masked(real_ref, m1g[at(4, 20), :], 4, 20), 4, 20)
    weight_grad(x2, m1g[at(own, last), :], 1)
    now = gelu_slope(c1[at(5, 19), :]) * conv_back(k12, 5, 19)
    fill(g3, now, 5, 19)
    weight_grad(x1, now[at(own - 5, last - 5)], 0)
    now = gelu_slope(start(own, last)) * conv_back(k11, own, last)
    grad_ref[...] = (m1g[at(own, last), :] + now).astype(BF16)


def merge(tab, windows, kernels, out_weight, cycle_size):
    window = SLOTS + 2 * REACH
    vmem = pl.BlockSpec(memory_space=pltpu.VMEM)
    padded = (window + 2) * PITCH
    share_rows = 4 * (9 * CH // cycle_size) + CH // cycle_size
    small = pltpu.VMEM((window * PITCH, 128), F32)
    large = pltpu.VMEM((window * PITCH, CH), F32)
    return pl.pallas_call(
        functools.partial(merge_kernel, cycle_size),
        grid_spec=pltpu.PrefetchScalarGridSpec(
            num_scalar_prefetch=3,
            in_specs=[vmem] * 6,
            out_specs=[vmem] * 3,
            scratch_shapes=[pltpu.VMEM((padded, 3 * CH), BF16)] * 5 + [small] * 3 + [large] * 5,
        ),
        out_shape=[
            jax.ShapeDtypeStruct((SLOTS * PITCH, CH), BF16),
            jax.ShapeDtypeStruct((SLOTS * PITCH, CH), BF16),
            jax.ShapeDtypeStruct((cycle_size * share_rows, CH), BF16),
        ],
        cost_estimate=cost(25),
        compiler_params=pltpu.CompilerParams(vmem_limit_bytes=VMEM),
        name="merge",
    )(tab.wwidth, tab.wup, tab.wdown, windows, *kernels, out_weight)


def attend(tab, query, key_weight, value_weight, norms, sorted_keys, units, items, heads):
    feats = heads * HEAD
    cols = heads * QROWS
    width = query.shape[1]
    groups = width // feats
    blocks8 = (query.shape[0] // QROWS + 7) // 8 * 8
    once = pl.Buffered(1) if units > 16 else None

    def part(rows, columns=feats):
        return pl.BlockSpec((rows, columns), lambda group, *_: (0, group), pipeline_mode=once)

    def whole(rows, columns):
        return pl.BlockSpec(
            (rows, columns), lambda group, *_: (0, 0), pipeline_mode=pl.Buffered(1)
        )

    return pl.pallas_call(
        functools.partial(attend_kernel, heads, units, items),
        grid_spec=pltpu.PrefetchScalarGridSpec(
            num_scalar_prefetch=TABLES,
            grid=(groups,),
            in_specs=[part(query.shape[0]), part(width), part(width)]
            + [whole(*norm.shape) for norm in norms],
            out_specs=[
                part(SLOTS * ROWW),
                part(query.shape[0]),
                part(blocks8, cols),
                whole(sorted_keys, width),
                whole(sorted_keys, 128),
                part(sorted_keys),
                part(sorted_keys),
            ],
            scratch_shapes=[
                pltpu.VMEM((2 * cols, feats), F32),
                pltpu.VMEM((8, 2 * cols), F32),
                pltpu.VMEM((8, 2 * cols), F32),
                pltpu.VMEM((query.shape[0], SLOTS * ROWW), BF16),
            ],
        ),
        out_shape=[
            jax.ShapeDtypeStruct((SLOTS * ROWW, width), BF16),
            jax.ShapeDtypeStruct(query.shape, F32),
            jax.ShapeDtypeStruct((blocks8, groups * cols), F32),
            jax.ShapeDtypeStruct((sorted_keys, width), BF16),
            jax.ShapeDtypeStruct((sorted_keys, 128), BF16),
            jax.ShapeDtypeStruct((sorted_keys, width), BF16),
            jax.ShapeDtypeStruct((sorted_keys, width), BF16),
        ],
        cost_estimate=cost(70),
        compiler_params=pltpu.CompilerParams(vmem_limit_bytes=VMEM),
        name="attend",
    )(*tab, query, key_weight, value_weight, *norms)


def attend_back(
    tab, query, grads, outputs, lse, ks, vs, key_weight, value_weight, ns, bias,
    unit_size, units, items, heads,
):
    feats = heads * HEAD
    cols = heads * QROWS
    rows, width = query.shape
    groups = width // feats
    blocks = rows // QROWS
    once = pl.Buffered(1) if units > 16 else None

    def part(rows, columns=feats):
        return pl.BlockSpec((rows, columns), lambda group, *_: (0, group), pipeline_mode=once)

    def whole(rows, columns):
        return pl.BlockSpec(
            (rows, columns), lambda group, *_: (0, 0), pipeline_mode=pl.Buffered(1)
        )

    return pl.pallas_call(
        functools.partial(attend_back_kernel, heads, units, items, unit_size),
        grid_spec=pltpu.PrefetchScalarGridSpec(
            num_scalar_prefetch=TABLES,
            grid=(groups,),
            in_specs=[
                part(rows),
                part(grads.shape[0]),
                part(rows),
                part(lse.shape[0], cols),
                part(ks.shape[0]),
                part(ks.shape[0]),
                part(width),
                part(width),
                whole(*ns.shape),
                whole(*bias.shape),
            ],
            out_specs=[
                part(grads.shape[0]),
                part(width),
                part(width),
                whole(units * HALF * ROWW, width),
            ],
            scratch_shapes=[
                pltpu.VMEM((blocks, cols, feats), BF16),
                pltpu.VMEM((blocks, cols, feats), BF16),
                pltpu.VMEM((blocks, 8, cols), F32),
                pltpu.VMEM((blocks, cols, feats), F32),
                pltpu.VMEM((SPARE_KEYS, feats), F32),
                pltpu.VMEM((SPARE_KEYS, feats), F32),
                pltpu.VMEM((width, feats), F32),
                pltpu.VMEM((width, feats), F32),
                pltpu.VMEM(ns.shape, BF16),
                pltpu.VMEM((rows, grads.shape[0]), BF16),
                pltpu.VMEM((rows, feats), BF16),
                pltpu.VMEM((rows, feats), BF16),
                pltpu.VMEM((unit_size, width), BF16),
            ],
        ),
        out_shape=[
            jax.ShapeDtypeStruct(grads.shape, BF16),
            jax.ShapeDtypeStruct((width, width), BF16),
            jax.ShapeDtypeStruct((width, width), BF16),
            jax.ShapeDtypeStruct((units * HALF * ROWW, width), BF16),
        ],
        cost_estimate=cost(90),
        compiler_params=pltpu.CompilerParams(vmem_limit_bytes=VMEM),
        name="attend_back",
    )(*tab, query, grads, outputs, lse, ks, vs, key_weight, value_weight, ns, bias)


@functools.cache
def most_rows(cycle_size, item_count):
    rows = np.arange(SLOTS)[:, None] * cycle_size + np.arange(cycle_size)
    most_keys = most_unit = most_queries = 0
    lists = [()]
    while lists:
        heights = lists.pop()
        if len(heights) < item_count:
            for height in (24, 30):
                if sum(heights) + height <= SLOTS * cycle_size:
                    lists.append(heights + (height,))
        if not heights:
            continue
        ends = np.cumsum(heights)
        number = np.searchsorted(ends, rows, side="right")
        wide = np.array([24 if height == 24 else ROWW for height in heights] + [0])[number]
        kinds = np.arange(len(heights))
        counts = [((number == kind) * wide) for kind in kinds] + [ROWW - wide]
        counts = np.stack(counts)

        def rounded(values, align):
            return -(-values // align) * align

        units = rounded(counts.reshape(len(counts), 2, HALF, cycle_size).sum(2), 16)
        most_unit = max(most_unit, units.sum(0).max())
        keys = units.sum((1, 2))
        keys = rounded(keys[:-1], KEYS).sum() + rounded(keys[-1], SPARE_KEYS)
        most_keys = max(most_keys, keys)
        most_queries = max(most_queries, rounded(counts.sum(1), QROWS).sum(0).max())
    return int(most_keys), int(most_unit), int(most_queries)


def passed(value, axis, target):
    pairs = [(source, target(source)) for source in range(lax.axis_size(axis))]
    return lax.ppermute(value, axis, pairs)


def passed_along(value, axis, steps):
    count = lax.axis_size(axis)
    return passed(value, axis, lambda source: (source + steps) % count)


def tied(*values):
    return lax.optimization_barrier(values)


def to_sibling(value):
    return passed(value, "blk", lambda source: source ^ 1)


def gelu_tanh(values):
    return (
        0.5
        * values
        * (1.0 + jnp.tanh(0.7978845608028654 * (values + 0.044715 * values * values * values)))
    )


def gelu_back(values, gradient):
    return jax.vjp(gelu_tanh, values)[1](gradient)[0]


def item_facts(lengths):
    facts, start = [], 0
    for item in range(lengths.shape[0]):
        length = lengths[item]
        height = jnp.where(length == 1200, 30, jnp.where(length == 576, 24, 0))
        width = jnp.where(length == 1200, 40, 24)
        facts.append((start, start + height, height, width))
        start = start + height
    return facts


def row_facts(facts, rows):
    number = jnp.full_like(rows, len(facts))
    local, height, width = rows, jnp.zeros_like(rows), jnp.zeros_like(rows)
    for item, (start, end, item_height, item_width) in enumerate(facts):
        inside = (rows >= start) & (rows < end)
        number = jnp.where(inside, item, number)
        local = jnp.where(inside, rows - start, local)
        height = jnp.where(inside, item_height, height)
        width = jnp.where(inside, item_width, width)
    return number, local, height, width


def tap_masks(local_row, height, width):
    column = lax.broadcasted_iota(jnp.int32, (1, ROWW), 1)
    is_real = column < width
    all_masks = []
    for row_step in (-1, 0, 1):
        rows_fine = (local_row + row_step >= 0) & (local_row + row_step < height)
        for col_step in (-1, 0, 1):
            cols_fine = (column + col_step >= 0) & (column + col_step < width)
            all_masks.append(is_real & rows_fine & cols_fine)
    return is_real, all_masks


def side_shift(values, col_step):
    if col_step == 0:
        return values
    empty_col = jnp.zeros_like(values[:, :1])
    if col_step < 0:
        return jnp.concatenate([empty_col, values[:, :-1]], axis=1)
    return jnp.concatenate([values[:, 1:], empty_col], axis=1)


def from_above(values, cycle_pos):
    got = passed_along(values, "blk", 1)
    empty_row = jnp.zeros_like(values[:1])
    return jnp.where(cycle_pos == 0, jnp.concatenate([empty_row, got[:-1]], axis=0), got)


def from_below(values, cycle_pos, cycle_size):
    got = passed_along(values, "blk", -1)
    empty_row = jnp.zeros_like(values[:1])
    return jnp.where(
        cycle_pos == cycle_size - 1, jnp.concatenate([got[1:], empty_row], axis=0), got
    )


def upsample_forward(values, all_masks, cycle_pos, cycle_size):
    center = values.astype(F32)
    row_above = from_above(values, cycle_pos)
    row_below = from_below(values, cycle_pos, cycle_size)
    upper_value = jnp.where(all_masks[1][:, :, None], row_above, values).astype(F32)
    lower_value = jnp.where(all_masks[7][:, :, None], row_below, values).astype(F32)
    pieces = []
    for half_rows in (0.75 * center + 0.25 * upper_value, 0.75 * center + 0.25 * lower_value):
        left_value = jnp.where(all_masks[3][:, :, None], side_shift(half_rows, -1), half_rows)
        right_value = jnp.where(all_masks[5][:, :, None], side_shift(half_rows, 1), half_rows)
        pieces.append(0.75 * half_rows + 0.25 * left_value)
        pieces.append(0.75 * half_rows + 0.25 * right_value)
    joined = jnp.concatenate(pieces, axis=2)
    return joined.reshape(-1, joined.shape[2])


def upsample_back_columns(gradient, all_masks):
    channels = gradient.shape[2] // 4
    left_fine = all_masks[3][:, :, None]
    right_fine = all_masks[5][:, :, None]
    halves = []
    for half in (0, 1):
        left_part = gradient[:, :, 2 * half * channels : (2 * half + 1) * channels].astype(F32)
        right_part = gradient[:, :, (2 * half + 1) * channels : (2 * half + 2) * channels].astype(
            F32
        )
        side = jnp.where(right_fine, side_shift(left_part, 1), 0.0)
        side = side + jnp.where(left_fine, 0.0, left_part)
        side = side + jnp.where(left_fine, side_shift(right_part, -1), 0.0)
        side = side + jnp.where(right_fine, 0.0, right_part)
        halves.append(0.75 * (left_part + right_part) + 0.25 * side)
    return [half.astype(BF16) for half in halves]


def upsample_back_rows(upper, lower, upper_next, lower_prev, all_masks):
    up_fine = all_masks[1][:, :, None]
    down_fine = all_masks[7][:, :, None]
    rows = jnp.where(down_fine, upper_next, lower).astype(F32)
    rows = rows + jnp.where(up_fine, lower_prev, upper).astype(F32)
    return 0.75 * (upper.astype(F32) + lower.astype(F32)) + 0.25 * rows


def first_slot(begin, device, cycle_size):
    return -((device - begin) // cycle_size)


def to_windows(values, cycle_pos, cycle_size):
    window = SLOTS + 2 * REACH
    many = -(-window // cycle_size)
    spare = many + 1
    padded = jnp.pad(values, ((spare, spare), (0, 0), (0, 0)))
    sends = []
    for target in range(cycle_size):
        slot = first_slot(SLOTS * target - REACH, cycle_pos, cycle_size) + spare
        sends.append(lax.dynamic_slice_in_dim(padded, slot, many, axis=0))
    got = lax.all_to_all(jnp.stack(sends), "blk", 0, 0)
    got = jnp.swapaxes(got, 0, 1)
    begin = SLOTS * cycle_pos - REACH
    turn = begin - (begin // cycle_size) * cycle_size
    got = lax.dynamic_slice_in_dim(jnp.concatenate([got, got], axis=1), turn, cycle_size, axis=1)
    return got.reshape((many * cycle_size,) + values.shape[1:])[:window]


def from_windows(values, cycle_pos, cycle_size):
    many = -(-SLOTS // cycle_size)
    padded = jnp.pad(values, ((0, many * cycle_size), (0, 0), (0, 0)))
    begin = SLOTS * cycle_pos
    sends = []
    for target in range(cycle_size):
        slot = first_slot(begin, target, cycle_size)
        for extra in range(many):
            row = (slot + extra) * cycle_size + target - begin
            sends.append(lax.dynamic_slice_in_dim(padded, row, 1, axis=0))
    sends = jnp.concatenate(sends, axis=0).reshape((cycle_size, many) + values.shape[1:])
    got = lax.all_to_all(sends, "blk", 0, 0).reshape((cycle_size * many,) + values.shape[1:])
    rows = []
    for slot in range(SLOTS):
        row = slot * cycle_size + cycle_pos
        source = row // SLOTS
        extra = slot - first_slot(source * SLOTS, cycle_pos, cycle_size)
        rows.append(lax.dynamic_slice_in_dim(got, source * many + extra, 1, axis=0))
    return jnp.concatenate(rows, axis=0)


def dot32(left, right, **more):
    return jnp.dot(left, right, preferred_element_type=F32, **more)


def dot_t(left, right):
    return lax.dot_general(left, right, NT, preferred_element_type=F32)


def t_dot(left, right):
    return lax.dot_general(left, right, (((0,), (0,)), ((), ())), preferred_element_type=F32)


def halved(values, device, bit, axis, pairs_axis):
    half = values.shape[axis] // 2
    mine = (device >> bit) & 1
    keep = lax.dynamic_slice_in_dim(values, mine * half, half, axis=axis)
    send = lax.dynamic_slice_in_dim(values, (1 - mine) * half, half, axis=axis)
    got = passed(send, pairs_axis, lambda source: source ^ (1 << bit))
    return (keep.astype(F32) + got.astype(F32)).astype(BF16)


def core_summed(shares, core):
    cycle_size, rows, width = shares.shape
    paired = shares.reshape(cycle_size // 2, 2, rows, width)
    keep = lax.dynamic_index_in_dim(paired, core, 1, keepdims=False)
    send = lax.dynamic_index_in_dim(paired, 1 - core, 1, keepdims=False)
    return (keep.astype(F32) + to_sibling(send).astype(F32)).astype(BF16)


def added_over_chips(values, chip):
    chips, rows, _ = values.shape
    half = rows // 2
    both = []
    for part, way in ((values[:, :half], 1), (values[:, half:], -1)):

        def block(offset, part=part, way=way):
            return lax.dynamic_index_in_dim(
                part, (chip - way * offset) % chips, 0, keepdims=False
            ).astype(F32)

        moving = block(1)
        for step in range(2, chips + 1):
            moving = passed_along(moving.astype(BF16), "blk", 2 * way).astype(F32) + block(step)
        both.append(moving.astype(BF16))
    return jnp.concatenate(both, axis=0)


def gathered_over_groups(values, dp_pos):
    groups = lax.axis_size("dp")
    bits = groups.bit_length() - 1
    half = values.shape[0] // 2
    both = []
    for part, order in ((values[:half], range(bits)), (values[half:], range(bits - 1, -1, -1))):
        held = part[(None,) * bits]
        for bit in order:
            axis = bits - 1 - bit
            got = passed(held, "dp", lambda source, bit=bit: source ^ (1 << bit))
            mine = (dp_pos >> bit) & 1
            held = jnp.where(
                mine == 0,
                jnp.concatenate([held, got], axis=axis),
                jnp.concatenate([got, held], axis=axis),
            )
        both.append(held.reshape((groups,) + part.shape))
    return jnp.concatenate(both, axis=1)


def small_sums(values, core, chip, dp_pos):
    values = core_summed(values, core)
    for bit in range(lax.axis_size("dp").bit_length() - 1):
        got = passed(values, "dp", lambda source, bit=bit: source ^ (1 << bit))
        values = (values.astype(F32) + got.astype(F32)).astype(BF16)
    chips = values.shape[0]
    total = lax.dynamic_index_in_dim(values, chip, 0, keepdims=False).astype(F32)
    for step in range(1, chips):
        send = lax.dynamic_index_in_dim(values, (chip + step) % chips, 0, keepdims=False)
        total = total + passed_along(send, "blk", 2 * step).astype(F32)
    return total


def finished(late, orders, chip, dp_pos):
    groups = lax.axis_size("dp")
    bits = groups.bit_length() - 1
    chips = late[0].shape[0]
    joined = jnp.concatenate([part.reshape(chips, -1, 256) for part in late], axis=1)
    whole = gathered_over_groups(added_over_chips(joined, chip), dp_pos)
    out, place = [], 0
    for part, order in zip(late, orders):
        rows, width = part.shape[1:]
        size = rows * width // 256
        pieces = []
        for turn in range(groups):
            device = sum(((turn >> (bits - 1 - index)) & 1) << bit for index, bit in enumerate(order))
            pieces.append(whole[device, place : place + size].reshape(rows, width))
        out.append(jnp.concatenate(pieces, axis=0).astype(F32))
        place += size
    return out


def shards(
    tokens,
    item_lengths,
    dataset_ids,
    dataset_table,
    norm1_gain,
    norm1_bias,
    query_weight,
    key_weight,
    value_weight,
    out_weight,
    norm2_gain,
    norm2_bias,
    fc1_weight,
    fc2_weight,
    project_weight,
    unit1_first,
    unit1_second,
    unit2_first,
    unit2_second,
    output_weight,
    block_cotangent,
    merged_cotangent,
):
    cycle_size = lax.axis_size("blk")
    cycle_pos = lax.axis_index("blk")
    chips = cycle_size // 2
    chip, core = cycle_pos // 2, cycle_pos % 2
    lengths = item_lengths[0]
    item_count = lengths.shape[0]
    kinds = item_count + 1
    width_model = tokens.shape[1]
    heads = 4 if cycle_size <= 8 else 2
    half_tokens = HALF * ROWW
    token_count = tokens.shape[0]

    facts = item_facts(lengths)
    own_rows = lax.broadcasted_iota(jnp.int32, (SLOTS, 1), 0) * cycle_size + cycle_pos
    number, local_row, height, width = row_facts(facts, own_rows)
    is_real, all_masks = tap_masks(local_row, height, width)
    units = 4 * chips
    most_keys, most_unit, query_rows = most_rows(cycle_size, item_count)
    unit_size = most_unit + 48
    sorted_keys = (most_keys + 128 + ROWS - 1) // ROWS * ROWS
    tab = geometry(lengths, cycle_pos, cycle_size, unit_size)
    ids = dataset_ids[0]
    gain_one, bias_one = norm1_gain.reshape(1, -1), norm1_bias.reshape(1, -1)

    stream_start, normed_one, query = own_start(
        tab, ids, tokens, dataset_table, gain_one, bias_one, query_weight, query_rows
    )
    ahead, behind = tokens[:half_tokens], tokens[half_tokens:]
    sorted_norms = []
    for step in range(chips):
        if step:
            ahead = passed_along(ahead, "blk", 2)
            behind = passed_along(behind, "blk", -2)
            ahead, behind, sorted_norms[-1] = tied(ahead, behind, sorted_norms[-1])
        if step == 1:
            ahead, behind, merged_cotangent, stream_start, normed_one, query = tied(
                ahead, behind, merged_cotangent, stream_start, normed_one, query
            )
        mine = jnp.concatenate([ahead, behind], axis=0)
        sorted_norms.append(
            sort_step(
                step, tab, ids, mine, to_sibling(mine), dataset_table, gain_one, bias_one, unit_size
            )
        )
    upper, lower = upsample_back_columns(
        merged_cotangent.reshape(SLOTS, ROWW, -1), all_masks
    )
    sorted_norms[-1], upper, lower = tied(sorted_norms[-1], upper, lower)
    upper_next = from_below(upper, cycle_pos, cycle_size)
    lower_prev = from_above(lower, cycle_pos)
    attended, outputs, lse, sorted_norm, bias, ks, vs = attend(
        tab, query, key_weight, value_weight, sorted_norms, sorted_keys, units, kinds, heads
    )

    attended, upper_next, lower_prev = tied(attended, upper_next, lower_prev)

    def as_cells(flattened):
        return flattened.reshape(SLOTS, ROWW, flattened.shape[-1])

    after_attn = stream_start + dot32(attended, out_weight)
    normed_two = layer_norm(after_attn, norm2_gain, norm2_bias).astype(BF16)
    pre_act = dot32(normed_two, fc1_weight)
    hidden = gelu_tanh(pre_act).astype(BF16)
    block_out = (after_attn + dot32(hidden, fc2_weight)).astype(BF16)
    reassembled_own = dot32(block_out, project_weight).astype(BF16)

    mapped_grad_own = upsample_back_rows(
        upper, lower, upper_next, lower_prev, all_masks
    ).astype(BF16)
    channels = mapped_grad_own.shape[-1]
    arrived = to_windows(
        jnp.concatenate([as_cells(reassembled_own), mapped_grad_own], axis=2), cycle_pos, cycle_size
    )
    windows = jnp.pad(arrived, ((0, 0), (0, PITCH - ROWW), (0, 0))).reshape(-1, 2 * channels)
    reassembled_grad, mapped, conv_shares = merge(
        tab, windows, (unit1_first, unit1_second, unit2_first, unit2_second), output_weight, cycle_size
    )
    conv_shares = conv_shares.reshape(cycle_size, -1, channels)

    def own_window(values):
        return values.reshape(SLOTS, PITCH, channels)[:, :ROWW]

    def shared_out(*gradients):
        parts = []
        for gradient in gradients:
            parts.append(gradient.astype(BF16).reshape(cycle_size, -1, gradient.shape[-1]))
        return jnp.concatenate(parts, axis=1) if len(parts) > 1 else parts[0]

    dp_pos = lax.axis_index("dp")
    groups = lax.axis_size("dp")
    bits = groups.bit_length() - 1
    one_way = list(range(bits))
    other_way = one_way[::-1]

    def wide(gradient):
        return gradient.reshape(cycle_size, -1, width_model)

    def scattered(shares):
        count, share_rows, share_width = shares.shape
        parts = shares.reshape(count, groups, share_rows // groups, share_width)
        parts = jnp.swapaxes(parts, 0, 1).reshape(-1, share_width)
        part = lax.psum_scatter(parts, "dp", scatter_dimension=0, tiled=True)
        return part.reshape(count, -1, 256)

    def dp_halved(values, order, index):
        return halved(values, dp_pos, order[index], 1, "dp")

    returned = from_windows(
        jnp.concatenate([own_window(reassembled_grad), own_window(mapped)], axis=2),
        cycle_pos,
        cycle_size,
    )
    reassembled_grad = returned[:, :, :channels].reshape(-1, channels)
    merged = upsample_forward(returned[:, :, channels:], all_masks, cycle_pos, cycle_size).astype(
        BF16
    )

    project_grad = t_dot(block_out, reassembled_grad)
    block_grad = block_cotangent.astype(F32) + dot_t(reassembled_grad, project_weight)
    mlp_grad = block_grad.astype(BF16)
    fc2_grad = t_dot(hidden, mlp_grad)
    conv_sums = core_summed(conv_shares, core)
    pre_grad = gelu_back(pre_act, dot_t(mlp_grad, fc2_weight)).astype(BF16)
    fc1_grad = t_dot(normed_two, pre_grad)
    normed_two_grad = dot_t(pre_grad, fc1_weight)
    norm_two_pull = jax.vjp(layer_norm, after_attn, norm2_gain, norm2_bias)[1]
    attn_side, norm2_gain_grad, norm2_bias_grad = norm_two_pull(normed_two_grad)
    after_grad = block_grad + attn_side
    branch_grad = after_grad.astype(BF16)
    out_proj_grad = t_dot(attended, branch_grad)
    attended_grad = dot_t(branch_grad, out_weight).astype(BF16)

    rows = width_model // cycle_size
    rows = width_model // cycle_size
    model_sums = scattered(shared_out(fc2_grad, out_proj_grad, wide(project_grad)))
    fc1_sums = scattered(shared_out(fc1_grad))
    early = [model_sums, fc1_sums]
    early_sums = jnp.concatenate(early, axis=1)
    attended_grad, conv_sums = tied(attended_grad, conv_sums)
    conv_sums = dp_halved(conv_sums, one_way, 0)
    query_low, key_grad, value_grad, unit_grad = attend_back(
        tab, query, attended_grad, outputs, lse, ks, vs, key_weight, value_weight, sorted_norm,
        bias, unit_size, units, kinds, heads,
    )
    query_low, key_grad, value_grad, unit_grad, conv_sums = tied(
        query_low, key_grad, value_grad, unit_grad, conv_sums
    )
    query_grad = t_dot(normed_one, query_low)
    key_sums = core_summed(shared_out(key_grad, value_grad), core)
    query_sums = core_summed(shared_out(query_grad), core)

    def unit_part(step):
        part = unit_grad[4 * step * half_tokens : 4 * (step + 1) * half_tokens]
        part = part.reshape(4, half_tokens, width_model)
        return part[:2].astype(F32) + to_sibling(part[2:]).astype(F32)

    ahead = behind = None
    for step in range(chips - 1, -1, -1):
        part = unit_part(step)
        if ahead is None:
            ahead, behind = part[0], part[1]
        else:
            ahead = passed_along(ahead.astype(BF16), "blk", -2).astype(F32) + part[0]
            behind = passed_along(behind.astype(BF16), "blk", 2).astype(F32) + part[1]
            turn = chips - 1 - step
            if turn < bits:
                conv_sums = dp_halved(conv_sums, one_way, turn)
            if turn <= bits:
                key_sums = dp_halved(key_sums, one_way, turn - 1)
                query_sums = dp_halved(query_sums, other_way, turn - 1)
                ahead, behind, key_sums, query_sums, conv_sums = tied(
                    ahead, behind, key_sums, query_sums, conv_sums
                )
                if turn == 1:
                    early_sums = lax.psum_scatter(
                        early_sums.reshape(-1, 256), "blk", scatter_dimension=0, tiled=True
                    )
    normed_one_grad = jnp.concatenate([ahead, behind], axis=0) + dot_t(query_low, query_weight)

    norm_one_pull = jax.vjp(layer_norm, stream_start, norm1_gain, norm1_bias)[1]
    start_side, norm1_gain_grad, norm1_bias_grad = norm_one_pull(normed_one_grad)
    tokens_grad = after_grad + start_side
    table_rows = dataset_table.shape[0]
    dataset = jnp.full_like(number, -1)
    for item in range(item_count):
        dataset = jnp.where(number == item, ids[item], dataset)
    dataset = jnp.where(is_real, dataset, -1).reshape(1, -1)
    onehot = (dataset == lax.broadcasted_iota(jnp.int32, (table_rows, 1), 0)).astype(F32)
    table_grad = jnp.dot(onehot, tokens_grad, precision=HIGH)
    table_split = jnp.swapaxes(table_grad.reshape(table_rows, cycle_size, rows), 0, 1)
    small = [table_split.reshape(cycle_size, -1)] + [
        gradient.reshape(cycle_size, -1)
        for gradient in (norm1_gain_grad, norm1_bias_grad, norm2_gain_grad, norm2_bias_grad)
    ]
    small = jnp.concatenate(small, axis=1).astype(BF16)
    small_rows = -(-small.shape[1] // 1024) * 8
    small = jnp.pad(small, ((0, 0), (0, small_rows * 128 - small.shape[1])))
    small = small_sums(small.reshape(cycle_size, small_rows, 128), core, chip, dp_pos).reshape(-1)
    table_size = table_rows * rows
    norms = [small[table_size + index * rows :][:rows] for index in range(4)]

    unit_share = 9 * channels // cycle_size
    out_share = channels // cycle_size
    fc2_share = fc2_weight.shape[0] // cycle_size
    convs, keys_values, query_share = finished(
        [conv_sums, key_sums, query_sums], [one_way, one_way, other_way], chip, dp_pos
    )
    whole = gathered_over_groups(early_sums, dp_pos)
    shares, spot = [], 0
    for part, columns in zip(early, (width_model, fc1_weight.shape[1])):
        size = part.shape[1]
        shares.append(whole[:, spot : spot + size].reshape(-1, columns).astype(F32))
        spot += size
    models, fc1_share = shares
    return (
        block_out,
        merged,
        tokens_grad,
        small[:table_size].reshape(table_rows, rows),
        norms[0],
        norms[1],
        query_share,
        keys_values[:rows],
        keys_values[rows:],
        models[fc2_share : fc2_share + rows],
        norms[2],
        norms[3],
        fc1_share,
        models[:fc2_share],
        models[fc2_share + rows :].reshape(rows, channels),
        convs[:unit_share],
        convs[unit_share : 2 * unit_share],
        convs[2 * unit_share : 3 * unit_share],
        convs[3 * unit_share : 4 * unit_share],
        convs[4 * unit_share :],
    )


def solution(mesh):
    split = P(("dp", "blk"), None)
    placed = (split, P("dp", None), P("dp", None)) + (P(),) * 17 + (split, split)
    rows, line = P("blk", None), P("blk")
    return jax.shard_map(
        shards,
        mesh=mesh,
        in_specs=placed,
        out_specs=(
            split, split, split, P(None, "blk"), line, line, rows, rows, rows, rows, line, line,
            rows, rows, rows, rows, rows, rows, rows, rows,
        ),
        check_vma=False,
    )
```

time: 752 us -> 632 us (0.84)
  other arithmetic: 95.9 us -> 32.2 us
  Pallas kernels: 173 us -> 218 us
  matrix products: 89.8 us -> 49.1 us
  waiting for transfers between devices: 179 us -> 139 us
  local copies, waits for them, and re-layouts: 107 us -> 75 us
  between operations: 5.94 us -> 21.9 us
    ppermute x50 -> x53, waiting for transfers between devices: 159 us -> 89.9 us  [passed(): return lax.ppermute(value, axis, pairs)]
    pallas_call x1 -> x8, Pallas kernels: 92.6 us -> 144 us  [the longest x1 94 us: attend_back(): pl.pallas_call(functools.partial(attend_back_kernel, heads, units, items,...]
    convert_element_type x22 -> x14, other arithmetic: 26.9 us -> 6.09 us  [the longest x4 2.85 us: core_summed(): return (keep.astype(F32) + to_sibling(send).astype(F32)).astype(BF16)]
    dot_general x14 -> x1, matrix products: 17.5 us -> 0.6 us  [shards(): table_grad = jnp.dot(onehot, tokens_grad, precision=HIGH)]
    dot_general x15 -> x4, matrix products: 30.6 us -> 14 us  [dot32(): return jnp.dot(left, right, preferred_element_type=F32, **more)]
    dot_general x12 -> x5, matrix products: 24.7 us -> 9.7 us  [t_dot(): lax.dot_general(left, right, (((0,), (0,)), ((), ())), preferred_element_...]
    unnamed x52 -> x2, other arithmetic: 13.3 us -> 0.01 us
    all_to_all x1, waiting for transfers between devices: 11.1 us -> 24.5 us  [to_windows(): got = lax.all_to_all(jnp.stack(sends), 'blk', 0, 0)]
  transfers between devices with their start and end apart: 52 -> 58, of which waited for: 27 -> 28; matrix products, arithmetic and copies ran while one was open for 21% -> 13% of each run, Pallas kernels for 12% -> 31%
where the time goes in v2:
time: 632 us; the launch traced here: 623 us
  Pallas kernels  218 us (34%)
  waiting for transfers between devices  139 us (22%)
  starting transfers between devices  88.7 us (14%)
  local copies, waits for them, and re-layouts  75 us (12%)
  matrix products  49.1 us (8%)
  other arithmetic  32.2 us (5%)
  between operations  21.9 us (3%)
    pallas_call x1, Pallas kernels, attend_back(): pl.pallas_call(functools.partial(attend_back_kernel, heads, units, items,...  94 us
    ppermute x53, waiting for transfers between devices, passed(): return lax.ppermute(value, axis, pairs)  89.9 us
    ppermute x53, starting transfers between devices, passed(): return lax.ppermute(value, axis, pairs)  79.7 us
    pallas_call x1, Pallas kernels, attend(): pl.pallas_call(functools.partial(attend_kernel, heads, units, items), gri...  73.4 us
    dot_general x5, matrix products, dot_t(): return lax.dot_general(left, right, NT, preferred_element_type=F32)  24.8 us
    all_to_all x1, waiting for transfers between devices, to_windows(): got = lax.all_to_all(jnp.stack(sends), 'blk', 0, 0)  24.5 us
    unnamed x172, local copies, waits for them, and re-layouts  24.4 us
    pallas_call x4, Pallas kernels, sort_step(): pl.pallas_call(functools.partial(sort_step_kernel, step), grid_spec=pltpu...  20.1 us
  transfers between devices with their start and end apart: 58, of which 28 were waited for; matrix products, arithmetic and copies ran while one was open for 13% of the time, Pallas kernels for 31%

profile of v2, /device:TPU:0, one launch (start us, length us, event | category | flops | bytes accessed | tf_op | source)
XLA Modules:
  0.0 623.3 jit_solution(10248329580697897056)
XLA Ops:
  8.9 4.7 collective-permute-start.1
  14.8 4.9 geometry.1
  19.7 5.4 own_start.1
  26.0 5.0 sort_step.4.refs_21_
  38.2 3.1 compare_select_fusion.3
  42.4 2.7 collective-permute-start.4
  45.1 5.0 sort_step.5.refs_22_
  50.1 4.4 collective-permute-done.3
  54.5 6.4 %collective-permute-done.4 = bf16[240,768]{1,0:T(8,128)(2,1)S(1)} collective-permute-done((bf16[240,768]{1,0:T(8,128)(2,1)S(1)}, bf16[240,768]{1,0:T(8,128)(2,1)S(1)}, u32[]{:S(2)}, u32[]{:S(2)}) %collective-permute-start.4) | collective-permute-done | bytes 368672 | tf_op jit(solution)/shard_map/ppermute | solution.py:873
  62.6 14.0 %collective-permute-start.7 = (bf16[240,768]{1,0:T(8,128)(2,1)S(1)}, bf16[240,768]{1,0:T(8,128)(2,1)S(1)}, u32[]{:S(2)}, u32[]{:S(2)}) collective-permute-start(bf16[240,768]{1,0:T(8,128)(2,1)S(1)} %collective-permute-done.4), channel_id=1, source_target_pairs={{0,6},{1,7},{2,0},{3,1},{4,2},{5,3},{6,4},{7,5},{8,14},{9,15},{10,... | collective-permute-start | bytes 1105928 | tf_op jit(solution)/shard_map/ppermute | solution.py:873
  76.6 5.0 sort_step.6.refs_23_
  81.6 3.3 collective-permute-done.7
  88.1 5.0 sort_step.7.refs_24_
  93.1 3.9 collective-permute-start.10
  97.0 73.4 %attend.1 = (bf16[480,768]{1,0:T(8,128)(2,1)}, f32[704,768]{1,0:T(8,128)}, f32[16,768]{1,0:T(8,128)}, bf16[5120,768]{1,0:T(8,128)(2,1)}, bf16[5120,128]{1,0:T(8,...) custom-call(s32[80]{0:T(128)} %get-tuple-element.107.refs_0_, s32[80]{0:T(128)} %get-tuple-element.108.refs_1_, ...), custom_call_target="tpu_custom_call" | custom-call | flops 70000001024 | bytes 1000000 | tf_op jit(solution)/shard_map/attend/pallas_call | solution.py:731
  175.2 4.9 fusion.63
  180.1 8.0 %add_convert_fusion.1 = bf16[480,768]{1,0:T(8,128)(2,1)S(1)} fusion(f32[480,768]{1,0:T(8,128)S(1)} %get-tuple-element.266, bf16[3072,768]{1,0:T(8,128)(2,1)} %param.35, f32[480,3072]{1,0:T(8,128)S(1)} %fusion.63), kind=kOutput, calls=%fused_computation.51 | convolution fusion | flops 2278932480 | bytes 12828672 | tf_op jit(solution)/shard_map/dot_general | solution.py:1044
  194.3 4.7 all-to-all-start
  199.3 24.5 %all-to-all-done = bf16[8,3,40,512]{3,2,1,0:T(8,128)(2,1)} async-done(((bf16[8,3,40,512]{3,2,1,0:T(8,128)(2,1)}), bf16[8,3,40,512]{3,2,1,0:T(8,128)(2,1)}, u32[]{:S(2)}, u32[]{:S(2)}) %all-to-all-start) | async-done | bytes 983072 | tf_op jit(solution)/shard_map/all_to_all | solution.py:1014
  226.5 20.0 %merge.1 = (bf16[576,256]{1,0:T(8,128)(2,1)}, bf16[576,256]{1,0:T(8,128)(2,1)}, bf16[9472,256]{1,0:T(8,128)(2,1)}) custom-call(s32[24]{0:T(128)} %get-tuple-element.114.refs_15_.wwidth, s32[24]{0:T(128)} %get-tuple-element.115.refs_16_.wup, s32[24]{0:T(128)} %get-tuple-element.116.refs_17_.wdown, bf16[1152,512]{1,0:T(8,128)(2,1)} %bitcast.241, ...), custom_call_target="tpu_custom_call" | custom-call | flops 24999999488 | bytes 1000000 | tf_op jit(solution)/shard_map/merge/pallas_call | solution.py:696
  249.7 4.2 all-to-all-start.1
  254.5 17.6 %all-to-all-done.1 = bf16[8,2,40,512]{3,2,1,0:T(8,128)(2,1)} async-done(((bf16[8,2,40,512]{3,2,1,0:T(8,128)(2,1)}), bf16[8,2,40,512]{3,2,1,0:T(8,128)(2,1)}, u32[]{:S(2)}, u32[]{:S(2)}) %all-to-all-start.1) | async-done | bytes 655392 | tf_op jit(solution)/shard_map/all_to_all | solution.py:1033
  283.5 11.2 %fusion.3 = bf16[480,3072]{1,0:T(8,128)(2,1)S(1)} fusion(f32[480,3072]{1,0:T(8,128)} %copy-done.61, bf16[3072,768]{1,0:T(8,128)(2,1)} %param.35, f32[480,768]{1,0:T(8,128)S(1)} %convert_add_fusion.6), kind=kOutput, calls=%fused_computation.8 | convolution fusion | flops 2300682240 | bytes 15040512 | tf_op jit(solution)/shard_map/dot_general | solution.py:1048
  294.7 3.4 convolution_convert_fusion
  298.1 2.6 copy.53
  302.5 3.5 dynamic-slice_bitcast_fusion
  306.5 3.2 collective-permute-start.13
  310.9 1.9 convert_element_type.518
  312.9 7.7 %multiply_reduce_fusion = (bf16[768]{0:T(1024)(128)(2,1)S(1)}, f32[480]{0:T(512)S(1)}, bf16[768]{0:T(1024)(128)(2,1)S(1)}, f32[480,768]{1,0:T(8,128)}) fusion(f32[480,768]{1,0:T(8,128)} %copy-done.3, f32[480]{0:T(512)S(1)} %fusion.59, f32[480]{0:T(512)S(1)} %broadcast_multiply_fusion.1, f32[768]{0:T(1024)S(1)} %copy-done.51, ...), kind=kOutput, calls=%fused_computation.43 | convolution fusion | flops 2267871232 | bytes 10628736 | tf_op jit(solution)/shard_map/dot_general | solution.py:1048
  321.4 2.7 fusion.65
  326.4 3.5 convolution_convert_fusion.1
  330.4 3.0 copy.52
  333.6 3.2 convolution_convert_fusion.4.refs_19_
  342.2 2.4 fusion.6
  347.6 94.0 %attend_back.1 = (bf16[480,768]{1,0:T(8,128)(2,1)}, bf16[768,768]{1,0:T(8,128)(2,1)}, bf16[768,768]{1,0:T(8,128)(2,1)}, bf16[3840,768]{1,0:T(8,128)(2,1)}) custom-call(s32[80]{0:T(128)} %get-tuple-element.107.refs_0_, s32[80]{0:T(128)} %get-tuple-element.108.refs_1_, s32[80]{0:T(128)} %get-tuple-element.109.refs_2_, s32[6]{0:T(128)} %get-tuple-element.110.refs_3_, ...), custom_call_target="tpu_custom_call" | custom-call | flops 89999998976 | bytes 1000000 | tf_op jit(solution)/shard_map/attend_back/pallas_call | solution.py:788
  449.6 11.1 %collective-permute-done.24 = bf16[4,296,256]{2,1,0:T(8,128)(2,1)S(1)} collective-permute-done((bf16[4,296,256]{2,1,0:T(8,128)(2,1)S(1)}, bf16[4,296,256]{2,1,0:T(8,128)(2,1)S(1)}, u32[]{:S(2)}, u32[]{:S(2)}) %collective-permute-start.24) | collective-permute-done | bytes 606240 | tf_op jit(solution)/shard_map/ppermute | solution.py:873
  462.8 2.6 collective-permute-start.17
  465.7 7.4 %collective-permute-start.21 = (bf16[4,96,768]{2,1,0:T(8,128)(2,1)S(1)}, bf16[4,96,768]{2,1,0:T(8,128)(2,1)S(1)}, u32[]{:S(2)}, u32[]{:S(2)}) collective-permute-start(bf16[4,96,768]{2,1,0:T(8,128)(2,1)S(1)} %constant_dynamic-slice_fusion.10), channel_id=1, source_target_pairs={{0,8},{8,0},{16,24},{24,16},{1,9},{9,1},{17,25},{25,17},{2,10},{10... | collective-permute-start | bytes 1769480 | tf_op jit(solution)/shard_map/ppermute | solution.py:873
  474.7 6.0 collective-permute-done.17
  480.8 4.8 collective-permute-done.21
  485.9 1.8 collective-permute-start.29
  491.6 3.2 collective-permute-done.28
  494.9 5.2 collective-permute-done.25
  500.2 7.1 %collective-permute-done.27 = bf16[240,768]{1,0:T(8,128)(2,1)S(1)} collective-permute-done((bf16[240,768]{1,0:T(8,128)(2,1)S(1)}, bf16[240,768]{1,0:T(8,128)(2,1)S(1)}, u32[]{:S(2)}, u32[]{:S(2)}) %collective-permute-start.27) | collective-permute-done | bytes 368672 | tf_op jit(solution)/shard_map/ppermute | solution.py:873
  513.9 3.5 collective-permute-start.30
  517.5 3.9 collective-permute-start.40
  521.9 4.4 collective-permute-start.49
  526.3 2.8 collective-permute-done.30
  529.1 8.5 %collective-permute-done.32 = bf16[240,768]{1,0:T(8,128)(2,1)S(1)} collective-permute-done((bf16[240,768]{1,0:T(8,128)(2,1)S(1)}, bf16[240,768]{1,0:T(8,128)(2,1)S(1)}, u32[]{:S(2)}, u32[]{:S(2)}) %collective-permute-start.32) | collective-permute-done | bytes 368672 | tf_op jit(solution)/shard_map/ppermute | solution.py:873
  537.9 2.2 multiply_reduce_fusion.1
  540.3 2.8 reshape.992
  543.1 3.8 reshape.990
  546.9 3.1 pad_maximum_fusion.1
  550.1 2.0 fusion.64
  557.1 2.4 collective-permute-done.34
  560.4 3.5 collective-permute-done.41
  564.7 3.6 collective-permute-start.38
  568.3 2.0 collective-permute-done.50
  570.4 2.6 collective-permute-done.37
  576.7 4.3 collective-permute-done.43
  584.6 6.4 %reduce-scatter.8.cloned.1.call-done = bf16[672,256]{1,0:T(8,128)(2,1)} async-done(((bf16[5376,256]{1,0:T(8,128)(2,1)}), bf16[672,256]{1,0:T(8,128)(2,1)}) %reduce-scatter.8.cloned.1.call-update) | async-done | bytes 344080 | tf_op jit(solution)/shard_map/reduce_scatter | solution.py:1340
  594.6 2.9 collective-permute-done.46
  601.7 4.6 collective-permute-done.47
  611.9 2.7 reshape.1007
  (413 shorter events, 107.8 us)
Async XLA Ops:
  7.2 166.4 %copy-start = (bf16[768,768]{1,0:T(8,128)(2,1)S(1)}, bf16[768,768]{1,0:T(8,128)(2,1)}, u32[]{:S(2)}) copy-start(bf16[768,768]{1,0:T(8,128)(2,1)} %param.31) | copy-start | bytes 3538948
  7.2 17.9 %collective-permute-start.2 = (bf16[480,768]{1,0:T(8,128)(2,1)}, bf16[480,768]{1,0:T(8,128)(2,1)S(1)}, u32[]{:S(2)}, u32[]{:S(2)}) collective-permute-start(bf16[480,768]{1,0:T(8,128)(2,1)} %refs_0_.2), channel_id=1, source_target_pairs={{0,1},{1,0},{2,3},{3,2},{4,5},{5,4},{6,7},{7,6},{8,9},{9,8},{10,11... | collective-permute-start | bytes 2211848 | tf_op jit(solution)/shard_map/ppermute | solution.py:873
  8.9 22.1 %collective-permute-start.1 = (bf16[240,768]{1,0:T(8,128)(2,1)S(1)}, bf16[240,768]{1,0:T(8,128)(2,1)S(1)}, u32[]{:S(2)}, u32[]{:S(2)}) collective-permute-start(bf16[240,768]{1,0:T(8,128)(2,1)S(1)} %get-tuple-element.213), channel_id=1, source_target_pairs={{0,6},{1,7},{2,0},{3,1},{4,2},{5,3},{6,4},{7,5},{8,14},{9,15},{10,... | collective-permute-start | bytes 1105928 | tf_op jit(solution)/shard_map/ppermute | solution.py:873
  13.6 17.4 %collective-permute-start = (bf16[240,768]{1,0:T(8,128)(2,1)S(1)}, bf16[240,768]{1,0:T(8,128)(2,1)S(1)}, u32[]{:S(2)}, u32[]{:S(2)}) collective-permute-start(bf16[240,768]{1,0:T(8,128)(2,1)S(1)} %get-tuple-element.214), channel_id=1, source_target_pairs={{0,2},{1,3},{2,4},{3,5},{4,6},{5,7},{6,0},{7,1},{8,10},{9,11},{10,... | collective-permute-start | bytes 1105928 | tf_op jit(solution)/shard_map/ppermute | solution.py:873
  31.1 14.0 %copy-start.39 = (bf16[480,768]{1,0:T(8,128)(2,1)}, bf16[480,768]{1,0:T(8,128)(2,1)S(1)}, u32[]{:S(2)}) copy-start(bf16[480,768]{1,0:T(8,128)(2,1)S(1)} %constant_dynamic-update-slice_fusion.refs_0_) | copy-start | bytes 2211844
  31.1 14.0 %collective-permute-start.5 = (bf16[480,768]{1,0:T(8,128)(2,1)S(1)}, bf16[480,768]{1,0:T(8,128)(2,1)}, u32[]{:S(2)}, u32[]{:S(2)}) collective-permute-start(bf16[480,768]{1,0:T(8,128)(2,1)S(1)} %constant_dynamic-update-slice_fusion.refs_0_), channel_id=1, source_target_pairs={{0,1},{1,0},{2,3},{3,2},{4,5},{5,4},{6,7},{7,6},{8,9},{9,8},{10,11... | collective-permute-start | bytes 2211848 | tf_op jit(solution)/shard_map/ppermute | solution.py:873
  41.3 13.3 %collective-permute-start.3 = (bf16[240,768]{1,0:T(8,128)(2,1)S(1)}, bf16[240,768]{1,0:T(8,128)(2,1)S(1)}, u32[]{:S(2)}, u32[]{:S(2)}) collective-permute-start(bf16[240,768]{1,0:T(8,128)(2,1)S(1)} %collective-permute-done), channel_id=1, source_target_pairs={{0,2},{1,3},{2,4},{3,5},{4,6},{5,7},{6,0},{7,1},{8,10},{9,11},{10,... | collective-permute-start | bytes 1105928 | tf_op jit(solution)/shard_map/ppermute | solution.py:873
  42.4 18.5 %collective-permute-start.4 = (bf16[240,768]{1,0:T(8,128)(2,1)S(1)}, bf16[240,768]{1,0:T(8,128)(2,1)S(1)}, u32[]{:S(2)}, u32[]{:S(2)}) collective-permute-start(bf16[240,768]{1,0:T(8,128)(2,1)S(1)} %collective-permute-done.1), channel_id=1, source_target_pairs={{0,6},{1,7},{2,0},{3,1},{4,2},{5,3},{6,4},{7,5},{8,14},{9,15},{10,... | collective-permute-start | bytes 1105928 | tf_op jit(solution)/shard_map/ppermute | solution.py:873
  60.9 15.6 %copy-start.40 = (bf16[480,768]{1,0:T(8,128)(2,1)}, bf16[480,768]{1,0:T(8,128)(2,1)S(1)}, u32[]{:S(2)}) copy-start(bf16[480,768]{1,0:T(8,128)(2,1)S(1)} %constant_dynamic-update-slice_fusion.2.refs_0_) | copy-start | bytes 2211844
  61.0 15.6 %collective-permute-start.8 = (bf16[480,768]{1,0:T(8,128)(2,1)S(1)}, bf16[480,768]{1,0:T(8,128)(2,1)}, u32[]{:S(2)}, u32[]{:S(2)}) collective-permute-start(bf16[480,768]{1,0:T(8,128)(2,1)S(1)} %constant_dynamic-update-slice_fusion.2.refs_0_), channel_id=1, source_target_pairs={{0,1},{1,0},{2,3},{3,2},{4,5},{5,4},{6,7},{7,6},{8,9},{9,8},{10,11... | collective-permute-start | bytes 2211848 | tf_op jit(solution)/shard_map/ppermute | solution.py:873
  61.1 20.5 %collective-permute-start.6 = (bf16[240,768]{1,0:T(8,128)(2,1)S(1)}, bf16[240,768]{1,0:T(8,128)(2,1)S(1)}, u32[]{:S(2)}, u32[]{:S(2)}) collective-permute-start(bf16[240,768]{1,0:T(8,128)(2,1)S(1)} %collective-permute-done.3), channel_id=1, source_target_pairs={{0,2},{1,3},{2,4},{3,5},{4,6},{5,7},{6,0},{7,1},{8,10},{9,11},{10,... | collective-permute-start | bytes 1105928 | tf_op jit(solution)/shard_map/ppermute | solution.py:873
  62.6 22.3 %collective-permute-start.7 = (bf16[240,768]{1,0:T(8,128)(2,1)S(1)}, bf16[240,768]{1,0:T(8,128)(2,1)S(1)}, u32[]{:S(2)}, u32[]{:S(2)}) collective-permute-start(bf16[240,768]{1,0:T(8,128)(2,1)S(1)} %collective-permute-done.4), channel_id=1, source_target_pairs={{0,6},{1,7},{2,0},{3,1},{4,2},{5,3},{6,4},{7,5},{8,14},{9,15},{10,... | collective-permute-start | bytes 1105928 | tf_op jit(solution)/shard_map/ppermute | solution.py:873
  85.0 2.3 collective-permute-start.9
  93.1 77.4 %collective-permute-start.10 = (bf16[12,40,256]{2,1,0:T(8,128)(2,1)S(1)}, bf16[12,40,256]{2,1,0:T(8,128)(2,1)}, u32[]{:S(2)}, u32[]{:S(2)}) collective-permute-start(bf16[12,40,256]{2,1,0:T(8,128)(2,1)S(1)} %get-tuple-element.130), channel_id=1, source_target_pairs={{0,7},{1,0},{2,1},{3,2},{4,3},{5,4},{6,5},{7,6},{8,15},{9,8},{10,9... | collective-permute-start | bytes 737288 | tf_op jit(solution)/shard_map/ppermute | solution.py:873
  97.0 74.6 %collective-permute-start.11 = (bf16[12,40,256]{2,1,0:T(8,128)(2,1)S(1)}, bf16[12,40,256]{2,1,0:T(8,128)(2,1)}, u32[]{:S(2)}, u32[]{:S(2)}) collective-permute-start(bf16[12,40,256]{2,1,0:T(8,128)(2,1)S(1)} %get-tuple-element.131), channel_id=1, source_target_pairs={{0,1},{1,2},{2,3},{3,4},{4,5},{5,6},{6,7},{7,0},{8,9},{9,10},{10,1... | collective-permute-start | bytes 737288 | tf_op jit(solution)/shard_map/ppermute | solution.py:873
  194.3 29.4 %all-to-all-start = ((bf16[8,3,40,512]{3,2,1,0:T(8,128)(2,1)}), bf16[8,3,40,512]{3,2,1,0:T(8,128)(2,1)}, u32[]{:S(2)}, u32[]{:S(2)}) async-start(bf16[8,3,40,512]{3,2,1,0:T(8,128)(2,1)} %bitcast_dynamic-update-slice_fusion), calls=%async_computation | async-start | bytes 1966080 | tf_op jit(solution)/shard_map/all_to_all | solution.py:1014
  249.7 22.4 %all-to-all-start.1 = ((bf16[8,2,40,512]{3,2,1,0:T(8,128)(2,1)}), bf16[8,2,40,512]{3,2,1,0:T(8,128)(2,1)}, u32[]{:S(2)}, u32[]{:S(2)}) async-start(bf16[8,2,40,512]{3,2,1,0:T(8,128)(2,1)} %bitcast.248), calls=%async_computation.1 | async-start | bytes 1310720 | tf_op jit(solution)/shard_map/all_to_all | solution.py:1033
  253.9 286.4 %reduce-scatter.6.cloned.1.call-start = ((), (), s32[]{:S(2)}) async-start(), calls=%async_computation.6 | async-start | bytes 5898240 | tf_op jit(solution)/shard_map/reduce_scatter | solution.py:1267
  300.7 242.4 %reduce-scatter.4.cloned.1.call-start = ((), (), s32[]{:S(2)}) async-start(), calls=%async_computation.5 | async-start | bytes 7864320 | tf_op jit(solution)/shard_map/reduce_scatter | solution.py:1267
  306.0 36.2 %collective-permute-start.14 = (bf16[4,1184,256]{2,1,0:T(8,128)(2,1)}, bf16[4,1184,256]{2,1,0:T(8,128)(2,1)}, u32[]{:S(2)}, u32[]{:S(2)}) collective-permute-start(bf16[4,1184,256]{2,1,0:T(8,128)(2,1)} %dynamic-slice_bitcast_fusion), channel_id=1, source_target_pairs={{0,1},{1,0},{2,3},{3,2},{4,5},{5,4},{6,7},{7,6},{8,9},{9,8},{10,11... | collective-permute-start | bytes 7274504 | tf_op jit(solution)/shard_map/ppermute | solution.py:873
  306.0 30.8 %collective-permute-start.12 = (bf16[12,40,256]{2,1,0:T(8,128)(2,1)}, bf16[12,40,256]{2,1,0:T(8,128)(2,1)}, u32[]{:S(2)}, u32[]{:S(2)}) collective-permute-start(bf16[12,40,256]{2,1,0:T(8,128)(2,1)} %get-tuple-element.228), channel_id=1, source_target_pairs={{0,1},{1,2},{2,3},{3,4},{4,5},{5,6},{6,7},{7,0},{8,9},{9,10},{10,1... | collective-permute-start | bytes 737288 | tf_op jit(solution)/shard_map/ppermute | solution.py:873
  306.5 31.2 %collective-permute-start.13 = (bf16[12,40,256]{2,1,0:T(8,128)(2,1)}, bf16[12,40,256]{2,1,0:T(8,128)(2,1)}, u32[]{:S(2)}, u32[]{:S(2)}) collective-permute-start(bf16[12,40,256]{2,1,0:T(8,128)(2,1)} %get-tuple-element.228), channel_id=1, source_target_pairs={{0,7},{1,0},{2,1},{3,2},{4,3},{5,4},{6,5},{7,6},{8,15},{9,8},{10,9... | collective-permute-start | bytes 737288 | tf_op jit(solution)/shard_map/ppermute | solution.py:873
  333.5 257.5 %reduce-scatter.8.cloned.1.call-start = ((), (), s32[]{:S(2)}) async-start(), calls=%async_computation.7 | async-start | bytes 3096576 | tf_op jit(solution)/shard_map/reduce_scatter | solution.py:1340
  347.2 94.5 %collective-permute-start.15 = (bf16[4,592,256]{2,1,0:T(8,128)(2,1)}, bf16[4,592,256]{2,1,0:T(8,128)(2,1)S(1)}, u32[]{:S(2)}, u32[]{:S(2)}) collective-permute-start(bf16[4,592,256]{2,1,0:T(8,128)(2,1)} %constant_dynamic-slice_fusion.11), channel_id=1, source_target_pairs={{0,8},{8,0},{16,24},{24,16},{1,9},{9,1},{17,25},{25,17},{2,10},{10... | collective-permute-start | bytes 3637256 | tf_op jit(solution)/shard_map/ppermute | solution.py:873
  444.3 5.0 collective-permute-start.22
  444.5 16.1 %collective-permute-start.24 = (bf16[4,296,256]{2,1,0:T(8,128)(2,1)S(1)}, bf16[4,296,256]{2,1,0:T(8,128)(2,1)S(1)}, u32[]{:S(2)}, u32[]{:S(2)}) collective-permute-start(bf16[4,296,256]{2,1,0:T(8,128)(2,1)S(1)} %constant_dynamic-slice_fusion.8), channel_id=1, source_target_pairs={{0,16},{8,24},{16,0},{24,8},{1,17},{9,25},{17,1},{25,9},{2,18},{10... | collective-permute-start | bytes 1818632 | tf_op jit(solution)/shard_map/ppermute | solution.py:873
  446.4 14.6 %collective-permute-start.16 = (bf16[2,240,768]{2,1,0:T(8,128)(2,1)S(1)}, bf16[2,240,768]{2,1,0:T(8,128)(2,1)S(1)}, u32[]{:S(2)}, u32[]{:S(2)}) collective-permute-start(bf16[2,240,768]{2,1,0:T(8,128)(2,1)S(1)} %bitcast.251), channel_id=1, source_target_pairs={{0,1},{1,0},{2,3},{3,2},{4,5},{5,4},{6,7},{7,6},{8,9},{9,8},{10,11... | collective-permute-start | bytes 2211848 | tf_op jit(solution)/shard_map/ppermute | solution.py:873
  446.6 16.2 %collective-permute-start.20 = (bf16[4,192,768]{2,1,0:T(8,128)(2,1)S(1)}, bf16[4,192,768]{2,1,0:T(8,128)(2,1)S(1)}, u32[]{:S(2)}, u32[]{:S(2)}) collective-permute-start(bf16[4,192,768]{2,1,0:T(8,128)(2,1)S(1)} %fusion.15), channel_id=1, source_target_pairs={{0,1},{1,0},{2,3},{3,2},{4,5},{5,4},{6,7},{7,6},{8,9},{9,8},{10,11... | collective-permute-start | bytes 3538952 | tf_op jit(solution)/shard_map/ppermute | solution.py:873
  448.9 63.3 %collective-permute-start.31 = (bf16[2,240,768]{2,1,0:T(8,128)(2,1)}, bf16[2,240,768]{2,1,0:T(8,128)(2,1)}, u32[]{:S(2)}, u32[]{:S(2)}) collective-permute-start(bf16[2,240,768]{2,1,0:T(8,128)(2,1)} %bitcast.53), channel_id=1, source_target_pairs={{0,1},{1,0},{2,3},{3,2},{4,5},{5,4},{6,7},{7,6},{8,9},{9,8},{10,11... | collective-permute-start | bytes 2211848 | tf_op jit(solution)/shard_map/ppermute | solution.py:873
  449.4 16.4 %collective-permute-start.18 = (bf16[2,240,768]{2,1,0:T(8,128)(2,1)S(1)}, bf16[2,240,768]{2,1,0:T(8,128)(2,1)S(1)}, u32[]{:S(2)}, u32[]{:S(2)}) collective-permute-start(bf16[2,240,768]{2,1,0:T(8,128)(2,1)S(1)} %bitcast.250), channel_id=1, source_target_pairs={{0,1},{1,0},{2,3},{3,2},{4,5},{5,4},{6,7},{7,6},{8,9},{9,8},{10,11... | collective-permute-start | bytes 2211848 | tf_op jit(solution)/shard_map/ppermute | solution.py:873
  460.6 12.6 %collective-permute-start.23 = (bf16[4,48,768]{2,1,0:T(8,128)(2,1)S(1)}, bf16[4,48,768]{2,1,0:T(8,128)(2,1)S(1)}, u32[]{:S(2)}, u32[]{:S(2)}) collective-permute-start(bf16[4,48,768]{2,1,0:T(8,128)(2,1)S(1)} %constant_dynamic-slice_fusion.9), channel_id=1, source_target_pairs={{0,16},{8,24},{16,0},{24,8},{1,17},{9,25},{17,1},{25,9},{2,18},{10... | collective-permute-start | bytes 884744 | tf_op jit(solution)/shard_map/ppermute | solution.py:873
  461.3 13.4 %collective-permute-start.19 = (bf16[240,768]{1,0:T(8,128)(2,1)S(1)}, bf16[240,768]{1,0:T(8,128)(2,1)S(1)}, u32[]{:S(2)}, u32[]{:S(2)}) collective-permute-start(bf16[240,768]{1,0:T(8,128)(2,1)S(1)} %get-tuple-element.211), channel_id=1, source_target_pairs={{0,2},{1,3},{2,4},{3,5},{4,6},{5,7},{6,0},{7,1},{8,10},{9,11},{10,... | collective-permute-start | bytes 1105928 | tf_op jit(solution)/shard_map/ppermute | solution.py:873
  462.8 17.9 %collective-permute-start.17 = (bf16[240,768]{1,0:T(8,128)(2,1)S(1)}, bf16[240,768]{1,0:T(8,128)(2,1)S(1)}, u32[]{:S(2)}, u32[]{:S(2)}) collective-permute-start(bf16[240,768]{1,0:T(8,128)(2,1)S(1)} %get-tuple-element.212), channel_id=1, source_target_pairs={{0,6},{1,7},{2,0},{3,1},{4,2},{5,3},{6,4},{7,5},{8,14},{9,15},{10,... | collective-permute-start | bytes 1105928 | tf_op jit(solution)/shard_map/ppermute | solution.py:873
  465.7 19.9 %collective-permute-start.21 = (bf16[4,96,768]{2,1,0:T(8,128)(2,1)S(1)}, bf16[4,96,768]{2,1,0:T(8,128)(2,1)S(1)}, u32[]{:S(2)}, u32[]{:S(2)}) collective-permute-start(bf16[4,96,768]{2,1,0:T(8,128)(2,1)S(1)} %constant_dynamic-slice_fusion.10), channel_id=1, source_target_pairs={{0,8},{8,0},{16,24},{24,16},{1,9},{9,1},{17,25},{25,17},{2,10},{10... | collective-permute-start | bytes 1769480 | tf_op jit(solution)/shard_map/ppermute | solution.py:873
  473.3 16.0 %collective-permute-start.26 = (bf16[2,240,768]{2,1,0:T(8,128)(2,1)S(1)}, bf16[2,240,768]{2,1,0:T(8,128)(2,1)S(1)}, u32[]{:S(2)}, u32[]{:S(2)}) collective-permute-start(bf16[2,240,768]{2,1,0:T(8,128)(2,1)S(1)} %bitcast.249), channel_id=1, source_target_pairs={{0,1},{1,0},{2,3},{3,2},{4,5},{5,4},{6,7},{7,6},{8,9},{9,8},{10,11... | collective-permute-start | bytes 2211848 | tf_op jit(solution)/shard_map/ppermute | solution.py:873
  485.9 5.7 collective-permute-start.29
  487.7 7.2 %collective-permute-start.28 = (bf16[4,48,768]{2,1,0:T(8,128)(2,1)S(1)}, bf16[4,48,768]{2,1,0:T(8,128)(2,1)S(1)}, u32[]{:S(2)}, u32[]{:S(2)}) collective-permute-start(bf16[4,48,768]{2,1,0:T(8,128)(2,1)S(1)} %constant_dynamic-slice_fusion.7), channel_id=1, source_target_pairs={{0,16},{8,24},{16,0},{24,8},{1,17},{9,25},{17,1},{25,9},{2,18},{10... | collective-permute-start | bytes 884744 | tf_op jit(solution)/shard_map/ppermute | solution.py:873
  489.5 10.7 %collective-permute-start.25 = (bf16[240,768]{1,0:T(8,128)(2,1)S(1)}, bf16[240,768]{1,0:T(8,128)(2,1)S(1)}, u32[]{:S(2)}, u32[]{:S(2)}) collective-permute-start(bf16[240,768]{1,0:T(8,128)(2,1)S(1)} %get-tuple-element.156), channel_id=1, source_target_pairs={{0,6},{1,7},{2,0},{3,1},{4,2},{5,3},{6,4},{7,5},{8,14},{9,15},{10,... | collective-permute-start | bytes 1105928 | tf_op jit(solution)/shard_map/ppermute | solution.py:873
  491.1 16.1 %collective-permute-start.27 = (bf16[240,768]{1,0:T(8,128)(2,1)S(1)}, bf16[240,768]{1,0:T(8,128)(2,1)S(1)}, u32[]{:S(2)}, u32[]{:S(2)}) collective-permute-start(bf16[240,768]{1,0:T(8,128)(2,1)S(1)} %get-tuple-element.157), channel_id=1, source_target_pairs={{0,2},{1,3},{2,4},{3,5},{4,6},{5,7},{6,0},{7,1},{8,10},{9,11},{10,... | collective-permute-start | bytes 1105928 | tf_op jit(solution)/shard_map/ppermute | solution.py:873
  510.4 7.1 %collective-permute-start.39 = (bf16[256,256]{1,0:T(8,128)(2,1)S(1)}, bf16[256,256]{1,0:T(8,128)(2,1)S(1)}, u32[]{:S(2)}, u32[]{:S(2)}) collective-permute-start(bf16[256,256]{1,0:T(8,128)(2,1)S(1)} %dynamic-slice_bitcast_fusion.3), channel_id=1, source_target_pairs={{0,6},{1,7},{2,0},{3,1},{4,2},{5,3},{6,4},{7,5},{8,14},{9,15},{10,... | collective-permute-start | bytes 393224 | tf_op jit(solution)/shard_map/ppermute | solution.py:873
  513.5 8.3 %collective-permute-start.48 = (bf16[256,256]{1,0:T(8,128)(2,1)S(1)}, bf16[256,256]{1,0:T(8,128)(2,1)S(1)}, u32[]{:S(2)}, u32[]{:S(2)}) collective-permute-start(bf16[256,256]{1,0:T(8,128)(2,1)S(1)} %dynamic-slice_bitcast_fusion.2), channel_id=1, source_target_pairs={{0,2},{1,3},{2,4},{3,5},{4,6},{5,7},{6,0},{7,1},{8,10},{9,11},{10,... | collective-permute-start | bytes 393224 | tf_op jit(solution)/shard_map/ppermute | solution.py:873
  513.9 15.3 %collective-permute-start.30 = (bf16[240,768]{1,0:T(8,128)(2,1)S(1)}, bf16[240,768]{1,0:T(8,128)(2,1)S(1)}, u32[]{:S(2)}, u32[]{:S(2)}) collective-permute-start(bf16[240,768]{1,0:T(8,128)(2,1)S(1)} %copy-done.37), channel_id=1, source_target_pairs={{0,6},{1,7},{2,0},{3,1},{4,2},{5,3},{6,4},{7,5},{8,14},{9,15},{10,... | collective-permute-start | bytes 1105928 | tf_op jit(solution)/shard_map/ppermute | solution.py:873
  517.4 20.2 %collective-permute-start.32 = (bf16[240,768]{1,0:T(8,128)(2,1)S(1)}, bf16[240,768]{1,0:T(8,128)(2,1)S(1)}, u32[]{:S(2)}, u32[]{:S(2)}) collective-permute-start(bf16[240,768]{1,0:T(8,128)(2,1)S(1)} %copy-done.36), channel_id=1, source_target_pairs={{0,2},{1,3},{2,4},{3,5},{4,6},{5,7},{6,0},{7,1},{8,10},{9,11},{10,... | collective-permute-start | bytes 1105928 | tf_op jit(solution)/shard_map/ppermute | solution.py:873
  517.5 37.0 %collective-permute-start.40 = (bf16[256,256]{1,0:T(8,128)(2,1)S(1)}, bf16[256,256]{1,0:T(8,128)(2,1)S(1)}, u32[]{:S(2)}, u32[]{:S(2)}) collective-permute-start(bf16[256,256]{1,0:T(8,128)(2,1)S(1)} %fusion.41), channel_id=1, source_target_pairs={{0,6},{1,7},{2,0},{3,1},{4,2},{5,3},{6,4},{7,5},{8,14},{9,15},{10,... | collective-permute-start | bytes 393224 | tf_op jit(solution)/shard_map/ppermute | solution.py:873
  521.9 16.0 %copy-start.46 = (f32[768]{0:T(1024)S(1)}, f32[768]{0:T(1024)}, u32[]{:S(2)}) copy-start(f32[768]{0:T(1024)} %param.26) | copy-start | bytes 9220
  521.9 16.0 %copy-start.54 = (bf16[768,768]{1,0:T(8,128)(2,1)S(1)}, bf16[768,768]{1,0:T(8,128)(2,1)}, u32[]{:S(2)}) copy-start(bf16[768,768]{1,0:T(8,128)(2,1)} %refs_4_.1) | copy-start | bytes 3538948
  521.9 16.0 %copy-start.59 = (bf16[480,768]{1,0:T(8,128)(2,1)S(1)}, bf16[480,768]{1,0:T(8,128)(2,1)}, u32[]{:S(2)}) copy-start(bf16[480,768]{1,0:T(8,128)(2,1)} %get-tuple-element.154) | copy-start | bytes 2211844
  521.9 34.2 %collective-permute-start.49 = (bf16[256,256]{1,0:T(8,128)(2,1)S(1)}, bf16[256,256]{1,0:T(8,128)(2,1)S(1)}, u32[]{:S(2)}, u32[]{:S(2)}) collective-permute-start(bf16[256,256]{1,0:T(8,128)(2,1)S(1)} %fusion.38), channel_id=1, source_target_pairs={{0,2},{1,3},{2,4},{3,5},{4,6},{5,7},{6,0},{7,1},{8,10},{9,11},{10,... | collective-permute-start | bytes 393224 | tf_op jit(solution)/shard_map/ppermute | solution.py:873
  554.4 1.3 collective-permute-start.33
  554.6 9.3 %collective-permute-start.41 = (bf16[256,256]{1,0:T(8,128)(2,1)S(1)}, bf16[256,256]{1,0:T(8,128)(2,1)S(1)}, u32[]{:S(2)}, u32[]{:S(2)}) collective-permute-start(bf16[256,256]{1,0:T(8,128)(2,1)S(1)} %fusion.40), channel_id=1, source_target_pairs={{0,6},{1,7},{2,0},{3,1},{4,2},{5,3},{6,4},{7,5},{8,14},{9,15},{10,... | collective-permute-start | bytes 393224 | tf_op jit(solution)/shard_map/ppermute | solution.py:873
  555.8 3.8 collective-permute-start.34
  556.2 14.1 %collective-permute-start.50 = (bf16[256,256]{1,0:T(8,128)(2,1)S(1)}, bf16[256,256]{1,0:T(8,128)(2,1)S(1)}, u32[]{:S(2)}, u32[]{:S(2)}) collective-permute-start(bf16[256,256]{1,0:T(8,128)(2,1)S(1)} %fusion.37), channel_id=1, source_target_pairs={{0,2},{1,3},{2,4},{3,5},{4,6},{5,7},{6,0},{7,1},{8,10},{9,11},{10,... | collective-permute-start | bytes 393224 | tf_op jit(solution)/shard_map/ppermute | solution.py:873
  559.6 4.8 collective-permute-start.35
  563.9 10.3 %collective-permute-start.42 = (bf16[1,1,256,256]{3,2,1,0:T(8,128)(2,1)S(1)}, bf16[1,1,256,256]{3,2,1,0:T(8,128)(2,1)S(1)}, u32[]{:S(2)}, u32[]{:S(2)}) collective-permute-start(bf16[1,1,256,256]{3,2,1,0:T(8,128)(2,1)S(1)} %fusion.43), channel_id=1, source_target_pairs={{0,16},{8,24},{16,0},{24,8},{1,17},{9,25},{17,1},{25,9},{2,18},{10... | collective-permute-start | bytes 393224 | tf_op jit(solution)/shard_map/ppermute | solution.py:873
  564.4 6.0 collective-permute-start.36
  564.7 5.8 collective-permute-start.38
  568.2 4.8 collective-permute-start.37
  570.3 5.0 collective-permute-start.51
  574.3 6.7 %collective-permute-start.43 = (bf16[2,1,256,256]{3,2,1,0:T(8,128)(2,1)S(1)}, bf16[2,1,256,256]{3,2,1,0:T(8,128)(2,1)S(1)}, u32[]{:S(2)}, u32[]{:S(2)}) collective-permute-start(bf16[2,1,256,256]{3,2,1,0:T(8,128)(2,1)S(1)} %maximum_select_fusion.6), channel_id=1, source_target_pairs={{0,8},{8,0},{16,24},{24,16},{1,9},{9,1},{17,25},{25,17},{2,10},{10... | collective-permute-start | bytes 786440 | tf_op jit(solution)/shard_map/ppermute | solution.py:873
  575.4 7.0 %collective-permute-start.52 = (bf16[1,2,256,256]{3,2,1,0:T(8,128)(2,1)S(1)}, bf16[1,2,256,256]{3,2,1,0:T(8,128)(2,1)S(1)}, u32[]{:S(2)}, u32[]{:S(2)}) collective-permute-start(bf16[1,2,256,256]{3,2,1,0:T(8,128)(2,1)S(1)} %maximum_select_fusion.7), channel_id=1, source_target_pairs={{0,16},{8,24},{16,0},{24,8},{1,17},{9,25},{17,1},{25,9},{2,18},{10... | collective-permute-start | bytes 786440 | tf_op jit(solution)/shard_map/ppermute | solution.py:873
  592.0 5.5 collective-permute-start.46
  593.6 7.3 %collective-permute-start.44 = (bf16[1,1,336,256]{3,2,1,0:T(8,128)(2,1)S(1)}, bf16[1,1,336,256]{3,2,1,0:T(8,128)(2,1)S(1)}, u32[]{:S(2)}, u32[]{:S(2)}) collective-permute-start(bf16[1,1,336,256]{3,2,1,0:T(8,128)(2,1)S(1)} %get-tuple-element.239), channel_id=1, source_target_pairs={{0,8},{8,0},{16,24},{24,16},{1,9},{9,1},{17,25},{25,17},{2,10},{10... | collective-permute-start | bytes 516104 | tf_op jit(solution)/shard_map/ppermute | solution.py:873
  597.6 8.7 %collective-permute-start.47 = (bf16[2,1,336,256]{3,2,1,0:T(8,128)(2,1)S(1)}, bf16[2,1,336,256]{3,2,1,0:T(8,128)(2,1)S(1)}, u32[]{:S(2)}, u32[]{:S(2)}) collective-permute-start(bf16[2,1,336,256]{3,2,1,0:T(8,128)(2,1)S(1)} %maximum_select_fusion.5), channel_id=1, source_target_pairs={{0,8},{8,0},{16,24},{24,16},{1,9},{9,1},{17,25},{25,17},{2,10},{10... | collective-permute-start | bytes 1032200 | tf_op jit(solution)/shard_map/ppermute | solution.py:873
  600.9 7.3 %collective-permute-start.45 = (bf16[1,2,336,256]{3,2,1,0:T(8,128)(2,1)S(1)}, bf16[1,2,336,256]{3,2,1,0:T(8,128)(2,1)S(1)}, u32[]{:S(2)}, u32[]{:S(2)}) collective-permute-start(bf16[1,2,336,256]{3,2,1,0:T(8,128)(2,1)S(1)} %maximum_select_fusion.4), channel_id=1, source_target_pairs={{0,16},{8,24},{16,0},{24,8},{1,17},{9,25},{17,1},{25,9},{2,18},{10... | collective-permute-start | bytes 1032200 | tf_op jit(solution)/shard_map/ppermute | solution.py:873
  (63 other events, 219.8 us)
Sparse Core Ops, SparseCore 0:
  300.8 60.8 reduce-scatter.5
  364.8 77.1 reduce-scatter.3
  550.2 40.8 reduce-scatter.7

commit v3 on v2

--- a/solution.py
+++ b/solution.py
@@ -25,7 +25,7 @@
 KEYS = 672
 SPARE_KEYS = 768
 QROWS = 64
-ROWS = 512
+ROWS = 1024
 VMEM = 60 * 1024 * 1024
 NT = (((1,), (1,)), ((), ()))
 FLIP = (((0,), (0,)), ((), ()))
@@ -79,9 +79,36 @@
     wwidth: jax.Array
     wup: jax.Array
     wdown: jax.Array
+    wgroup: jax.Array
+    wcame: jax.Array
+    sent: jax.Array
+    back: jax.Array
+    came: jax.Array
+    around: jax.Array
 
 
 TABLES = len(Tables._fields)
+
+
+def pieces(cycle_size):
+    return -(-(SLOTS + 2 * REACH) // cycle_size), -(-SLOTS // cycle_size)
+
+
+def floor_div(value, by):
+    return lax.div(value + 16 * by, by) - 16
+
+
+def first_slot(begin, device, cycle_size):
+    return -floor_div(device - begin, cycle_size)
+
+
+def unit_source(unit, me, chips):
+    chip, core = lax.div(me, 2), lax.rem(me, 2)
+    turn, half = lax.div(unit, 4), lax.rem(unit, 2)
+    other = lax.rem(lax.div(unit, 2), 2)
+    turn = jnp.where(half == 0, -turn, turn)
+    source = 2 * lax.rem(chip + turn + chips, chips) + jnp.where(other == 0, core, 1 - core)
+    return source, half
 
 
 def geometry_kernel(cycle_size, unit_size, lengths, place, *refs):
@@ -91,7 +118,7 @@
     chips = cycle_size // 2
     units = 4 * chips
     me = place[0]
-    chip, core = lax.div(me, 2), lax.rem(me, 2)
+    many, few = pieces(cycle_size)
     facts, start = [], 0
     for item in range(item_count):
         length = lengths[item]
@@ -134,10 +161,7 @@
         return counts, offsets
 
     def one_unit(unit, lens):
-        turn, half = lax.div(unit, 4), lax.rem(unit, 2)
-        other = lax.rem(lax.div(unit, 2), 2)
-        turn = jnp.where(half == 0, -turn, turn)
-        source = 2 * lax.rem(chip + turn + chips, chips) + jnp.where(other == 0, core, 1 - core)
+        source, half = unit_source(unit, me, chips)
         rows = [(half * HALF + slot) * cycle_size + source for slot in range(HALF)]
         counts, offsets = sort(
             rows, 16, tab.ubase, tab.uspare, tab.uwidth, tab.uitem, unit * HALF
@@ -175,6 +199,29 @@
         tab.wwidth[index] = width
         tab.wup[index] = above
         tab.wdown[index] = below
+        inner = jnp.clip(row, 0, SLOTS * cycle_size - 1)
+        slot = lax.div(inner, cycle_size)
+        device = inner - slot * cycle_size
+        tab.wgroup[index] = (device * SLOTS + slot) * PITCH
+        slot = floor_div(row, cycle_size)
+        device = row - slot * cycle_size
+        turn = slot - first_slot(SLOTS * me - REACH, device, cycle_size)
+        tab.wcame[index] = (device * many + turn) * PITCH
+    for device in range(cycle_size):
+        first = first_slot(SLOTS * device - REACH, me, cycle_size)
+        for turn in range(many):
+            tab.sent[device * many + turn] = first + turn
+        first = first_slot(SLOTS * me, device, cycle_size)
+        for turn in range(few):
+            tab.back[device * few + turn] = (first + turn) * cycle_size + device - SLOTS * me
+    for slot in range(SLOTS):
+        row = slot * cycle_size + me
+        source = lax.div(row, SLOTS)
+        turn = slot - first_slot(source * SLOTS, me, cycle_size)
+        tab.came[slot] = (source * few + turn) * PITCH
+        for turn in range(3):
+            near = jnp.clip(row + turn - 1, 0, SLOTS * cycle_size - 1)
+            tab.around[turn * SLOTS + slot] = near * PITCH
     rows = [slot * cycle_size + me for slot in range(SLOTS)]
     counts, offsets = sort(rows, QROWS, tab.qbase, tab.qspare, tab.qwidth, tab.qitem, 0)
     for item in range(items):
@@ -186,7 +233,9 @@
     items = lengths.shape[0] + 1
     units = 2 * cycle_size
     sizes = [units * items] * 3 + [items + 1] + [items] * 3 + [units * HALF] * 4 + [SLOTS] * 4
-    sizes += [SLOTS + 2 * REACH] * 3
+    sizes += [SLOTS + 2 * REACH] * 5
+    many, few = pieces(cycle_size)
+    sizes += [cycle_size * many, cycle_size * few, SLOTS, 3 * SLOTS]
     smem = pl.BlockSpec(memory_space=pltpu.SMEM)
     return Tables(
         *pl.pallas_call(
@@ -441,7 +490,7 @@
     ).astype(BF16)
 
 
-def attend_back_kernel(heads, units, items, unit_size, *refs):
+def attend_back_kernel(heads, units, items, unit_size, me, *refs):
     tab, refs = Tables(*refs[:TABLES]), refs[TABLES:]
     koff, kcnt, kdst, kstart, klen, qfirst, qcount = tab[:7]
     q_ref, grad_ref, o_ref, lse_ref, ks_ref, vs_ref, wk_ref, wv_ref, ns_ref, bias_ref = refs[:10]
@@ -552,7 +601,9 @@
 
             lax.fori_loop(0, items, one_item, 0)
             place = places(tab.ubase, tab.uspare, tab.uwidth, unit * HALF, HALF)
-            dn_ref[pl.ds(pl.multiple_of(unit * count, 16), count), :] = lax.dot_general(
+            source, half = unit_source(unit, me[0], units // 4)
+            spot = (2 * source + half) * count
+            dn_ref[pl.ds(pl.multiple_of(spot, 16), count), :] = lax.dot_general(
                 sorter(place, unit_size), unit_rows[...], flip, preferred_element_type=F32
             ).astype(BF16)
             return none
@@ -576,14 +627,16 @@
 
 
 def merge_kernel(
-    cycle_size, wwidth, wup, wdown,
-    win_ref, k11, k12, k21, k22, out_weight, grad_ref, mapped_ref, shares_ref,
-    x1, x2, x3, x4, g3, real_ref, up_ref, down_ref, c1, m1, c3, m2g, m1g,
+    cycle_size, wwidth, wup, wdown, wgroup, wcame, back,
+    came_ref, group_ref, k11, k12, k21, k22, out_weight, grad_ref, mapped_ref, shares_ref,
+    x1, x2, x3, x4, g3, real_ref, up_ref, down_ref, c1, m1, c3, m2g, m1g, win_ref, rows_ref,
 ):
     window = SLOTS + 2 * REACH
     column = lax.broadcasted_iota(jnp.int32, (PITCH, 128), 0)
     for row in range(window):
         spots = pl.ds(row * PITCH, PITCH)
+        win_ref[spots, :CH] = came_ref[pl.ds(pl.multiple_of(wcame[row], 16), PITCH), :]
+        win_ref[spots, CH:] = group_ref[pl.ds(pl.multiple_of(wgroup[row], 16), PITCH), :]
         real = jnp.where(column < wwidth[row], 1.0, 0.0)
         real_ref[spots, :] = real
         up_ref[spots, :] = real * wup[row].astype(F32)
@@ -660,6 +713,14 @@
     c3[at(3, 21), :] = conv(x3, k21, 3, 21)
     fill(x4, masked(real_ref, gelu(c3[at(3, 21), :]), 3, 21), 3, 21)
     merged = (m1[at(own, last), :] + conv(x4, k22, own, last)).astype(BF16)
+
+    def send(values, ref):
+        rows_ref[...] = values
+        for piece in range(back.shape[0]):
+            row = jnp.minimum(back[piece], SLOTS - 1)
+            block = rows_ref[pl.ds(pl.multiple_of(row * PITCH, PITCH), PITCH), :]
+            ref[piece * PITCH : (piece + 1) * PITCH, :] = block.astype(BF16)
+
     mapped_ref[...] = jnp.dot(merged, out_weight[...], preferred_element_type=F32).astype(BF16)
     block = lax.dot_general(
         merged, win_ref[at(own, last), CH:], FLIP, preferred_element_type=F32
@@ -683,10 +744,60 @@
     fill(g3, now, 5, 19)
     weight_grad(x1, now[at(own - 5, last - 5)], 0)
     now = gelu_slope(start(own, last)) * conv_back(k11, own, last)
-    grad_ref[...] = (m1g[at(own, last), :] + now).astype(BF16)
-
-
-def merge(tab, windows, kernels, out_weight, cycle_size):
+    send(m1g[at(own, last), :] + now, grad_ref)
+
+
+def pack_kernel(sent, block_ref, weight_ref, out_ref, rows_ref):
+    rows_ref[...] = jnp.dot(block_ref[...], weight_ref[...], preferred_element_type=F32)
+    blank = jnp.zeros((PITCH - ROWW, CH), F32)
+    for piece in range(sent.shape[0]):
+        slot = jnp.clip(sent[piece], 0, SLOTS - 1)
+        block = rows_ref[pl.ds(pl.multiple_of(slot * ROWW, 8), ROWW), :]
+        out_ref[piece * PITCH : (piece + 1) * PITCH, :] = jnp.concatenate(
+            [block, blank], axis=0
+        ).astype(BF16)
+
+
+def pack(tab, block_out, weight):
+    vmem = pl.BlockSpec(memory_space=pltpu.VMEM)
+    return pl.pallas_call(
+        pack_kernel,
+        grid_spec=pltpu.PrefetchScalarGridSpec(
+            num_scalar_prefetch=1,
+            in_specs=[vmem] * 2,
+            out_specs=vmem,
+            scratch_shapes=[pltpu.VMEM((block_out.shape[0], CH), F32)],
+        ),
+        out_shape=jax.ShapeDtypeStruct((tab.sent.shape[0] * PITCH, CH), BF16),
+        cost_estimate=cost(2),
+        compiler_params=pltpu.CompilerParams(vmem_limit_bytes=VMEM),
+        name="pack",
+    )(tab.sent, block_out, weight)
+
+
+def unpack_kernel(came, rows_ref, out_ref):
+    parts = []
+    for slot in range(came.shape[0]):
+        block = rows_ref[pl.ds(pl.multiple_of(came[slot], 16), PITCH), :].astype(F32)
+        parts.append(block[:ROWW])
+    out_ref[...] = jnp.concatenate(parts, axis=0).astype(BF16)
+
+
+def unpack(came, rows):
+    vmem = pl.BlockSpec(memory_space=pltpu.VMEM)
+    return pl.pallas_call(
+        unpack_kernel,
+        grid_spec=pltpu.PrefetchScalarGridSpec(
+            num_scalar_prefetch=1, in_specs=[vmem], out_specs=vmem
+        ),
+        out_shape=jax.ShapeDtypeStruct((came.shape[0] * ROWW, CH), BF16),
+        cost_estimate=cost(1),
+        compiler_params=pltpu.CompilerParams(vmem_limit_bytes=VMEM),
+        name="unpack",
+    )(came, rows)
+
+
+def merge(tab, came, group, kernels, out_weight, cycle_size):
     window = SLOTS + 2 * REACH
     vmem = pl.BlockSpec(memory_space=pltpu.VMEM)
     padded = (window + 2) * PITCH
@@ -696,20 +807,29 @@
     return pl.pallas_call(
         functools.partial(merge_kernel, cycle_size),
         grid_spec=pltpu.PrefetchScalarGridSpec(
-            num_scalar_prefetch=3,
-            in_specs=[vmem] * 6,
+            num_scalar_prefetch=6,
+            in_specs=[vmem] * 7,
             out_specs=[vmem] * 3,
-            scratch_shapes=[pltpu.VMEM((padded, 3 * CH), BF16)] * 5 + [small] * 3 + [large] * 5,
+            scratch_shapes=[pltpu.VMEM((padded, 3 * CH), BF16)] * 5
+            + [small] * 3
+            + [large] * 5
+            + [
+                pltpu.VMEM((window * PITCH, 2 * CH), BF16),
+                pltpu.VMEM((SLOTS * PITCH, CH), F32),
+            ],
         ),
         out_shape=[
-            jax.ShapeDtypeStruct((SLOTS * PITCH, CH), BF16),
+            jax.ShapeDtypeStruct((tab.back.shape[0] * PITCH, CH), BF16),
             jax.ShapeDtypeStruct((SLOTS * PITCH, CH), BF16),
             jax.ShapeDtypeStruct((cycle_size * share_rows, CH), BF16),
         ],
         cost_estimate=cost(25),
         compiler_params=pltpu.CompilerParams(vmem_limit_bytes=VMEM),
         name="merge",
-    )(tab.wwidth, tab.wup, tab.wdown, windows, *kernels, out_weight)
+    )(
+        tab.wwidth, tab.wup, tab.wdown, tab.wgroup, tab.wcame, tab.back,
+        came, group, *kernels, out_weight,
+    )
 
 
 def attend(tab, query, key_weight, value_weight, norms, sorted_keys, units, items, heads):
@@ -767,7 +887,7 @@
 
 
 def attend_back(
-    tab, query, grads, outputs, lse, ks, vs, key_weight, value_weight, ns, bias,
+    tab, cycle_pos, query, grads, outputs, lse, ks, vs, key_weight, value_weight, ns, bias,
     unit_size, units, items, heads,
 ):
     feats = heads * HEAD
@@ -788,7 +908,7 @@
     return pl.pallas_call(
         functools.partial(attend_back_kernel, heads, units, items, unit_size),
         grid_spec=pltpu.PrefetchScalarGridSpec(
-            num_scalar_prefetch=TABLES,
+            num_scalar_prefetch=TABLES + 1,
             grid=(groups,),
             in_specs=[
                 part(rows),
@@ -833,7 +953,7 @@
         cost_estimate=cost(90),
         compiler_params=pltpu.CompilerParams(vmem_limit_bytes=VMEM),
         name="attend_back",
-    )(*tab, query, grads, outputs, lse, ks, vs, key_weight, value_weight, ns, bias)
+    )(cycle_pos.reshape(1), *tab, query, grads, outputs, lse, ks, vs, key_weight, value_weight, ns, bias)
 
 
 @functools.cache
@@ -956,10 +1076,8 @@
     )
 
 
-def upsample_forward(values, all_masks, cycle_pos, cycle_size):
+def upsample_forward(row_above, values, row_below, all_masks):
     center = values.astype(F32)
-    row_above = from_above(values, cycle_pos)
-    row_below = from_below(values, cycle_pos, cycle_size)
     upper_value = jnp.where(all_masks[1][:, :, None], row_above, values).astype(F32)
     lower_value = jnp.where(all_masks[7][:, :, None], row_below, values).astype(F32)
     pieces = []
@@ -998,48 +1116,6 @@
     return 0.75 * (upper.astype(F32) + lower.astype(F32)) + 0.25 * rows
 
 
-def first_slot(begin, device, cycle_size):
-    return -((device - begin) // cycle_size)
-
-
-def to_windows(values, cycle_pos, cycle_size):
-    window = SLOTS + 2 * REACH
-    many = -(-window // cycle_size)
-    spare = many + 1
-    padded = jnp.pad(values, ((spare, spare), (0, 0), (0, 0)))
-    sends = []
-    for target in range(cycle_size):
-        slot = first_slot(SLOTS * target - REACH, cycle_pos, cycle_size) + spare
-        sends.append(lax.dynamic_slice_in_dim(padded, slot, many, axis=0))
-    got = lax.all_to_all(jnp.stack(sends), "blk", 0, 0)
-    got = jnp.swapaxes(got, 0, 1)
-    begin = SLOTS * cycle_pos - REACH
-    turn = begin - (begin // cycle_size) * cycle_size
-    got = lax.dynamic_slice_in_dim(jnp.concatenate([got, got], axis=1), turn, cycle_size, axis=1)
-    return got.reshape((many * cycle_size,) + values.shape[1:])[:window]
-
-
-def from_windows(values, cycle_pos, cycle_size):
-    many = -(-SLOTS // cycle_size)
-    padded = jnp.pad(values, ((0, many * cycle_size), (0, 0), (0, 0)))
-    begin = SLOTS * cycle_pos
-    sends = []
-    for target in range(cycle_size):
-        slot = first_slot(begin, target, cycle_size)
-        for extra in range(many):
-            row = (slot + extra) * cycle_size + target - begin
-            sends.append(lax.dynamic_slice_in_dim(padded, row, 1, axis=0))
-    sends = jnp.concatenate(sends, axis=0).reshape((cycle_size, many) + values.shape[1:])
-    got = lax.all_to_all(sends, "blk", 0, 0).reshape((cycle_size * many,) + values.shape[1:])
-    rows = []
-    for slot in range(SLOTS):
-        row = slot * cycle_size + cycle_pos
-        source = row // SLOTS
-        extra = slot - first_slot(source * SLOTS, cycle_pos, cycle_size)
-        rows.append(lax.dynamic_slice_in_dim(got, source * many + extra, 1, axis=0))
-    return jnp.concatenate(rows, axis=0)
-
-
 def dot32(left, right, **more):
     return jnp.dot(left, right, preferred_element_type=F32, **more)
 
@@ -1052,12 +1128,15 @@
     return lax.dot_general(left, right, (((0,), (0,)), ((), ())), preferred_element_type=F32)
 
 
-def halved(values, device, bit, axis, pairs_axis):
+def halving(values, device, bit, axis, pairs_axis):
     half = values.shape[axis] // 2
     mine = (device >> bit) & 1
     keep = lax.dynamic_slice_in_dim(values, mine * half, half, axis=axis)
     send = lax.dynamic_slice_in_dim(values, (1 - mine) * half, half, axis=axis)
-    got = passed(send, pairs_axis, lambda source: source ^ (1 << bit))
+    return keep, passed(send, pairs_axis, lambda source: source ^ (1 << bit))
+
+
+def summed(keep, got):
     return (keep.astype(F32) + got.astype(F32)).astype(BF16)
 
 
@@ -1069,49 +1148,69 @@
     return (keep.astype(F32) + to_sibling(send).astype(F32)).astype(BF16)
 
 
-def added_over_chips(values, chip):
-    chips, rows, _ = values.shape
-    half = rows // 2
-    both = []
-    for part, way in ((values[:, :half], 1), (values[:, half:], -1)):
-
-        def block(offset, part=part, way=way):
-            return lax.dynamic_index_in_dim(
-                part, (chip - way * offset) % chips, 0, keepdims=False
-            ).astype(F32)
-
-        moving = block(1)
-        for step in range(2, chips + 1):
-            moving = passed_along(moving.astype(BF16), "blk", 2 * way).astype(F32) + block(step)
-        both.append(moving.astype(BF16))
-    return jnp.concatenate(both, axis=0)
+class ChipSums:
+    def __init__(self, values, chip):
+        half = values.shape[1] // 2
+        self.chip, self.chips = chip, values.shape[0]
+        self.parts = [(values[:, :half], 1), (values[:, half:], -1)]
+        self.moving = [self.block(part, way, 1).astype(BF16) for part, way in self.parts]
+
+    def block(self, part, way, offset):
+        spot = (self.chip - way * offset) % self.chips
+        return lax.dynamic_index_in_dim(part, spot, 0, keepdims=False).astype(F32)
+
+    def step(self, number):
+        moved = []
+        for value, (part, way) in zip(self.moving, self.parts):
+            got = passed_along(value, "blk", 2 * way).astype(F32)
+            moved.append((got + self.block(part, way, number + 1)).astype(BF16))
+        self.moving = moved
+
+    def result(self):
+        return jnp.concatenate(self.moving, axis=0)
+
+
+class GroupGather:
+    def __init__(self, values, dp_pos):
+        self.dp_pos, self.bits = dp_pos, lax.axis_size("dp").bit_length() - 1
+        half = values.shape[0] // 2
+        self.held = [part[(None,) * self.bits] for part in (values[:half], values[half:])]
+
+    def step(self, number):
+        held = []
+        for value, bit in zip(self.held, (number, self.bits - 1 - number)):
+            axis = self.bits - 1 - bit
+            got = passed(value, "dp", lambda source, bit=bit: source ^ (1 << bit))
+            mine = (self.dp_pos >> bit) & 1
+            held.append(
+                jnp.where(
+                    mine == 0,
+                    jnp.concatenate([value, got], axis=axis),
+                    jnp.concatenate([got, value], axis=axis),
+                )
+            )
+        self.held = held
+
+    def result(self):
+        shape = (1 << self.bits,)
+        return jnp.concatenate(
+            [value.reshape(shape + value.shape[self.bits :]) for value in self.held], axis=1
+        )
 
 
 def gathered_over_groups(values, dp_pos):
-    groups = lax.axis_size("dp")
-    bits = groups.bit_length() - 1
-    half = values.shape[0] // 2
-    both = []
-    for part, order in ((values[:half], range(bits)), (values[half:], range(bits - 1, -1, -1))):
-        held = part[(None,) * bits]
-        for bit in order:
-            axis = bits - 1 - bit
-            got = passed(held, "dp", lambda source, bit=bit: source ^ (1 << bit))
-            mine = (dp_pos >> bit) & 1
-            held = jnp.where(
-                mine == 0,
-                jnp.concatenate([held, got], axis=axis),
-                jnp.concatenate([got, held], axis=axis),
-            )
-        both.append(held.reshape((groups,) + part.shape))
-    return jnp.concatenate(both, axis=1)
-
-
-def small_sums(values, core, chip, dp_pos):
-    values = core_summed(values, core)
-    for bit in range(lax.axis_size("dp").bit_length() - 1):
-        got = passed(values, "dp", lambda source, bit=bit: source ^ (1 << bit))
-        values = (values.astype(F32) + got.astype(F32)).astype(BF16)
+    gather = GroupGather(values, dp_pos)
+    for number in range(gather.bits):
+        gather.step(number)
+    return gather.result()
+
+
+def over_groups(values, bit):
+    got = passed(values, "dp", lambda source: source ^ (1 << bit))
+    return (values.astype(F32) + got.astype(F32)).astype(BF16)
+
+
+def sum_over_chips(values, chip):
     chips = values.shape[0]
     total = lax.dynamic_index_in_dim(values, chip, 0, keepdims=False).astype(F32)
     for step in range(1, chips):
@@ -1120,14 +1219,11 @@
     return total
 
 
-def finished(late, orders, chip, dp_pos):
-    groups = lax.axis_size("dp")
+def whole_shares(whole, parts, orders):
+    groups = whole.shape[0]
     bits = groups.bit_length() - 1
-    chips = late[0].shape[0]
-    joined = jnp.concatenate([part.reshape(chips, -1, 256) for part in late], axis=1)
-    whole = gathered_over_groups(added_over_chips(joined, chip), dp_pos)
     out, place = [], 0
-    for part, order in zip(late, orders):
+    for part, order in zip(parts, orders):
         rows, width = part.shape[1:]
         size = rows * width // 256
         pieces = []
@@ -1198,26 +1294,36 @@
             behind = passed_along(behind, "blk", -2)
             ahead, behind, sorted_norms[-1] = tied(ahead, behind, sorted_norms[-1])
         if step == 1:
-            ahead, behind, merged_cotangent, stream_start, normed_one, query = tied(
-                ahead, behind, merged_cotangent, stream_start, normed_one, query
+            ahead, behind, stream_start, normed_one, query = tied(
+                ahead, behind, stream_start, normed_one, query
             )
+            ahead, behind, merged_cotangent = tied(ahead, behind, merged_cotangent)
+            upper, lower = upsample_back_columns(
+                merged_cotangent.reshape(SLOTS, ROWW, -1), all_masks
+            )
+        if step == 2:
+            ahead, behind, upper, lower = tied(ahead, behind, upper, lower)
+            upper_next = from_below(upper, cycle_pos, cycle_size)
+            lower_prev = from_above(lower, cycle_pos)
+        if step == chips - 1:
+            ahead, behind, upper_next, lower_prev = tied(ahead, behind, upper_next, lower_prev)
+            mapped_grad = upsample_back_rows(
+                upper, lower, upper_next, lower_prev, all_masks
+            ).astype(BF16)
+            mapped_grad = jnp.pad(mapped_grad, ((0, 0), (0, PITCH - ROWW), (0, 0)))
+            mapped_grad = mapped_grad.reshape(SLOTS * PITCH, -1)
         mine = jnp.concatenate([ahead, behind], axis=0)
         sorted_norms.append(
             sort_step(
                 step, tab, ids, mine, to_sibling(mine), dataset_table, gain_one, bias_one, unit_size
             )
         )
-    upper, lower = upsample_back_columns(
-        merged_cotangent.reshape(SLOTS, ROWW, -1), all_masks
-    )
-    sorted_norms[-1], upper, lower = tied(sorted_norms[-1], upper, lower)
-    upper_next = from_below(upper, cycle_pos, cycle_size)
-    lower_prev = from_above(lower, cycle_pos)
+    sorted_norms[-1], mapped_grad = tied(sorted_norms[-1], mapped_grad)
+    group_grad = lax.all_gather(mapped_grad, "blk", tiled=True)
     attended, outputs, lse, sorted_norm, bias, ks, vs = attend(
         tab, query, key_weight, value_weight, sorted_norms, sorted_keys, units, kinds, heads
     )
-
-    attended, upper_next, lower_prev = tied(attended, upper_next, lower_prev)
+    attended, group_grad = tied(attended, group_grad)
 
     def as_cells(flattened):
         return flattened.reshape(SLOTS, ROWW, flattened.shape[-1])
@@ -1227,23 +1333,23 @@
     pre_act = dot32(normed_two, fc1_weight)
     hidden = gelu_tanh(pre_act).astype(BF16)
     block_out = (after_attn + dot32(hidden, fc2_weight)).astype(BF16)
-    reassembled_own = dot32(block_out, project_weight).astype(BF16)
-
-    mapped_grad_own = upsample_back_rows(
-        upper, lower, upper_next, lower_prev, all_masks
-    ).astype(BF16)
-    channels = mapped_grad_own.shape[-1]
-    arrived = to_windows(
-        jnp.concatenate([as_cells(reassembled_own), mapped_grad_own], axis=2), cycle_pos, cycle_size
-    )
-    windows = jnp.pad(arrived, ((0, 0), (0, PITCH - ROWW), (0, 0))).reshape(-1, 2 * channels)
-    reassembled_grad, mapped, conv_shares = merge(
-        tab, windows, (unit1_first, unit1_second, unit2_first, unit2_second), output_weight, cycle_size
+    channels = project_weight.shape[1]
+
+    def exchanged(values):
+        values = values.reshape(cycle_size, -1, channels)
+        return lax.all_to_all(values, "blk", 0, 0).reshape(-1, channels)
+
+    grad_rows, mapped_rows, conv_shares = merge(
+        tab,
+        exchanged(pack(tab, block_out, project_weight)),
+        group_grad,
+        (unit1_first, unit1_second, unit2_first, unit2_second),
+        output_weight,
+        cycle_size,
     )
     conv_shares = conv_shares.reshape(cycle_size, -1, channels)
-
-    def own_window(values):
-        return values.reshape(SLOTS, PITCH, channels)[:, :ROWW]
+    group_mapped = lax.all_gather(mapped_rows, "blk", tiled=True)
+    reassembled_grad = unpack(tab.came, exchanged(grad_rows))
 
     def shared_out(*gradients):
         parts = []
@@ -1260,30 +1366,26 @@
     def wide(gradient):
         return gradient.reshape(cycle_size, -1, width_model)
 
-    def scattered(shares):
+    def scattering(shares):
         count, share_rows, share_width = shares.shape
         parts = shares.reshape(count, groups, share_rows // groups, share_width)
-        parts = jnp.swapaxes(parts, 0, 1).reshape(-1, share_width)
-        part = lax.psum_scatter(parts, "dp", scatter_dimension=0, tiled=True)
-        return part.reshape(count, -1, 256)
+        return jnp.swapaxes(parts, 0, 1).reshape(-1, share_width)
+
+    def scattered(parts):
+        return lax.psum_scatter(parts, "dp", scatter_dimension=0, tiled=True)
+
+    def dp_halving(values, order, index):
+        return halving(values, dp_pos, order[index], 1, "dp")
 
     def dp_halved(values, order, index):
-        return halved(values, dp_pos, order[index], 1, "dp")
-
-    returned = from_windows(
-        jnp.concatenate([own_window(reassembled_grad), own_window(mapped)], axis=2),
-        cycle_pos,
-        cycle_size,
-    )
-    reassembled_grad = returned[:, :, :channels].reshape(-1, channels)
-    merged = upsample_forward(returned[:, :, channels:], all_masks, cycle_pos, cycle_size).astype(
-        BF16
-    )
+        return summed(*dp_halving(values, order, index))
 
     project_grad = t_dot(block_out, reassembled_grad)
     block_grad = block_cotangent.astype(F32) + dot_t(reassembled_grad, project_weight)
     mlp_grad = block_grad.astype(BF16)
-    fc2_grad = t_dot(hidden, mlp_grad)
+    fc2_parts = scattering(shared_out(t_dot(hidden, mlp_grad)))
+    mlp_grad, fc2_parts = tied(mlp_grad, fc2_parts)
+    fc2_sums = scattered(fc2_parts)
     conv_sums = core_summed(conv_shares, core)
     pre_grad = gelu_back(pre_act, dot_t(mlp_grad, fc2_weight)).astype(BF16)
     fc1_grad = t_dot(normed_two, pre_grad)
@@ -1297,50 +1399,52 @@
 
     rows = width_model // cycle_size
     rows = width_model // cycle_size
-    model_sums = scattered(shared_out(fc2_grad, out_proj_grad, wide(project_grad)))
-    fc1_sums = scattered(shared_out(fc1_grad))
-    early = [model_sums, fc1_sums]
-    early_sums = jnp.concatenate(early, axis=1)
-    attended_grad, conv_sums = tied(attended_grad, conv_sums)
-    conv_sums = dp_halved(conv_sums, one_way, 0)
-    query_low, key_grad, value_grad, unit_grad = attend_back(
-        tab, query, attended_grad, outputs, lse, ks, vs, key_weight, value_weight, sorted_norm,
+    fc1_sums = core_summed(shared_out(fc1_grad), core)
+    out_sums = core_summed(shared_out(out_proj_grad, wide(project_grad)), core)
+    attended_grad, conv_sums, fc1_sums, out_sums, fc2_sums = tied(
+        attended_grad, conv_sums, fc1_sums, out_sums, fc2_sums
+    )
+    conv_sums, conv_got = dp_halving(conv_sums, one_way, 0)
+    fc1_sums, fc1_got = dp_halving(fc1_sums, other_way, 0)
+    out_sums, out_got = dp_halving(out_sums, one_way, 0)
+    fc2_sums = lax.psum_scatter(fc2_sums, "blk", scatter_dimension=0, tiled=True)
+    query_low, key_grad, value_grad, token_grad = attend_back(
+        tab, cycle_pos, query, attended_grad, outputs, lse, ks, vs, key_weight, value_weight, sorted_norm,
         bias, unit_size, units, kinds, heads,
     )
-    query_low, key_grad, value_grad, unit_grad, conv_sums = tied(
-        query_low, key_grad, value_grad, unit_grad, conv_sums
+    query_low, key_grad, value_grad, token_grad, conv_got, fc1_got, out_got, fc2_sums = tied(
+        query_low, key_grad, value_grad, token_grad, conv_got, fc1_got, out_got, fc2_sums
     )
+    normed_one_grad = lax.psum_scatter(token_grad, "blk", scatter_dimension=0, tiled=True)
+    conv_sums = summed(conv_sums, conv_got)
+    fc1_sums = summed(fc1_sums, fc1_got)
+    out_sums = summed(out_sums, out_got)
     query_grad = t_dot(normed_one, query_low)
     key_sums = core_summed(shared_out(key_grad, value_grad), core)
     query_sums = core_summed(shared_out(query_grad), core)
 
-    def unit_part(step):
-        part = unit_grad[4 * step * half_tokens : 4 * (step + 1) * half_tokens]
-        part = part.reshape(4, half_tokens, width_model)
-        return part[:2].astype(F32) + to_sibling(part[2:]).astype(F32)
-
-    ahead = behind = None
-    for step in range(chips - 1, -1, -1):
-        part = unit_part(step)
-        if ahead is None:
-            ahead, behind = part[0], part[1]
-        else:
-            ahead = passed_along(ahead.astype(BF16), "blk", -2).astype(F32) + part[0]
-            behind = passed_along(behind.astype(BF16), "blk", 2).astype(F32) + part[1]
-            turn = chips - 1 - step
-            if turn < bits:
-                conv_sums = dp_halved(conv_sums, one_way, turn)
-            if turn <= bits:
-                key_sums = dp_halved(key_sums, one_way, turn - 1)
-                query_sums = dp_halved(query_sums, other_way, turn - 1)
-                ahead, behind, key_sums, query_sums, conv_sums = tied(
-                    ahead, behind, key_sums, query_sums, conv_sums
-                )
-                if turn == 1:
-                    early_sums = lax.psum_scatter(
-                        early_sums.reshape(-1, 256), "blk", scatter_dimension=0, tiled=True
-                    )
-    normed_one_grad = jnp.concatenate([ahead, behind], axis=0) + dot_t(query_low, query_weight)
+    for index in range(bits):
+        if index:
+            conv_sums = dp_halved(conv_sums, one_way, index)
+            fc1_sums = dp_halved(fc1_sums, other_way, index)
+            out_sums = dp_halved(out_sums, one_way, index)
+        key_sums = dp_halved(key_sums, one_way, index)
+        query_sums = dp_halved(query_sums, other_way, index)
+    late = [conv_sums, fc1_sums, out_sums, key_sums, query_sums]
+    late_orders = [one_way, other_way, one_way, one_way, other_way]
+    chip_sums = ChipSums(
+        jnp.concatenate([part.reshape(chips, -1, 256) for part in late], axis=1), chip
+    )
+    for turn in range(1, chips):
+        chip_sums.step(turn)
+    around = unpack(tab.around, group_mapped).reshape(3, SLOTS, ROWW, channels)
+    merged = upsample_forward(around[0], around[1], around[2], all_masks).astype(BF16)
+    fc2_all = gathered_over_groups(fc2_sums, dp_pos)
+    normed_one_grad, fc2_all, *chip_sums.moving = tied(
+        normed_one_grad, fc2_all, *chip_sums.moving
+    )
+    gather = GroupGather(chip_sums.result(), dp_pos)
+    normed_one_grad = normed_one_grad.astype(F32) + dot_t(query_low, query_weight)
 
     norm_one_pull = jax.vjp(layer_norm, stream_start, norm1_gain, norm1_bias)[1]
     start_side, norm1_gain_grad, norm1_bias_grad = norm_one_pull(normed_one_grad)
@@ -1360,23 +1464,20 @@
     small = jnp.concatenate(small, axis=1).astype(BF16)
     small_rows = -(-small.shape[1] // 1024) * 8
     small = jnp.pad(small, ((0, 0), (0, small_rows * 128 - small.shape[1])))
-    small = small_sums(small.reshape(cycle_size, small_rows, 128), core, chip, dp_pos).reshape(-1)
+    small = small.reshape(cycle_size, small_rows, 128)
+    small = core_summed(small, core)
+    for bit in range(bits):
+        gather.step(bit)
+        small = over_groups(small, bit)
+    small = sum_over_chips(small, chip).reshape(-1)
     table_size = table_rows * rows
     norms = [small[table_size + index * rows :][:rows] for index in range(4)]
 
     unit_share = 9 * channels // cycle_size
     out_share = channels // cycle_size
-    fc2_share = fc2_weight.shape[0] // cycle_size
-    convs, keys_values, query_share = finished(
-        [conv_sums, key_sums, query_sums], [one_way, one_way, other_way], chip, dp_pos
+    convs, fc1_share, outs, keys_values, query_share = whole_shares(
+        gather.result(), late, late_orders
     )
-    whole = gathered_over_groups(early_sums, dp_pos)
-    shares, spot = [], 0
-    for part, columns in zip(early, (width_model, fc1_weight.shape[1])):
-        size = part.shape[1]
-        shares.append(whole[:, spot : spot + size].reshape(-1, columns).astype(F32))
-        spot += size
-    models, fc1_share = shares
     return (
         block_out,
         merged,
@@ -1387,12 +1488,12 @@
         query_share,
         keys_values[:rows],
         keys_values[rows:],
-        models[fc2_share : fc2_share + rows],
+        outs[:rows],
         norms[2],
         norms[3],
         fc1_share,
-        models[:fc2_share],
-        models[fc2_share + rows :].reshape(rows, channels),
+        fc2_all.reshape(-1, width_model).astype(F32),
+        outs[rows:].reshape(rows, channels),
         convs[:unit_share],
         convs[unit_share : 2 * unit_share],
         convs[2 * unit_share : 3 * unit_share],

time: 632 us -> 604 us (0.956)
  waiting for transfers between devices: 139 us -> 88.1 us
  blocking collectives: 0 us -> 37.6 us
  other arithmetic: 32.2 us -> 54.3 us
  starting transfers between devices: 88.7 us -> 68.2 us
  local copies, waits for them, and re-layouts: 75 us -> 55.6 us
    all_to_all x2 -> x0, waiting for transfers between devices: 42.1 us -> none  [the longest x1 24.5 us: to_windows(): got = lax.all_to_all(jnp.stack(sends), 'blk', 0, 0)]
    all_to_all x0 -> x2, blocking collectives: none -> 37.6 us  [exchanged(): return lax.all_to_all(values, 'blk', 0, 0).reshape(-1, channels)]
    ppermute x53 -> x47, waiting for transfers between devices: 89.9 us -> 76.5 us  [passed(): return lax.ppermute(value, axis, pairs)]
    ppermute x53 -> x47, starting transfers between devices: 79.7 us -> 68 us  [passed(): return lax.ppermute(value, axis, pairs)]
    convert_element_type x18 -> x25, other arithmetic: 4.95 us -> 16.4 us  [the longest x10 10.2 us: summed(): return (keep.astype(F32) + got.astype(F32)).astype(BF16)]
    unnamed x172 -> x161, local copies, waits for them, and re-layouts: 24.4 us -> 13 us
    convert_element_type x4 -> x6, other arithmetic: 2.85 us -> 14 us  [core_summed(): return (keep.astype(F32) + to_sibling(send).astype(F32)).astype(BF16)]
    all_to_all x2 -> x0, starting transfers between devices: 8.86 us -> none  [the longest x1 4.65 us: to_windows(): got = lax.all_to_all(jnp.stack(sends), 'blk', 0, 0)]
  transfers between devices with their start and end apart: 58 -> 52, of which waited for: 28 -> 20; matrix products, arithmetic and copies ran while one was open for 13% -> 17% of each run, Pallas kernels for 31% -> 32%
where the time goes in v3:
time: 604 us; the launch traced here: 594 us
  Pallas kernels  220 us (36%)
  waiting for transfers between devices  88.1 us (15%)
  starting transfers between devices  68.2 us (11%)
  local copies, waits for them, and re-layouts  55.6 us (9%)
  other arithmetic  54.3 us (9%)
  matrix products  50.1 us (8%)
  blocking collectives  37.6 us (6%)
  between operations  20.9 us (3%)
    pallas_call x1, Pallas kernels, attend_back(): pl.pallas_call(functools.partial(attend_back_kernel, heads, units, items,...  92.3 us
    ppermute x47, waiting for transfers between devices, passed(): return lax.ppermute(value, axis, pairs)  76.5 us
    ppermute x47, starting transfers between devices, passed(): return lax.ppermute(value, axis, pairs)  68 us
    pallas_call x1, Pallas kernels, attend(): pl.pallas_call(functools.partial(attend_kernel, heads, units, items), gri...  67 us
    all_to_all x2, blocking collectives, exchanged(): return lax.all_to_all(values, 'blk', 0, 0).reshape(-1, channels)  37.6 us
    dot_general x5, matrix products, dot_t(): return lax.dot_general(left, right, NT, preferred_element_type=F32)  22.5 us
    pallas_call x1, Pallas kernels, merge(): pl.pallas_call(functools.partial(merge_kernel, cycle_size), grid_spec=plt...  20.6 us
    pallas_call x4, Pallas kernels, sort_step(): pl.pallas_call(functools.partial(sort_step_kernel, step), grid_spec=pltpu...  20.1 us
  transfers between devices with their start and end apart: 52, of which 20 were waited for; matrix products, arithmetic and copies ran while one was open for 17% of the time, Pallas kernels for 32%

profile of v3, /device:TPU:0, one launch (start us, length us, event | category | flops | bytes accessed | tf_op | source)
XLA Modules:
  0.0 594.3 jit_solution(16681414244131413874)
XLA Ops:
  9.0 4.7 collective-permute-start.1
  20.1 3.1 compare_select_fusion.3
  24.4 5.3 geometry.1
  29.8 5.4 own_start.1
  36.1 5.1 sort_step.4.refs_27_
  41.7 3.8 collective-permute-start.4
  46.4 5.0 sort_step.5.refs_28_
  51.4 3.5 collective-permute-done.3
  54.9 5.5 collective-permute-done.4
  62.0 3.9 collective-permute-start.9
  65.9 14.9 %collective-permute-start.7 = (bf16[240,768]{1,0:T(8,128)(2,1)S(1)}, bf16[240,768]{1,0:T(8,128)(2,1)}, u32[]{:S(2)}, u32[]{:S(2)}) collective-permute-start(bf16[240,768]{1,0:T(8,128)(2,1)S(1)} %collective-permute-done.4), channel_id=1, source_target_pairs={{0,6},{1,7},{2,0},{3,1},{4,2},{5,3},{6,4},{7,5},{8,14},{9,15},{10,... | collective-permute-start | bytes 1105928 | tf_op jit(solution)/shard_map/ppermute | solution.py:993
  80.8 5.0 sort_step.6.refs_29_
  85.9 3.3 collective-permute-done.7
  93.4 5.0 sort_step.7.refs_30_
  98.5 67.0 %attend.1 = (bf16[480,768]{1,0:T(8,128)(2,1)}, f32[704,768]{1,0:T(8,128)}, f32[16,768]{1,0:T(8,128)}, bf16[5120,768]{1,0:T(8,128)(2,1)}, bf16[5120,128]{1,0:T(8,...) custom-call(s32[80]{0:T(128)} %get-tuple-element.123.refs_0_, s32[80]{0:T(128)} %get-tuple-element.124.refs_1_, ...), custom_call_target="tpu_custom_call" | custom-call | flops 70000001024 | bytes 1000000 | tf_op jit(solution)/shard_map/attend/pallas_call | solution.py:851
  165.5 1.9 fusion.67
  168.2 4.9 fusion.51
  173.1 2.6 copy-done.75
  175.7 6.7 %add_convert_fusion.2.block_ref = bf16[480,768]{1,0:T(8,128)(2,1)} fusion(f32[480,768]{1,0:T(8,128)S(1)} %get-tuple-element.288, bf16[3072,768]{1,0:T(8,128)(2,1)} %param.35, f32[480,3072]{1,0:T(8,128)S(1)} %fusion.51), kind=kOutput, calls=%fused_computation.46 | convolution fusion | flops 2278932480 | bytes 12828672 | tf_op jit(solution)/shard_map/dot_general | solution.py:1120
  182.4 3.1 pack.1
  185.5 20.9 %all_to_all.10 = bf16[8,144,256]{2,1,0:T(8,128)(2,1)} all-to-all(bf16[8,144,256]{2,1,0:T(8,128)(2,1)} %bitcast.196), channel_id=1, replica_groups=mesh['dp'=4,'blk'=8] {'blk'}, dimensions={0} | all-to-all | bytes 1179648 | tf_op jit(solution)/shard_map/all_to_all | solution.py:1340
  206.5 20.6 %merge.1 = (bf16[768,256]{1,0:T(8,128)(2,1)}, bf16[576,256]{1,0:T(8,128)(2,1)}, bf16[9472,256]{1,0:T(8,128)(2,1)}) custom-call(s32[24]{0:T(128)} %get-tuple-element.130.refs_15_.wwidth, s32[24]{0:T(128)} %get-tuple-element.131.refs_16_.wup, s32[24]{0:T(128)} %get-tuple-element.132.refs_17_.wdown, s32[24]{0:T(128)} %get-tuple-element.133.refs_18_.wgroup, ...), custom_call_target="tpu_custom_call" | custom-call | flops 24999999488 | bytes 1000000 | tf_op jit(solution)/shard_map/merge/pallas_call | solution.py:807
  227.0 16.6 %all_to_all.11 = bf16[8,96,256]{2,1,0:T(8,128)(2,1)} all-to-all(bf16[8,96,256]{2,1,0:T(8,128)(2,1)} %bitcast.197), channel_id=1, replica_groups=mesh['dp'=4,'blk'=8] {'blk'}, dimensions={0} | all-to-all | bytes 786432 | tf_op jit(solution)/shard_map/all_to_all | solution.py:1340
  243.7 2.5 unpack.3
  246.2 2.5 fusion.68
  248.6 5.9 convolution_convert_fusion.1
  254.5 2.5 copy.42
  257.1 3.4 dynamic-slice_bitcast_fusion
  261.7 10.7 %fusion.3 = bf16[480,3072]{1,0:T(8,128)(2,1)S(1)} fusion(f32[480,3072]{1,0:T(8,128)} %copy-done.75, bf16[480,768]{1,0:T(8,128)(2,1)S(1)} %get-tuple-element.167, bf16[3072,768]{1,0:T(8,128)(2,1)} %param.35), kind=kOutput, calls=%fused_computation.7 | convolution fusion | flops 2300313600 | bytes 14303232 | tf_op jit(solution)/shard_map/dot_general | solution.py:1124
  272.4 4.8 convolution_convert_fusion
  277.3 3.5 dynamic-slice_bitcast_fusion.1
  280.8 3.9 multiply_reduce_fusion
  285.2 2.0 fusion.53
  293.8 2.2 fusion.9
  296.0 3.0 fusion.6
  299.0 5.6 fusion.7
  304.6 10.9 %reduce-scatter.4.cloned.1.call-done = bf16[768,768]{1,0:T(8,128)(2,1)} async-done(((bf16[3072,768]{1,0:T(8,128)(2,1)}), bf16[768,768]{1,0:T(8,128)(2,1)}) %reduce-scatter.4.cloned.1.call-update) | async-done | bytes 1179664 | tf_op jit(solution)/shard_map/reduce_scatter | solution.py:1375
  317.7 2.5 constant_dynamic-slice_fusion.12
  323.2 92.3 %attend_back.1 = (bf16[480,768]{1,0:T(8,128)(2,1)}, bf16[768,768]{1,0:T(8,128)(2,1)}, bf16[768,768]{1,0:T(8,128)(2,1)}, bf16[3840,768]{1,0:T(8,128)(2,1)}) custom-call(s32[1]{0:T(128)} %bitcast.1.place.me, s32[80]{0:T(128)} %get-tuple-element.123.refs_0_, s32[80]{0:T(128)} %get-tuple-element.124.refs_1_, s32[80]{0:T(128)} %get-tuple-element.125.refs_2_, ...), custom_call_target="tpu_custom_call" | custom-call | flops 89999998976 | bytes 1000000 | tf_op jit(solution)/shard_map/attend_back/pallas_call | solution.py:908
  417.6 3.2 unpack.2
  424.3 8.4 %collective-permute-start.18 = (bf16[1,1,48,768]{3,2,1,0:T(8,128)(2,1)S(1)}, bf16[1,1,48,768]{3,2,1,0:T(8,128)(2,1)S(1)}, u32[]{:S(2)}, u32[]{:S(2)}) collective-permute-start(bf16[1,1,48,768]{3,2,1,0:T(8,128)(2,1)S(1)} %get-tuple-element.261), channel_id=1, source_target_pairs={{0,8},{8,0},{16,24},{24,16},{1,9},{9,1},{17,25},{25,17},{2,10},{10... | collective-permute-start | bytes 221192 | tf_op jit(solution)/shard_map/ppermute | solution.py:993
  433.0 2.0 collective-permute-start.27
  445.5 1.8 collective-permute-start.22
  448.8 1.9 collective-permute-start.19
  452.5 3.2 collective-permute-done.21
  456.8 8.0 %collective-permute-done.19 = bf16[1,2,48,768]{3,2,1,0:T(8,128)(2,1)} collective-permute-done((bf16[1,2,48,768]{3,2,1,0:T(8,128)(2,1)}, bf16[1,2,48,768]{3,2,1,0:T(8,128)(2,1)}, u32[]{:S(2)}, u32[]{:S(2)}) %collective-permute-start.19) | collective-permute-done | bytes 147488 | tf_op jit(solution)/shard_map/ppermute | solution.py:993
  466.9 2.0 add_convert_fusion.6
  470.2 2.1 reshape.943
  474.1 2.0 fusion.8
  477.7 3.1 collective-permute-done.32
  482.6 9.6 %collective-permute-done.29 = bf16[4,96,768]{2,1,0:T(8,128)(2,1)S(1)} collective-permute-done((bf16[4,96,768]{2,1,0:T(8,128)(2,1)S(1)}, bf16[4,96,768]{2,1,0:T(8,128)(2,1)S(1)}, u32[]{:S(2)}, u32[]{:S(2)}) %collective-permute-start.29) | collective-permute-done | bytes 589856 | tf_op jit(solution)/shard_map/ppermute | solution.py:993
  499.0 1.9 collective-permute-done.30
  500.9 1.8 add_convert_fusion.9
  502.7 1.8 reshape.945
  508.8 11.4 %collective-permute-done.34 = bf16[448,256]{1,0:T(8,128)(2,1)S(1)} collective-permute-done((bf16[448,256]{1,0:T(8,128)(2,1)S(1)}, bf16[448,256]{1,0:T(8,128)(2,1)S(1)}, u32[]{:S(2)}, u32[]{:S(2)}) %collective-permute-start.34) | collective-permute-done | bytes 229408 | tf_op jit(solution)/shard_map/ppermute | solution.py:993
  520.5 2.1 collective-permute-start.26
  522.5 7.6 %collective-permute-done.35 = bf16[448,256]{1,0:T(8,128)(2,1)S(1)} collective-permute-done((bf16[448,256]{1,0:T(8,128)(2,1)S(1)}, bf16[448,256]{1,0:T(8,128)(2,1)S(1)}, u32[]{:S(2)}, u32[]{:S(2)}) %collective-permute-start.35) | collective-permute-done | bytes 229408 | tf_op jit(solution)/shard_map/ppermute | solution.py:993
  531.1 5.2 collective-permute-done.36
  537.1 3.8 multiply_reduce_fusion.1
  541.0 3.1 fusion.52
  551.1 1.8 collective-permute-done.38
  558.3 3.3 collective-permute-start.42
  563.0 3.1 collective-permute-done.41
  570.1 5.4 collective-permute-done.44
  (390 shorter events, 97.6 us)
Async XLA Ops:
  7.2 158.3 %copy-start = (bf16[768,768]{1,0:T(8,128)(2,1)S(1)}, bf16[768,768]{1,0:T(8,128)(2,1)}, u32[]{:S(2)}) copy-start(bf16[768,768]{1,0:T(8,128)(2,1)} %param.31) | copy-start | bytes 3538948
  7.2 16.0 %copy-start.67 = (f32[768]{0:T(1024)S(1)}, f32[768]{0:T(1024)}, u32[]{:S(2)}) copy-start(f32[768]{0:T(1024)} %param.27) | copy-start | bytes 9220
  7.2 16.6 %copy-start.60 = (f32[768]{0:T(1024)S(1)}, f32[768]{0:T(1024)}, u32[]{:S(2)}) copy-start(f32[768]{0:T(1024)} %param.26) | copy-start | bytes 9220
  7.3 158.2 %all-gather.3.cloned.1.call-start = ((), (), s32[]{:S(2)}) async-start(), calls=%async_computation.5 | async-start | bytes 2654208 | tf_op jit(solution)/shard_map/all_gather | solution.py:1322
  7.3 27.9 %collective-permute-start.2 = (bf16[480,768]{1,0:T(8,128)(2,1)}, bf16[480,768]{1,0:T(8,128)(2,1)S(1)}, u32[]{:S(2)}, u32[]{:S(2)}) collective-permute-start(bf16[480,768]{1,0:T(8,128)(2,1)} %refs_0_.2), channel_id=1, source_target_pairs={{0,1},{1,0},{2,3},{3,2},{4,5},{5,4},{6,7},{7,6},{8,9},{9,8},{10,11... | collective-permute-start | bytes 2211848 | tf_op jit(solution)/shard_map/ppermute | solution.py:993
  9.0 32.2 %collective-permute-start.1 = (bf16[240,768]{1,0:T(8,128)(2,1)S(1)}, bf16[240,768]{1,0:T(8,128)(2,1)S(1)}, u32[]{:S(2)}, u32[]{:S(2)}) collective-permute-start(bf16[240,768]{1,0:T(8,128)(2,1)S(1)} %get-tuple-element.247), channel_id=1, source_target_pairs={{0,6},{1,7},{2,0},{3,1},{4,2},{5,3},{6,4},{7,5},{8,14},{9,15},{10,... | collective-permute-start | bytes 1105928 | tf_op jit(solution)/shard_map/ppermute | solution.py:993
  13.6 27.5 %collective-permute-start = (bf16[240,768]{1,0:T(8,128)(2,1)S(1)}, bf16[240,768]{1,0:T(8,128)(2,1)S(1)}, u32[]{:S(2)}, u32[]{:S(2)}) collective-permute-start(bf16[240,768]{1,0:T(8,128)(2,1)S(1)} %get-tuple-element.248), channel_id=1, source_target_pairs={{0,2},{1,3},{2,4},{3,5},{4,6},{5,7},{6,0},{7,1},{8,10},{9,11},{10,... | collective-permute-start | bytes 1105928 | tf_op jit(solution)/shard_map/ppermute | solution.py:993
  23.2 18.3 %copy-start.64 = (s32[12]{0:T(128)}, s32[12]{0:T(128)S(1)}, u32[]{:S(2)}) copy-start(s32[12]{0:T(128)S(1)} %select_select_fusion.1) | copy-start | bytes 148
  41.2 5.2 collective-permute-start.5
  41.6 48.8 %copy-start.52 = (pred[12,40]{1,0:T(8,128)(4,1)}, pred[12,40]{1,0:T(8,128)(4,1)S(1)}, u32[]{:S(2)}) copy-start(pred[12,40]{1,0:T(8,128)(4,1)S(1)} %get-tuple-element.275) | copy-start | bytes 1444
  41.6 48.8 %copy-start.54 = (pred[12,40]{1,0:T(8,128)(4,1)}, pred[12,40]{1,0:T(8,128)(4,1)S(1)}, u32[]{:S(2)}) copy-start(pred[12,40]{1,0:T(8,128)(4,1)S(1)} %get-tuple-element.276) | copy-start | bytes 1444
  41.6 13.3 %collective-permute-start.3 = (bf16[240,768]{1,0:T(8,128)(2,1)S(1)}, bf16[240,768]{1,0:T(8,128)(2,1)S(1)}, u32[]{:S(2)}, u32[]{:S(2)}) collective-permute-start(bf16[240,768]{1,0:T(8,128)(2,1)S(1)} %collective-permute-done), channel_id=1, source_target_pairs={{0,2},{1,3},{2,4},{3,5},{4,6},{5,7},{6,0},{7,1},{8,10},{9,11},{10,... | collective-permute-start | bytes 1105928 | tf_op jit(solution)/shard_map/ppermute | solution.py:993
  41.7 18.7 %collective-permute-start.4 = (bf16[240,768]{1,0:T(8,128)(2,1)S(1)}, bf16[240,768]{1,0:T(8,128)(2,1)S(1)}, u32[]{:S(2)}, u32[]{:S(2)}) collective-permute-start(bf16[240,768]{1,0:T(8,128)(2,1)S(1)} %collective-permute-done.1), channel_id=1, source_target_pairs={{0,6},{1,7},{2,0},{3,1},{4,2},{5,3},{6,4},{7,5},{8,14},{9,15},{10,... | collective-permute-start | bytes 1105928 | tf_op jit(solution)/shard_map/ppermute | solution.py:993
  62.0 18.9 %collective-permute-start.8 = (bf16[480,768]{1,0:T(8,128)(2,1)}, bf16[480,768]{1,0:T(8,128)(2,1)}, u32[]{:S(2)}, u32[]{:S(2)}) collective-permute-start(bf16[480,768]{1,0:T(8,128)(2,1)} %constant_dynamic-update-slice_fusion.2.refs_0_), channel_id=1, source_target_pairs={{0,1},{1,0},{2,3},{3,2},{4,5},{5,4},{6,7},{7,6},{8,9},{9,8},{10,11... | collective-permute-start | bytes 2211848 | tf_op jit(solution)/shard_map/ppermute | solution.py:993
  62.0 18.7 %collective-permute-start.9 = (bf16[12,40,256]{2,1,0:T(8,128)(2,1)S(1)}, bf16[12,40,256]{2,1,0:T(8,128)(2,1)S(1)}, u32[]{:S(2)}, u32[]{:S(2)}) collective-permute-start(bf16[12,40,256]{2,1,0:T(8,128)(2,1)S(1)} %get-tuple-element.154), channel_id=1, source_target_pairs={{0,7},{1,0},{2,1},{3,2},{4,3},{5,4},{6,5},{7,6},{8,15},{9,8},{10,9... | collective-permute-start | bytes 737288 | tf_op jit(solution)/shard_map/ppermute | solution.py:993
  65.8 14.9 %collective-permute-start.10 = (bf16[12,40,256]{2,1,0:T(8,128)(2,1)S(1)}, bf16[12,40,256]{2,1,0:T(8,128)(2,1)S(1)}, u32[]{:S(2)}, u32[]{:S(2)}) collective-permute-start(bf16[12,40,256]{2,1,0:T(8,128)(2,1)S(1)} %get-tuple-element.155), channel_id=1, source_target_pairs={{0,1},{1,2},{2,3},{3,4},{4,5},{5,6},{6,7},{7,0},{8,9},{9,10},{10,1... | collective-permute-start | bytes 737288 | tf_op jit(solution)/shard_map/ppermute | solution.py:993
  65.9 20.0 %collective-permute-start.6 = (bf16[240,768]{1,0:T(8,128)(2,1)S(1)}, bf16[240,768]{1,0:T(8,128)(2,1)S(1)}, u32[]{:S(2)}, u32[]{:S(2)}) collective-permute-start(bf16[240,768]{1,0:T(8,128)(2,1)S(1)} %collective-permute-done.3), channel_id=1, source_target_pairs={{0,2},{1,3},{2,4},{3,5},{4,6},{5,7},{6,0},{7,1},{8,10},{9,11},{10,... | collective-permute-start | bytes 1105928 | tf_op jit(solution)/shard_map/ppermute | solution.py:993
  65.9 23.3 %collective-permute-start.7 = (bf16[240,768]{1,0:T(8,128)(2,1)S(1)}, bf16[240,768]{1,0:T(8,128)(2,1)}, u32[]{:S(2)}, u32[]{:S(2)}) collective-permute-start(bf16[240,768]{1,0:T(8,128)(2,1)S(1)} %collective-permute-done.4), channel_id=1, source_target_pairs={{0,6},{1,7},{2,0},{3,1},{4,2},{5,3},{6,4},{7,5},{8,14},{9,15},{10,... | collective-permute-start | bytes 1105928 | tf_op jit(solution)/shard_map/ppermute | solution.py:993
  90.2 2.3 collective-permute-start.11
  98.4 217.1 %reduce-scatter.4.cloned.1.call-start = ((), (), s32[]{:S(2)}) async-start(), calls=%async_computation.7 | async-start | bytes 5898240 | tf_op jit(solution)/shard_map/reduce_scatter | solution.py:1375
  98.5 67.1 %copy-start.2 = (f32[480,768]{1,0:T(8,128)S(1)}, f32[480,768]{1,0:T(8,128)}, u32[]{:S(2)}) copy-start(f32[480,768]{1,0:T(8,128)} %get-tuple-element.122) | copy-start | bytes 4423684
  257.0 158.5 %reduce-scatter.6.cloned.1.call-start = ((), (), s32[]{:S(2)}) async-start(), calls=%async_computation.8 | async-start | bytes 1327104 | tf_op jit(solution)/shard_map/reduce_scatter | solution.py:1410
  257.1 23.6 %slice-start = ((s8[4718592]{0:T(1024)(128)(4,1)}), s8[4194304]{0:T(1024)(128)(4,1)S(1)}, s32[]{:S(2)}) async-start(s8[4718592]{0:T(1024)(128)(4,1)} %bitcast.210), calls=%async_computation.10 | async-start | bytes 8388608
  260.5 35.5 %collective-permute-start.12 = (bf16[4,1184,256]{2,1,0:T(8,128)(2,1)}, bf16[4,1184,256]{2,1,0:T(8,128)(2,1)}, u32[]{:S(2)}, u32[]{:S(2)}) collective-permute-start(bf16[4,1184,256]{2,1,0:T(8,128)(2,1)} %dynamic-slice_bitcast_fusion), channel_id=1, source_target_pairs={{0,1},{1,0},{2,3},{3,2},{4,5},{5,4},{6,7},{7,6},{8,9},{9,8},{10,11... | collective-permute-start | bytes 7274504 | tf_op jit(solution)/shard_map/ppermute | solution.py:993
  261.7 19.0 %slice-start.1 = ((s8[4718592]{0:T(1024)(128)(4,1)}), s8[524288]{0:T(1024)(128)(4,1)S(1)}, s32[]{:S(2)}) async-start(s8[4718592]{0:T(1024)(128)(4,1)} %bitcast.210), calls=%async_computation.11 | async-start | bytes 1048576
  284.8 14.2 %collective-permute-start.13 = (bf16[4,96,3072]{2,1,0:T(8,128)(2,1)}, bf16[4,96,3072]{2,1,0:T(8,128)(2,1)}, u32[]{:S(2)}, u32[]{:S(2)}) collective-permute-start(bf16[4,96,3072]{2,1,0:T(8,128)(2,1)} %dynamic-slice_bitcast_fusion.1), channel_id=1, source_target_pairs={{0,1},{1,0},{2,3},{3,2},{4,5},{5,4},{6,7},{7,6},{8,9},{9,8},{10,11... | collective-permute-start | bytes 7077896 | tf_op jit(solution)/shard_map/ppermute | solution.py:993
  291.2 2.6 collective-permute-start.14
  299.0 21.8 %copy-start.10 = (bf16[4,1184,256]{2,1,0:T(8,128)(2,1)}, bf16[4,1184,256]{2,1,0:T(8,128)(2,1)S(1)}, u32[]{:S(2)}) copy-start(bf16[4,1184,256]{2,1,0:T(8,128)(2,1)S(1)} %fusion.6) | copy-start | bytes 7274500
  315.6 102.1 %all-gather.5.cloned.1.call-start = ((), (), s32[]{:S(2)}) async-start(), calls=%async_computation.6 | async-start | bytes 2654208 | tf_op jit(solution)/shard_map/all_gather | solution.py:1351
  316.1 220.9 %reduce-scatter.8.cloned.1.call-start = ((), (), s32[]{:S(2)}) async-start(), calls=%async_computation.9 | async-start | bytes 6635520 | tf_op jit(solution)/shard_map/reduce_scatter | solution.py:1418
  316.2 99.3 %collective-permute-start.17 = (bf16[4,64,768]{2,1,0:T(8,128)(2,1)S(1)}, bf16[4,64,768]{2,1,0:T(8,128)(2,1)S(1)}, u32[]{:S(2)}, u32[]{:S(2)}) collective-permute-start(bf16[4,64,768]{2,1,0:T(8,128)(2,1)S(1)} %constant_dynamic-slice_fusion.11), channel_id=1, source_target_pairs={{0,8},{8,0},{16,24},{24,16},{1,9},{9,1},{17,25},{25,17},{2,10},{10... | collective-permute-start | bytes 1179656 | tf_op jit(solution)/shard_map/ppermute | solution.py:993
  320.1 95.4 %collective-permute-start.16 = (bf16[4,48,3072]{2,1,0:T(8,128)(2,1)}, bf16[4,48,3072]{2,1,0:T(8,128)(2,1)}, u32[]{:S(2)}, u32[]{:S(2)}) collective-permute-start(bf16[4,48,3072]{2,1,0:T(8,128)(2,1)} %constant_dynamic-slice_fusion.12), channel_id=1, source_target_pairs={{0,16},{8,24},{16,0},{24,8},{1,17},{9,25},{17,1},{25,9},{2,18},{10... | collective-permute-start | bytes 3538952 | tf_op jit(solution)/shard_map/ppermute | solution.py:993
  321.9 93.7 %collective-permute-start.15 = (bf16[4,592,256]{2,1,0:T(8,128)(2,1)}, bf16[4,592,256]{2,1,0:T(8,128)(2,1)}, u32[]{:S(2)}, u32[]{:S(2)}) collective-permute-start(bf16[4,592,256]{2,1,0:T(8,128)(2,1)} %constant_dynamic-slice_fusion.13), channel_id=1, source_target_pairs={{0,8},{8,0},{16,24},{24,16},{1,9},{9,1},{17,25},{25,17},{2,10},{10... | collective-permute-start | bytes 3637256 | tf_op jit(solution)/shard_map/ppermute | solution.py:993
  424.3 23.7 %collective-permute-start.18 = (bf16[1,1,48,768]{3,2,1,0:T(8,128)(2,1)S(1)}, bf16[1,1,48,768]{3,2,1,0:T(8,128)(2,1)S(1)}, u32[]{:S(2)}, u32[]{:S(2)}) collective-permute-start(bf16[1,1,48,768]{3,2,1,0:T(8,128)(2,1)S(1)} %get-tuple-element.261), channel_id=1, source_target_pairs={{0,8},{8,0},{16,24},{24,16},{1,9},{9,1},{17,25},{25,17},{2,10},{10... | collective-permute-start | bytes 221192 | tf_op jit(solution)/shard_map/ppermute | solution.py:993
  432.7 12.8 %collective-permute-start.20 = (bf16[1,1,48,768]{3,2,1,0:T(8,128)(2,1)S(1)}, bf16[1,1,48,768]{3,2,1,0:T(8,128)(2,1)S(1)}, u32[]{:S(2)}, u32[]{:S(2)}) collective-permute-start(bf16[1,1,48,768]{3,2,1,0:T(8,128)(2,1)S(1)} %get-tuple-element.262), channel_id=1, source_target_pairs={{0,16},{8,24},{16,0},{24,8},{1,17},{9,25},{17,1},{25,9},{2,18},{10... | collective-permute-start | bytes 221192 | tf_op jit(solution)/shard_map/ppermute | solution.py:993
  433.0 15.9 %collective-permute-start.27 = (bf16[4,32,768]{2,1,0:T(8,128)(2,1)S(1)}, bf16[4,32,768]{2,1,0:T(8,128)(2,1)S(1)}, u32[]{:S(2)}, u32[]{:S(2)}) collective-permute-start(bf16[4,32,768]{2,1,0:T(8,128)(2,1)S(1)} %constant_dynamic-slice_fusion.8), channel_id=1, source_target_pairs={{0,16},{8,24},{16,0},{24,8},{1,17},{9,25},{17,1},{25,9},{2,18},{10... | collective-permute-start | bytes 589832 | tf_op jit(solution)/shard_map/ppermute | solution.py:993
  438.6 28.3 %collective-permute-start.23 = (bf16[4,24,3072]{2,1,0:T(8,128)(2,1)}, bf16[4,24,3072]{2,1,0:T(8,128)(2,1)}, u32[]{:S(2)}, u32[]{:S(2)}) collective-permute-start(bf16[4,24,3072]{2,1,0:T(8,128)(2,1)} %constant_dynamic-slice_fusion.9), channel_id=1, source_target_pairs={{0,8},{8,0},{16,24},{24,16},{1,9},{9,1},{17,25},{25,17},{2,10},{10... | collective-permute-start | bytes 1769480 | tf_op jit(solution)/shard_map/ppermute | solution.py:993
  440.5 28.5 %collective-permute-start.31 = (bf16[4,96,768]{2,1,0:T(8,128)(2,1)}, bf16[4,96,768]{2,1,0:T(8,128)(2,1)}, u32[]{:S(2)}, u32[]{:S(2)}) collective-permute-start(bf16[4,96,768]{2,1,0:T(8,128)(2,1)} %dynamic-slice_bitcast_fusion.2), channel_id=1, source_target_pairs={{0,1},{1,0},{2,3},{3,2},{4,5},{5,4},{6,7},{7,6},{8,9},{9,8},{10,11... | collective-permute-start | bytes 1769480 | tf_op jit(solution)/shard_map/ppermute | solution.py:993
  445.5 31.0 %collective-permute-start.22 = (bf16[4,296,256]{2,1,0:T(8,128)(2,1)}, bf16[4,296,256]{2,1,0:T(8,128)(2,1)}, u32[]{:S(2)}, u32[]{:S(2)}) collective-permute-start(bf16[4,296,256]{2,1,0:T(8,128)(2,1)} %constant_dynamic-slice_fusion.10), channel_id=1, source_target_pairs={{0,16},{8,24},{16,0},{24,8},{1,17},{9,25},{17,1},{25,9},{2,18},{10... | collective-permute-start | bytes 1818632 | tf_op jit(solution)/shard_map/ppermute | solution.py:993
  448.0 7.6 %collective-permute-start.21 = (bf16[2,1,48,768]{3,2,1,0:T(8,128)(2,1)}, bf16[2,1,48,768]{3,2,1,0:T(8,128)(2,1)}, u32[]{:S(2)}, u32[]{:S(2)}) collective-permute-start(bf16[2,1,48,768]{3,2,1,0:T(8,128)(2,1)} %maximum_select_fusion.7), channel_id=1, source_target_pairs={{0,8},{8,0},{16,24},{24,16},{1,9},{9,1},{17,25},{25,17},{2,10},{10... | collective-permute-start | bytes 442376 | tf_op jit(solution)/shard_map/ppermute | solution.py:993
  448.8 16.0 %collective-permute-start.19 = (bf16[1,2,48,768]{3,2,1,0:T(8,128)(2,1)}, bf16[1,2,48,768]{3,2,1,0:T(8,128)(2,1)}, u32[]{:S(2)}, u32[]{:S(2)}) collective-permute-start(bf16[1,2,48,768]{3,2,1,0:T(8,128)(2,1)} %maximum_select_fusion.6), channel_id=1, source_target_pairs={{0,16},{8,24},{16,0},{24,8},{1,17},{9,25},{17,1},{25,9},{2,18},{10... | collective-permute-start | bytes 442376 | tf_op jit(solution)/shard_map/ppermute | solution.py:993
  452.5 14.5 %copy-start.21 = (bf16[4,48,3072]{2,1,0:T(8,128)(2,1)S(1)}, bf16[4,48,3072]{2,1,0:T(8,128)(2,1)}, u32[]{:S(2)}) copy-start(bf16[4,48,3072]{2,1,0:T(8,128)(2,1)} %copy-done.20) | copy-start | bytes 3538948
  455.6 18.5 %collective-permute-start.28 = (bf16[4,192,768]{2,1,0:T(8,128)(2,1)}, bf16[4,192,768]{2,1,0:T(8,128)(2,1)}, u32[]{:S(2)}, u32[]{:S(2)}) collective-permute-start(bf16[4,192,768]{2,1,0:T(8,128)(2,1)} %fusion.11), channel_id=1, source_target_pairs={{0,1},{1,0},{2,3},{3,2},{4,5},{5,4},{6,7},{7,6},{8,9},{9,8},{10,11... | collective-permute-start | bytes 3538952 | tf_op jit(solution)/shard_map/ppermute | solution.py:993
  472.3 8.5 %collective-permute-start.32 = (bf16[4,48,768]{2,1,0:T(8,128)(2,1)S(1)}, bf16[4,48,768]{2,1,0:T(8,128)(2,1)S(1)}, u32[]{:S(2)}, u32[]{:S(2)}) collective-permute-start(bf16[4,48,768]{2,1,0:T(8,128)(2,1)S(1)} %constant_dynamic-slice_fusion.5), channel_id=1, source_target_pairs={{0,16},{8,24},{16,0},{24,8},{1,17},{9,25},{17,1},{25,9},{2,18},{10... | collective-permute-start | bytes 884744 | tf_op jit(solution)/shard_map/ppermute | solution.py:993
  476.2 15.9 %collective-permute-start.29 = (bf16[4,96,768]{2,1,0:T(8,128)(2,1)S(1)}, bf16[4,96,768]{2,1,0:T(8,128)(2,1)S(1)}, u32[]{:S(2)}, u32[]{:S(2)}) collective-permute-start(bf16[4,96,768]{2,1,0:T(8,128)(2,1)S(1)} %constant_dynamic-slice_fusion.7), channel_id=1, source_target_pairs={{0,8},{8,0},{16,24},{24,16},{1,9},{9,1},{17,25},{25,17},{2,10},{10... | collective-permute-start | bytes 1769480 | tf_op jit(solution)/shard_map/ppermute | solution.py:993
  480.9 15.8 %collective-permute-start.33 = (bf16[4,24,768]{2,1,0:T(8,128)(2,1)S(1)}, bf16[4,24,768]{2,1,0:T(8,128)(2,1)S(1)}, u32[]{:S(2)}, u32[]{:S(2)}) collective-permute-start(bf16[4,24,768]{2,1,0:T(8,128)(2,1)S(1)} %constant_dynamic-slice_fusion.4), channel_id=1, source_target_pairs={{0,8},{8,0},{16,24},{24,16},{1,9},{9,1},{17,25},{25,17},{2,10},{10... | collective-permute-start | bytes 442376 | tf_op jit(solution)/shard_map/ppermute | solution.py:993
  493.9 7.0 %collective-permute-start.30 = (bf16[4,48,768]{2,1,0:T(8,128)(2,1)}, bf16[4,48,768]{2,1,0:T(8,128)(2,1)}, u32[]{:S(2)}, u32[]{:S(2)}) collective-permute-start(bf16[4,48,768]{2,1,0:T(8,128)(2,1)} %constant_dynamic-slice_fusion.6), channel_id=1, source_target_pairs={{0,16},{8,24},{16,0},{24,8},{1,17},{9,25},{17,1},{25,9},{2,18},{10... | collective-permute-start | bytes 884744 | tf_op jit(solution)/shard_map/ppermute | solution.py:993
  495.0 11.0 %collective-permute-start.24 = (bf16[448,256]{1,0:T(8,128)(2,1)}, bf16[448,256]{1,0:T(8,128)(2,1)}, u32[]{:S(2)}, u32[]{:S(2)}) collective-permute-start(bf16[448,256]{1,0:T(8,128)(2,1)} %fusion.30), channel_id=1, source_target_pairs={{0,2},{1,3},{2,4},{3,5},{4,6},{5,7},{6,0},{7,1},{8,10},{9,11},{10,... | collective-permute-start | bytes 688136 | tf_op jit(solution)/shard_map/ppermute | solution.py:993
  505.7 14.6 %collective-permute-start.34 = (bf16[448,256]{1,0:T(8,128)(2,1)S(1)}, bf16[448,256]{1,0:T(8,128)(2,1)S(1)}, u32[]{:S(2)}, u32[]{:S(2)}) collective-permute-start(bf16[448,256]{1,0:T(8,128)(2,1)S(1)} %dynamic-slice_bitcast_fusion.3), channel_id=1, source_target_pairs={{0,6},{1,7},{2,0},{3,1},{4,2},{5,3},{6,4},{7,5},{8,14},{9,15},{10,... | collective-permute-start | bytes 688136 | tf_op jit(solution)/shard_map/ppermute | solution.py:993
  507.0 13.4 %collective-permute-start.25 = (bf16[448,256]{1,0:T(8,128)(2,1)S(1)}, bf16[448,256]{1,0:T(8,128)(2,1)S(1)}, u32[]{:S(2)}, u32[]{:S(2)}) collective-permute-start(bf16[448,256]{1,0:T(8,128)(2,1)S(1)} %fusion.24), channel_id=1, source_target_pairs={{0,2},{1,3},{2,4},{3,5},{4,6},{5,7},{6,0},{7,1},{8,10},{9,11},{10,... | collective-permute-start | bytes 688136 | tf_op jit(solution)/shard_map/ppermute | solution.py:993
  520.3 9.9 %collective-permute-start.35 = (bf16[448,256]{1,0:T(8,128)(2,1)S(1)}, bf16[448,256]{1,0:T(8,128)(2,1)S(1)}, u32[]{:S(2)}, u32[]{:S(2)}) collective-permute-start(bf16[448,256]{1,0:T(8,128)(2,1)S(1)} %fusion.21), channel_id=1, source_target_pairs={{0,6},{1,7},{2,0},{3,1},{4,2},{5,3},{6,4},{7,5},{8,14},{9,15},{10,... | collective-permute-start | bytes 688136 | tf_op jit(solution)/shard_map/ppermute | solution.py:993
  520.5 16.6 %copy-start.61 = (f32[768]{0:T(1024)S(1)}, f32[768]{0:T(1024)}, u32[]{:S(2)}) copy-start(f32[768]{0:T(1024)} %param.26) | copy-start | bytes 9220
  520.5 9.8 %collective-permute-start.26 = (bf16[448,256]{1,0:T(8,128)(2,1)S(1)}, bf16[448,256]{1,0:T(8,128)(2,1)S(1)}, u32[]{:S(2)}, u32[]{:S(2)}) collective-permute-start(bf16[448,256]{1,0:T(8,128)(2,1)S(1)} %fusion.23), channel_id=1, source_target_pairs={{0,2},{1,3},{2,4},{3,5},{4,6},{5,7},{6,0},{7,1},{8,10},{9,11},{10,... | collective-permute-start | bytes 688136 | tf_op jit(solution)/shard_map/ppermute | solution.py:993
  530.3 6.1 %collective-permute-start.36 = (bf16[448,256]{1,0:T(8,128)(2,1)S(1)}, bf16[448,256]{1,0:T(8,128)(2,1)S(1)}, u32[]{:S(2)}, u32[]{:S(2)}) collective-permute-start(bf16[448,256]{1,0:T(8,128)(2,1)S(1)} %fusion.20), channel_id=1, source_target_pairs={{0,6},{1,7},{2,0},{3,1},{4,2},{5,3},{6,4},{7,5},{8,14},{9,15},{10,... | collective-permute-start | bytes 688136 | tf_op jit(solution)/shard_map/ppermute | solution.py:993
  547.8 1.2 collective-permute-start.37
  549.1 3.8 collective-permute-start.38
  552.9 4.6 collective-permute-start.39
  555.3 10.8 %collective-permute-start.43 = (bf16[1,1,448,256]{3,2,1,0:T(8,128)(2,1)S(1)}, bf16[1,1,448,256]{3,2,1,0:T(8,128)(2,1)S(1)}, u32[]{:S(2)}, u32[]{:S(2)}) collective-permute-start(bf16[1,1,448,256]{3,2,1,0:T(8,128)(2,1)S(1)} %bitcast.193), channel_id=1, source_target_pairs={{0,16},{8,24},{16,0},{24,8},{1,17},{9,25},{17,1},{25,9},{2,18},{10... | collective-permute-start | bytes 688136 | tf_op jit(solution)/shard_map/ppermute | solution.py:993
  556.1 12.7 %collective-permute-start.45 = (bf16[1,1,448,256]{3,2,1,0:T(8,128)(2,1)S(1)}, bf16[1,1,448,256]{3,2,1,0:T(8,128)(2,1)S(1)}, u32[]{:S(2)}, u32[]{:S(2)}) collective-permute-start(bf16[1,1,448,256]{3,2,1,0:T(8,128)(2,1)S(1)} %bitcast.191), channel_id=1, source_target_pairs={{0,8},{8,0},{16,24},{24,16},{1,9},{9,1},{17,25},{25,17},{2,10},{10... | collective-permute-start | bytes 688136 | tf_op jit(solution)/shard_map/ppermute | solution.py:993
  557.5 5.5 collective-permute-start.40
  558.3 4.7 collective-permute-start.42
  561.6 4.5 collective-permute-start.41
  566.2 9.2 %collective-permute-start.44 = (bf16[2,1,448,256]{3,2,1,0:T(8,128)(2,1)S(1)}, bf16[2,1,448,256]{3,2,1,0:T(8,128)(2,1)S(1)}, u32[]{:S(2)}, u32[]{:S(2)}) collective-permute-start(bf16[2,1,448,256]{3,2,1,0:T(8,128)(2,1)S(1)} %maximum_select_fusion.2), channel_id=1, source_target_pairs={{0,8},{8,0},{16,24},{24,16},{1,9},{9,1},{17,25},{25,17},{2,10},{10... | collective-permute-start | bytes 1376264 | tf_op jit(solution)/shard_map/ppermute | solution.py:993
  568.8 8.9 %collective-permute-start.46 = (bf16[1,2,448,256]{3,2,1,0:T(8,128)(2,1)S(1)}, bf16[1,2,448,256]{3,2,1,0:T(8,128)(2,1)S(1)}, u32[]{:S(2)}, u32[]{:S(2)}) collective-permute-start(bf16[1,2,448,256]{3,2,1,0:T(8,128)(2,1)S(1)} %maximum_select_fusion.3), channel_id=1, source_target_pairs={{0,16},{8,24},{16,0},{24,8},{1,17},{9,25},{17,1},{25,9},{2,18},{10... | collective-permute-start | bytes 1376264 | tf_op jit(solution)/shard_map/ppermute | solution.py:993
  (66 other events, 231.2 us)
Sparse Core Ops, SparseCore 0:
  98.5 33.2 all-gather.2
  257.2 58.3 reduce-scatter.3
  317.8 32.7 reduce-scatter.5
  352.7 29.2 all-gather.4
  415.8 71.1 reduce-scatter.7

commit v4 on v3

--- a/solution.py
+++ b/solution.py
@@ -25,6 +25,8 @@
 KEYS = 672
 SPARE_KEYS = 768
 QROWS = 64
+TOGETHER = 5
+TOGETHER_BACK = 2
 ROWS = 1024
 VMEM = 60 * 1024 * 1024
 NT = (((1,), (1,)), ((), ()))
@@ -346,16 +348,18 @@
     )(tab.qbase, tab.qspare, tab.qwidth, tab.qitem, ids, tokens, table, gain, bias, weight)
 
 
-def query_blocks(first, many, body):
-    def pair(number, none):
-        body(first + 2 * number, 2)
+def query_blocks(first, many, most, body):
+    def run(number, none):
+        body(first + most * number, most)
         return none
 
-    lax.fori_loop(0, many // 2, pair, 0)
-
-    @pl.when(many % 2 == 1)
-    def _():
-        body(first + many - 1, 1)
+    runs = lax.div(many, most)
+    lax.fori_loop(0, runs, run, 0)
+    for count in range(1, most):
+
+        @pl.when(many - most * runs == count)
+        def _(count=count):
+            body(first + most * runs, count)
 
 
 def for_items(items, klen, body):
@@ -482,7 +486,7 @@
                     out[part], heads
                 )
 
-        query_blocks(qfirst[item], qcount[item], some_queries)
+        query_blocks(qfirst[item], qcount[item], TOGETHER, some_queries)
 
     for_items(items, klen, one_item)
     att_ref[...] = lax.dot_general(
@@ -552,7 +556,7 @@
                 part = lax.dot_general(score_grads, keys, flip, preferred_element_type=F32)
                 dq_acc[spot] += part.reshape(count, cols, feats)
 
-            query_blocks(qfirst[item], qcount[item], some_queries)
+            query_blocks(qfirst[item], qcount[item], TOGETHER_BACK, some_queries)
             dk = dk_acc[:size].astype(BF16)
             dv = dv_acc[:size].astype(BF16)
             dn_acc[here, :] += (
@@ -865,9 +869,9 @@
                 part(sorted_keys),
             ],
             scratch_shapes=[
-                pltpu.VMEM((2 * cols, feats), F32),
-                pltpu.VMEM((8, 2 * cols), F32),
-                pltpu.VMEM((8, 2 * cols), F32),
+                pltpu.VMEM((TOGETHER * cols, feats), F32),
+                pltpu.VMEM((8, TOGETHER * cols), F32),
+                pltpu.VMEM((8, TOGETHER * cols), F32),
                 pltpu.VMEM((query.shape[0], SLOTS * ROWW), BF16),
             ],
         ),

time: 604 us -> 597 us (0.988)
  starting transfers between devices: 68.2 us -> 54.7 us
  waiting for transfers between devices: 88.1 us -> 96.1 us
    ppermute x47, starting transfers between devices: 68 us -> 54.5 us  [passed(): return lax.ppermute(value, axis, pairs)]
    ppermute x47, waiting for transfers between devices: 76.5 us -> 87 us  [passed(): return lax.ppermute(value, axis, pairs)]
  transfers between devices with their start and end apart: 52 -> 52, of which waited for: 20 -> 22; matrix products, arithmetic and copies ran while one was open for 17% -> 17% of each run, Pallas kernels for 32% -> 31%
where the time goes in v4:
time: 597 us; the launch traced here: 588 us
  Pallas kernels  216 us (36%)
  waiting for transfers between devices  96.1 us (16%)
  local copies, waits for them, and re-layouts  55.2 us (9%)
  other arithmetic  55.1 us (9%)
  starting transfers between devices  54.7 us (9%)
  matrix products  50.9 us (9%)
  blocking collectives  38.7 us (6%)
  between operations  20.9 us (4%)
    pallas_call x1, Pallas kernels, attend_back(): pl.pallas_call(functools.partial(attend_back_kernel, heads, units, items,...  94.1 us
    ppermute x47, waiting for transfers between devices, passed(): return lax.ppermute(value, axis, pairs)  87 us
    pallas_call x1, Pallas kernels, attend(): pl.pallas_call(functools.partial(attend_kernel, heads, units, items), gri...  61.7 us
    ppermute x47, starting transfers between devices, passed(): return lax.ppermute(value, axis, pairs)  54.5 us
    all_to_all x2, blocking collectives, exchanged(): return lax.all_to_all(values, 'blk', 0, 0).reshape(-1, channels)  38.7 us
    dot_general x5, matrix products, dot_t(): return lax.dot_general(left, right, NT, preferred_element_type=F32)  23.3 us
    pallas_call x1, Pallas kernels, merge(): pl.pallas_call(functools.partial(merge_kernel, cycle_size), grid_spec=plt...  20.8 us
    pallas_call x4, Pallas kernels, sort_step(): pl.pallas_call(functools.partial(sort_step_kernel, step), grid_spec=pltpu...  20.1 us
  transfers between devices with their start and end apart: 52, of which 22 were waited for; matrix products, arithmetic and copies ran while one was open for 17% of the time, Pallas kernels for 31%

profile of v4, /device:TPU:0, one launch (start us, length us, event | category | flops | bytes accessed | tf_op | source)
XLA Modules:
  0.0 588.0 jit_solution(9383033998962024215)
XLA Ops:
  9.0 4.7 collective-permute-start.1
  20.1 3.1 compare_select_fusion.3
  24.4 5.3 geometry.1
  29.8 5.4 own_start.1
  36.1 5.1 sort_step.4.refs_27_
  41.7 3.8 collective-permute-start.4
  46.4 5.0 sort_step.5.refs_28_
  51.4 3.5 collective-permute-done.3
  54.9 5.5 collective-permute-done.4
  62.0 3.9 collective-permute-start.9
  65.9 4.0 collective-permute-start.7
  69.9 2.4 collective-permute-done.9
  72.3 3.2 collective-permute-done.10
  75.6 5.0 sort_step.6.refs_29_
  80.6 7.2 %collective-permute-done.7 = bf16[240,768]{1,0:T(8,128)(2,1)} collective-permute-done((bf16[240,768]{1,0:T(8,128)(2,1)S(1)}, bf16[240,768]{1,0:T(8,128)(2,1)}, u32[]{:S(2)}, u32[]{:S(2)}) %collective-permute-start.7) | collective-permute-done | bytes 368672 | tf_op jit(solution)/shard_map/ppermute | solution.py:997
  92.0 5.0 sort_step.7.refs_30_
  97.1 61.7 %attend.1 = (bf16[480,768]{1,0:T(8,128)(2,1)}, f32[704,768]{1,0:T(8,128)}, f32[16,768]{1,0:T(8,128)}, bf16[5120,768]{1,0:T(8,128)(2,1)}, bf16[5120,128]{1,0:T(8,...) custom-call(s32[80]{0:T(128)} %get-tuple-element.123.refs_0_, s32[80]{0:T(128)} %get-tuple-element.124.refs_1_, ...), custom_call_target="tpu_custom_call" | custom-call | flops 70000001024 | bytes 1000000 | tf_op jit(solution)/shard_map/attend/pallas_call | solution.py:855
  158.8 1.9 fusion.67
  161.6 4.9 fusion.51
  166.5 2.6 copy-done.75
  169.0 6.7 %add_convert_fusion.2.block_ref = bf16[480,768]{1,0:T(8,128)(2,1)} fusion(f32[480,768]{1,0:T(8,128)S(1)} %get-tuple-element.288, bf16[3072,768]{1,0:T(8,128)(2,1)} %param.35, f32[480,3072]{1,0:T(8,128)S(1)} %fusion.51), kind=kOutput, calls=%fused_computation.46 | convolution fusion | flops 2278932480 | bytes 12828672 | tf_op jit(solution)/shard_map/dot_general | solution.py:1124
  175.7 3.1 pack.1
  178.8 22.1 %all_to_all.10 = bf16[8,144,256]{2,1,0:T(8,128)(2,1)} all-to-all(bf16[8,144,256]{2,1,0:T(8,128)(2,1)} %bitcast.196), channel_id=1, replica_groups=mesh['dp'=4,'blk'=8] {'blk'}, dimensions={0} | all-to-all | bytes 1179648 | tf_op jit(solution)/shard_map/all_to_all | solution.py:1344
  200.9 20.8 %merge.1 = (bf16[768,256]{1,0:T(8,128)(2,1)}, bf16[576,256]{1,0:T(8,128)(2,1)}, bf16[9472,256]{1,0:T(8,128)(2,1)}) custom-call(s32[24]{0:T(128)} %get-tuple-element.130.refs_15_.wwidth, s32[24]{0:T(128)} %get-tuple-element.131.refs_16_.wup, s32[24]{0:T(128)} %get-tuple-element.132.refs_17_.wdown, s32[24]{0:T(128)} %get-tuple-element.133.refs_18_.wgroup, ...), custom_call_target="tpu_custom_call" | custom-call | flops 24999999488 | bytes 1000000 | tf_op jit(solution)/shard_map/merge/pallas_call | solution.py:811
  221.7 16.6 %all_to_all.11 = bf16[8,96,256]{2,1,0:T(8,128)(2,1)} all-to-all(bf16[8,96,256]{2,1,0:T(8,128)(2,1)} %bitcast.197), channel_id=1, replica_groups=mesh['dp'=4,'blk'=8] {'blk'}, dimensions={0} | all-to-all | bytes 786432 | tf_op jit(solution)/shard_map/all_to_all | solution.py:1344
  238.3 2.5 unpack.3
  240.9 2.5 fusion.68
  243.3 5.9 convolution_convert_fusion.1
  249.2 2.5 copy.42
  251.8 3.4 dynamic-slice_bitcast_fusion
  256.4 11.5 %fusion.3 = bf16[480,3072]{1,0:T(8,128)(2,1)S(1)} fusion(f32[480,3072]{1,0:T(8,128)} %copy-done.75, bf16[480,768]{1,0:T(8,128)(2,1)S(1)} %get-tuple-element.167, bf16[3072,768]{1,0:T(8,128)(2,1)} %param.35), kind=kOutput, calls=%fused_computation.7 | convolution fusion | flops 2300313600 | bytes 14303232 | tf_op jit(solution)/shard_map/dot_general | solution.py:1128
  267.9 4.8 convolution_convert_fusion
  272.7 3.2 dynamic-slice_bitcast_fusion.1
  275.9 3.9 multiply_reduce_fusion
  280.6 2.1 fusion.53
  289.3 2.2 fusion.9
  291.5 3.7 fusion.6
  295.3 5.6 fusion.7
  300.8 8.5 %reduce-scatter.4.cloned.1.call-done = bf16[768,768]{1,0:T(8,128)(2,1)} async-done(((bf16[3072,768]{1,0:T(8,128)(2,1)}), bf16[768,768]{1,0:T(8,128)(2,1)}) %reduce-scatter.4.cloned.1.call-update) | async-done | bytes 1179664 | tf_op jit(solution)/shard_map/reduce_scatter | solution.py:1379
  311.4 2.5 constant_dynamic-slice_fusion.12
  317.0 94.1 %attend_back.1 = (bf16[480,768]{1,0:T(8,128)(2,1)}, bf16[768,768]{1,0:T(8,128)(2,1)}, bf16[768,768]{1,0:T(8,128)(2,1)}, bf16[3840,768]{1,0:T(8,128)(2,1)}) custom-call(s32[1]{0:T(128)} %bitcast.1.place.me, s32[80]{0:T(128)} %get-tuple-element.123.refs_0_, s32[80]{0:T(128)} %get-tuple-element.124.refs_1_, s32[80]{0:T(128)} %get-tuple-element.125.refs_2_, ...), custom_call_target="tpu_custom_call" | custom-call | flops 89999998976 | bytes 1000000 | tf_op jit(solution)/shard_map/attend_back/pallas_call | solution.py:912
  413.2 3.2 unpack.2
  419.9 7.8 %collective-permute-start.20 = (bf16[1,1,48,768]{3,2,1,0:T(8,128)(2,1)S(1)}, bf16[1,1,48,768]{3,2,1,0:T(8,128)(2,1)S(1)}, u32[]{:S(2)}, u32[]{:S(2)}) collective-permute-start(bf16[1,1,48,768]{3,2,1,0:T(8,128)(2,1)S(1)} %get-tuple-element.262), channel_id=1, source_target_pairs={{0,16},{8,24},{16,0},{24,8},{1,17},{9,25},{17,1},{25,9},{2,18},{10... | collective-permute-start | bytes 221192 | tf_op jit(solution)/shard_map/ppermute | solution.py:997
  439.0 1.9 collective-permute-start.22
  445.5 3.1 collective-permute-done.21
  449.8 8.7 %collective-permute-done.19 = bf16[1,2,48,768]{3,2,1,0:T(8,128)(2,1)} collective-permute-done((bf16[1,2,48,768]{3,2,1,0:T(8,128)(2,1)}, bf16[1,2,48,768]{3,2,1,0:T(8,128)(2,1)}, u32[]{:S(2)}, u32[]{:S(2)}) %collective-permute-start.19) | collective-permute-done | bytes 147488 | tf_op jit(solution)/shard_map/ppermute | solution.py:997
  460.6 2.0 add_convert_fusion.6
  463.8 2.0 reshape.943
  465.9 1.8 collective-permute-start.32
  467.8 2.0 fusion.8
  472.5 2.0 collective-permute-done.32
  476.0 9.8 %collective-permute-done.29 = bf16[4,96,768]{2,1,0:T(8,128)(2,1)S(1)} collective-permute-done((bf16[4,96,768]{2,1,0:T(8,128)(2,1)S(1)}, bf16[4,96,768]{2,1,0:T(8,128)(2,1)S(1)}, u32[]{:S(2)}, u32[]{:S(2)}) %collective-permute-start.29) | collective-permute-done | bytes 589856 | tf_op jit(solution)/shard_map/ppermute | solution.py:997
  492.5 2.1 collective-permute-done.30
  494.5 1.8 add_convert_fusion.9
  496.4 1.8 reshape.945
  502.5 11.4 %collective-permute-done.34 = bf16[448,256]{1,0:T(8,128)(2,1)S(1)} collective-permute-done((bf16[448,256]{1,0:T(8,128)(2,1)S(1)}, bf16[448,256]{1,0:T(8,128)(2,1)S(1)}, u32[]{:S(2)}, u32[]{:S(2)}) %collective-permute-start.34) | collective-permute-done | bytes 229408 | tf_op jit(solution)/shard_map/ppermute | solution.py:997
  514.1 2.1 collective-permute-start.26
  516.2 7.7 %collective-permute-done.35 = bf16[448,256]{1,0:T(8,128)(2,1)S(1)} collective-permute-done((bf16[448,256]{1,0:T(8,128)(2,1)S(1)}, bf16[448,256]{1,0:T(8,128)(2,1)S(1)}, u32[]{:S(2)}, u32[]{:S(2)}) %collective-permute-start.35) | collective-permute-done | bytes 229408 | tf_op jit(solution)/shard_map/ppermute | solution.py:997
  524.7 5.2 collective-permute-done.36
  530.7 3.8 multiply_reduce_fusion.1
  534.6 3.1 fusion.52
  552.3 3.0 collective-permute-start.42
  556.7 3.2 collective-permute-done.41
  562.9 6.3 %collective-permute-done.44 = bf16[2,1,448,256]{3,2,1,0:T(8,128)(2,1)S(1)} collective-permute-done((bf16[2,1,448,256]{3,2,1,0:T(8,128)(2,1)S(1)}, bf16[2,1,448,256]{3,2,1,0:T(8,128)(2,1)S(1)}, u32[]{:S(2)}, u32[]{:S(2)}) %collective-permute-start.44) | collective-permute-done | bytes 458784 | tf_op jit(solution)/shard_map/ppermute | solution.py:997
  (390 shorter events, 99.8 us)
Async XLA Ops:
  7.2 151.6 %copy-start = (bf16[768,768]{1,0:T(8,128)(2,1)S(1)}, bf16[768,768]{1,0:T(8,128)(2,1)}, u32[]{:S(2)}) copy-start(bf16[768,768]{1,0:T(8,128)(2,1)} %param.31) | copy-start | bytes 3538948
  7.2 16.0 %copy-start.67 = (f32[768]{0:T(1024)S(1)}, f32[768]{0:T(1024)}, u32[]{:S(2)}) copy-start(f32[768]{0:T(1024)} %param.27) | copy-start | bytes 9220
  7.2 16.6 %copy-start.60 = (f32[768]{0:T(1024)S(1)}, f32[768]{0:T(1024)}, u32[]{:S(2)}) copy-start(f32[768]{0:T(1024)} %param.26) | copy-start | bytes 9220
  7.3 151.6 %all-gather.3.cloned.1.call-start = ((), (), s32[]{:S(2)}) async-start(), calls=%async_computation.5 | async-start | bytes 2654208 | tf_op jit(solution)/shard_map/all_gather | solution.py:1326
  7.3 27.9 %collective-permute-start.2 = (bf16[480,768]{1,0:T(8,128)(2,1)}, bf16[480,768]{1,0:T(8,128)(2,1)S(1)}, u32[]{:S(2)}, u32[]{:S(2)}) collective-permute-start(bf16[480,768]{1,0:T(8,128)(2,1)} %refs_0_.2), channel_id=1, source_target_pairs={{0,1},{1,0},{2,3},{3,2},{4,5},{5,4},{6,7},{7,6},{8,9},{9,8},{10,11... | collective-permute-start | bytes 2211848 | tf_op jit(solution)/shard_map/ppermute | solution.py:997
  9.0 32.2 %collective-permute-start.1 = (bf16[240,768]{1,0:T(8,128)(2,1)S(1)}, bf16[240,768]{1,0:T(8,128)(2,1)S(1)}, u32[]{:S(2)}, u32[]{:S(2)}) collective-permute-start(bf16[240,768]{1,0:T(8,128)(2,1)S(1)} %get-tuple-element.247), channel_id=1, source_target_pairs={{0,6},{1,7},{2,0},{3,1},{4,2},{5,3},{6,4},{7,5},{8,14},{9,15},{10,... | collective-permute-start | bytes 1105928 | tf_op jit(solution)/shard_map/ppermute | solution.py:997
  13.6 27.5 %collective-permute-start = (bf16[240,768]{1,0:T(8,128)(2,1)S(1)}, bf16[240,768]{1,0:T(8,128)(2,1)S(1)}, u32[]{:S(2)}, u32[]{:S(2)}) collective-permute-start(bf16[240,768]{1,0:T(8,128)(2,1)S(1)} %get-tuple-element.248), channel_id=1, source_target_pairs={{0,2},{1,3},{2,4},{3,5},{4,6},{5,7},{6,0},{7,1},{8,10},{9,11},{10,... | collective-permute-start | bytes 1105928 | tf_op jit(solution)/shard_map/ppermute | solution.py:997
  23.2 18.3 %copy-start.64 = (s32[12]{0:T(128)}, s32[12]{0:T(128)S(1)}, u32[]{:S(2)}) copy-start(s32[12]{0:T(128)S(1)} %select_select_fusion.1) | copy-start | bytes 148
  41.2 5.2 collective-permute-start.5
  41.6 47.3 %copy-start.52 = (pred[12,40]{1,0:T(8,128)(4,1)}, pred[12,40]{1,0:T(8,128)(4,1)S(1)}, u32[]{:S(2)}) copy-start(pred[12,40]{1,0:T(8,128)(4,1)S(1)} %get-tuple-element.275) | copy-start | bytes 1444
  41.6 47.3 %copy-start.54 = (pred[12,40]{1,0:T(8,128)(4,1)}, pred[12,40]{1,0:T(8,128)(4,1)S(1)}, u32[]{:S(2)}) copy-start(pred[12,40]{1,0:T(8,128)(4,1)S(1)} %get-tuple-element.276) | copy-start | bytes 1444
  41.6 13.3 %collective-permute-start.3 = (bf16[240,768]{1,0:T(8,128)(2,1)S(1)}, bf16[240,768]{1,0:T(8,128)(2,1)S(1)}, u32[]{:S(2)}, u32[]{:S(2)}) collective-permute-start(bf16[240,768]{1,0:T(8,128)(2,1)S(1)} %collective-permute-done), channel_id=1, source_target_pairs={{0,2},{1,3},{2,4},{3,5},{4,6},{5,7},{6,0},{7,1},{8,10},{9,11},{10,... | collective-permute-start | bytes 1105928 | tf_op jit(solution)/shard_map/ppermute | solution.py:997
  41.7 18.7 %collective-permute-start.4 = (bf16[240,768]{1,0:T(8,128)(2,1)S(1)}, bf16[240,768]{1,0:T(8,128)(2,1)S(1)}, u32[]{:S(2)}, u32[]{:S(2)}) collective-permute-start(bf16[240,768]{1,0:T(8,128)(2,1)S(1)} %collective-permute-done.1), channel_id=1, source_target_pairs={{0,6},{1,7},{2,0},{3,1},{4,2},{5,3},{6,4},{7,5},{8,14},{9,15},{10,... | collective-permute-start | bytes 1105928 | tf_op jit(solution)/shard_map/ppermute | solution.py:997
  62.0 13.6 %collective-permute-start.8 = (bf16[480,768]{1,0:T(8,128)(2,1)}, bf16[480,768]{1,0:T(8,128)(2,1)}, u32[]{:S(2)}, u32[]{:S(2)}) collective-permute-start(bf16[480,768]{1,0:T(8,128)(2,1)} %constant_dynamic-update-slice_fusion.2.refs_0_), channel_id=1, source_target_pairs={{0,1},{1,0},{2,3},{3,2},{4,5},{5,4},{6,7},{7,6},{8,9},{9,8},{10,11... | collective-permute-start | bytes 2211848 | tf_op jit(solution)/shard_map/ppermute | solution.py:997
  62.0 10.3 %collective-permute-start.9 = (bf16[12,40,256]{2,1,0:T(8,128)(2,1)S(1)}, bf16[12,40,256]{2,1,0:T(8,128)(2,1)S(1)}, u32[]{:S(2)}, u32[]{:S(2)}) collective-permute-start(bf16[12,40,256]{2,1,0:T(8,128)(2,1)S(1)} %get-tuple-element.154), channel_id=1, source_target_pairs={{0,7},{1,0},{2,1},{3,2},{4,3},{5,4},{6,5},{7,6},{8,15},{9,8},{10,9... | collective-permute-start | bytes 737288 | tf_op jit(solution)/shard_map/ppermute | solution.py:997
  65.8 9.7 %collective-permute-start.10 = (bf16[12,40,256]{2,1,0:T(8,128)(2,1)S(1)}, bf16[12,40,256]{2,1,0:T(8,128)(2,1)S(1)}, u32[]{:S(2)}, u32[]{:S(2)}) collective-permute-start(bf16[12,40,256]{2,1,0:T(8,128)(2,1)S(1)} %get-tuple-element.155), channel_id=1, source_target_pairs={{0,1},{1,2},{2,3},{3,4},{4,5},{5,6},{6,7},{7,0},{8,9},{9,10},{10,1... | collective-permute-start | bytes 737288 | tf_op jit(solution)/shard_map/ppermute | solution.py:997
  65.9 14.8 %collective-permute-start.6 = (bf16[240,768]{1,0:T(8,128)(2,1)S(1)}, bf16[240,768]{1,0:T(8,128)(2,1)S(1)}, u32[]{:S(2)}, u32[]{:S(2)}) collective-permute-start(bf16[240,768]{1,0:T(8,128)(2,1)S(1)} %collective-permute-done.3), channel_id=1, source_target_pairs={{0,2},{1,3},{2,4},{3,5},{4,6},{5,7},{6,0},{7,1},{8,10},{9,11},{10,... | collective-permute-start | bytes 1105928 | tf_op jit(solution)/shard_map/ppermute | solution.py:997
  65.9 22.0 %collective-permute-start.7 = (bf16[240,768]{1,0:T(8,128)(2,1)S(1)}, bf16[240,768]{1,0:T(8,128)(2,1)}, u32[]{:S(2)}, u32[]{:S(2)}) collective-permute-start(bf16[240,768]{1,0:T(8,128)(2,1)S(1)} %collective-permute-done.4), channel_id=1, source_target_pairs={{0,6},{1,7},{2,0},{3,1},{4,2},{5,3},{6,4},{7,5},{8,14},{9,15},{10,... | collective-permute-start | bytes 1105928 | tf_op jit(solution)/shard_map/ppermute | solution.py:997
  88.9 2.3 collective-permute-start.11
  97.1 212.2 %reduce-scatter.4.cloned.1.call-start = ((), (), s32[]{:S(2)}) async-start(), calls=%async_computation.7 | async-start | bytes 5898240 | tf_op jit(solution)/shard_map/reduce_scatter | solution.py:1379
  97.1 61.7 %copy-start.2 = (f32[480,768]{1,0:T(8,128)S(1)}, f32[480,768]{1,0:T(8,128)}, u32[]{:S(2)}) copy-start(f32[480,768]{1,0:T(8,128)} %get-tuple-element.122) | copy-start | bytes 4423684
  251.7 159.4 %reduce-scatter.6.cloned.1.call-start = ((), (), s32[]{:S(2)}) async-start(), calls=%async_computation.8 | async-start | bytes 1327104 | tf_op jit(solution)/shard_map/reduce_scatter | solution.py:1414
  251.8 24.1 %slice-start = ((s8[4718592]{0:T(1024)(128)(4,1)}), s8[4194304]{0:T(1024)(128)(4,1)S(1)}, s32[]{:S(2)}) async-start(s8[4718592]{0:T(1024)(128)(4,1)} %bitcast.210), calls=%async_computation.10 | async-start | bytes 8388608
  255.2 36.3 %collective-permute-start.12 = (bf16[4,1184,256]{2,1,0:T(8,128)(2,1)}, bf16[4,1184,256]{2,1,0:T(8,128)(2,1)}, u32[]{:S(2)}, u32[]{:S(2)}) collective-permute-start(bf16[4,1184,256]{2,1,0:T(8,128)(2,1)} %dynamic-slice_bitcast_fusion), channel_id=1, source_target_pairs={{0,1},{1,0},{2,3},{3,2},{4,5},{5,4},{6,7},{7,6},{8,9},{9,8},{10,11... | collective-permute-start | bytes 7274504 | tf_op jit(solution)/shard_map/ppermute | solution.py:997
  256.4 19.5 %slice-start.1 = ((s8[4718592]{0:T(1024)(128)(4,1)}), s8[524288]{0:T(1024)(128)(4,1)S(1)}, s32[]{:S(2)}) async-start(s8[4718592]{0:T(1024)(128)(4,1)} %bitcast.210), calls=%async_computation.11 | async-start | bytes 1048576
  280.0 15.3 %collective-permute-start.13 = (bf16[4,96,3072]{2,1,0:T(8,128)(2,1)}, bf16[4,96,3072]{2,1,0:T(8,128)(2,1)}, u32[]{:S(2)}, u32[]{:S(2)}) collective-permute-start(bf16[4,96,3072]{2,1,0:T(8,128)(2,1)} %dynamic-slice_bitcast_fusion.1), channel_id=1, source_target_pairs={{0,1},{1,0},{2,3},{3,2},{4,5},{5,4},{6,7},{7,6},{8,9},{9,8},{10,11... | collective-permute-start | bytes 7077896 | tf_op jit(solution)/shard_map/ppermute | solution.py:997
  286.6 2.6 collective-permute-start.14
  295.2 19.3 %copy-start.10 = (bf16[4,1184,256]{2,1,0:T(8,128)(2,1)}, bf16[4,1184,256]{2,1,0:T(8,128)(2,1)S(1)}, u32[]{:S(2)}) copy-start(bf16[4,1184,256]{2,1,0:T(8,128)(2,1)S(1)} %fusion.6) | copy-start | bytes 7274500
  309.3 103.9 %all-gather.5.cloned.1.call-start = ((), (), s32[]{:S(2)}) async-start(), calls=%async_computation.6 | async-start | bytes 2654208 | tf_op jit(solution)/shard_map/all_gather | solution.py:1355
  309.9 220.9 %reduce-scatter.8.cloned.1.call-start = ((), (), s32[]{:S(2)}) async-start(), calls=%async_computation.9 | async-start | bytes 6635520 | tf_op jit(solution)/shard_map/reduce_scatter | solution.py:1422
  310.0 101.1 %collective-permute-start.17 = (bf16[4,64,768]{2,1,0:T(8,128)(2,1)S(1)}, bf16[4,64,768]{2,1,0:T(8,128)(2,1)S(1)}, u32[]{:S(2)}, u32[]{:S(2)}) collective-permute-start(bf16[4,64,768]{2,1,0:T(8,128)(2,1)S(1)} %constant_dynamic-slice_fusion.11), channel_id=1, source_target_pairs={{0,8},{8,0},{16,24},{24,16},{1,9},{9,1},{17,25},{25,17},{2,10},{10... | collective-permute-start | bytes 1179656 | tf_op jit(solution)/shard_map/ppermute | solution.py:997
  313.9 97.2 %collective-permute-start.16 = (bf16[4,48,3072]{2,1,0:T(8,128)(2,1)}, bf16[4,48,3072]{2,1,0:T(8,128)(2,1)}, u32[]{:S(2)}, u32[]{:S(2)}) collective-permute-start(bf16[4,48,3072]{2,1,0:T(8,128)(2,1)} %constant_dynamic-slice_fusion.12), channel_id=1, source_target_pairs={{0,16},{8,24},{16,0},{24,8},{1,17},{9,25},{17,1},{25,9},{2,18},{10... | collective-permute-start | bytes 3538952 | tf_op jit(solution)/shard_map/ppermute | solution.py:997
  315.6 95.5 %collective-permute-start.15 = (bf16[4,592,256]{2,1,0:T(8,128)(2,1)}, bf16[4,592,256]{2,1,0:T(8,128)(2,1)}, u32[]{:S(2)}, u32[]{:S(2)}) collective-permute-start(bf16[4,592,256]{2,1,0:T(8,128)(2,1)} %constant_dynamic-slice_fusion.13), channel_id=1, source_target_pairs={{0,8},{8,0},{16,24},{24,16},{1,9},{9,1},{17,25},{25,17},{2,10},{10... | collective-permute-start | bytes 3637256 | tf_op jit(solution)/shard_map/ppermute | solution.py:997
  419.8 21.8 %collective-permute-start.18 = (bf16[1,1,48,768]{3,2,1,0:T(8,128)(2,1)S(1)}, bf16[1,1,48,768]{3,2,1,0:T(8,128)(2,1)S(1)}, u32[]{:S(2)}, u32[]{:S(2)}) collective-permute-start(bf16[1,1,48,768]{3,2,1,0:T(8,128)(2,1)S(1)} %get-tuple-element.261), channel_id=1, source_target_pairs={{0,8},{8,0},{16,24},{24,16},{1,9},{9,1},{17,25},{25,17},{2,10},{10... | collective-permute-start | bytes 221192 | tf_op jit(solution)/shard_map/ppermute | solution.py:997
  419.9 19.1 %collective-permute-start.20 = (bf16[1,1,48,768]{3,2,1,0:T(8,128)(2,1)S(1)}, bf16[1,1,48,768]{3,2,1,0:T(8,128)(2,1)S(1)}, u32[]{:S(2)}, u32[]{:S(2)}) collective-permute-start(bf16[1,1,48,768]{3,2,1,0:T(8,128)(2,1)S(1)} %get-tuple-element.262), channel_id=1, source_target_pairs={{0,16},{8,24},{16,0},{24,8},{1,17},{9,25},{17,1},{25,9},{2,18},{10... | collective-permute-start | bytes 221192 | tf_op jit(solution)/shard_map/ppermute | solution.py:997
  427.8 15.8 %collective-permute-start.27 = (bf16[4,32,768]{2,1,0:T(8,128)(2,1)S(1)}, bf16[4,32,768]{2,1,0:T(8,128)(2,1)S(1)}, u32[]{:S(2)}, u32[]{:S(2)}) collective-permute-start(bf16[4,32,768]{2,1,0:T(8,128)(2,1)S(1)} %constant_dynamic-slice_fusion.8), channel_id=1, source_target_pairs={{0,16},{8,24},{16,0},{24,8},{1,17},{9,25},{17,1},{25,9},{2,18},{10... | collective-permute-start | bytes 589832 | tf_op jit(solution)/shard_map/ppermute | solution.py:997
  431.6 28.9 %collective-permute-start.23 = (bf16[4,24,3072]{2,1,0:T(8,128)(2,1)}, bf16[4,24,3072]{2,1,0:T(8,128)(2,1)}, u32[]{:S(2)}, u32[]{:S(2)}) collective-permute-start(bf16[4,24,3072]{2,1,0:T(8,128)(2,1)} %constant_dynamic-slice_fusion.9), channel_id=1, source_target_pairs={{0,8},{8,0},{16,24},{24,16},{1,9},{9,1},{17,25},{25,17},{2,10},{10... | collective-permute-start | bytes 1769480 | tf_op jit(solution)/shard_map/ppermute | solution.py:997
  434.0 28.6 %collective-permute-start.31 = (bf16[4,96,768]{2,1,0:T(8,128)(2,1)}, bf16[4,96,768]{2,1,0:T(8,128)(2,1)}, u32[]{:S(2)}, u32[]{:S(2)}) collective-permute-start(bf16[4,96,768]{2,1,0:T(8,128)(2,1)} %dynamic-slice_bitcast_fusion.2), channel_id=1, source_target_pairs={{0,1},{1,0},{2,3},{3,2},{4,5},{5,4},{6,7},{7,6},{8,9},{9,8},{10,11... | collective-permute-start | bytes 1769480 | tf_op jit(solution)/shard_map/ppermute | solution.py:997
  439.0 32.2 %collective-permute-start.22 = (bf16[4,296,256]{2,1,0:T(8,128)(2,1)}, bf16[4,296,256]{2,1,0:T(8,128)(2,1)}, u32[]{:S(2)}, u32[]{:S(2)}) collective-permute-start(bf16[4,296,256]{2,1,0:T(8,128)(2,1)} %constant_dynamic-slice_fusion.10), channel_id=1, source_target_pairs={{0,16},{8,24},{16,0},{24,8},{1,17},{9,25},{17,1},{25,9},{2,18},{10... | collective-permute-start | bytes 1818632 | tf_op jit(solution)/shard_map/ppermute | solution.py:997
  441.6 7.0 %collective-permute-start.21 = (bf16[2,1,48,768]{3,2,1,0:T(8,128)(2,1)}, bf16[2,1,48,768]{3,2,1,0:T(8,128)(2,1)}, u32[]{:S(2)}, u32[]{:S(2)}) collective-permute-start(bf16[2,1,48,768]{3,2,1,0:T(8,128)(2,1)} %maximum_select_fusion.7), channel_id=1, source_target_pairs={{0,8},{8,0},{16,24},{24,16},{1,9},{9,1},{17,25},{25,17},{2,10},{10... | collective-permute-start | bytes 442376 | tf_op jit(solution)/shard_map/ppermute | solution.py:997
  443.6 14.9 %collective-permute-start.19 = (bf16[1,2,48,768]{3,2,1,0:T(8,128)(2,1)}, bf16[1,2,48,768]{3,2,1,0:T(8,128)(2,1)}, u32[]{:S(2)}, u32[]{:S(2)}) collective-permute-start(bf16[1,2,48,768]{3,2,1,0:T(8,128)(2,1)} %maximum_select_fusion.6), channel_id=1, source_target_pairs={{0,16},{8,24},{16,0},{24,8},{1,17},{9,25},{17,1},{25,9},{2,18},{10... | collective-permute-start | bytes 442376 | tf_op jit(solution)/shard_map/ppermute | solution.py:997
  445.5 15.1 %copy-start.21 = (bf16[4,48,3072]{2,1,0:T(8,128)(2,1)S(1)}, bf16[4,48,3072]{2,1,0:T(8,128)(2,1)}, u32[]{:S(2)}) copy-start(bf16[4,48,3072]{2,1,0:T(8,128)(2,1)} %copy-done.20) | copy-start | bytes 3538948
  448.6 19.1 %collective-permute-start.28 = (bf16[4,192,768]{2,1,0:T(8,128)(2,1)}, bf16[4,192,768]{2,1,0:T(8,128)(2,1)}, u32[]{:S(2)}, u32[]{:S(2)}) collective-permute-start(bf16[4,192,768]{2,1,0:T(8,128)(2,1)} %fusion.11), channel_id=1, source_target_pairs={{0,1},{1,0},{2,3},{3,2},{4,5},{5,4},{6,7},{7,6},{8,9},{9,8},{10,11... | collective-permute-start | bytes 3538952 | tf_op jit(solution)/shard_map/ppermute | solution.py:997
  465.9 8.6 %collective-permute-start.32 = (bf16[4,48,768]{2,1,0:T(8,128)(2,1)S(1)}, bf16[4,48,768]{2,1,0:T(8,128)(2,1)S(1)}, u32[]{:S(2)}, u32[]{:S(2)}) collective-permute-start(bf16[4,48,768]{2,1,0:T(8,128)(2,1)S(1)} %constant_dynamic-slice_fusion.5), channel_id=1, source_target_pairs={{0,16},{8,24},{16,0},{24,8},{1,17},{9,25},{17,1},{25,9},{2,18},{10... | collective-permute-start | bytes 884744 | tf_op jit(solution)/shard_map/ppermute | solution.py:997
  469.8 16.0 %collective-permute-start.29 = (bf16[4,96,768]{2,1,0:T(8,128)(2,1)S(1)}, bf16[4,96,768]{2,1,0:T(8,128)(2,1)S(1)}, u32[]{:S(2)}, u32[]{:S(2)}) collective-permute-start(bf16[4,96,768]{2,1,0:T(8,128)(2,1)S(1)} %constant_dynamic-slice_fusion.7), channel_id=1, source_target_pairs={{0,8},{8,0},{16,24},{24,16},{1,9},{9,1},{17,25},{25,17},{2,10},{10... | collective-permute-start | bytes 1769480 | tf_op jit(solution)/shard_map/ppermute | solution.py:997
  474.6 15.5 %collective-permute-start.33 = (bf16[4,24,768]{2,1,0:T(8,128)(2,1)S(1)}, bf16[4,24,768]{2,1,0:T(8,128)(2,1)S(1)}, u32[]{:S(2)}, u32[]{:S(2)}) collective-permute-start(bf16[4,24,768]{2,1,0:T(8,128)(2,1)S(1)} %constant_dynamic-slice_fusion.4), channel_id=1, source_target_pairs={{0,8},{8,0},{16,24},{24,16},{1,9},{9,1},{17,25},{25,17},{2,10},{10... | collective-permute-start | bytes 442376 | tf_op jit(solution)/shard_map/ppermute | solution.py:997
  487.5 7.0 %collective-permute-start.30 = (bf16[4,48,768]{2,1,0:T(8,128)(2,1)}, bf16[4,48,768]{2,1,0:T(8,128)(2,1)}, u32[]{:S(2)}, u32[]{:S(2)}) collective-permute-start(bf16[4,48,768]{2,1,0:T(8,128)(2,1)} %constant_dynamic-slice_fusion.6), channel_id=1, source_target_pairs={{0,16},{8,24},{16,0},{24,8},{1,17},{9,25},{17,1},{25,9},{2,18},{10... | collective-permute-start | bytes 884744 | tf_op jit(solution)/shard_map/ppermute | solution.py:997
  488.7 11.0 %collective-permute-start.24 = (bf16[448,256]{1,0:T(8,128)(2,1)}, bf16[448,256]{1,0:T(8,128)(2,1)}, u32[]{:S(2)}, u32[]{:S(2)}) collective-permute-start(bf16[448,256]{1,0:T(8,128)(2,1)} %fusion.30), channel_id=1, source_target_pairs={{0,2},{1,3},{2,4},{3,5},{4,6},{5,7},{6,0},{7,1},{8,10},{9,11},{10,... | collective-permute-start | bytes 688136 | tf_op jit(solution)/shard_map/ppermute | solution.py:997
  499.3 14.6 %collective-permute-start.34 = (bf16[448,256]{1,0:T(8,128)(2,1)S(1)}, bf16[448,256]{1,0:T(8,128)(2,1)S(1)}, u32[]{:S(2)}, u32[]{:S(2)}) collective-permute-start(bf16[448,256]{1,0:T(8,128)(2,1)S(1)} %dynamic-slice_bitcast_fusion.3), channel_id=1, source_target_pairs={{0,6},{1,7},{2,0},{3,1},{4,2},{5,3},{6,4},{7,5},{8,14},{9,15},{10,... | collective-permute-start | bytes 688136 | tf_op jit(solution)/shard_map/ppermute | solution.py:997
  500.7 13.3 %collective-permute-start.25 = (bf16[448,256]{1,0:T(8,128)(2,1)S(1)}, bf16[448,256]{1,0:T(8,128)(2,1)S(1)}, u32[]{:S(2)}, u32[]{:S(2)}) collective-permute-start(bf16[448,256]{1,0:T(8,128)(2,1)S(1)} %fusion.24), channel_id=1, source_target_pairs={{0,2},{1,3},{2,4},{3,5},{4,6},{5,7},{6,0},{7,1},{8,10},{9,11},{10,... | collective-permute-start | bytes 688136 | tf_op jit(solution)/shard_map/ppermute | solution.py:997
  514.0 9.9 %collective-permute-start.35 = (bf16[448,256]{1,0:T(8,128)(2,1)S(1)}, bf16[448,256]{1,0:T(8,128)(2,1)S(1)}, u32[]{:S(2)}, u32[]{:S(2)}) collective-permute-start(bf16[448,256]{1,0:T(8,128)(2,1)S(1)} %fusion.21), channel_id=1, source_target_pairs={{0,6},{1,7},{2,0},{3,1},{4,2},{5,3},{6,4},{7,5},{8,14},{9,15},{10,... | collective-permute-start | bytes 688136 | tf_op jit(solution)/shard_map/ppermute | solution.py:997
  514.1 16.6 %copy-start.61 = (f32[768]{0:T(1024)S(1)}, f32[768]{0:T(1024)}, u32[]{:S(2)}) copy-start(f32[768]{0:T(1024)} %param.26) | copy-start | bytes 9220
  514.1 9.8 %collective-permute-start.26 = (bf16[448,256]{1,0:T(8,128)(2,1)S(1)}, bf16[448,256]{1,0:T(8,128)(2,1)S(1)}, u32[]{:S(2)}, u32[]{:S(2)}) collective-permute-start(bf16[448,256]{1,0:T(8,128)(2,1)S(1)} %fusion.23), channel_id=1, source_target_pairs={{0,2},{1,3},{2,4},{3,5},{4,6},{5,7},{6,0},{7,1},{8,10},{9,11},{10,... | collective-permute-start | bytes 688136 | tf_op jit(solution)/shard_map/ppermute | solution.py:997
  523.9 6.1 %collective-permute-start.36 = (bf16[448,256]{1,0:T(8,128)(2,1)S(1)}, bf16[448,256]{1,0:T(8,128)(2,1)S(1)}, u32[]{:S(2)}, u32[]{:S(2)}) collective-permute-start(bf16[448,256]{1,0:T(8,128)(2,1)S(1)} %fusion.20), channel_id=1, source_target_pairs={{0,6},{1,7},{2,0},{3,1},{4,2},{5,3},{6,4},{7,5},{8,14},{9,15},{10,... | collective-permute-start | bytes 688136 | tf_op jit(solution)/shard_map/ppermute | solution.py:997
  541.5 1.2 collective-permute-start.37
  542.7 3.8 collective-permute-start.38
  546.6 4.6 collective-permute-start.39
  548.0 11.8 %collective-permute-start.43 = (bf16[1,1,448,256]{3,2,1,0:T(8,128)(2,1)S(1)}, bf16[1,1,448,256]{3,2,1,0:T(8,128)(2,1)S(1)}, u32[]{:S(2)}, u32[]{:S(2)}) collective-permute-start(bf16[1,1,448,256]{3,2,1,0:T(8,128)(2,1)S(1)} %bitcast.193), channel_id=1, source_target_pairs={{0,16},{8,24},{16,0},{24,8},{1,17},{9,25},{17,1},{25,9},{2,18},{10... | collective-permute-start | bytes 688136 | tf_op jit(solution)/shard_map/ppermute | solution.py:997
  549.7 12.8 %collective-permute-start.45 = (bf16[1,1,448,256]{3,2,1,0:T(8,128)(2,1)S(1)}, bf16[1,1,448,256]{3,2,1,0:T(8,128)(2,1)S(1)}, u32[]{:S(2)}, u32[]{:S(2)}) collective-permute-start(bf16[1,1,448,256]{3,2,1,0:T(8,128)(2,1)S(1)} %bitcast.191), channel_id=1, source_target_pairs={{0,8},{8,0},{16,24},{24,16},{1,9},{9,1},{17,25},{25,17},{2,10},{10... | collective-permute-start | bytes 688136 | tf_op jit(solution)/shard_map/ppermute | solution.py:997
  551.2 5.5 collective-permute-start.40
  552.3 4.4 collective-permute-start.42
  555.3 4.5 collective-permute-start.41
  559.9 9.2 %collective-permute-start.44 = (bf16[2,1,448,256]{3,2,1,0:T(8,128)(2,1)S(1)}, bf16[2,1,448,256]{3,2,1,0:T(8,128)(2,1)S(1)}, u32[]{:S(2)}, u32[]{:S(2)}) collective-permute-start(bf16[2,1,448,256]{3,2,1,0:T(8,128)(2,1)S(1)} %maximum_select_fusion.2), channel_id=1, source_target_pairs={{0,8},{8,0},{16,24},{24,16},{1,9},{9,1},{17,25},{25,17},{2,10},{10... | collective-permute-start | bytes 1376264 | tf_op jit(solution)/shard_map/ppermute | solution.py:997
  562.6 8.8 %collective-permute-start.46 = (bf16[1,2,448,256]{3,2,1,0:T(8,128)(2,1)S(1)}, bf16[1,2,448,256]{3,2,1,0:T(8,128)(2,1)S(1)}, u32[]{:S(2)}, u32[]{:S(2)}) collective-permute-start(bf16[1,2,448,256]{3,2,1,0:T(8,128)(2,1)S(1)} %maximum_select_fusion.3), channel_id=1, source_target_pairs={{0,16},{8,24},{16,0},{24,8},{1,17},{9,25},{17,1},{25,9},{2,18},{10... | collective-permute-start | bytes 1376264 | tf_op jit(solution)/shard_map/ppermute | solution.py:997
  (66 other events, 224.5 us)
Sparse Core Ops, SparseCore 0:
  97.2 32.1 all-gather.2
  251.9 57.3 reduce-scatter.3
  311.6 32.9 reduce-scatter.5
  346.7 29.4 all-gather.4
  411.3 69.8 reduce-scatter.7

commit v5 on v4

--- a/solution.py
+++ b/solution.py
@@ -260,6 +260,21 @@
     return place
 
 
+def unsorter(base, spare, width, first, slots, rows):
+    token = lax.broadcasted_iota(jnp.int32, (slots * ROWW, 1), 0)
+    place = jnp.zeros_like(token)
+    for slot in range(slots):
+        column = token - slot * ROWW
+        here = jnp.where(column < width[first + slot], base[first + slot], spare[first + slot])
+        place = jnp.where((column >= 0) & (column < ROWW), here + column, place)
+    spot = lax.broadcasted_iota(jnp.int32, (slots * ROWW, rows), 1)
+    return jnp.where(spot == place, 1.0, 0.0).astype(BF16)
+
+
+def query_unsorter(tab, rows):
+    return unsorter(tab.qbase, tab.qspare, tab.qwidth, 0, SLOTS, rows)
+
+
 def sorter(place, rows):
     spot = lax.broadcasted_iota(jnp.int32, (rows, place.shape[1]), 0)
     return jnp.where(spot == place, 1.0, 0.0).astype(BF16)
@@ -393,7 +408,7 @@
 
     @pl.when(pl.program_id(0) == 0)
     def _():
-        matrix[...] = query_sorter(tab, o_ref.shape[0])
+        matrix[...] = query_unsorter(tab, o_ref.shape[0])
 
         def one_item(item, size, blocks):
             def one_unit(turn, unit, none):
@@ -489,8 +504,8 @@
         query_blocks(qfirst[item], qcount[item], TOGETHER, some_queries)
 
     for_items(items, klen, one_item)
-    att_ref[...] = lax.dot_general(
-        matrix[...], o_ref[...].astype(BF16), FLIP, preferred_element_type=F32
+    att_ref[...] = jnp.dot(
+        matrix[...], o_ref[...].astype(BF16), preferred_element_type=F32
     ).astype(BF16)
 
 
@@ -501,7 +516,7 @@
     dq_ref, gk_ref, gv_ref, dn_ref = refs[10:14]
     (
         spread_q, spread_do, delta, dq_acc, dk_acc, dv_acc, gk_acc, gv_acc, dn_acc,
-        matrix, do_ref, dqs, unit_rows,
+        matrix, back_matrix, do_ref, dqs, unit_rows,
     ) = refs[14:]
     feats = heads * HEAD
     cols = heads * QROWS
@@ -515,6 +530,7 @@
     def _():
         dn_acc[...] = jnp.zeros_like(dn_acc)
         matrix[...] = query_sorter(tab, q_ref.shape[0])
+        back_matrix[...] = query_unsorter(tab, q_ref.shape[0])
 
     do_ref[...] = jnp.dot(matrix[...], grad_ref[...], preferred_element_type=F32).astype(BF16)
 
@@ -579,9 +595,7 @@
         return none
 
     lax.fori_loop(0, used, finish, 0)
-    dq_ref[...] = lax.dot_general(
-        matrix[...], dqs[...], flip, preferred_element_type=F32
-    ).astype(BF16)
+    dq_ref[...] = jnp.dot(back_matrix[...], dqs[...], preferred_element_type=F32).astype(BF16)
     gk_ref[...] = gk_acc[...].astype(BF16)
     gv_ref[...] = gv_acc[...].astype(BF16)
 
@@ -604,11 +618,11 @@
                 return lax.fori_loop(0, (kcnt[entry] + 63) // 64, step, none)
 
             lax.fori_loop(0, items, one_item, 0)
-            place = places(tab.ubase, tab.uspare, tab.uwidth, unit * HALF, HALF)
+            back = unsorter(tab.ubase, tab.uspare, tab.uwidth, unit * HALF, HALF, unit_size)
             source, half = unit_source(unit, me[0], units // 4)
             spot = (2 * source + half) * count
-            dn_ref[pl.ds(pl.multiple_of(spot, 16), count), :] = lax.dot_general(
-                sorter(place, unit_size), unit_rows[...], flip, preferred_element_type=F32
+            dn_ref[pl.ds(pl.multiple_of(spot, 16), count), :] = jnp.dot(
+                back, unit_rows[...], preferred_element_type=F32
             ).astype(BF16)
             return none
 
@@ -872,7 +886,7 @@
                 pltpu.VMEM((TOGETHER * cols, feats), F32),
                 pltpu.VMEM((8, TOGETHER * cols), F32),
                 pltpu.VMEM((8, TOGETHER * cols), F32),
-                pltpu.VMEM((query.shape[0], SLOTS * ROWW), BF16),
+                pltpu.VMEM((SLOTS * ROWW, query.shape[0]), BF16),
             ],
         ),
         out_shape=[
@@ -943,6 +957,7 @@
                 pltpu.VMEM((width, feats), F32),
                 pltpu.VMEM(ns.shape, BF16),
                 pltpu.VMEM((rows, grads.shape[0]), BF16),
+                pltpu.VMEM((grads.shape[0], rows), BF16),
                 pltpu.VMEM((rows, feats), BF16),
                 pltpu.VMEM((rows, feats), BF16),
                 pltpu.VMEM((unit_size, width), BF16),
@@ -1209,9 +1224,12 @@
     return gather.result()
 
 
-def over_groups(values, bit):
-    got = passed(values, "dp", lambda source: source ^ (1 << bit))
-    return (values.astype(F32) + got.astype(F32)).astype(BF16)
+def over_groups(values):
+    total = values.astype(F32)
+    for partner in range(1, lax.axis_size("dp")):
+        got = passed(values, "dp", lambda source, partner=partner: source ^ partner)
+        total = total + got.astype(F32)
+    return total.astype(BF16)
 
 
 def sum_over_chips(values, chip):
@@ -1439,7 +1457,7 @@
     chip_sums = ChipSums(
         jnp.concatenate([part.reshape(chips, -1, 256) for part in late], axis=1), chip
     )
-    for turn in range(1, chips):
+    for turn in range(1, chips - 1):
         chip_sums.step(turn)
     around = unpack(tab.around, group_mapped).reshape(3, SLOTS, ROWW, channels)
     merged = upsample_forward(around[0], around[1], around[2], all_masks).astype(BF16)
@@ -1447,6 +1465,7 @@
     normed_one_grad, fc2_all, *chip_sums.moving = tied(
         normed_one_grad, fc2_all, *chip_sums.moving
     )
+    chip_sums.step(chips - 1)
     gather = GroupGather(chip_sums.result(), dp_pos)
     normed_one_grad = normed_one_grad.astype(F32) + dot_t(query_low, query_weight)
 
@@ -1469,10 +1488,9 @@
     small_rows = -(-small.shape[1] // 1024) * 8
     small = jnp.pad(small, ((0, 0), (0, small_rows * 128 - small.shape[1])))
     small = small.reshape(cycle_size, small_rows, 128)
-    small = core_summed(small, core)
+    small = over_groups(core_summed(small, core))
     for bit in range(bits):
         gather.step(bit)
-        small = over_groups(small, bit)
     small = sum_over_chips(small, chip).reshape(-1)
     table_size = table_rows * rows
     norms = [small[table_size + index * rows :][:rows] for index in range(4)]

time: 597 us -> 585 us (0.980)
  starting transfers between devices: 54.7 us -> 67.2 us
  Pallas kernels: 216 us -> 208 us
  waiting for transfers between devices: 96.1 us -> 89.2 us
    ppermute x47 -> x48, starting transfers between devices: 54.5 us -> 67 us  [passed(): return lax.ppermute(value, axis, pairs)]
    ppermute x47 -> x48, waiting for transfers between devices: 87 us -> 75.6 us  [passed(): return lax.ppermute(value, axis, pairs)]
    pallas_call x1, Pallas kernels: 94.1 us -> 87.5 us  [attend_back(): pl.pallas_call(functools.partial(attend_back_kernel, heads, units, items,...]
  transfers between devices with their start and end apart: 52 -> 53, of which waited for: 22 -> 20; matrix products, arithmetic and copies ran while one was open for 17% -> 16% of each run, Pallas kernels for 31% -> 31%
where the time goes in v5:
time: 585 us; the launch traced here: 573 us
  Pallas kernels  208 us (36%)
  waiting for transfers between devices  89.2 us (15%)
  starting transfers between devices  67.2 us (11%)
  other arithmetic  51.4 us (9%)
  local copies, waits for them, and re-layouts  50.8 us (9%)
  matrix products  48.7 us (8%)
  blocking collectives  37.7 us (6%)
  between operations  21 us (4%)
    pallas_call x1, Pallas kernels, attend_back(): pl.pallas_call(functools.partial(attend_back_kernel, heads, units, items,...  87.5 us
    ppermute x48, waiting for transfers between devices, passed(): return lax.ppermute(value, axis, pairs)  75.6 us
    ppermute x48, starting transfers between devices, passed(): return lax.ppermute(value, axis, pairs)  67 us
    pallas_call x1, Pallas kernels, attend(): pl.pallas_call(functools.partial(attend_kernel, heads, units, items), gri...  59.4 us
    all_to_all x2, blocking collectives, exchanged(): return lax.all_to_all(values, 'blk', 0, 0).reshape(-1, channels)  37.7 us
    dot_general x5, matrix products, dot_t(): return lax.dot_general(left, right, NT, preferred_element_type=F32)  22.5 us
    pallas_call x1, Pallas kernels, merge(): pl.pallas_call(functools.partial(merge_kernel, cycle_size), grid_spec=plt...  20.8 us
    pallas_call x4, Pallas kernels, sort_step(): pl.pallas_call(functools.partial(sort_step_kernel, step), grid_spec=pltpu...  20.1 us
  transfers between devices with their start and end apart: 53, of which 20 were waited for; matrix products, arithmetic and copies ran while one was open for 16% of the time, Pallas kernels for 31%

profile of v5, /device:TPU:0, one launch (start us, length us, event | category | flops | bytes accessed | tf_op | source)
XLA Modules:
  0.0 573.4 jit_solution(4486468632883492450)
XLA Ops:
  9.0 4.7 collective-permute-start.1
  20.1 3.2 compare_select_fusion.3
  24.5 5.3 geometry.1
  29.8 5.5 own_start.1
  36.2 5.0 sort_step.4.refs_27_
  41.8 3.8 collective-permute-start.4
  46.5 5.1 sort_step.5.refs_28_
  51.5 3.4 collective-permute-done.3
  55.0 5.5 collective-permute-done.4
  62.0 3.9 collective-permute-start.9
  65.9 4.0 collective-permute-start.7
  69.9 2.4 collective-permute-done.9
  72.3 3.2 collective-permute-done.10
  75.7 5.0 sort_step.6.refs_29_
  80.7 7.2 %collective-permute-done.7 = bf16[240,768]{1,0:T(8,128)(2,1)} collective-permute-done((bf16[240,768]{1,0:T(8,128)(2,1)S(1)}, bf16[240,768]{1,0:T(8,128)(2,1)}, u32[]{:S(2)}, u32[]{:S(2)}) %collective-permute-start.7) | collective-permute-done | bytes 368672 | tf_op jit(solution)/shard_map/ppermute | solution.py:1012
  92.1 5.0 sort_step.7.refs_30_
  97.2 59.4 %attend.1 = (bf16[480,768]{1,0:T(8,128)(2,1)}, f32[704,768]{1,0:T(8,128)}, f32[16,768]{1,0:T(8,128)}, bf16[5120,768]{1,0:T(8,128)(2,1)}, bf16[5120,128]{1,0:T(8,...) custom-call(s32[80]{0:T(128)} %get-tuple-element.123.refs_0_, s32[80]{0:T(128)} %get-tuple-element.124.refs_1_, ...), custom_call_target="tpu_custom_call" | custom-call | flops 70000001024 | bytes 1000000 | tf_op jit(solution)/shard_map/attend/pallas_call | solution.py:869
  156.7 1.9 fusion.69
  159.4 4.9 fusion.53
  164.3 2.5 copy-done.75
  166.8 6.7 %add_convert_fusion.2.block_ref = bf16[480,768]{1,0:T(8,128)(2,1)} fusion(f32[480,768]{1,0:T(8,128)S(1)} %get-tuple-element.288, bf16[3072,768]{1,0:T(8,128)(2,1)} %param.35, f32[480,3072]{1,0:T(8,128)S(1)} %fusion.53), kind=kOutput, calls=%fused_computation.46 | convolution fusion | flops 2278932480 | bytes 12828672 | tf_op jit(solution)/shard_map/dot_general | solution.py:1139
  173.5 3.1 pack.1
  176.6 21.0 %all_to_all.10 = bf16[8,144,256]{2,1,0:T(8,128)(2,1)} all-to-all(bf16[8,144,256]{2,1,0:T(8,128)(2,1)} %bitcast.196), channel_id=1, replica_groups=mesh['dp'=4,'blk'=8] {'blk'}, dimensions={0} | all-to-all | bytes 1179648 | tf_op jit(solution)/shard_map/all_to_all | solution.py:1362
  197.6 20.8 %merge.1 = (bf16[768,256]{1,0:T(8,128)(2,1)}, bf16[576,256]{1,0:T(8,128)(2,1)}, bf16[9472,256]{1,0:T(8,128)(2,1)}) custom-call(s32[24]{0:T(128)} %get-tuple-element.130.refs_15_.wwidth, s32[24]{0:T(128)} %get-tuple-element.131.refs_16_.wup, s32[24]{0:T(128)} %get-tuple-element.132.refs_17_.wdown, s32[24]{0:T(128)} %get-tuple-element.133.refs_18_.wgroup, ...), custom_call_target="tpu_custom_call" | custom-call | flops 24999999488 | bytes 1000000 | tf_op jit(solution)/shard_map/merge/pallas_call | solution.py:825
  218.4 16.6 %all_to_all.11 = bf16[8,96,256]{2,1,0:T(8,128)(2,1)} all-to-all(bf16[8,96,256]{2,1,0:T(8,128)(2,1)} %bitcast.197), channel_id=1, replica_groups=mesh['dp'=4,'blk'=8] {'blk'}, dimensions={0} | all-to-all | bytes 786432 | tf_op jit(solution)/shard_map/all_to_all | solution.py:1362
  235.0 2.5 unpack.3
  237.5 2.5 fusion.70
  240.0 5.9 %convolution_convert_fusion.1 = bf16[3072,768]{1,0:T(8,128)(2,1)S(1)} fusion(bf16[480,768]{1,0:T(8,128)(2,1)S(1)} %get-tuple-element.167, f32[480,3072]{1,0:T(8,128)} %copy-done.75), kind=kOutput, calls=%fused_computation.12 | convolution fusion | flops 2280554496 | bytes 11354112 | tf_op jit(solution)/shard_map/dot_general | solution.py:1147
  245.9 2.5 copy.42
  248.5 3.4 dynamic-slice_bitcast_fusion
  253.1 10.7 %fusion.3 = bf16[480,3072]{1,0:T(8,128)(2,1)S(1)} fusion(f32[480,3072]{1,0:T(8,128)} %copy-done.75, bf16[480,768]{1,0:T(8,128)(2,1)S(1)} %get-tuple-element.167, bf16[3072,768]{1,0:T(8,128)(2,1)} %param.35), kind=kOutput, calls=%fused_computation.7 | convolution fusion | flops 2300313600 | bytes 14303232 | tf_op jit(solution)/shard_map/dot_general | solution.py:1143
  263.9 3.4 convolution_convert_fusion
  267.2 2.2 copy-done.19
  271.0 3.9 multiply_reduce_fusion
  275.7 2.0 fusion.55
  285.7 4.7 fusion.6
  290.4 3.5 fusion.7
  293.9 12.9 %reduce-scatter.4.cloned.1.call-done = bf16[768,768]{1,0:T(8,128)(2,1)} async-done(((bf16[3072,768]{1,0:T(8,128)(2,1)}), bf16[768,768]{1,0:T(8,128)(2,1)}) %reduce-scatter.4.cloned.1.call-update) | async-done | bytes 1179664 | tf_op jit(solution)/shard_map/reduce_scatter | solution.py:1397
  312.0 87.5 %attend_back.1 = (bf16[480,768]{1,0:T(8,128)(2,1)}, bf16[768,768]{1,0:T(8,128)(2,1)}, bf16[768,768]{1,0:T(8,128)(2,1)}, bf16[3840,768]{1,0:T(8,128)(2,1)}) custom-call(s32[1]{0:T(128)} %bitcast.1.place.me, s32[80]{0:T(128)} %get-tuple-element.123.refs_0_, s32[80]{0:T(128)} %get-tuple-element.124.refs_1_, s32[80]{0:T(128)} %get-tuple-element.125.refs_2_, ...), custom_call_target="tpu_custom_call" | custom-call | flops 89999998976 | bytes 1000000 | tf_op jit(solution)/shard_map/attend_back/pallas_call | solution.py:926
  401.6 3.2 unpack.2
  408.6 6.0 %collective-permute-start.18 = (bf16[1,1,48,768]{3,2,1,0:T(8,128)(2,1)S(1)}, bf16[1,1,48,768]{3,2,1,0:T(8,128)(2,1)S(1)}, u32[]{:S(2)}, u32[]{:S(2)}) collective-permute-start(bf16[1,1,48,768]{3,2,1,0:T(8,128)(2,1)S(1)} %get-tuple-element.261), channel_id=1, source_target_pairs={{0,8},{8,0},{16,24},{24,16},{1,9},{9,1},{17,25},{25,17},{2,10},{10... | collective-permute-start | bytes 221192 | tf_op jit(solution)/shard_map/ppermute | solution.py:1012
  415.9 2.0 collective-permute-start.26
  427.6 1.9 collective-permute-start.22
  429.8 1.9 collective-permute-start.19
  432.5 3.9 collective-permute-done.21
  437.4 9.7 %collective-permute-done.19 = bf16[1,2,48,768]{3,2,1,0:T(8,128)(2,1)} collective-permute-done((bf16[1,2,48,768]{3,2,1,0:T(8,128)(2,1)S(1)}, bf16[1,2,48,768]{3,2,1,0:T(8,128)(2,1)}, u32[]{:S(2)}, u32[]{:S(2)}) %collective-permute-start.19) | collective-permute-done | bytes 147488 | tf_op jit(solution)/shard_map/ppermute | solution.py:1012
  449.0 2.1 add_convert_fusion.6
  452.3 2.1 reshape.943
  456.2 2.0 fusion.8
  459.8 3.2 collective-permute-done.31
  464.6 9.6 %collective-permute-done.28 = bf16[4,96,768]{2,1,0:T(8,128)(2,1)S(1)} collective-permute-done((bf16[4,96,768]{2,1,0:T(8,128)(2,1)S(1)}, bf16[4,96,768]{2,1,0:T(8,128)(2,1)S(1)}, u32[]{:S(2)}, u32[]{:S(2)}) %collective-permute-start.28) | collective-permute-done | bytes 589856 | tf_op jit(solution)/shard_map/ppermute | solution.py:1012
  477.2 4.0 collective-permute-start.24
  486.2 5.9 %collective-permute-start.33 = (bf16[448,256]{1,0:T(8,128)(2,1)S(1)}, bf16[448,256]{1,0:T(8,128)(2,1)S(1)}, u32[]{:S(2)}, u32[]{:S(2)}) collective-permute-start(bf16[448,256]{1,0:T(8,128)(2,1)S(1)} %dynamic-slice_bitcast_fusion.3), channel_id=1, source_target_pairs={{0,6},{1,7},{2,0},{3,1},{4,2},{5,3},{6,4},{7,5},{8,14},{9,15},{10,... | collective-permute-start | bytes 688136 | tf_op jit(solution)/shard_map/ppermute | solution.py:1012
  493.2 5.2 collective-permute-done.33
  498.4 2.8 collective-permute-start.34
  502.6 3.0 collective-permute-done.34
  506.3 3.8 multiply_reduce_fusion.1
  510.2 3.0 fusion.54
  513.3 2.0 add_add_fusion.2
  524.0 3.5 collective-permute-start.42
  528.2 3.6 collective-permute-start.41
  533.5 4.3 collective-permute-done.39
  541.0 4.1 collective-permute-done.43
  549.2 6.3 %collective-permute-done.44 = bf16[2,1,448,256]{3,2,1,0:T(8,128)(2,1)S(1)} collective-permute-done((bf16[2,1,448,256]{3,2,1,0:T(8,128)(2,1)S(1)}, bf16[2,1,448,256]{3,2,1,0:T(8,128)(2,1)S(1)}, u32[]{:S(2)}, u32[]{:S(2)}) %collective-permute-start.44) | collective-permute-done | bytes 458784 | tf_op jit(solution)/shard_map/ppermute | solution.py:1012
  (391 shorter events, 96.4 us)
Async XLA Ops:
  7.2 149.5 %copy-start = (bf16[768,768]{1,0:T(8,128)(2,1)S(1)}, bf16[768,768]{1,0:T(8,128)(2,1)}, u32[]{:S(2)}) copy-start(bf16[768,768]{1,0:T(8,128)(2,1)} %param.31) | copy-start | bytes 3538948
  7.2 16.7 %copy-start.60 = (f32[768]{0:T(1024)S(1)}, f32[768]{0:T(1024)}, u32[]{:S(2)}) copy-start(f32[768]{0:T(1024)} %param.26) | copy-start | bytes 9220
  7.3 149.4 %all-gather.3.cloned.1.call-start = ((), (), s32[]{:S(2)}) async-start(), calls=%async_computation.5 | async-start | bytes 2654208 | tf_op jit(solution)/shard_map/all_gather | solution.py:1344
  7.3 28.0 %collective-permute-start.2 = (bf16[480,768]{1,0:T(8,128)(2,1)}, bf16[480,768]{1,0:T(8,128)(2,1)S(1)}, u32[]{:S(2)}, u32[]{:S(2)}) collective-permute-start(bf16[480,768]{1,0:T(8,128)(2,1)} %refs_0_.2), channel_id=1, source_target_pairs={{0,1},{1,0},{2,3},{3,2},{4,5},{5,4},{6,7},{7,6},{8,9},{9,8},{10,11... | collective-permute-start | bytes 2211848 | tf_op jit(solution)/shard_map/ppermute | solution.py:1012
  9.0 32.2 %collective-permute-start.1 = (bf16[240,768]{1,0:T(8,128)(2,1)S(1)}, bf16[240,768]{1,0:T(8,128)(2,1)S(1)}, u32[]{:S(2)}, u32[]{:S(2)}) collective-permute-start(bf16[240,768]{1,0:T(8,128)(2,1)S(1)} %get-tuple-element.247), channel_id=1, source_target_pairs={{0,6},{1,7},{2,0},{3,1},{4,2},{5,3},{6,4},{7,5},{8,14},{9,15},{10,... | collective-permute-start | bytes 1105928 | tf_op jit(solution)/shard_map/ppermute | solution.py:1012
  13.6 27.6 %collective-permute-start = (bf16[240,768]{1,0:T(8,128)(2,1)S(1)}, bf16[240,768]{1,0:T(8,128)(2,1)S(1)}, u32[]{:S(2)}, u32[]{:S(2)}) collective-permute-start(bf16[240,768]{1,0:T(8,128)(2,1)S(1)} %get-tuple-element.248), channel_id=1, source_target_pairs={{0,2},{1,3},{2,4},{3,5},{4,6},{5,7},{6,0},{7,1},{8,10},{9,11},{10,... | collective-permute-start | bytes 1105928 | tf_op jit(solution)/shard_map/ppermute | solution.py:1012
  23.3 18.3 %copy-start.64 = (s32[12]{0:T(128)}, s32[12]{0:T(128)S(1)}, u32[]{:S(2)}) copy-start(s32[12]{0:T(128)S(1)} %select_select_fusion.1) | copy-start | bytes 148
  41.3 5.2 collective-permute-start.5
  41.7 47.3 %copy-start.52 = (pred[12,40]{1,0:T(8,128)(4,1)}, pred[12,40]{1,0:T(8,128)(4,1)S(1)}, u32[]{:S(2)}) copy-start(pred[12,40]{1,0:T(8,128)(4,1)S(1)} %get-tuple-element.275) | copy-start | bytes 1444
  41.7 47.3 %copy-start.54 = (pred[12,40]{1,0:T(8,128)(4,1)}, pred[12,40]{1,0:T(8,128)(4,1)S(1)}, u32[]{:S(2)}) copy-start(pred[12,40]{1,0:T(8,128)(4,1)S(1)} %get-tuple-element.276) | copy-start | bytes 1444
  41.7 13.3 %collective-permute-start.3 = (bf16[240,768]{1,0:T(8,128)(2,1)S(1)}, bf16[240,768]{1,0:T(8,128)(2,1)S(1)}, u32[]{:S(2)}, u32[]{:S(2)}) collective-permute-start(bf16[240,768]{1,0:T(8,128)(2,1)S(1)} %collective-permute-done), channel_id=1, source_target_pairs={{0,2},{1,3},{2,4},{3,5},{4,6},{5,7},{6,0},{7,1},{8,10},{9,11},{10,... | collective-permute-start | bytes 1105928 | tf_op jit(solution)/shard_map/ppermute | solution.py:1012
  41.8 18.7 %collective-permute-start.4 = (bf16[240,768]{1,0:T(8,128)(2,1)S(1)}, bf16[240,768]{1,0:T(8,128)(2,1)S(1)}, u32[]{:S(2)}, u32[]{:S(2)}) collective-permute-start(bf16[240,768]{1,0:T(8,128)(2,1)S(1)} %collective-permute-done.1), channel_id=1, source_target_pairs={{0,6},{1,7},{2,0},{3,1},{4,2},{5,3},{6,4},{7,5},{8,14},{9,15},{10,... | collective-permute-start | bytes 1105928 | tf_op jit(solution)/shard_map/ppermute | solution.py:1012
  62.0 13.6 %collective-permute-start.8 = (bf16[480,768]{1,0:T(8,128)(2,1)}, bf16[480,768]{1,0:T(8,128)(2,1)}, u32[]{:S(2)}, u32[]{:S(2)}) collective-permute-start(bf16[480,768]{1,0:T(8,128)(2,1)} %constant_dynamic-update-slice_fusion.2.refs_0_), channel_id=1, source_target_pairs={{0,1},{1,0},{2,3},{3,2},{4,5},{5,4},{6,7},{7,6},{8,9},{9,8},{10,11... | collective-permute-start | bytes 2211848 | tf_op jit(solution)/shard_map/ppermute | solution.py:1012
  62.0 10.3 %collective-permute-start.9 = (bf16[12,40,256]{2,1,0:T(8,128)(2,1)S(1)}, bf16[12,40,256]{2,1,0:T(8,128)(2,1)S(1)}, u32[]{:S(2)}, u32[]{:S(2)}) collective-permute-start(bf16[12,40,256]{2,1,0:T(8,128)(2,1)S(1)} %get-tuple-element.154), channel_id=1, source_target_pairs={{0,7},{1,0},{2,1},{3,2},{4,3},{5,4},{6,5},{7,6},{8,15},{9,8},{10,9... | collective-permute-start | bytes 737288 | tf_op jit(solution)/shard_map/ppermute | solution.py:1012
  65.9 9.7 %collective-permute-start.10 = (bf16[12,40,256]{2,1,0:T(8,128)(2,1)S(1)}, bf16[12,40,256]{2,1,0:T(8,128)(2,1)S(1)}, u32[]{:S(2)}, u32[]{:S(2)}) collective-permute-start(bf16[12,40,256]{2,1,0:T(8,128)(2,1)S(1)} %get-tuple-element.155), channel_id=1, source_target_pairs={{0,1},{1,2},{2,3},{3,4},{4,5},{5,6},{6,7},{7,0},{8,9},{9,10},{10,1... | collective-permute-start | bytes 737288 | tf_op jit(solution)/shard_map/ppermute | solution.py:1012
  65.9 14.7 %collective-permute-start.6 = (bf16[240,768]{1,0:T(8,128)(2,1)S(1)}, bf16[240,768]{1,0:T(8,128)(2,1)S(1)}, u32[]{:S(2)}, u32[]{:S(2)}) collective-permute-start(bf16[240,768]{1,0:T(8,128)(2,1)S(1)} %collective-permute-done.3), channel_id=1, source_target_pairs={{0,2},{1,3},{2,4},{3,5},{4,6},{5,7},{6,0},{7,1},{8,10},{9,11},{10,... | collective-permute-start | bytes 1105928 | tf_op jit(solution)/shard_map/ppermute | solution.py:1012
  65.9 22.0 %collective-permute-start.7 = (bf16[240,768]{1,0:T(8,128)(2,1)S(1)}, bf16[240,768]{1,0:T(8,128)(2,1)}, u32[]{:S(2)}, u32[]{:S(2)}) collective-permute-start(bf16[240,768]{1,0:T(8,128)(2,1)S(1)} %collective-permute-done.4), channel_id=1, source_target_pairs={{0,6},{1,7},{2,0},{3,1},{4,2},{5,3},{6,4},{7,5},{8,14},{9,15},{10,... | collective-permute-start | bytes 1105928 | tf_op jit(solution)/shard_map/ppermute | solution.py:1012
  88.9 2.3 collective-permute-start.11
  97.1 209.7 %reduce-scatter.4.cloned.1.call-start = ((), (), s32[]{:S(2)}) async-start(), calls=%async_computation.7 | async-start | bytes 5898240 | tf_op jit(solution)/shard_map/reduce_scatter | solution.py:1397
  97.2 59.5 %copy-start.2 = (f32[480,768]{1,0:T(8,128)S(1)}, f32[480,768]{1,0:T(8,128)}, u32[]{:S(2)}) copy-start(f32[480,768]{1,0:T(8,128)} %get-tuple-element.122) | copy-start | bytes 4423684
  248.4 151.2 %reduce-scatter.6.cloned.1.call-start = ((), (), s32[]{:S(2)}) async-start(), calls=%async_computation.8 | async-start | bytes 1327104 | tf_op jit(solution)/shard_map/reduce_scatter | solution.py:1432
  248.5 22.5 %slice-start = ((s8[4718592]{0:T(1024)(128)(4,1)}), s8[4194304]{0:T(1024)(128)(4,1)S(1)}, s32[]{:S(2)}) async-start(s8[4718592]{0:T(1024)(128)(4,1)} %bitcast.210), calls=%async_computation.10 | async-start | bytes 8388608
  251.9 33.8 %collective-permute-start.12 = (bf16[4,1184,256]{2,1,0:T(8,128)(2,1)}, bf16[4,1184,256]{2,1,0:T(8,128)(2,1)}, u32[]{:S(2)}, u32[]{:S(2)}) collective-permute-start(bf16[4,1184,256]{2,1,0:T(8,128)(2,1)} %dynamic-slice_bitcast_fusion), channel_id=1, source_target_pairs={{0,1},{1,0},{2,3},{3,2},{4,5},{5,4},{6,7},{7,6},{8,9},{9,8},{10,11... | collective-permute-start | bytes 7274504 | tf_op jit(solution)/shard_map/ppermute | solution.py:1012
  253.1 17.8 %slice-start.1 = ((s8[4718592]{0:T(1024)(128)(4,1)}), s8[524288]{0:T(1024)(128)(4,1)S(1)}, s32[]{:S(2)}) async-start(s8[4718592]{0:T(1024)(128)(4,1)} %bitcast.210), calls=%async_computation.11 | async-start | bytes 1048576
  275.1 15.3 %collective-permute-start.13 = (bf16[4,96,3072]{2,1,0:T(8,128)(2,1)}, bf16[4,96,3072]{2,1,0:T(8,128)(2,1)}, u32[]{:S(2)}, u32[]{:S(2)}) collective-permute-start(bf16[4,96,3072]{2,1,0:T(8,128)(2,1)} %dynamic-slice_bitcast_fusion.1), channel_id=1, source_target_pairs={{0,1},{1,0},{2,3},{3,2},{4,5},{5,4},{6,7},{7,6},{8,9},{9,8},{10,11... | collective-permute-start | bytes 7077896 | tf_op jit(solution)/shard_map/ppermute | solution.py:1012
  281.7 2.6 collective-permute-start.14
  285.7 21.8 %copy-start.26 = (bf16[4,128,768]{2,1,0:T(8,128)(2,1)}, bf16[4,128,768]{2,1,0:T(8,128)(2,1)S(1)}, u32[]{:S(2)}) copy-start(bf16[4,128,768]{2,1,0:T(8,128)(2,1)S(1)} %fusion.9) | copy-start | bytes 2359300
  306.9 94.7 %all-gather.5.cloned.1.call-start = ((), (), s32[]{:S(2)}) async-start(), calls=%async_computation.6 | async-start | bytes 2654208 | tf_op jit(solution)/shard_map/all_gather | solution.py:1373
  307.5 198.9 %reduce-scatter.8.cloned.1.call-start = ((), (), s32[]{:S(2)}) async-start(), calls=%async_computation.9 | async-start | bytes 6635520 | tf_op jit(solution)/shard_map/reduce_scatter | solution.py:1440
  308.3 91.2 %collective-permute-start.17 = (bf16[4,64,768]{2,1,0:T(8,128)(2,1)}, bf16[4,64,768]{2,1,0:T(8,128)(2,1)}, u32[]{:S(2)}, u32[]{:S(2)}) collective-permute-start(bf16[4,64,768]{2,1,0:T(8,128)(2,1)} %constant_dynamic-slice_fusion.11), channel_id=1, source_target_pairs={{0,8},{8,0},{16,24},{24,16},{1,9},{9,1},{17,25},{25,17},{2,10},{10... | collective-permute-start | bytes 1179656 | tf_op jit(solution)/shard_map/ppermute | solution.py:1012
  309.8 89.8 %collective-permute-start.16 = (bf16[4,48,3072]{2,1,0:T(8,128)(2,1)S(1)}, bf16[4,48,3072]{2,1,0:T(8,128)(2,1)}, u32[]{:S(2)}, u32[]{:S(2)}) collective-permute-start(bf16[4,48,3072]{2,1,0:T(8,128)(2,1)S(1)} %constant_dynamic-slice_fusion.12), channel_id=1, source_target_pairs={{0,16},{8,24},{16,0},{24,8},{1,17},{9,25},{17,1},{25,9},{2,18},{10... | collective-permute-start | bytes 3538952 | tf_op jit(solution)/shard_map/ppermute | solution.py:1012
  310.6 89.0 %collective-permute-start.15 = (bf16[4,592,256]{2,1,0:T(8,128)(2,1)S(1)}, bf16[4,592,256]{2,1,0:T(8,128)(2,1)}, u32[]{:S(2)}, u32[]{:S(2)}) collective-permute-start(bf16[4,592,256]{2,1,0:T(8,128)(2,1)S(1)} %constant_dynamic-slice_fusion.13), channel_id=1, source_target_pairs={{0,8},{8,0},{16,24},{24,16},{1,9},{9,1},{17,25},{25,17},{2,10},{10... | collective-permute-start | bytes 3637256 | tf_op jit(solution)/shard_map/ppermute | solution.py:1012
  408.6 20.9 %collective-permute-start.18 = (bf16[1,1,48,768]{3,2,1,0:T(8,128)(2,1)S(1)}, bf16[1,1,48,768]{3,2,1,0:T(8,128)(2,1)S(1)}, u32[]{:S(2)}, u32[]{:S(2)}) collective-permute-start(bf16[1,1,48,768]{3,2,1,0:T(8,128)(2,1)S(1)} %get-tuple-element.261), channel_id=1, source_target_pairs={{0,8},{8,0},{16,24},{24,16},{1,9},{9,1},{17,25},{25,17},{2,10},{10... | collective-permute-start | bytes 221192 | tf_op jit(solution)/shard_map/ppermute | solution.py:1012
  414.7 13.0 %collective-permute-start.20 = (bf16[1,1,48,768]{3,2,1,0:T(8,128)(2,1)S(1)}, bf16[1,1,48,768]{3,2,1,0:T(8,128)(2,1)S(1)}, u32[]{:S(2)}, u32[]{:S(2)}) collective-permute-start(bf16[1,1,48,768]{3,2,1,0:T(8,128)(2,1)S(1)} %get-tuple-element.262), channel_id=1, source_target_pairs={{0,16},{8,24},{16,0},{24,8},{1,17},{9,25},{17,1},{25,9},{2,18},{10... | collective-permute-start | bytes 221192 | tf_op jit(solution)/shard_map/ppermute | solution.py:1012
  415.9 13.8 %collective-permute-start.26 = (bf16[4,32,768]{2,1,0:T(8,128)(2,1)S(1)}, bf16[4,32,768]{2,1,0:T(8,128)(2,1)S(1)}, u32[]{:S(2)}, u32[]{:S(2)}) collective-permute-start(bf16[4,32,768]{2,1,0:T(8,128)(2,1)S(1)} %constant_dynamic-slice_fusion.8), channel_id=1, source_target_pairs={{0,16},{8,24},{16,0},{24,8},{1,17},{9,25},{17,1},{25,9},{2,18},{10... | collective-permute-start | bytes 589832 | tf_op jit(solution)/shard_map/ppermute | solution.py:1012
  419.7 29.3 %collective-permute-start.23 = (bf16[4,24,3072]{2,1,0:T(8,128)(2,1)S(1)}, bf16[4,24,3072]{2,1,0:T(8,128)(2,1)}, u32[]{:S(2)}, u32[]{:S(2)}) collective-permute-start(bf16[4,24,3072]{2,1,0:T(8,128)(2,1)S(1)} %constant_dynamic-slice_fusion.9), channel_id=1, source_target_pairs={{0,8},{8,0},{16,24},{24,16},{1,9},{9,1},{17,25},{25,17},{2,10},{10... | collective-permute-start | bytes 1769480 | tf_op jit(solution)/shard_map/ppermute | solution.py:1012
  421.6 29.4 %collective-permute-start.30 = (bf16[4,96,768]{2,1,0:T(8,128)(2,1)}, bf16[4,96,768]{2,1,0:T(8,128)(2,1)}, u32[]{:S(2)}, u32[]{:S(2)}) collective-permute-start(bf16[4,96,768]{2,1,0:T(8,128)(2,1)} %dynamic-slice_bitcast_fusion.2), channel_id=1, source_target_pairs={{0,1},{1,0},{2,3},{3,2},{4,5},{5,4},{6,7},{7,6},{8,9},{9,8},{10,11... | collective-permute-start | bytes 1769480 | tf_op jit(solution)/shard_map/ppermute | solution.py:1012
  427.6 30.9 %collective-permute-start.22 = (bf16[4,296,256]{2,1,0:T(8,128)(2,1)}, bf16[4,296,256]{2,1,0:T(8,128)(2,1)}, u32[]{:S(2)}, u32[]{:S(2)}) collective-permute-start(bf16[4,296,256]{2,1,0:T(8,128)(2,1)} %constant_dynamic-slice_fusion.10), channel_id=1, source_target_pairs={{0,16},{8,24},{16,0},{24,8},{1,17},{9,25},{17,1},{25,9},{2,18},{10... | collective-permute-start | bytes 1818632 | tf_op jit(solution)/shard_map/ppermute | solution.py:1012
  429.6 6.8 %collective-permute-start.21 = (bf16[2,1,48,768]{3,2,1,0:T(8,128)(2,1)S(1)}, bf16[2,1,48,768]{3,2,1,0:T(8,128)(2,1)}, u32[]{:S(2)}, u32[]{:S(2)}) collective-permute-start(bf16[2,1,48,768]{3,2,1,0:T(8,128)(2,1)S(1)} %maximum_select_fusion.7), channel_id=1, source_target_pairs={{0,8},{8,0},{16,24},{24,16},{1,9},{9,1},{17,25},{25,17},{2,10},{10... | collective-permute-start | bytes 442376 | tf_op jit(solution)/shard_map/ppermute | solution.py:1012
  429.8 17.3 %collective-permute-start.19 = (bf16[1,2,48,768]{3,2,1,0:T(8,128)(2,1)S(1)}, bf16[1,2,48,768]{3,2,1,0:T(8,128)(2,1)}, u32[]{:S(2)}, u32[]{:S(2)}) collective-permute-start(bf16[1,2,48,768]{3,2,1,0:T(8,128)(2,1)S(1)} %maximum_select_fusion.6), channel_id=1, source_target_pairs={{0,16},{8,24},{16,0},{24,8},{1,17},{9,25},{17,1},{25,9},{2,18},{10... | collective-permute-start | bytes 442376 | tf_op jit(solution)/shard_map/ppermute | solution.py:1012
  432.5 16.5 %copy-start.23 = (bf16[4,48,3072]{2,1,0:T(8,128)(2,1)S(1)}, bf16[4,48,3072]{2,1,0:T(8,128)(2,1)}, u32[]{:S(2)}) copy-start(bf16[4,48,3072]{2,1,0:T(8,128)(2,1)} %copy-done.22) | copy-start | bytes 3538948
  436.4 19.8 %collective-permute-start.27 = (bf16[4,192,768]{2,1,0:T(8,128)(2,1)}, bf16[4,192,768]{2,1,0:T(8,128)(2,1)}, u32[]{:S(2)}, u32[]{:S(2)}) collective-permute-start(bf16[4,192,768]{2,1,0:T(8,128)(2,1)} %fusion.11), channel_id=1, source_target_pairs={{0,1},{1,0},{2,3},{3,2},{4,5},{5,4},{6,7},{7,6},{8,9},{9,8},{10,11... | collective-permute-start | bytes 3538952 | tf_op jit(solution)/shard_map/ppermute | solution.py:1012
  454.4 8.6 %collective-permute-start.31 = (bf16[4,48,768]{2,1,0:T(8,128)(2,1)S(1)}, bf16[4,48,768]{2,1,0:T(8,128)(2,1)S(1)}, u32[]{:S(2)}, u32[]{:S(2)}) collective-permute-start(bf16[4,48,768]{2,1,0:T(8,128)(2,1)S(1)} %constant_dynamic-slice_fusion.5), channel_id=1, source_target_pairs={{0,16},{8,24},{16,0},{24,8},{1,17},{9,25},{17,1},{25,9},{2,18},{10... | collective-permute-start | bytes 884744 | tf_op jit(solution)/shard_map/ppermute | solution.py:1012
  458.3 16.0 %collective-permute-start.28 = (bf16[4,96,768]{2,1,0:T(8,128)(2,1)S(1)}, bf16[4,96,768]{2,1,0:T(8,128)(2,1)S(1)}, u32[]{:S(2)}, u32[]{:S(2)}) collective-permute-start(bf16[4,96,768]{2,1,0:T(8,128)(2,1)S(1)} %constant_dynamic-slice_fusion.7), channel_id=1, source_target_pairs={{0,8},{8,0},{16,24},{24,16},{1,9},{9,1},{17,25},{25,17},{2,10},{10... | collective-permute-start | bytes 1769480 | tf_op jit(solution)/shard_map/ppermute | solution.py:1012
  463.1 18.2 %collective-permute-start.32 = (bf16[4,24,768]{2,1,0:T(8,128)(2,1)S(1)}, bf16[4,24,768]{2,1,0:T(8,128)(2,1)S(1)}, u32[]{:S(2)}, u32[]{:S(2)}) collective-permute-start(bf16[4,24,768]{2,1,0:T(8,128)(2,1)S(1)} %constant_dynamic-slice_fusion.4), channel_id=1, source_target_pairs={{0,8},{8,0},{16,24},{24,16},{1,9},{9,1},{17,25},{25,17},{2,10},{10... | collective-permute-start | bytes 442376 | tf_op jit(solution)/shard_map/ppermute | solution.py:1012
  476.0 7.0 %collective-permute-start.29 = (bf16[4,48,768]{2,1,0:T(8,128)(2,1)}, bf16[4,48,768]{2,1,0:T(8,128)(2,1)}, u32[]{:S(2)}, u32[]{:S(2)}) collective-permute-start(bf16[4,48,768]{2,1,0:T(8,128)(2,1)} %constant_dynamic-slice_fusion.6), channel_id=1, source_target_pairs={{0,16},{8,24},{16,0},{24,8},{1,17},{9,25},{17,1},{25,9},{2,18},{10... | collective-permute-start | bytes 884744 | tf_op jit(solution)/shard_map/ppermute | solution.py:1012
  477.2 14.9 %collective-permute-start.24 = (bf16[448,256]{1,0:T(8,128)(2,1)}, bf16[448,256]{1,0:T(8,128)(2,1)}, u32[]{:S(2)}, u32[]{:S(2)}) collective-permute-start(bf16[448,256]{1,0:T(8,128)(2,1)} %fusion.32), channel_id=1, source_target_pairs={{0,2},{1,3},{2,4},{3,5},{4,6},{5,7},{6,0},{7,1},{8,10},{9,11},{10,... | collective-permute-start | bytes 688136 | tf_op jit(solution)/shard_map/ppermute | solution.py:1012
  486.1 19.4 %copy-start.25 = (bf16[4,448,256]{2,1,0:T(8,128)(2,1)}, bf16[4,448,256]{2,1,0:T(8,128)(2,1)S(1)}, u32[]{:S(2)}) copy-start(bf16[4,448,256]{2,1,0:T(8,128)(2,1)S(1)} %pad_maximum_fusion.1) | copy-start | bytes 2752516
  486.2 12.2 %collective-permute-start.33 = (bf16[448,256]{1,0:T(8,128)(2,1)S(1)}, bf16[448,256]{1,0:T(8,128)(2,1)S(1)}, u32[]{:S(2)}, u32[]{:S(2)}) collective-permute-start(bf16[448,256]{1,0:T(8,128)(2,1)S(1)} %dynamic-slice_bitcast_fusion.3), channel_id=1, source_target_pairs={{0,6},{1,7},{2,0},{3,1},{4,2},{5,3},{6,4},{7,5},{8,14},{9,15},{10,... | collective-permute-start | bytes 688136 | tf_op jit(solution)/shard_map/ppermute | solution.py:1012
  493.1 9.4 %collective-permute-start.25 = (bf16[448,256]{1,0:T(8,128)(2,1)S(1)}, bf16[448,256]{1,0:T(8,128)(2,1)S(1)}, u32[]{:S(2)}, u32[]{:S(2)}) collective-permute-start(bf16[448,256]{1,0:T(8,128)(2,1)S(1)} %fusion.24), channel_id=1, source_target_pairs={{0,2},{1,3},{2,4},{3,5},{4,6},{5,7},{6,0},{7,1},{8,10},{9,11},{10,... | collective-permute-start | bytes 688136 | tf_op jit(solution)/shard_map/ppermute | solution.py:1012
  498.4 7.1 %collective-permute-start.34 = (bf16[448,256]{1,0:T(8,128)(2,1)S(1)}, bf16[448,256]{1,0:T(8,128)(2,1)S(1)}, u32[]{:S(2)}, u32[]{:S(2)}) collective-permute-start(bf16[448,256]{1,0:T(8,128)(2,1)S(1)} %fusion.22), channel_id=1, source_target_pairs={{0,6},{1,7},{2,0},{3,1},{4,2},{5,3},{6,4},{7,5},{8,14},{9,15},{10,... | collective-permute-start | bytes 688136 | tf_op jit(solution)/shard_map/ppermute | solution.py:1012
  517.4 2.0 collective-permute-start.35
  519.4 8.1 %collective-permute-start.38 = (bf16[4,16,128]{2,1,0:T(8,128)(2,1)S(1)}, bf16[4,16,128]{2,1,0:T(8,128)(2,1)S(1)}, u32[]{:S(2)}, u32[]{:S(2)}) collective-permute-start(bf16[4,16,128]{2,1,0:T(8,128)(2,1)S(1)} %fusion.37), channel_id=1, source_target_pairs={{0,24},{8,16},{16,8},{24,0},{1,25},{9,17},{17,9},{25,1},{2,26},{10... | collective-permute-start | bytes 49160 | tf_op jit(solution)/shard_map/ppermute | solution.py:1012
  521.0 6.6 %collective-permute-start.37 = (bf16[4,16,128]{2,1,0:T(8,128)(2,1)S(1)}, bf16[4,16,128]{2,1,0:T(8,128)(2,1)S(1)}, u32[]{:S(2)}, u32[]{:S(2)}) collective-permute-start(bf16[4,16,128]{2,1,0:T(8,128)(2,1)S(1)} %fusion.37), channel_id=1, source_target_pairs={{0,16},{8,24},{16,0},{24,8},{1,17},{9,25},{17,1},{25,9},{2,18},{10... | collective-permute-start | bytes 49160 | tf_op jit(solution)/shard_map/ppermute | solution.py:1012
  522.2 5.3 collective-permute-start.36
  524.0 13.8 %collective-permute-start.42 = (bf16[448,256]{1,0:T(8,128)(2,1)S(1)}, bf16[448,256]{1,0:T(8,128)(2,1)S(1)}, u32[]{:S(2)}, u32[]{:S(2)}) collective-permute-start(bf16[448,256]{1,0:T(8,128)(2,1)S(1)} %copy-done.42), channel_id=1, source_target_pairs={{0,6},{1,7},{2,0},{3,1},{4,2},{5,3},{6,4},{7,5},{8,14},{9,15},{10,... | collective-permute-start | bytes 688136 | tf_op jit(solution)/shard_map/ppermute | solution.py:1012
  527.5 11.7 %collective-permute-start.45 = (bf16[448,256]{1,0:T(8,128)(2,1)S(1)}, bf16[448,256]{1,0:T(8,128)(2,1)S(1)}, u32[]{:S(2)}, u32[]{:S(2)}) collective-permute-start(bf16[448,256]{1,0:T(8,128)(2,1)S(1)} %fusion.23), channel_id=1, source_target_pairs={{0,2},{1,3},{2,4},{3,5},{4,6},{5,7},{6,0},{7,1},{8,10},{9,11},{10,... | collective-permute-start | bytes 688136 | tf_op jit(solution)/shard_map/ppermute | solution.py:1012
  527.6 10.2 %collective-permute-start.39 = (bf16[16,128]{1,0:T(8,128)(2,1)S(1)}, bf16[16,128]{1,0:T(8,128)(2,1)S(1)}, u32[]{:S(2)}, u32[]{:S(2)}) collective-permute-start(bf16[16,128]{1,0:T(8,128)(2,1)S(1)} %get-tuple-element.263), channel_id=1, source_target_pairs={{0,2},{1,3},{2,4},{3,5},{4,6},{5,7},{6,0},{7,1},{8,10},{9,11},{10,... | collective-permute-start | bytes 12296 | tf_op jit(solution)/shard_map/ppermute | solution.py:1012
  528.2 9.6 %collective-permute-start.41 = (bf16[16,128]{1,0:T(8,128)(2,1)S(1)}, bf16[16,128]{1,0:T(8,128)(2,1)S(1)}, u32[]{:S(2)}, u32[]{:S(2)}) collective-permute-start(bf16[16,128]{1,0:T(8,128)(2,1)S(1)} %get-tuple-element.264), channel_id=1, source_target_pairs={{0,6},{1,7},{2,0},{3,1},{4,2},{5,3},{6,4},{7,5},{8,14},{9,15},{10,... | collective-permute-start | bytes 12296 | tf_op jit(solution)/shard_map/ppermute | solution.py:1012
  531.8 6.0 %collective-permute-start.40 = (bf16[16,128]{1,0:T(8,128)(2,1)S(1)}, bf16[16,128]{1,0:T(8,128)(2,1)S(1)}, u32[]{:S(2)}, u32[]{:S(2)}) collective-permute-start(bf16[16,128]{1,0:T(8,128)(2,1)S(1)} %get-tuple-element.265), channel_id=1, source_target_pairs={{0,4},{1,5},{2,6},{3,7},{4,0},{5,1},{6,2},{7,3},{8,12},{9,13},{10,... | collective-permute-start | bytes 12296 | tf_op jit(solution)/shard_map/ppermute | solution.py:1012
  538.8 6.3 %collective-permute-start.43 = (bf16[1,1,448,256]{3,2,1,0:T(8,128)(2,1)S(1)}, bf16[1,1,448,256]{3,2,1,0:T(8,128)(2,1)S(1)}, u32[]{:S(2)}, u32[]{:S(2)}) collective-permute-start(bf16[1,1,448,256]{3,2,1,0:T(8,128)(2,1)S(1)} %fusion.27), channel_id=1, source_target_pairs={{0,16},{8,24},{16,0},{24,8},{1,17},{9,25},{17,1},{25,9},{2,18},{10... | collective-permute-start | bytes 688136 | tf_op jit(solution)/shard_map/ppermute | solution.py:1012
  539.3 8.7 %collective-permute-start.46 = (bf16[1,1,448,256]{3,2,1,0:T(8,128)(2,1)S(1)}, bf16[1,1,448,256]{3,2,1,0:T(8,128)(2,1)S(1)}, u32[]{:S(2)}, u32[]{:S(2)}) collective-permute-start(bf16[1,1,448,256]{3,2,1,0:T(8,128)(2,1)S(1)} %fusion.28), channel_id=1, source_target_pairs={{0,8},{8,0},{16,24},{24,16},{1,9},{9,1},{17,25},{25,17},{2,10},{10... | collective-permute-start | bytes 688136 | tf_op jit(solution)/shard_map/ppermute | solution.py:1012
  545.2 10.3 %collective-permute-start.44 = (bf16[2,1,448,256]{3,2,1,0:T(8,128)(2,1)S(1)}, bf16[2,1,448,256]{3,2,1,0:T(8,128)(2,1)S(1)}, u32[]{:S(2)}, u32[]{:S(2)}) collective-permute-start(bf16[2,1,448,256]{3,2,1,0:T(8,128)(2,1)S(1)} %maximum_select_fusion.2), channel_id=1, source_target_pairs={{0,8},{8,0},{16,24},{24,16},{1,9},{9,1},{17,25},{25,17},{2,10},{10... | collective-permute-start | bytes 1376264 | tf_op jit(solution)/shard_map/ppermute | solution.py:1012
  548.0 9.4 %collective-permute-start.47 = (bf16[1,2,448,256]{3,2,1,0:T(8,128)(2,1)S(1)}, bf16[1,2,448,256]{3,2,1,0:T(8,128)(2,1)S(1)}, u32[]{:S(2)}, u32[]{:S(2)}) collective-permute-start(bf16[1,2,448,256]{3,2,1,0:T(8,128)(2,1)S(1)} %maximum_select_fusion.3), channel_id=1, source_target_pairs={{0,16},{8,24},{16,0},{24,8},{1,17},{9,25},{17,1},{25,9},{2,18},{10... | collective-permute-start | bytes 1376264 | tf_op jit(solution)/shard_map/ppermute | solution.py:1012
  (67 other events, 234.5 us)
Sparse Core Ops, SparseCore 0:
  97.2 32.1 all-gather.2
  248.5 58.2 reduce-scatter.3
  309.2 32.7 reduce-scatter.5
  344.0 29.9 all-gather.4
  399.8 73.1 reduce-scatter.7
